TPU v7x, 512 devices: a whole 4x4x16 slice. The times are simulated.
512 devices in a mesh: pairs: 64 (over x, z), tensor: 8 (over y, core).
Axes of the slice: x: 4, y: 4, z: 16, core: 2. Of those that a mesh axis runs over, the one named last changes fastest.
Arguments:
- tokens: bfloat16 [8192, 4096], P('pairs', 'tensor'), may hold values from -6 to 6
- norm_gain: bfloat16 [4096], replicated, may hold values from 0.099609375 to 1.8984375
- wq: bfloat16 [4096, 4096], P('pairs', 'tensor'), may hold values from -0.09375 to 0.09375
- wk: bfloat16 [4096, 1024], P('pairs', 'tensor'), may hold values from -0.09375 to 0.09375
- wv: bfloat16 [4096, 1024], P('pairs', 'tensor'), may hold values from -0.09375 to 0.09375
- doc_cache: bfloat16 [128, 128, 2048], P('pairs', None, 'tensor'), may hold values from -140 to 140
- doc_lists: int32 [64, 16], replicated, may hold values from 0 to 127, as said below
- doc_place: int32 [128], replicated, may hold values from 0 to 127, as said below
- block_use: int32 [128, 16], P('pairs'), may hold values 0 or 1
Outputs:
- attended: bfloat16 [8192, 4096], P('pairs', 'tensor')
Inputs may be any that keep to these rules, and one draw needn't show every extreme that they name: `doc_lists`: in each row the documents are distinct; a group takes exactly 2 documents from each owner (storage places k*2 to k*2 + 1) that it names, and none from the others. `doc_place`: A permutation of the documents.
All inputs are finite; a program needn't handle non-finite values. No bound on the sum of `block_use` on one device may be relied on, other than what follows from the above.
Results may differ from a plain program's by a relative error of at most 0.0085.
The roundings to bfloat16 on the way count: a program that leaves them out, or rounds other values in their place, can miss the bound.
Values may be sent and summed in bfloat16 or wider, within the bound.
No kernel may reach another device: no remote copies, remote signals or barrier semaphores. Data moves between devices by JAX's collectives and lax.ppermute only.
A program may use at most 64 MiB of HBM per device.

v0:
```python
import jax
import jax.numpy as jnp
from jax import lax
from jax.sharding import PartitionSpec as P

HEAD_DIM = 128
PAIRS_DEV = 1
SEQ = 128
QBLK = 64
BLK = 128
PICKS_PAIR = 16


def attend(query, key_own, value_own, key_doc, value_doc, use):
    head_size = query.shape[-1]
    scale = head_size ** (-0.5)
    s_doc = (
        jnp.einsum("psvgd,pkvd->pvgsk", query, key_doc, preferred_element_type=jnp.float32) * scale
    )
    s_own = (
        jnp.einsum("psvgd,ptvd->pvgst", query, key_own, preferred_element_type=jnp.float32) * scale
    )
    keep_doc = jnp.repeat(jnp.repeat(use, QBLK, axis=1), BLK, axis=2) > 0
    causal = jnp.arange(SEQ)[:, None] >= jnp.arange(SEQ)[None, :]
    s_doc = jnp.where(keep_doc[:, None, None], s_doc, -1e30)
    s_own = jnp.where(causal[None, None, None], s_own, -1e30)
    scores = jnp.concatenate([s_doc, s_own], axis=-1)
    top = jnp.max(scores, axis=-1, keepdims=True)
    expo = jnp.exp(scores - top)
    probs = (expo / jnp.sum(expo, axis=-1, keepdims=True)).astype(jnp.bfloat16)
    values = jnp.concatenate([value_doc, value_own], axis=1)
    out = jnp.einsum("pvgsk,pkvd->psvgd", probs, values, preferred_element_type=jnp.float32)
    return out.astype(jnp.bfloat16)


def shards(tokens, norm_gain, wq, wk, wv, doc_cache, doc_lists, doc_place, block_use):
    gathered = lax.all_gather(tokens, "tensor", axis=1, tiled=True)
    feats = gathered.astype(jnp.float32)
    power = jnp.mean(feats * feats, axis=-1, keepdims=True)
    normed = (feats * lax.rsqrt(power + 1e-05) * norm_gain.astype(jnp.float32)).astype(jnp.bfloat16)
    row_count = normed.shape[0]
    q_sum = jnp.dot(
        normed, lax.all_gather(wq, "pairs", axis=0, tiled=True), preferred_element_type=jnp.float32
    )
    k_sum = jnp.dot(
        normed, lax.all_gather(wk, "pairs", axis=0, tiled=True), preferred_element_type=jnp.float32
    )
    v_sum = jnp.dot(
        normed, lax.all_gather(wv, "pairs", axis=0, tiled=True), preferred_element_type=jnp.float32
    )
    query = q_sum.astype(jnp.bfloat16)
    key_own = k_sum.astype(jnp.bfloat16)
    value_own = v_sum.astype(jnp.bfloat16)
    group_total = lax.axis_size("pairs")
    my_group = lax.axis_index("pairs")
    pick_count = doc_lists.shape[1]
    doc_local = doc_cache.shape[0]
    doc_total = doc_place.shape[0]
    capacity = max(2, -(-pick_count // group_total))
    width = doc_cache.shape[1] * doc_cache.shape[2]
    matches = doc_lists[:, :, None] == jnp.arange(doc_total, dtype=jnp.int32)[None, None, :]
    places_all = jnp.sum(jnp.where(matches, doc_place[None, None, :], 0), axis=-1)
    my_places = lax.dynamic_index_in_dim(places_all, my_group, 0, keepdims=False)
    owner_all = places_all // doc_local
    local_all = places_all % doc_local
    order = jnp.arange(pick_count, dtype=jnp.int32)
    earlier = (owner_all[:, :, None] == owner_all[:, None, :]) & (
        order[None, None, :] < order[None, :, None]
    )
    rank_all = jnp.sum(earlier.astype(jnp.int32), axis=-1)
    mine = owner_all == my_group
    pick_slot = (
        rank_all[:, :, None, None] == jnp.arange(capacity, dtype=jnp.int32)[None, None, :, None]
    )
    pick_local = (
        local_all[:, :, None, None] == jnp.arange(doc_local, dtype=jnp.int32)[None, None, None, :]
    )
    selector = jnp.sum((mine[:, :, None, None] & pick_slot & pick_local).astype(jnp.int32), axis=1)
    flat_cache = doc_cache.reshape(doc_local, width)
    outgoing = jnp.einsum(
        "gcl,lx->gcx", selector.astype(jnp.bfloat16), flat_cache, preferred_element_type=jnp.float32
    ).astype(jnp.bfloat16)
    incoming = lax.all_to_all(outgoing, "pairs", split_axis=0, concat_axis=0, tiled=True)
    flat_in = incoming.reshape(group_total * capacity, width)
    my_rank = lax.dynamic_index_in_dim(rank_all, my_group, 0, keepdims=False)
    slots = my_places // doc_local * capacity + my_rank
    blocks = jnp.take(flat_in, slots, axis=0)
    kv_local = key_own.shape[1] // HEAD_DIM
    ratio = query.shape[1] // HEAD_DIM // kv_local
    q_rows = query.reshape(PAIRS_DEV, SEQ, kv_local, ratio, HEAD_DIM)
    k_rows = key_own.reshape(PAIRS_DEV, SEQ, kv_local, HEAD_DIM)
    v_rows = value_own.reshape(PAIRS_DEV, SEQ, kv_local, HEAD_DIM)
    doc_parts = blocks.reshape(PAIRS_DEV, PICKS_PAIR * BLK, kv_local, 2, HEAD_DIM)
    use = block_use.reshape(PAIRS_DEV, SEQ // QBLK, PICKS_PAIR)
    out = attend(q_rows, k_rows, v_rows, doc_parts[:, :, :, 0], doc_parts[:, :, :, 1], use)
    return out.reshape(row_count, query.shape[1])


def solution(mesh):
    placed = (
        P("pairs", "tensor"),
        P(),
        P("pairs", "tensor"),
        P("pairs", "tensor"),
        P("pairs", "tensor"),
        P("pairs", None, "tensor"),
        P(),
        P(),
        P("pairs", None),
    )
    return jax.shard_map(
        shards, mesh=mesh, in_specs=placed, out_specs=P("pairs", "tensor"), check_vma=False
    )
```

profile of v0, /device:TPU:24, one launch (start us, length us, event | category | flops | bytes accessed | tf_op | source)
XLA Modules:
  0.0 639.7 jit_solution(1647812005859428946)
XLA Ops:
  6.5 0.8 copy.61
  7.3 2.0 select_reduce_fusion
  9.4 0.9 reshape.377
  10.5 2.4 convolution_convert_fusion
  12.9 16.3 %copy.66 = bf16[64,2,32768]{2,1,0:T(2,128)(2,1)} copy(bf16[64,2,32768]{2,0,1:T(8,128)(2,1)S(1)} %convolution_convert_fusion) | data formatting | bytes 16777216 | tf_op jit(solution)/shard_map/convert_element_type | solution.py:82
  29.2 19.0 %all-to-all-start = ((bf16[64,2,32768]{2,1,0:T(2,128)(2,1)}), bf16[64,2,32768]{2,1,0:T(2,128)(2,1)}, u32[]{:S(2)}, u32[]{:S(2)}) async-start(bf16[64,2,32768]{2,1,0:T(2,128)(2,1)} %copy.66), calls=%async_computation | async-start | bytes 16777216 | tf_op jit(solution)/shard_map/all_to_all | solution.py:83
  48.2 0.7 all-gather.5.cloned.1.call-update
  49.0 0.7 all-gather.7.cloned.1.call-update
  49.7 0.7 all-gather.9.cloned.1.call-update
  51.6 30.0 %all-gather.5.cloned.1.call-done = bf16[128,4096]{1,0:T(8,128)(2,1)} async-done(((bf16[128,512]{1,0:T(8,128)(2,1)}), bf16[128,4096]{1,0:T(8,128)(2,1)}) %all-gather.5.cloned.1.call-update) | async-done | bytes 1048592 | tf_op jit(solution)/shard_map/all_gather | solution.py:37
  81.6 1.5 fusion.7
  83.1 181.1 %all-gather.7.cloned.1.call-done = bf16[4096,128]{1,0:T(8,128)(2,1)} async-done(((bf16[64,128]{1,0:T(8,128)(2,1)}), bf16[4096,128]{1,0:T(8,128)(2,1)}) %all-gather.7.cloned.1.call-update) | async-done | bytes 1048592 | tf_op jit(solution)/shard_map/all_gather | solution.py:49
  264.3 2.1 fusion.16
  266.3 202.9 %all-gather.9.cloned.1.call-done = bf16[4096,512]{1,0:T(8,128)(2,1)} async-done(((bf16[64,512]{1,0:T(8,128)(2,1)}), bf16[4096,512]{1,0:T(8,128)(2,1)}) %all-gather.9.cloned.1.call-update) | async-done | bytes 4194320 | tf_op jit(solution)/shard_map/all_gather | solution.py:43
  469.2 3.3 fusion.15
  472.5 134.4 %all-gather.11.cloned.1.call-done = bf16[4096,128]{1,0:T(8,128)(2,1)} async-done(((bf16[64,128]{1,0:T(8,128)(2,1)}), bf16[4096,128]{1,0:T(8,128)(2,1)}) %all-gather.11.cloned.1.call-update) | async-done | bytes 1048592 | tf_op jit(solution)/shard_map/all_gather | solution.py:46
  606.9 1.9 fusion.36
  608.8 13.2 %reshape.363 = bf16[128,32768]{1,0:T(8,128)(2,1)} reshape(bf16[64,2,32768]{2,1,0:T(2,128)(2,1)} %all-to-all-done) | data formatting | bytes 16777216 | tf_op jit(solution)/shard_map/reshape | solution.py:84
  621.9 6.6 %gather_fusion = bf16[16,32768]{1,0:T(8,128)(2,1)S(1)} fusion(bf16[128,32768]{1,0:T(8,128)(2,1)} %reshape.363, s32[1024]{0:T(1024)S(1)} %pad_clamp_fusion), kind=kCustom, calls=%fused_computation | custom fusion | bytes 2097216 | tf_op jit(solution)/shard_map/jit(_take)/gather | solution.py:87
  628.5 0.8 gather.7
  629.3 0.7 copy_select_fusion
  630.1 0.7 fusion.35
  631.4 1.0 fusion.11
  632.4 0.8 copy.73
  (35 shorter events, 2.3 us)
Async XLA Ops:
  29.2 21.8 %copy-start.1 = (bf16[4096]{0:T(1024)(128)(2,1)S(1)}, bf16[4096]{0:T(1024)(128)(2,1)}, u32[]{:S(2)}) copy-start(bf16[4096]{0:T(1024)(128)(2,1)} %param.10) | copy-start | bytes 24580
  29.2 21.8 %copy-start.2 = (s32[2,16]{1,0:T(2,128)S(1)}, s32[2,16]{1,0:T(2,128)}, u32[]{:S(2)}) copy-start(s32[2,16]{1,0:T(2,128)} %param.17) | copy-start | bytes 388
  29.2 579.6 %all-to-all-start = ((bf16[64,2,32768]{2,1,0:T(2,128)(2,1)}), bf16[64,2,32768]{2,1,0:T(2,128)(2,1)}, u32[]{:S(2)}, u32[]{:S(2)}) async-start(bf16[64,2,32768]{2,1,0:T(2,128)(2,1)} %copy.66), calls=%async_computation | async-start | bytes 16777216 | tf_op jit(solution)/shard_map/all_to_all | solution.py:83
  48.2 33.4 %all-gather.5.cloned.1.call-start = ((), (), s32[]{:S(2)}) async-start(), calls=%async_computation.1 | async-start | bytes 1179648 | tf_op jit(solution)/shard_map/all_gather | solution.py:37
  48.9 215.3 %all-gather.7.cloned.1.call-start = ((), (), s32[]{:S(2)}) async-start(), calls=%async_computation.2 | async-start | bytes 1064960 | tf_op jit(solution)/shard_map/all_gather | solution.py:49
  49.7 419.5 %all-gather.9.cloned.1.call-start = ((), (), s32[]{:S(2)}) async-start(), calls=%async_computation.3 | async-start | bytes 4259840 | tf_op jit(solution)/shard_map/all_gather | solution.py:43
  50.4 556.5 %all-gather.11.cloned.1.call-start = ((), (), s32[]{:S(2)}) async-start(), calls=%async_computation.4 | async-start | bytes 1064960 | tf_op jit(solution)/shard_map/all_gather | solution.py:46
  83.1 523.8 %copy-start = (bf16[128,4096]{1,0:T(8,128)(2,1)S(1)}, bf16[128,4096]{1,0:T(8,128)(2,1)}, u32[]{:S(2)}) copy-start(bf16[128,4096]{1,0:T(8,128)(2,1)} %all-gather.5.cloned.1.call-done) | copy-start | bytes 3145732
Sparse Core Ops, SparseCore 0:
  51.1 30.4 all-gather.4
  84.6 179.6 all-gather.6
  267.2 201.9 all-gather.8
  472.0 134.8 all-gather.10
where the time goes:
time: 641 us; the launch traced here: 640 us
  waiting for transfers between devices  551 us (86%)
  local copies, waits for them, and re-layouts  40 us (6%)
  starting transfers between devices  19.3 us (3%)
  between operations  13.3 us (2%)
  matrix products  11.3 us (2%)
    all_gather x1, waiting for transfers between devices, shards(): lax.all_gather(wq, 'pairs', axis=0, tiled=True)  203 us
    all_gather x1, waiting for transfers between devices, shards(): lax.all_gather(wv, 'pairs', axis=0, tiled=True)  181 us
    all_gather x1, waiting for transfers between devices, shards(): lax.all_gather(wk, 'pairs', axis=0, tiled=True)  134 us
    all_gather x1, waiting for transfers between devices, shards(): gathered = lax.all_gather(tokens, 'tensor', axis=1, tiled=True)  30 us
    all_to_all x1, starting transfers between devices, shards(): lax.all_to_all(outgoing, 'pairs', split_axis=0, concat_axis=0, tiled=True)  19 us
    convert_element_type x1, local copies, waits for them, and re-layouts, shards(): outgoing = jnp.einsum('gcl,lx->gcx', selector.astype(jnp.bfloat16), flat_...  16.3 us
    reshape x1, local copies, waits for them, and re-layouts, shards(): flat_in = incoming.reshape(group_total * capacity, width)  13.2 us
  transfers between devices with their start and end apart: 5, of which 4 were waited for; matrix products, arithmetic and copies ran while one was open for 1% of the time, Pallas kernels for 0%

commit v1 on v0

v1 whole, which is shorter than its diff:
```python
import jax
import jax.numpy as jnp
from jax import lax
from jax.experimental import pallas as pl
from jax.experimental.pallas import tpu as pltpu
from jax.sharding import Mesh
from jax.sharding import PartitionSpec as P

F32 = jnp.float32
BF16 = jnp.bfloat16
HEAD = 128
HALF = 64
SEQ = 128
RATIO = 4
NX = 4
NZ = 16
PICKS = 16
ROWS = NX * SEQ
COLS = RATIO * SEQ
SCALE = HEAD ** (-0.5)
LOW = -1e30
UNITS = 128

VMEM = pl.BlockSpec(memory_space=pltpu.VMEM)
SMEM = pl.BlockSpec(memory_space=pltpu.SMEM)
PARAMS = pltpu.CompilerParams(vmem_limit_bytes=40 * 1024 * 1024)


def call(kernel, outs, args, specs, out_specs=None, scratch=(), flops=0, moved=0):
    return pl.pallas_call(
        kernel,
        out_shape=outs,
        in_specs=specs,
        out_specs=VMEM if out_specs is None else out_specs,
        scratch_shapes=list(scratch),
        compiler_params=PARAMS,
        cost_estimate=pl.CostEstimate(flops=flops, bytes_accessed=moved, transcendentals=0),
    )(*args)


def side_by_side(left, right, left_at, right_at):
    left, right = left.astype(F32), right.astype(F32)
    lane = lax.broadcasted_iota(jnp.int32, left.shape, 1)
    left = pltpu.roll(left, HALF, 1) if left_at else left
    right = right if right_at else pltpu.roll(right, HALF, 1)
    return jnp.where(lane < HALF, left, right).astype(BF16)


def pack_kernel(wq, wk, wv, out):
    for part in range(NX):
        src = wk if part < 2 else wv
        at = HALF * (part % 2)
        packed = side_by_side(src[0:32, :], src[32:64, :], at, at)
        for copy in range(4):
            out[part, copy, 0:64, :] = wq[:, part * HEAD : (part + 1) * HEAD]
            out[part, copy, 64:96, :] = packed


def norm_kernel(where, mine, other, gain, out):
    core = where[3]
    for row in range(NX):
        rows = pl.ds(row * SEQ, SEQ)
        total = jnp.zeros((SEQ, HEAD), F32)
        for src in (mine, other):
            for y in range(4):
                for c in range(4):
                    feats = src[row, y, :, c * HEAD : (c + 1) * HEAD].astype(F32)
                    total = total + feats * feats
        power = jnp.sum(total, axis=-1, keepdims=True) * (1.0 / 4096.0)
        factor = lax.rsqrt(power + 1e-05)
        for src, flip in ((mine, 0), (other, 1)):
            side = core if flip == 0 else 1 - core
            for y in range(4):
                slot = 2 * y + side
                feats = src[row, y].astype(F32)
                out[slot, rows, :] = (feats * factor * gain[slot]).astype(BF16)


def route_kernel(where, lists, place, use, units, table):
    x, z = where[0], where[1]

    def clear(i, carry):
        table[i] = 0
        return carry

    lax.fori_loop(0, NX * NZ, clear, 0)

    def fill(i, carry):
        row, pick = i // PICKS, i % PICKS
        at = place[lists[row * NZ + z, pick]]
        owner, local = at // 2, at % 2
        bits = use[row * 2, pick] + 2 * use[row * 2 + 1, pick]
        entry = row * NZ + owner % NZ
        mine = jnp.where(owner // NZ == x, 1, 0)
        table[entry] = table[entry] + mine * bits * jnp.where(local == 1, 4, 1)
        return carry

    lax.fori_loop(0, NX * PICKS, fill, 0)

    def compact(i, count):
        bits = table[i]
        units[count + 1] = i * 16 + bits
        return count + jnp.where(bits > 0, 1, 0)

    units[0] = lax.fori_loop(0, NX * NZ, compact, 0)


def project_kernel(where, normed, near, ahead, far_a, far_b, behind, send, weights):
    lane_part = where[2]
    for step in range(4):
        row = lax.rem(lane_part + step, 4) * HALF
        for b in range(16):
            if step == 0:
                block = near[b]
            elif step == 1:
                block = ahead[b]
            elif step == 3:
                block = behind[b]
            else:
                block = far_a[b] if b < 8 else far_b[b - 8]
            base = pl.multiple_of(b * 256 + row, HALF)
            packed = block[64:96, :]
            weights[pl.ds(base, 64), 0:HEAD] = block[0:64, :]
            weights[pl.ds(base, 32), HEAD : 2 * HEAD] = packed
            weights[pl.ds(pl.multiple_of(base + 32, 32), 32), HEAD : 2 * HEAD] = pltpu.roll(
                packed.astype(F32), HALF, 1
            ).astype(BF16)
    total = jnp.zeros((ROWS, 2 * HEAD), F32)
    for slot in range(8):
        total = total + jnp.dot(
            normed[slot], weights[slot * 512 : (slot + 1) * 512, :], preferred_element_type=F32
        )
    query = total[:, 0:HEAD].astype(BF16)
    for dest in range(NX):
        own = total[dest * SEQ : (dest + 1) * SEQ, HEAD : 2 * HEAD]
        send[dest, 0:ROWS, :] = query
        send[dest, ROWS : ROWS + HALF, :] = side_by_side(own[0:HALF], own[HALF:SEQ], 0, 0)


def own_part(got, first):
    a, b = got[first, ROWS : ROWS + HALF, :], got[first + 1, ROWS : ROWS + HALF, :]
    return jnp.concatenate([side_by_side(a, b, 0, 0), side_by_side(a, b, HALF, HALF)], axis=0)


def queries(got, group):
    rows = pl.ds(pl.multiple_of(group * SEQ, SEQ), SEQ)
    return jnp.concatenate([got[head, rows, :] for head in range(RATIO)], axis=0)


def scores_of(keys, query):
    return (
        lax.dot_general(keys, query, (((1,), (1,)), ((), ())), preferred_element_type=F32) * SCALE
    )


def own_scores(got, group):
    scores = scores_of(own_part(got, 0), queries(got, group))
    key_at = lax.broadcasted_iota(jnp.int32, (SEQ, COLS), 0)
    row_at = lax.broadcasted_iota(jnp.int32, (SEQ, COLS), 1) % SEQ
    return jnp.where(row_at >= key_at, scores, LOW)


def unit_scores(code, got, docs):
    entry, bits = code // 16, code % 16
    group, owner = entry // NZ, entry % NZ
    keys = docs[pl.ds(owner * 2, 2), :, 0:HEAD].reshape(2 * SEQ, HEAD)
    scores = scores_of(keys, queries(got, group))
    second = (lax.broadcasted_iota(jnp.int32, (1, COLS), 1) % SEQ) // HALF
    kept = []
    for local in range(2):
        use_a, use_b = (bits // (4**local)) % 2, (bits // (2 * 4**local)) % 2
        keep = jnp.where(second == 0, use_a, use_b)
        kept.append(jnp.where(keep > 0, scores[local * SEQ : (local + 1) * SEQ], LOW))
    return group, owner, jnp.concatenate(kept, axis=0)


def stats_kernel(where, units, got, docs, send, stats):
    x = where[0]
    scores = own_scores(got, x)
    top = jnp.max(scores, axis=0, keepdims=True)
    stats[0:4, :] = jnp.full((4, COLS), LOW, F32)
    stats[4:8, :] = jnp.zeros((4, COLS), F32)
    stats[pl.ds(x, 1), :] = top
    stats[pl.ds(x + 4, 1), :] = jnp.sum(jnp.exp(scores - top), axis=0, keepdims=True)

    def unit(i, carry):
        group, owner, scores = unit_scores(units[i + 1], got, docs)
        before = stats[pl.ds(group, 1), :]
        top = jnp.maximum(before, jnp.max(scores, axis=0, keepdims=True))
        part = jnp.sum(jnp.exp(scores - top), axis=0, keepdims=True)
        stats[pl.ds(group, 1), :] = top
        stats[pl.ds(group + 4, 1), :] = stats[pl.ds(group + 4, 1), :] * jnp.exp(before - top) + part
        return carry

    lax.fori_loop(0, units[0], unit, 0)
    for dest in range(NX):
        send[dest] = stats[...]


def values_kernel(where, units, got, docs, all_stats, send, total):
    x = where[0]
    tops = [all_stats[src, 0:4, :] for src in range(NX)]
    top = jnp.maximum(jnp.maximum(tops[0], tops[1]), jnp.maximum(tops[2], tops[3]))
    sums = jnp.zeros((4, COLS), F32)
    for src in range(NX):
        sums = sums + all_stats[src, 4:8, :] * jnp.exp(tops[src] - top)
    total[0:4, :] = top
    total[4:8, :] = sums
    send[...] = jnp.zeros(send.shape, F32)

    def add(group, scores, values):
        expo = jnp.exp(scores - total[pl.ds(group, 1), :])
        probs = (expo / total[pl.ds(group + 4, 1), :]).astype(BF16)
        out = lax.dot_general(values, probs, (((0,), (0,)), ((), ())), preferred_element_type=F32)
        send[pl.ds(group, 1)] = send[pl.ds(group, 1)] + out[None]

    add(x, own_scores(got, x), own_part(got, 2))

    def unit(i, carry):
        group, owner, scores = unit_scores(units[i + 1], got, docs)
        values = docs[pl.ds(owner * 2, 2), :, HEAD : 2 * HEAD].reshape(2 * SEQ, HEAD)
        add(group, scores, values)
        return carry

    lax.fori_loop(0, units[0], unit, 0)


def finish_kernel(got, out):
    for head in range(RATIO):
        cols = slice(head * SEQ, (head + 1) * SEQ)
        total = (got[0, :, cols] + got[1, :, cols]) + (got[2, :, cols] + got[3, :, cols])
        out[:, cols] = total.T.astype(BF16)


def exchange(array, axes):
    return lax.all_to_all(array, axes, 0, 0, tiled=True)


def spread(array, axes, count):
    return exchange(jnp.broadcast_to(array[None], (count, *array.shape)), axes)


def shards(tokens, norm_gain, wq, wk, wv, doc_cache, doc_lists, doc_place, block_use):
    shape = jax.ShapeDtypeStruct
    z_axes = ("zh", "zl")
    docs = lax.all_gather(doc_cache, z_axes, axis=0, tiled=True)
    x, zh, zl = lax.axis_index("x"), lax.axis_index("zh"), lax.axis_index("zl")
    where = jnp.stack([x, zh * 4 + zl, zl, lax.axis_index("core")]).astype(jnp.int32)

    parts = call(pack_kernel, shape((4, 4, 96, HEAD), BF16), (wq, wk, wv), [VMEM] * 3)
    near = exchange(parts.reshape(16, 96, HEAD), ("x", "zh"))

    by_y = spread(tokens, "y", 4)
    mine = spread(by_y, "x", NX)
    other = lax.ppermute(mine, "core", [(0, 1), (1, 0)])
    gain = norm_gain.astype(F32).reshape(8, 1, 512)
    normed = call(
        norm_kernel,
        shape((8, ROWS, 512), BF16),
        (where, mine, other, gain),
        [SMEM, VMEM, VMEM, VMEM],
        flops=ROWS * 4096 * 8,
        moved=8 << 20,
    )
    use = spread(block_use, "x", NX).reshape(8, PICKS)
    units = call(
        route_kernel,
        shape((UNITS,), jnp.int32),
        (where, doc_lists, doc_place, use),
        [SMEM] * 4,
        out_specs=SMEM,
        scratch=[pltpu.SMEM((NX * NZ,), jnp.int32)],
    )

    def from_z(array, step):
        return lax.ppermute(array, z_axes, [((i + step) % NZ, i) for i in range(NZ)])

    ahead = from_z(near, 1)
    behind = from_z(near, -1)
    far_a = from_z(near[0:8], 2)
    far_b = from_z(near[8:16], -2)
    send = call(
        project_kernel,
        shape((NX, ROWS + HALF, HEAD), BF16),
        (where, normed, near, ahead, far_a, far_b, behind),
        [SMEM] + [VMEM] * 6,
        scratch=[pltpu.VMEM((4096, 2 * HEAD), BF16)],
        flops=2 * ROWS * 4096 * 256,
        moved=8 << 20,
    )
    got = exchange(send, "x")
    stats = call(
        stats_kernel,
        shape((NX, 8, COLS), F32),
        (where, units, got, docs),
        [SMEM, SMEM, VMEM, VMEM],
        scratch=[pltpu.VMEM((8, COLS), F32)],
    )
    all_stats = exchange(stats, "x")
    partial = call(
        values_kernel,
        shape((NX, HEAD, COLS), F32),
        (where, units, got, docs, all_stats),
        [SMEM, SMEM, VMEM, VMEM, VMEM],
        scratch=[pltpu.VMEM((8, COLS), F32)],
    )
    returned = exchange(partial, "x")
    return call(finish_kernel, shape((SEQ, COLS), BF16), (returned,), [VMEM])


def solution(mesh):
    fine = Mesh(mesh.devices.reshape(4, 4, 4, 4, 2), ("x", "zh", "zl", "y", "core"))
    pairs, tensor = ("x", "zh", "zl"), ("y", "core")
    placed = (
        P(pairs, tensor),
        P(),
        P(pairs, tensor),
        P(pairs, tensor),
        P(pairs, tensor),
        P(pairs, None, tensor),
        P(),
        P(),
        P(pairs, None),
    )
    return jax.shard_map(
        shards, mesh=fine, in_specs=placed, out_specs=P(pairs, tensor), check_vma=False
    )
```

time: 641 us -> 192 us (0.30)
  waiting for transfers between devices: 551 us -> 34.2 us
  blocking collectives: 0 us -> 85.2 us
  local copies, waits for them, and re-layouts: 40 us -> 5.53 us
  Pallas kernels: 0 us -> 24.1 us
  matrix products: 11.3 us -> 0 us
  starting transfers between devices: 19.3 us -> 26.4 us
    all_gather x4 -> x1, waiting for transfers between devices: 548 us -> 0.02 us  [shards(): docs = lax.all_gather(doc_cache, z_axes, axis=0, tiled=True)]
    all_to_all x0 -> x4, blocking collectives: none -> 85.2 us  [exchange(): return lax.all_to_all(array, axes, 0, 0, tiled=True)]
    all_to_all x1 -> x3, waiting for transfers between devices: 0.01 us -> 28.3 us  [exchange(): return lax.all_to_all(array, axes, 0, 0, tiled=True)]
    pallas_call x0 -> x7, Pallas kernels: none -> 24.1 us  [call(): pl.pallas_call(kernel, out_shape=outs, in_specs=specs, out_specs=VMEM if...]
    convert_element_type x1 -> x0, local copies, waits for them, and re-layouts: 16.3 us -> none  [shards(): outgoing = jnp.einsum('gcl,lx->gcx', selector.astype(jnp.bfloat16), flat_...]
    ppermute x0 -> x5, starting transfers between devices: none -> 15 us  [the longest x4 13.1 us: from_z(): lax.ppermute(array, z_axes, [((i + step) % NZ, i) for i in range(NZ)])]
    reshape x3 -> x0, local copies, waits for them, and re-layouts: 14.9 us -> none  [the longest x1 13.2 us: shards(): flat_in = incoming.reshape(group_total * capacity, width)]
    dot_general x6 -> x0, matrix products: 11.3 us -> none  [the longest x1 3.27 us: shards(): jnp.dot(normed, lax.all_gather(wq, 'pairs', axis=0, tiled=True), preferre...]
  transfers between devices with their start and end apart: 5 -> 9, of which waited for: 4 -> 4; matrix products, arithmetic and copies ran while one was open for 1% -> 1% of each run, Pallas kernels for 0% -> 6%
where the time goes in v1:
time: 192 us; the launch traced here: 189 us
  blocking collectives  85.2 us (44%)
  waiting for transfers between devices  34.2 us (18%)
  starting transfers between devices  26.4 us (14%)
  Pallas kernels  24.1 us (13%)
  between operations  13.6 us (7%)
  local copies, waits for them, and re-layouts  5.53 us (3%)
    all_to_all x4, blocking collectives, exchange(): return lax.all_to_all(array, axes, 0, 0, tiled=True)  85.2 us
    all_to_all x3, waiting for transfers between devices, exchange(): return lax.all_to_all(array, axes, 0, 0, tiled=True)  28.3 us
    pallas_call x7, Pallas kernels, call(): pl.pallas_call(kernel, out_shape=outs, in_specs=specs, out_specs=VMEM if...  24.1 us
    ppermute x4, starting transfers between devices, from_z(): lax.ppermute(array, z_axes, [((i + step) % NZ, i) for i in range(NZ)])  13.1 us
    all_to_all x3, starting transfers between devices, exchange(): return lax.all_to_all(array, axes, 0, 0, tiled=True)  11.4 us
    ppermute x4, waiting for transfers between devices, from_z(): lax.ppermute(array, z_axes, [((i + step) % NZ, i) for i in range(NZ)])  5.2 us
  transfers between devices with their start and end apart: 9, of which 4 were waited for; matrix products, arithmetic and copies ran while one was open for 1% of the time, Pallas kernels for 6%

profile of v1, /device:TPU:24, one launch (start us, length us, event | category | flops | bytes accessed | tf_op | source)
XLA Modules:
  0.0 189.1 jit_solution(10075426839758296014)
XLA Ops:
  6.5 0.9 broadcast_in_dim.7
  7.5 14.0 %all_to_all.35 = bf16[4,128,512]{2,1,0:T(8,128)(2,1)S(1)} all-to-all(bf16[4,128,512]{2,1,0:T(8,128)(2,1)S(1)} %broadcast_in_dim.7), channel_id=1, replica_groups=mesh['x'=4,'zh'=4,'zl'=4,'y'=4,'core'=2] {'y'}, dimensions={0} | all-to-all | bytes 1048576 | tf_op jit(solution)/shard_map/all_to_all | solution.py:236
  21.5 1.5 broadcast_in_dim.8
  23.0 3.7 %all-to-all-start.2 = ((bf16[4,4,128,512]{3,2,1,0:T(8,128)(2,1)}), bf16[4,4,128,512]{3,2,1,0:T(8,128)(2,1)S(1)}, u32[]{:S(2)}, u32[]{:S(2)}) async-start(bf16[4,4,128,512]{3,2,1,0:T(8,128)(2,1)} %broadcast_in_dim.8), calls=%async_computation.2 | async-start | bytes 4194304 | tf_op jit(solution)/shard_map/all_to_all | solution.py:236
  27.5 22.9 %all-to-all-done.2.mine = bf16[4,4,128,512]{3,2,1,0:T(8,128)(2,1)S(1)} async-done(((bf16[4,4,128,512]{3,2,1,0:T(8,128)(2,1)}), bf16[4,4,128,512]{3,2,1,0:T(8,128)(2,1)S(1)}, u32[]{:S(2)}, u32[]{:S(2)}) %all-to-all-start.2) | async-done | bytes 2097184 | tf_op jit(solution)/shard_map/all_to_all | solution.py:236
  50.5 1.9 %collective-permute-start = (bf16[4,4,128,512]{3,2,1,0:T(8,128)(2,1)S(1)}, bf16[4,4,128,512]{3,2,1,0:T(8,128)(2,1)}, u32[]{:S(2)}, u32[]{:S(2)}) collective-permute-start(bf16[4,4,128,512]{3,2,1,0:T(8,128)(2,1)S(1)} %all-to-all-done.2.mine), channel_id=1, source_target_pairs={{0,1},{1,0},{2,3},{3,2},{4,5},{5,4},{6,7},{7,6},{8,9},{9,8},{10,11... | collective-permute-start | bytes 6291464 | tf_op jit(solution)/shard_map/ppermute | solution.py:255
  52.5 47.7 %all_to_all.36.near = bf16[16,96,128]{2,1,0:T(8,128)(2,1)S(1)} all-to-all(bf16[16,96,128]{2,1,0:T(8,128)(2,1)S(1)} %bitcast.7), channel_id=1, replica_groups=mesh['x'=4,'zh'=4,'zl'=4,'y'=4,'core'=2] {'x','zh'}, dimensions={0} | all-to-all | bytes 786432 | tf_op jit(solution)/shard_map/all_to_all | solution.py:236
  100.2 1.9 %collective-permute-start.1 = (bf16[16,96,128]{2,1,0:T(8,128)(2,1)S(1)}, bf16[16,96,128]{2,1,0:T(8,128)(2,1)S(1)}, u32[]{:S(2)}, u32[]{:S(2)}) collective-permute-start(bf16[16,96,128]{2,1,0:T(8,128)(2,1)S(1)} %all_to_all.36.near), channel_id=1, source_target_pairs={{8,0},{16,8},{24,16},{32,24},{40,32},{48,40},{56,48},{64,56},{72,6... | collective-permute-start | bytes 1179656 | tf_op jit(solution)/shard_map/ppermute | solution.py:276
  102.1 4.4 %collective-permute-start.4 = (bf16[16,96,128]{2,1,0:T(8,128)(2,1)S(1)}, bf16[16,96,128]{2,1,0:T(8,128)(2,1)S(1)}, u32[]{:S(2)}, u32[]{:S(2)}) collective-permute-start(bf16[16,96,128]{2,1,0:T(8,128)(2,1)S(1)} %all_to_all.36.near), channel_id=1, source_target_pairs={{120,0},{0,8},{8,16},{16,24},{24,32},{32,40},{40,48},{48,56},{56,6... | collective-permute-start | bytes 1179656 | tf_op jit(solution)/shard_map/ppermute | solution.py:276
  107.3 1.9 %collective-permute-start.2 = (bf16[8,96,128]{2,1,0:T(8,128)(2,1)}, bf16[8,96,128]{2,1,0:T(8,128)(2,1)S(1)}, u32[]{:S(2)}, u32[]{:S(2)}) collective-permute-start(bf16[8,96,128]{2,1,0:T(8,128)(2,1)} %get-tuple-element.6), channel_id=1, source_target_pairs={{16,0},{24,8},{32,16},{40,24},{48,32},{56,40},{64,48},{72,56},{80,... | collective-permute-start | bytes 589832 | tf_op jit(solution)/shard_map/ppermute | solution.py:276
  109.2 4.8 %collective-permute-start.3 = (bf16[8,96,128]{2,1,0:T(8,128)(2,1)}, bf16[8,96,128]{2,1,0:T(8,128)(2,1)}, u32[]{:S(2)}, u32[]{:S(2)}) collective-permute-start(bf16[8,96,128]{2,1,0:T(8,128)(2,1)} %get-tuple-element.5), channel_id=1, source_target_pairs={{112,0},{120,8},{0,16},{8,24},{16,32},{24,40},{32,48},{40,56},{48,... | collective-permute-start | bytes 589832 | tf_op jit(solution)/shard_map/ppermute | solution.py:276
  114.7 3.2 %all-to-all-start = ((s32[4,2,16]{2,1,0:T(2,128)}), s32[4,2,16]{2,1,0:T(2,128)S(1)}, u32[]{:S(2)}, u32[]{:S(2)}) async-start(s32[4,2,16]{2,1,0:T(2,128)} %broadcast_in_dim.6), calls=%async_computation | async-start | bytes 8192 | tf_op jit(solution)/shard_map/all_to_all | solution.py:236
  118.1 3.6 %shard_map.92.normed = bf16[8,512,512]{2,1,0:T(8,128)(2,1)S(1)} custom-call(s32[4]{0:T(128)S(1)} %pad_add_fusion.where, bf16[4,4,128,512]{3,2,1,0:T(8,128)(2,1)S(1)} %all-to-all-done.2.mine, bf16[4,4,128,512]{3,2,1,0:T(8,128)(2,1)} %collective-permute-done.other, f32[8,1,512]{2,1,0:T(1,128)S(1)} %bitcast.8), custom_call_target="tpu_custom_call" | custom-call | flops 16777216 | bytes 8388608 | tf_op jit(solution)/shard_map/pallas_call | solution.py:30
  121.7 3.5 %collective-permute-done.2.far_a = bf16[8,96,128]{2,1,0:T(8,128)(2,1)S(1)} collective-permute-done((bf16[8,96,128]{2,1,0:T(8,128)(2,1)}, bf16[8,96,128]{2,1,0:T(8,128)(2,1)S(1)}, u32[]{:S(2)}, u32[]{:S(2)}) %collective-permute-start.2) | collective-permute-done | bytes 196640 | tf_op jit(solution)/shard_map/ppermute | solution.py:276
  125.2 1.7 collective-permute-done.3.far_b
  126.9 3.5 %shard_map.94 = bf16[4,576,128]{2,1,0:T(8,128)(2,1)} custom-call(s32[4]{0:T(128)S(1)} %pad_add_fusion.where, bf16[8,512,512]{2,1,0:T(8,128)(2,1)S(1)} %shard_map.92.normed, bf16[16,96,128]{2,1,0:T(8,128)(2,1)S(1)} %all_to_all.36.near, bf16[16,96,128]{2,1,0:T(8,128)(2,1)S(1)} %collective-permute-done.1.ahead, ...), custom_call_target="tpu_custom_call" | custom-call | flops 1073741824 | bytes 8388608 | tf_op jit(solution)/shard_map/pallas_call | solution.py:30
  130.4 4.4 %all-to-all-start.4 = ((bf16[4,576,128]{2,1,0:T(8,128)(2,1)}), bf16[4,576,128]{2,1,0:T(8,128)(2,1)S(1)}, u32[]{:S(2)}, u32[]{:S(2)}) async-start(bf16[4,576,128]{2,1,0:T(8,128)(2,1)} %shard_map.94), calls=%async_computation.4 | async-start | bytes 1179648 | tf_op jit(solution)/shard_map/all_to_all | solution.py:236
  134.9 4.7 %shard_map.91.units = s32[128]{0:T(128)S(1)} custom-call(s32[4]{0:T(128)S(1)} %pad_add_fusion.where, s32[64,16]{1,0:T(8,128)S(1)} %copy.11.lists, s32[128]{0:T(128)S(1)} %copy-done.4, s32[8,16]{1,0:T(8,128)S(1)} %bitcast.9), custom_call_target="tpu_custom_call" | custom-call | tf_op jit(solution)/shard_map/pallas_call | solution.py:30
  139.7 5.4 %all-to-all-done.4.got = bf16[4,576,128]{2,1,0:T(8,128)(2,1)S(1)} async-done(((bf16[4,576,128]{2,1,0:T(8,128)(2,1)}), bf16[4,576,128]{2,1,0:T(8,128)(2,1)S(1)}, u32[]{:S(2)}, u32[]{:S(2)}) %all-to-all-start.4) | async-done | bytes 589856 | tf_op jit(solution)/shard_map/all_to_all | solution.py:236
  145.0 1.6 copy-done
  146.6 5.0 %shard_map.95 = f32[4,8,512]{2,1,0:T(8,128)S(1)} custom-call(s32[4]{0:T(128)S(1)} %pad_add_fusion.where, s32[128]{0:T(128)S(1)} %shard_map.91.units, bf16[4,576,128]{2,1,0:T(8,128)(2,1)S(1)} %all-to-all-done.4.got, bf16[32,128,256]{2,1,0:T(8,128)(2,1)S(1)} %copy-done), custom_call_target="tpu_custom_call" | custom-call | tf_op jit(solution)/shard_map/pallas_call | solution.py:30
  151.6 8.0 %all_to_all.37.all_stats = f32[4,8,512]{2,1,0:T(8,128)S(1)} all-to-all(f32[4,8,512]{2,1,0:T(8,128)S(1)} %shard_map.95), channel_id=1, replica_groups=mesh['x'=4,'zh'=4,'zl'=4,'y'=4,'core'=2] {'x'}, dimensions={0} | all-to-all | bytes 131072 | tf_op jit(solution)/shard_map/all_to_all | solution.py:236
  159.6 6.4 %shard_map.96 = f32[4,128,512]{2,1,0:T(8,128)S(1)} custom-call(s32[4]{0:T(128)S(1)} %pad_add_fusion.where, s32[128]{0:T(128)S(1)} %shard_map.91.units, bf16[4,576,128]{2,1,0:T(8,128)(2,1)S(1)} %all-to-all-done.4.got, bf16[32,128,256]{2,1,0:T(8,128)(2,1)S(1)} %copy-done, f32[4,8,512]{2,1,0:T(8,128)S(1)} %all_to_all.37.all_stats), custom_call_target="tpu_custom_call" | custom-call | tf_op jit(solution)/shard_map/pallas_call | solution.py:30
  166.0 15.5 %all_to_all.38.got = f32[4,128,512]{2,1,0:T(8,128)S(1)} all-to-all(f32[4,128,512]{2,1,0:T(8,128)S(1)} %shard_map.96), channel_id=1, replica_groups=mesh['x'=4,'zh'=4,'zl'=4,'y'=4,'core'=2] {'x'}, dimensions={0} | all-to-all | bytes 2097152 | tf_op jit(solution)/shard_map/all_to_all | solution.py:236
  (29 shorter events, 3.2 us)
Async XLA Ops:
  23.0 29.4 %copy-start.1 = (bf16[64,512]{1,0:T(8,128)(2,1)S(1)}, bf16[64,512]{1,0:T(8,128)(2,1)}, u32[]{:S(2)}) copy-start(bf16[64,512]{1,0:T(8,128)(2,1)} %wq.1) | copy-start | bytes 196612
  23.0 29.4 %copy-start.2 = (bf16[64,128]{1,0:T(8,128)(2,1)S(1)}, bf16[64,128]{1,0:T(8,128)(2,1)}, u32[]{:S(2)}) copy-start(bf16[64,128]{1,0:T(8,128)(2,1)} %wk.1) | copy-start | bytes 49156
  23.0 29.4 %copy-start.3 = (bf16[64,128]{1,0:T(8,128)(2,1)S(1)}, bf16[64,128]{1,0:T(8,128)(2,1)}, u32[]{:S(2)}) copy-start(bf16[64,128]{1,0:T(8,128)(2,1)} %wv.1) | copy-start | bytes 49156
  23.0 27.5 %all-to-all-start.2 = ((bf16[4,4,128,512]{3,2,1,0:T(8,128)(2,1)}), bf16[4,4,128,512]{3,2,1,0:T(8,128)(2,1)S(1)}, u32[]{:S(2)}, u32[]{:S(2)}) async-start(bf16[4,4,128,512]{3,2,1,0:T(8,128)(2,1)} %broadcast_in_dim.8), calls=%async_computation.2 | async-start | bytes 4194304 | tf_op jit(solution)/shard_map/all_to_all | solution.py:236
  26.7 87.3 %copy-start.7 = (s32[2,16]{1,0:T(2,128)S(1)}, s32[2,16]{1,0:T(2,128)}, u32[]{:S(2)}) copy-start(s32[2,16]{1,0:T(2,128)} %param.17) | copy-start | bytes 388
  26.8 91.2 %copy-start.5 = (bf16[4096]{0:T(1024)(128)(2,1)S(1)}, bf16[4096]{0:T(1024)(128)(2,1)}, u32[]{:S(2)}) copy-start(bf16[4096]{0:T(1024)(128)(2,1)} %param.10) | copy-start | bytes 24580
  26.8 112.9 %all-gather.2.cloned.1.call-start = ((), (), s32[]{:S(2)}) async-start(), calls=%async_computation.7 | async-start | bytes 2228224 | tf_op jit(solution)/shard_map/all_gather | solution.py:246
  50.5 67.6 %collective-permute-start = (bf16[4,4,128,512]{3,2,1,0:T(8,128)(2,1)S(1)}, bf16[4,4,128,512]{3,2,1,0:T(8,128)(2,1)}, u32[]{:S(2)}, u32[]{:S(2)}) collective-permute-start(bf16[4,4,128,512]{3,2,1,0:T(8,128)(2,1)S(1)} %all-to-all-done.2.mine), channel_id=1, source_target_pairs={{0,1},{1,0},{2,3},{3,2},{4,5},{5,4},{6,7},{7,6},{8,9},{9,8},{10,11... | collective-permute-start | bytes 6291464 | tf_op jit(solution)/shard_map/ppermute | solution.py:255
  100.2 26.7 %collective-permute-start.1 = (bf16[16,96,128]{2,1,0:T(8,128)(2,1)S(1)}, bf16[16,96,128]{2,1,0:T(8,128)(2,1)S(1)}, u32[]{:S(2)}, u32[]{:S(2)}) collective-permute-start(bf16[16,96,128]{2,1,0:T(8,128)(2,1)S(1)} %all_to_all.36.near), channel_id=1, source_target_pairs={{8,0},{16,8},{24,16},{32,24},{40,32},{48,40},{56,48},{64,56},{72,6... | collective-permute-start | bytes 1179656 | tf_op jit(solution)/shard_map/ppermute | solution.py:276
  102.1 24.8 %collective-permute-start.4 = (bf16[16,96,128]{2,1,0:T(8,128)(2,1)S(1)}, bf16[16,96,128]{2,1,0:T(8,128)(2,1)S(1)}, u32[]{:S(2)}, u32[]{:S(2)}) collective-permute-start(bf16[16,96,128]{2,1,0:T(8,128)(2,1)S(1)} %all_to_all.36.near), channel_id=1, source_target_pairs={{120,0},{0,8},{8,16},{16,24},{24,32},{32,40},{40,48},{48,56},{56,6... | collective-permute-start | bytes 1179656 | tf_op jit(solution)/shard_map/ppermute | solution.py:276
  107.3 17.9 %collective-permute-start.2 = (bf16[8,96,128]{2,1,0:T(8,128)(2,1)}, bf16[8,96,128]{2,1,0:T(8,128)(2,1)S(1)}, u32[]{:S(2)}, u32[]{:S(2)}) collective-permute-start(bf16[8,96,128]{2,1,0:T(8,128)(2,1)} %get-tuple-element.6), channel_id=1, source_target_pairs={{16,0},{24,8},{32,16},{40,24},{48,32},{56,40},{64,48},{72,56},{80,... | collective-permute-start | bytes 589832 | tf_op jit(solution)/shard_map/ppermute | solution.py:276
  109.2 17.7 %collective-permute-start.3 = (bf16[8,96,128]{2,1,0:T(8,128)(2,1)}, bf16[8,96,128]{2,1,0:T(8,128)(2,1)}, u32[]{:S(2)}, u32[]{:S(2)}) collective-permute-start(bf16[8,96,128]{2,1,0:T(8,128)(2,1)} %get-tuple-element.5), channel_id=1, source_target_pairs={{112,0},{120,8},{0,16},{8,24},{16,32},{24,40},{32,48},{40,56},{48,... | collective-permute-start | bytes 589832 | tf_op jit(solution)/shard_map/ppermute | solution.py:276
  114.7 15.7 %all-to-all-start = ((s32[4,2,16]{2,1,0:T(2,128)}), s32[4,2,16]{2,1,0:T(2,128)S(1)}, u32[]{:S(2)}, u32[]{:S(2)}) async-start(s32[4,2,16]{2,1,0:T(2,128)} %broadcast_in_dim.6), calls=%async_computation | async-start | bytes 8192 | tf_op jit(solution)/shard_map/all_to_all | solution.py:236
  121.7 13.1 %copy-start.6 = (s32[64,16]{0,1:T(8,128)S(1)}, s32[64,16]{0,1:T(8,128)}, u32[]{:S(2)}) copy-start(s32[64,16]{0,1:T(8,128)} %param.15) | copy-start | bytes 12292
  121.7 13.2 %copy-start.4 = (s32[128]{0:T(128)S(1)}, s32[128]{0:T(128)}, u32[]{:S(2)}) copy-start(s32[128]{0:T(128)} %place.1) | copy-start | bytes 1540
  130.4 14.6 %all-to-all-start.4 = ((bf16[4,576,128]{2,1,0:T(8,128)(2,1)}), bf16[4,576,128]{2,1,0:T(8,128)(2,1)S(1)}, u32[]{:S(2)}, u32[]{:S(2)}) async-start(bf16[4,576,128]{2,1,0:T(8,128)(2,1)} %shard_map.94), calls=%async_computation.4 | async-start | bytes 1179648 | tf_op jit(solution)/shard_map/all_to_all | solution.py:236
  145.0 1.6 copy-start
Sparse Core Ops, SparseCore 0:
  29.7 92.7 all-gather.1

commit v2 on v1

--- a/solution.py
+++ b/solution.py
@@ -23,7 +23,7 @@
 
 VMEM = pl.BlockSpec(memory_space=pltpu.VMEM)
 SMEM = pl.BlockSpec(memory_space=pltpu.SMEM)
-PARAMS = pltpu.CompilerParams(vmem_limit_bytes=40 * 1024 * 1024)
+PARAMS = pltpu.CompilerParams(vmem_limit_bytes=24 * 1024 * 1024)
 
 
 def call(kernel, outs, args, specs, out_specs=None, scratch=(), flops=0, moved=0):
@@ -71,7 +71,7 @@
         for src, flip in ((mine, 0), (other, 1)):
             side = core if flip == 0 else 1 - core
             for y in range(4):
-                slot = 2 * y + side
+                slot = 2 * lax.rem(where[4] + y, 4) + side
                 feats = src[row, y].astype(F32)
                 out[slot, rows, :] = (feats * factor * gain[slot]).astype(BF16)
 
@@ -160,10 +160,20 @@
     return jnp.where(row_at >= key_at, scores, LOW)
 
 
-def unit_scores(code, got, docs):
+def documents(docs, owner, parity, part):
+    mine, up, down = docs
+    at, cols = (owner // 2) * 2, slice(part * HEAD, (part + 1) * HEAD)
+    from_mine = mine[pl.ds(at, 2), :, cols]
+    from_up = up[pl.ds(jnp.minimum(at, 6), 2), :, cols]
+    from_down = down[pl.ds(jnp.maximum(at - 8, 0), 2), :, cols]
+    other = jnp.where(at < 8, from_up, from_down)
+    return jnp.where(owner % 2 == parity, from_mine, other).reshape(2 * SEQ, HEAD)
+
+
+def unit_scores(code, got, docs, parity):
     entry, bits = code // 16, code % 16
     group, owner = entry // NZ, entry % NZ
-    keys = docs[pl.ds(owner * 2, 2), :, 0:HEAD].reshape(2 * SEQ, HEAD)
+    keys = documents(docs, owner, parity, 0)
     scores = scores_of(keys, queries(got, group))
     second = (lax.broadcasted_iota(jnp.int32, (1, COLS), 1) % SEQ) // HALF
     kept = []
@@ -174,8 +184,9 @@
     return group, owner, jnp.concatenate(kept, axis=0)
 
 
-def stats_kernel(where, units, got, docs, send, stats):
+def stats_kernel(where, units, got, docs_mine, docs_up, docs_down, send, stats):
     x = where[0]
+    docs = (docs_mine, docs_up, docs_down)
     scores = own_scores(got, x)
     top = jnp.max(scores, axis=0, keepdims=True)
     stats[0:4, :] = jnp.full((4, COLS), LOW, F32)
@@ -184,7 +195,7 @@
     stats[pl.ds(x + 4, 1), :] = jnp.sum(jnp.exp(scores - top), axis=0, keepdims=True)
 
     def unit(i, carry):
-        group, owner, scores = unit_scores(units[i + 1], got, docs)
+        group, owner, scores = unit_scores(units[i + 1], got, docs, where[1] % 2)
         before = stats[pl.ds(group, 1), :]
         top = jnp.maximum(before, jnp.max(scores, axis=0, keepdims=True))
         part = jnp.sum(jnp.exp(scores - top), axis=0, keepdims=True)
@@ -197,8 +208,9 @@
         send[dest] = stats[...]
 
 
-def values_kernel(where, units, got, docs, all_stats, send, total):
+def values_kernel(where, units, got, docs_mine, docs_up, docs_down, all_stats, send, total):
     x = where[0]
+    docs = (docs_mine, docs_up, docs_down)
     tops = [all_stats[src, 0:4, :] for src in range(NX)]
     top = jnp.maximum(jnp.maximum(tops[0], tops[1]), jnp.maximum(tops[2], tops[3]))
     sums = jnp.zeros((4, COLS), F32)
@@ -217,8 +229,8 @@
     add(x, own_scores(got, x), own_part(got, 2))
 
     def unit(i, carry):
-        group, owner, scores = unit_scores(units[i + 1], got, docs)
-        values = docs[pl.ds(owner * 2, 2), :, HEAD : 2 * HEAD].reshape(2 * SEQ, HEAD)
+        group, owner, scores = unit_scores(units[i + 1], got, docs, where[1] % 2)
+        values = documents(docs, owner, where[1] % 2, 1)
         add(group, scores, values)
         return carry
 
@@ -242,16 +254,32 @@
 
 def shards(tokens, norm_gain, wq, wk, wv, doc_cache, doc_lists, doc_place, block_use):
     shape = jax.ShapeDtypeStruct
-    z_axes = ("zh", "zl")
-    docs = lax.all_gather(doc_cache, z_axes, axis=0, tiled=True)
-    x, zh, zl = lax.axis_index("x"), lax.axis_index("zh"), lax.axis_index("zl")
-    where = jnp.stack([x, zh * 4 + zl, zl, lax.axis_index("core")]).astype(jnp.int32)
+    z_axes = ("zh", "zm", "zp")
+
+    def from_z(array, step):
+        return lax.ppermute(array, z_axes, [((i + step) % NZ, i) for i in range(NZ)])
+
+    docs_mine = lax.all_gather(doc_cache, ("zh", "zm"), axis=0, tiled=True)
+    x, zh = lax.axis_index("x"), lax.axis_index("zh")
+    zl = lax.axis_index("zm") * 2 + lax.axis_index("zp")
+    where = jnp.stack([x, zh * 4 + zl, zl, lax.axis_index("core"), lax.axis_index("y")]).astype(jnp.int32)
 
     parts = call(pack_kernel, shape((4, 4, 96, HEAD), BF16), (wq, wk, wv), [VMEM] * 3)
     near = exchange(parts.reshape(16, 96, HEAD), ("x", "zh"))
-
-    by_y = spread(tokens, "y", 4)
+    tokens, _ = lax.optimization_barrier((tokens, parts))
+    by_y = jnp.stack([tokens] + [lax.ppermute(tokens, "y", [((i + k) % 4, i) for i in range(4)]) for k in (1, 2, 3)])
+    by_y, near = lax.optimization_barrier((by_y, near))
     mine = spread(by_y, "x", NX)
+    ahead = from_z(near, 1)
+    behind = from_z(near, -1)
+    far_a = from_z(near[0:8], 2)
+    far_b = from_z(near[8:16], -2)
+    mine, ahead, behind, far_a, far_b, docs_mine = lax.optimization_barrier(
+        (mine, ahead, behind, far_a, far_b, docs_mine)
+    )
+    docs_up = from_z(docs_mine[0:8], 1)
+    docs_down = from_z(docs_mine[8:16], -1)
+    docs = (docs_mine, docs_up, docs_down)
     other = lax.ppermute(mine, "core", [(0, 1), (1, 0)])
     gain = norm_gain.astype(F32).reshape(8, 1, 512)
     normed = call(
@@ -272,13 +300,6 @@
         scratch=[pltpu.SMEM((NX * NZ,), jnp.int32)],
     )
 
-    def from_z(array, step):
-        return lax.ppermute(array, z_axes, [((i + step) % NZ, i) for i in range(NZ)])
-
-    ahead = from_z(near, 1)
-    behind = from_z(near, -1)
-    far_a = from_z(near[0:8], 2)
-    far_b = from_z(near[8:16], -2)
     send = call(
         project_kernel,
         shape((NX, ROWS + HALF, HEAD), BF16),
@@ -292,16 +313,16 @@
     stats = call(
         stats_kernel,
         shape((NX, 8, COLS), F32),
-        (where, units, got, docs),
-        [SMEM, SMEM, VMEM, VMEM],
+        (where, units, got, *docs),
+        [SMEM, SMEM] + [VMEM] * 4,
         scratch=[pltpu.VMEM((8, COLS), F32)],
     )
     all_stats = exchange(stats, "x")
     partial = call(
         values_kernel,
         shape((NX, HEAD, COLS), F32),
-        (where, units, got, docs, all_stats),
-        [SMEM, SMEM, VMEM, VMEM, VMEM],
+        (where, units, got, *docs, all_stats),
+        [SMEM, SMEM] + [VMEM] * 5,
         scratch=[pltpu.VMEM((8, COLS), F32)],
     )
     returned = exchange(partial, "x")
@@ -309,8 +330,8 @@
 
 
 def solution(mesh):
-    fine = Mesh(mesh.devices.reshape(4, 4, 4, 4, 2), ("x", "zh", "zl", "y", "core"))
-    pairs, tensor = ("x", "zh", "zl"), ("y", "core")
+    fine = Mesh(mesh.devices.reshape(4, 4, 2, 2, 4, 2), ("x", "zh", "zm", "zp", "y", "core"))
+    pairs, tensor = ("x", "zh", "zm", "zp"), ("y", "core")
     placed = (
         P(pairs, tensor),
         P(),

time: 192 us -> 177 us (0.922)
  blocking collectives: 85.2 us -> 23 us
  starting transfers between devices: 26.4 us -> 67.1 us
  local copies, waits for them, and re-layouts: 5.53 us -> 8.87 us
    all_to_all x4 -> x2, blocking collectives: 85.2 us -> 23 us  [exchange(): return lax.all_to_all(array, axes, 0, 0, tiled=True)]
    all_to_all x3 -> x4, starting transfers between devices: 11.4 us -> 32.7 us  [exchange(): return lax.all_to_all(array, axes, 0, 0, tiled=True)]
    all_to_all x3 -> x4, waiting for transfers between devices: 28.3 us -> 12.8 us  [exchange(): return lax.all_to_all(array, axes, 0, 0, tiled=True)]
    ppermute x4 -> x6, waiting for transfers between devices: 5.2 us -> 18.3 us  [from_z(): lax.ppermute(array, z_axes, [((i + step) % NZ, i) for i in range(NZ)])]
    ppermute x4 -> x6, starting transfers between devices: 13.1 us -> 22.9 us  [from_z(): lax.ppermute(array, z_axes, [((i + step) % NZ, i) for i in range(NZ)])]
    ppermute x0 -> x3, starting transfers between devices: none -> 9.6 us  [shards(): lax.ppermute(tokens, 'y', [((i + k) % 4, i) for i in range(4)])]
    ppermute x0 -> x3, waiting for transfers between devices: none -> 4.25 us  [shards(): lax.ppermute(tokens, 'y', [((i + k) % 4, i) for i in range(4)])]
    slice x0 -> x1, local copies, waits for them, and re-layouts: none -> 2.3 us  [shards(): docs_down = from_z(docs_mine[8:16], -1)]
  transfers between devices with their start and end apart: 9 -> 15, of which waited for: 4 -> 7; matrix products, arithmetic and copies ran while one was open for 1% -> 4% of each run, Pallas kernels for 6% -> 7%
where the time goes in v2:
time: 177 us; the launch traced here: 174 us
  starting transfers between devices  67.1 us (38%)
  waiting for transfers between devices  36 us (20%)
  Pallas kernels  23.9 us (14%)
  blocking collectives  23 us (13%)
  between operations  13.7 us (8%)
  local copies, waits for them, and re-layouts  8.87 us (5%)
    all_to_all x4, starting transfers between devices, exchange(): return lax.all_to_all(array, axes, 0, 0, tiled=True)  32.7 us
    pallas_call x7, Pallas kernels, call(): pl.pallas_call(kernel, out_shape=outs, in_specs=specs, out_specs=VMEM if...  23.9 us
    all_to_all x2, blocking collectives, exchange(): return lax.all_to_all(array, axes, 0, 0, tiled=True)  23 us
    ppermute x6, starting transfers between devices, from_z(): lax.ppermute(array, z_axes, [((i + step) % NZ, i) for i in range(NZ)])  22.9 us
    ppermute x6, waiting for transfers between devices, from_z(): lax.ppermute(array, z_axes, [((i + step) % NZ, i) for i in range(NZ)])  18.3 us
    all_to_all x4, waiting for transfers between devices, exchange(): return lax.all_to_all(array, axes, 0, 0, tiled=True)  12.8 us
    ppermute x3, starting transfers between devices, shards(): lax.ppermute(tokens, 'y', [((i + k) % 4, i) for i in range(4)])  9.6 us
    ppermute x3, waiting for transfers between devices, shards(): lax.ppermute(tokens, 'y', [((i + k) % 4, i) for i in range(4)])  4.25 us
  transfers between devices with their start and end apart: 15, of which 7 were waited for; matrix products, arithmetic and copies ran while one was open for 4% of the time, Pallas kernels for 7%

profile of v2, /device:TPU:24, one launch (start us, length us, event | category | flops | bytes accessed | tf_op | source)
XLA Modules:
  0.0 173.6 jit_solution(17661993833811924345)
XLA Ops:
  9.6 17.7 %all-to-all-start.1 = ((bf16[16,96,128]{2,1,0:T(8,128)(2,1)}), bf16[16,96,128]{2,1,0:T(8,128)(2,1)S(1)}, u32[]{:S(2)}, u32[]{:S(2)}) async-start(bf16[16,96,128]{2,1,0:T(8,128)(2,1)} %bitcast.10), calls=%async_computation.1 | async-start | bytes 786432 | tf_op jit(solution)/shard_map/all_to_all | solution.py:248
  28.0 2.7 %collective-permute-start = (bf16[128,512]{1,0:T(8,128)(2,1)}, bf16[128,512]{1,0:T(8,128)(2,1)S(1)}, u32[]{:S(2)}, u32[]{:S(2)}) collective-permute-start(bf16[128,512]{1,0:T(8,128)(2,1)} %param.9), channel_id=1, source_target_pairs={{2,0},{4,2},{6,4},{0,6},{3,1},{5,3},{7,5},{1,7},{10,8},{12,10},{14... | collective-permute-start | bytes 393224 | tf_op jit(solution)/shard_map/ppermute | solution.py:270
  30.7 2.9 %collective-permute-start.1 = (bf16[128,512]{1,0:T(8,128)(2,1)}, bf16[128,512]{1,0:T(8,128)(2,1)S(1)}, u32[]{:S(2)}, u32[]{:S(2)}) collective-permute-start(bf16[128,512]{1,0:T(8,128)(2,1)} %param.9), channel_id=1, source_target_pairs={{4,0},{6,2},{0,4},{2,6},{5,1},{7,3},{1,5},{3,7},{12,8},{14,10},{8,... | collective-permute-start | bytes 393224 | tf_op jit(solution)/shard_map/ppermute | solution.py:270
  33.6 4.1 %collective-permute-start.2 = (bf16[128,512]{1,0:T(8,128)(2,1)}, bf16[128,512]{1,0:T(8,128)(2,1)S(1)}, u32[]{:S(2)}, u32[]{:S(2)}) collective-permute-start(bf16[128,512]{1,0:T(8,128)(2,1)} %param.9), channel_id=1, source_target_pairs={{6,0},{0,2},{2,4},{4,6},{7,1},{1,3},{3,5},{5,7},{14,8},{8,10},{10,... | collective-permute-start | bytes 393224 | tf_op jit(solution)/shard_map/ppermute | solution.py:270
  39.3 2.6 %collective-permute-done.2 = bf16[128,512]{1,0:T(8,128)(2,1)S(1)} collective-permute-done((bf16[128,512]{1,0:T(8,128)(2,1)}, bf16[128,512]{1,0:T(8,128)(2,1)S(1)}, u32[]{:S(2)}, u32[]{:S(2)}) %collective-permute-start.2) | collective-permute-done | bytes 131104 | tf_op jit(solution)/shard_map/ppermute | solution.py:270
  42.9 7.8 %all-to-all-done.1.near = bf16[16,96,128]{2,1,0:T(8,128)(2,1)S(1)} async-done(((bf16[16,96,128]{2,1,0:T(8,128)(2,1)}), bf16[16,96,128]{2,1,0:T(8,128)(2,1)S(1)}, u32[]{:S(2)}, u32[]{:S(2)}) %all-to-all-start.1) | async-done | bytes 393248 | tf_op jit(solution)/shard_map/all_to_all | solution.py:248
  52.3 6.0 %all-to-all-start.2 = ((bf16[4,4,128,512]{3,2,1,0:T(8,128)(2,1)}), bf16[4,4,128,512]{3,2,1,0:T(8,128)(2,1)S(1)}, u32[]{:S(2)}, u32[]{:S(2)}) async-start(bf16[4,4,128,512]{3,2,1,0:T(8,128)(2,1)} %broadcast_in_dim.5), calls=%async_computation.2 | async-start | bytes 4194304 | tf_op jit(solution)/shard_map/all_to_all | solution.py:248
  58.3 4.3 %collective-permute-start.3 = (bf16[16,96,128]{2,1,0:T(8,128)(2,1)S(1)}, bf16[16,96,128]{2,1,0:T(8,128)(2,1)S(1)}, u32[]{:S(2)}, u32[]{:S(2)}) collective-permute-start(bf16[16,96,128]{2,1,0:T(8,128)(2,1)S(1)} %all-to-all-done.1.near), channel_id=1, source_target_pairs={{8,0},{16,8},{24,16},{32,24},{40,32},{48,40},{56,48},{64,56},{72,6... | collective-permute-start | bytes 1179656 | tf_op jit(solution)/shard_map/ppermute | solution.py:260
  62.5 4.0 %collective-permute-start.4 = (bf16[16,96,128]{2,1,0:T(8,128)(2,1)S(1)}, bf16[16,96,128]{2,1,0:T(8,128)(2,1)S(1)}, u32[]{:S(2)}, u32[]{:S(2)}) collective-permute-start(bf16[16,96,128]{2,1,0:T(8,128)(2,1)S(1)} %all-to-all-done.1.near), channel_id=1, source_target_pairs={{120,0},{0,8},{8,16},{16,24},{24,32},{32,40},{40,48},{48,56},{56,6... | collective-permute-start | bytes 1179656 | tf_op jit(solution)/shard_map/ppermute | solution.py:260
  68.7 4.7 %collective-permute-start.6 = (bf16[8,96,128]{2,1,0:T(8,128)(2,1)S(1)}, bf16[8,96,128]{2,1,0:T(8,128)(2,1)S(1)}, u32[]{:S(2)}, u32[]{:S(2)}) collective-permute-start(bf16[8,96,128]{2,1,0:T(8,128)(2,1)S(1)} %get-tuple-element.25), channel_id=1, source_target_pairs={{112,0},{120,8},{0,16},{8,24},{16,32},{24,40},{32,48},{40,56},{48,... | collective-permute-start | bytes 589832 | tf_op jit(solution)/shard_map/ppermute | solution.py:260
  73.3 16.0 %collective-permute-done.5.far_a = bf16[8,96,128]{2,1,0:T(8,128)(2,1)S(1)} collective-permute-done((bf16[8,96,128]{2,1,0:T(8,128)(2,1)S(1)}, bf16[8,96,128]{2,1,0:T(8,128)(2,1)S(1)}, u32[]{:S(2)}, u32[]{:S(2)}) %collective-permute-start.5) | collective-permute-done | bytes 196640 | tf_op jit(solution)/shard_map/ppermute | solution.py:260
  95.5 4.3 %all-to-all-start = ((s32[4,2,16]{2,1,0:T(2,128)}), s32[4,2,16]{2,1,0:T(2,128)}, u32[]{:S(2)}, u32[]{:S(2)}) async-start(s32[4,2,16]{2,1,0:T(2,128)} %broadcast_in_dim.4), calls=%async_computation | async-start | bytes 8192 | tf_op jit(solution)/shard_map/all_to_all | solution.py:248
  100.4 2.3 %fusion = (bf16[8,128,256]{2,1,0:T(8,128)(2,1)}, bf16[8,128,256]{2,1,0:T(8,128)(2,1)}) fusion(bf16[16,128,256]{2,1,0:T(8,128)(2,1)} %all-gather.2.cloned.1.call-done.docs_mine), kind=kLoop, calls=%fused_computation.1 | loop fusion | bytes 2097152 | tf_op jit(solution)/shard_map/slice | solution.py:281
  102.7 5.0 %collective-permute-start.8 = (bf16[8,128,256]{2,1,0:T(8,128)(2,1)}, bf16[8,128,256]{2,1,0:T(8,128)(2,1)S(1)}, u32[]{:S(2)}, u32[]{:S(2)}) collective-permute-start(bf16[8,128,256]{2,1,0:T(8,128)(2,1)} %get-tuple-element.24), channel_id=1, source_target_pairs={{8,0},{16,8},{24,16},{32,24},{40,32},{48,40},{56,48},{64,56},{72,6... | collective-permute-start | bytes 1572872 | tf_op jit(solution)/shard_map/ppermute | solution.py:260
  107.7 2.8 %collective-permute-start.9 = (bf16[8,128,256]{2,1,0:T(8,128)(2,1)}, bf16[8,128,256]{2,1,0:T(8,128)(2,1)S(1)}, u32[]{:S(2)}, u32[]{:S(2)}) collective-permute-start(bf16[8,128,256]{2,1,0:T(8,128)(2,1)} %get-tuple-element.23), channel_id=1, source_target_pairs={{120,0},{0,8},{8,16},{16,24},{24,32},{32,40},{40,48},{48,56},{56,6... | collective-permute-start | bytes 1572872 | tf_op jit(solution)/shard_map/ppermute | solution.py:260
  110.7 3.7 %shard_map.93.normed = bf16[8,512,512]{2,1,0:T(8,128)(2,1)S(1)} custom-call(s32[5]{0:T(128)S(1)} %copy-done.10, bf16[4,4,128,512]{3,2,1,0:T(8,128)(2,1)S(1)} %all-to-all-done.2.mine, bf16[4,4,128,512]{3,2,1,0:T(8,128)(2,1)} %collective-permute-done.7.other, f32[8,1,512]{2,1,0:T(1,128)S(1)} %bitcast.12), custom_call_target="tpu_custom_call" | custom-call | flops 16777216 | bytes 8388608 | tf_op jit(solution)/shard_map/pallas_call | solution.py:30
  114.5 3.1 %shard_map.94 = bf16[4,576,128]{2,1,0:T(8,128)(2,1)} custom-call(s32[5]{0:T(128)S(1)} %copy-done.10, bf16[8,512,512]{2,1,0:T(8,128)(2,1)S(1)} %shard_map.93.normed, bf16[16,96,128]{2,1,0:T(8,128)(2,1)S(1)} %all-to-all-done.1.near, bf16[16,96,128]{2,1,0:T(8,128)(2,1)S(1)} %copy-done.2, bf16[8,96,128]{2,1,0:T(8,128)(2,1)S(1)} %copy-done.6, ...), custom_call_target="tpu_custom_call" | custom-call | flops 1073741824 | bytes 8388608 | tf_op jit(solution)/shard_map/pallas_call | solution.py:30
  117.6 4.8 %all-to-all-start.3 = ((bf16[4,576,128]{2,1,0:T(8,128)(2,1)}), bf16[4,576,128]{2,1,0:T(8,128)(2,1)S(1)}, u32[]{:S(2)}, u32[]{:S(2)}) async-start(bf16[4,576,128]{2,1,0:T(8,128)(2,1)} %shard_map.94), calls=%async_computation.3 | async-start | bytes 1179648 | tf_op jit(solution)/shard_map/all_to_all | solution.py:248
  122.5 4.9 %shard_map.91.units = s32[128]{0:T(128)S(1)} custom-call(s32[5]{0:T(128)S(1)} %copy-done.11, s32[64,16]{1,0:T(8,128)S(1)} %copy.11.lists, s32[128]{0:T(128)S(1)} %copy-done.14, s32[8,16]{1,0:T(8,128)} %bitcast.5.use), custom_call_target="tpu_custom_call" | custom-call | tf_op jit(solution)/shard_map/pallas_call | solution.py:30
  127.4 5.0 %all-to-all-done.3.got = bf16[4,576,128]{2,1,0:T(8,128)(2,1)S(1)} async-done(((bf16[4,576,128]{2,1,0:T(8,128)(2,1)}), bf16[4,576,128]{2,1,0:T(8,128)(2,1)S(1)}, u32[]{:S(2)}, u32[]{:S(2)}) %all-to-all-start.3) | async-done | bytes 589856 | tf_op jit(solution)/shard_map/all_to_all | solution.py:248
  132.4 4.7 %shard_map.95 = f32[4,8,512]{2,1,0:T(8,128)S(1)} custom-call(s32[5]{0:T(128)S(1)} %copy-done.11, s32[128]{0:T(128)S(1)} %shard_map.91.units, bf16[4,576,128]{2,1,0:T(8,128)(2,1)S(1)} %all-to-all-done.3.got, bf16[16,128,256]{2,1,0:T(8,128)(2,1)S(1)} %copy-done, bf16[8,128,256]{2,1,0:T(8,128)(2,1)S(1)} %collective-permute-done.8.docs_up, ...), custom_call_target="tpu_custom_call" | custom-call | tf_op jit(solution)/shard_map/pallas_call | solution.py:30
  137.0 8.0 %all_to_all.30.all_stats = f32[4,8,512]{2,1,0:T(8,128)S(1)} all-to-all(f32[4,8,512]{2,1,0:T(8,128)S(1)} %shard_map.95), channel_id=1, replica_groups=mesh['x'=4,'zh'=4,'zm'=2,'zp'=2,'y'=4,'core'=2] {'x'}, dimensions={0} | all-to-all | bytes 131072 | tf_op jit(solution)/shard_map/all_to_all | solution.py:248
  145.0 6.0 %shard_map.96 = f32[4,128,512]{2,1,0:T(8,128)S(1)} custom-call(s32[5]{0:T(128)S(1)} %copy-done.11, s32[128]{0:T(128)S(1)} %shard_map.91.units, bf16[4,576,128]{2,1,0:T(8,128)(2,1)S(1)} %all-to-all-done.3.got, bf16[16,128,256]{2,1,0:T(8,128)(2,1)S(1)} %copy-done, bf16[8,128,256]{2,1,0:T(8,128)(2,1)S(1)} %collective-permute-done.8.docs_up, ...), custom_call_target="tpu_custom_call" | custom-call | tf_op jit(solution)/shard_map/pallas_call | solution.py:30
  151.0 15.0 %all_to_all.31.got = f32[4,128,512]{2,1,0:T(8,128)S(1)} all-to-all(f32[4,128,512]{2,1,0:T(8,128)S(1)} %shard_map.96), channel_id=1, replica_groups=mesh['x'=4,'zh'=4,'zm'=2,'zp'=2,'y'=4,'core'=2] {'x'}, dimensions={0} | all-to-all | bytes 2097152 | tf_op jit(solution)/shard_map/all_to_all | solution.py:248
  (60 shorter events, 17.8 us)
Async XLA Ops:
  9.6 41.1 %all-to-all-start.1 = ((bf16[16,96,128]{2,1,0:T(8,128)(2,1)}), bf16[16,96,128]{2,1,0:T(8,128)(2,1)S(1)}, u32[]{:S(2)}, u32[]{:S(2)}) async-start(bf16[16,96,128]{2,1,0:T(8,128)(2,1)} %bitcast.10), calls=%async_computation.1 | async-start | bytes 786432 | tf_op jit(solution)/shard_map/all_to_all | solution.py:248
  27.3 65.7 %all-gather.2.cloned.1.call-start = ((), (), s32[]{:S(2)}) async-start(), calls=%async_computation.6 | async-start | bytes 1179648 | tf_op jit(solution)/shard_map/all_gather | solution.py:262
  28.0 9.7 %collective-permute-start = (bf16[128,512]{1,0:T(8,128)(2,1)}, bf16[128,512]{1,0:T(8,128)(2,1)S(1)}, u32[]{:S(2)}, u32[]{:S(2)}) collective-permute-start(bf16[128,512]{1,0:T(8,128)(2,1)} %param.9), channel_id=1, source_target_pairs={{2,0},{4,2},{6,4},{0,6},{3,1},{5,3},{7,5},{1,7},{10,8},{12,10},{14... | collective-permute-start | bytes 393224 | tf_op jit(solution)/shard_map/ppermute | solution.py:270
  30.7 8.6 %collective-permute-start.1 = (bf16[128,512]{1,0:T(8,128)(2,1)}, bf16[128,512]{1,0:T(8,128)(2,1)S(1)}, u32[]{:S(2)}, u32[]{:S(2)}) collective-permute-start(bf16[128,512]{1,0:T(8,128)(2,1)} %param.9), channel_id=1, source_target_pairs={{4,0},{6,2},{0,4},{2,6},{5,1},{7,3},{1,5},{3,7},{12,8},{14,10},{8,... | collective-permute-start | bytes 393224 | tf_op jit(solution)/shard_map/ppermute | solution.py:270
  33.6 8.3 %collective-permute-start.2 = (bf16[128,512]{1,0:T(8,128)(2,1)}, bf16[128,512]{1,0:T(8,128)(2,1)S(1)}, u32[]{:S(2)}, u32[]{:S(2)}) collective-permute-start(bf16[128,512]{1,0:T(8,128)(2,1)} %param.9), channel_id=1, source_target_pairs={{6,0},{0,2},{2,4},{4,6},{7,1},{1,3},{3,5},{5,7},{14,8},{8,10},{10,... | collective-permute-start | bytes 393224 | tf_op jit(solution)/shard_map/ppermute | solution.py:270
  52.3 42.7 %copy-start.17 = (s32[2,16]{1,0:T(2,128)S(1)}, s32[2,16]{1,0:T(2,128)}, u32[]{:S(2)}) copy-start(s32[2,16]{1,0:T(2,128)} %param.17) | copy-start | bytes 388
  52.3 47.6 %copy-start.15 = (bf16[4096]{0:T(1024)(128)(2,1)S(1)}, bf16[4096]{0:T(1024)(128)(2,1)}, u32[]{:S(2)}) copy-start(bf16[4096]{0:T(1024)(128)(2,1)} %param.10) | copy-start | bytes 24580
  52.3 40.7 %all-to-all-start.2 = ((bf16[4,4,128,512]{3,2,1,0:T(8,128)(2,1)}), bf16[4,4,128,512]{3,2,1,0:T(8,128)(2,1)S(1)}, u32[]{:S(2)}, u32[]{:S(2)}) async-start(bf16[4,4,128,512]{3,2,1,0:T(8,128)(2,1)} %broadcast_in_dim.5), calls=%async_computation.2 | async-start | bytes 4194304 | tf_op jit(solution)/shard_map/all_to_all | solution.py:248
  58.3 34.7 %collective-permute-start.3 = (bf16[16,96,128]{2,1,0:T(8,128)(2,1)S(1)}, bf16[16,96,128]{2,1,0:T(8,128)(2,1)S(1)}, u32[]{:S(2)}, u32[]{:S(2)}) collective-permute-start(bf16[16,96,128]{2,1,0:T(8,128)(2,1)S(1)} %all-to-all-done.1.near), channel_id=1, source_target_pairs={{8,0},{16,8},{24,16},{32,24},{40,32},{48,40},{56,48},{64,56},{72,6... | collective-permute-start | bytes 1179656 | tf_op jit(solution)/shard_map/ppermute | solution.py:260
  62.5 30.5 %collective-permute-start.4 = (bf16[16,96,128]{2,1,0:T(8,128)(2,1)S(1)}, bf16[16,96,128]{2,1,0:T(8,128)(2,1)S(1)}, u32[]{:S(2)}, u32[]{:S(2)}) collective-permute-start(bf16[16,96,128]{2,1,0:T(8,128)(2,1)S(1)} %all-to-all-done.1.near), channel_id=1, source_target_pairs={{120,0},{0,8},{8,16},{16,24},{24,32},{32,40},{40,48},{48,56},{56,6... | collective-permute-start | bytes 1179656 | tf_op jit(solution)/shard_map/ppermute | solution.py:260
  66.6 22.7 %collective-permute-start.5 = (bf16[8,96,128]{2,1,0:T(8,128)(2,1)S(1)}, bf16[8,96,128]{2,1,0:T(8,128)(2,1)S(1)}, u32[]{:S(2)}, u32[]{:S(2)}) collective-permute-start(bf16[8,96,128]{2,1,0:T(8,128)(2,1)S(1)} %get-tuple-element.26), channel_id=1, source_target_pairs={{16,0},{24,8},{32,16},{40,24},{48,32},{56,40},{64,48},{72,56},{80,... | collective-permute-start | bytes 589832 | tf_op jit(solution)/shard_map/ppermute | solution.py:260
  68.7 23.6 %collective-permute-start.6 = (bf16[8,96,128]{2,1,0:T(8,128)(2,1)S(1)}, bf16[8,96,128]{2,1,0:T(8,128)(2,1)S(1)}, u32[]{:S(2)}, u32[]{:S(2)}) collective-permute-start(bf16[8,96,128]{2,1,0:T(8,128)(2,1)S(1)} %get-tuple-element.25), channel_id=1, source_target_pairs={{112,0},{120,8},{0,16},{8,24},{16,32},{24,40},{32,48},{40,56},{48,... | collective-permute-start | bytes 589832 | tf_op jit(solution)/shard_map/ppermute | solution.py:260
  93.0 9.8 %copy-start.1 = (bf16[16,96,128]{2,1,0:T(8,128)(2,1)}, bf16[16,96,128]{2,1,0:T(8,128)(2,1)S(1)}, u32[]{:S(2)}) copy-start(bf16[16,96,128]{2,1,0:T(8,128)(2,1)S(1)} %collective-permute-done.3.ahead) | copy-start | bytes 1179652
  93.0 9.8 %copy-start.3 = (bf16[16,96,128]{2,1,0:T(8,128)(2,1)}, bf16[16,96,128]{2,1,0:T(8,128)(2,1)S(1)}, u32[]{:S(2)}) copy-start(bf16[16,96,128]{2,1,0:T(8,128)(2,1)S(1)} %collective-permute-done.4.behind) | copy-start | bytes 1179652
  93.0 17.6 %collective-permute-start.7 = (bf16[4,4,128,512]{3,2,1,0:T(8,128)(2,1)S(1)}, bf16[4,4,128,512]{3,2,1,0:T(8,128)(2,1)}, u32[]{:S(2)}, u32[]{:S(2)}) collective-permute-start(bf16[4,4,128,512]{3,2,1,0:T(8,128)(2,1)S(1)} %all-to-all-done.2.mine), channel_id=1, source_target_pairs={{0,1},{1,0},{2,3},{3,2},{4,5},{5,4},{6,7},{7,6},{8,9},{9,8},{10,11... | collective-permute-start | bytes 6291464 | tf_op jit(solution)/shard_map/ppermute | solution.py:283
  95.5 22.0 %all-to-all-start = ((s32[4,2,16]{2,1,0:T(2,128)}), s32[4,2,16]{2,1,0:T(2,128)}, u32[]{:S(2)}, u32[]{:S(2)}) async-start(s32[4,2,16]{2,1,0:T(2,128)} %broadcast_in_dim.4), calls=%async_computation | async-start | bytes 8192 | tf_op jit(solution)/shard_map/all_to_all | solution.py:248
  100.4 10.2 %copy-start.10 = (s32[5]{0:T(128)S(1)}, s32[5]{0:T(128)}, u32[]{:S(2)}) copy-start(s32[5]{0:T(128)} %stack.38.where) | copy-start | bytes 64
  102.7 24.6 %collective-permute-start.8 = (bf16[8,128,256]{2,1,0:T(8,128)(2,1)}, bf16[8,128,256]{2,1,0:T(8,128)(2,1)S(1)}, u32[]{:S(2)}, u32[]{:S(2)}) collective-permute-start(bf16[8,128,256]{2,1,0:T(8,128)(2,1)} %get-tuple-element.24), channel_id=1, source_target_pairs={{8,0},{16,8},{24,16},{32,24},{40,32},{48,40},{56,48},{64,56},{72,6... | collective-permute-start | bytes 1572872 | tf_op jit(solution)/shard_map/ppermute | solution.py:260
  107.7 19.6 %collective-permute-start.9 = (bf16[8,128,256]{2,1,0:T(8,128)(2,1)}, bf16[8,128,256]{2,1,0:T(8,128)(2,1)S(1)}, u32[]{:S(2)}, u32[]{:S(2)}) collective-permute-start(bf16[8,128,256]{2,1,0:T(8,128)(2,1)} %get-tuple-element.23), channel_id=1, source_target_pairs={{120,0},{0,8},{8,16},{16,24},{24,32},{32,40},{40,48},{48,56},{56,6... | collective-permute-start | bytes 1572872 | tf_op jit(solution)/shard_map/ppermute | solution.py:260
  114.4 7.9 %copy-start.16 = (s32[64,16]{0,1:T(8,128)S(1)}, s32[64,16]{0,1:T(8,128)}, u32[]{:S(2)}) copy-start(s32[64,16]{0,1:T(8,128)} %param.15) | copy-start | bytes 12292
  114.5 8.0 %copy-start.11 = (s32[5]{0:T(128)S(1)}, s32[5]{0:T(128)}, u32[]{:S(2)}) copy-start(s32[5]{0:T(128)} %stack.38.where) | copy-start | bytes 64
  114.5 8.0 %copy-start.14 = (s32[128]{0:T(128)S(1)}, s32[128]{0:T(128)}, u32[]{:S(2)}) copy-start(s32[128]{0:T(128)} %place.1) | copy-start | bytes 1540
  114.5 17.9 %copy-start = (bf16[16,128,256]{2,1,0:T(8,128)(2,1)S(1)}, bf16[16,128,256]{2,1,0:T(8,128)(2,1)}, u32[]{:S(2)}) copy-start(bf16[16,128,256]{2,1,0:T(8,128)(2,1)} %all-gather.2.cloned.1.call-done.docs_mine) | copy-start | bytes 3145732
  117.6 14.8 %all-to-all-start.3 = ((bf16[4,576,128]{2,1,0:T(8,128)(2,1)}), bf16[4,576,128]{2,1,0:T(8,128)(2,1)S(1)}, u32[]{:S(2)}, u32[]{:S(2)}) async-start(bf16[4,576,128]{2,1,0:T(8,128)(2,1)} %shard_map.94), calls=%async_computation.3 | async-start | bytes 1179648 | tf_op jit(solution)/shard_map/all_to_all | solution.py:248
  (9 other events, 18.8 us)
Sparse Core Ops, SparseCore 0:
  30.2 57.1 all-gather.1

commit v3 on v1

--- a/solution.py
+++ b/solution.py
@@ -23,7 +23,7 @@
 
 VMEM = pl.BlockSpec(memory_space=pltpu.VMEM)
 SMEM = pl.BlockSpec(memory_space=pltpu.SMEM)
-PARAMS = pltpu.CompilerParams(vmem_limit_bytes=40 * 1024 * 1024)
+PARAMS = pltpu.CompilerParams(vmem_limit_bytes=24 * 1024 * 1024)
 
 
 def call(kernel, outs, args, specs, out_specs=None, scratch=(), flops=0, moved=0):
@@ -59,7 +59,7 @@
 def norm_kernel(where, mine, other, gain, out):
     core = where[3]
     for row in range(NX):
-        rows = pl.ds(row * SEQ, SEQ)
+        rows = pl.ds(pl.multiple_of(lax.rem(where[0] + row, NX) * SEQ, SEQ), SEQ)
         total = jnp.zeros((SEQ, HEAD), F32)
         for src in (mine, other):
             for y in range(4):
@@ -250,8 +250,20 @@
     parts = call(pack_kernel, shape((4, 4, 96, HEAD), BF16), (wq, wk, wv), [VMEM] * 3)
     near = exchange(parts.reshape(16, 96, HEAD), ("x", "zh"))
 
-    by_y = spread(tokens, "y", 4)
-    mine = spread(by_y, "x", NX)
+    def from_z(array, step):
+        return lax.ppermute(array, z_axes, [((i + step) % NZ, i) for i in range(NZ)])
+
+    tokens, _ = lax.optimization_barrier((tokens, parts))
+    by_y = lax.all_gather(tokens, "y")
+    def from_x(array, step):
+        return lax.ppermute(array, "x", [((i + step) % NX, i) for i in range(NX)])
+
+    mine = jnp.concatenate(
+        [by_y, from_x(by_y, 1), from_x(by_y[0:2], 2), from_x(by_y[2:4], -2), from_x(by_y, -1)]
+    ).reshape(4, 4, SEQ, 512)
+    ahead = from_z(near, 1)
+    behind = from_z(near, -1)
+    mine, ahead, behind = lax.optimization_barrier((mine, ahead, behind))
     other = lax.ppermute(mine, "core", [(0, 1), (1, 0)])
     gain = norm_gain.astype(F32).reshape(8, 1, 512)
     normed = call(
@@ -272,13 +284,8 @@
         scratch=[pltpu.SMEM((NX * NZ,), jnp.int32)],
     )
 
-    def from_z(array, step):
-        return lax.ppermute(array, z_axes, [((i + step) % NZ, i) for i in range(NZ)])
-
-    ahead = from_z(near, 1)
-    behind = from_z(near, -1)
-    far_a = from_z(near[0:8], 2)
-    far_b = from_z(near[8:16], -2)
+    far_a = from_z(ahead[0:8], 1)
+    far_b = from_z(behind[8:16], -1)
     send = call(
         project_kernel,
         shape((NX, ROWS + HALF, HEAD), BF16),

time: 192 us -> 166 us (0.86)
  blocking collectives: 85.2 us -> 36.5 us
  starting transfers between devices: 26.4 us -> 59 us
  waiting for transfers between devices: 34.2 us -> 16.1 us
  local copies, waits for them, and re-layouts: 5.53 us -> 12.1 us
  Pallas kernels: 24.1 us -> 26.5 us
    all_to_all x4 -> x2, blocking collectives: 85.2 us -> 22.8 us  [exchange(): return lax.all_to_all(array, axes, 0, 0, tiled=True)]
    all_to_all x3, waiting for transfers between devices: 28.3 us -> 4.95 us  [exchange(): return lax.all_to_all(array, axes, 0, 0, tiled=True)]
    all_to_all x3, starting transfers between devices: 11.4 us -> 26.9 us  [exchange(): return lax.all_to_all(array, axes, 0, 0, tiled=True)]
    ppermute x0 -> x4, starting transfers between devices: none -> 14.4 us  [from_x(): return lax.ppermute(array, 'x', [((i + step) % NX, i) for i in range(NX)])]
    all_gather x0 -> x1, blocking collectives: none -> 13.7 us  [shards(): by_y = lax.all_gather(tokens, 'y')]
    unnamed x17 -> x21, local copies, waits for them, and re-layouts: 1.71 us -> 7.12 us
    ppermute x4, waiting for transfers between devices: 5.2 us -> 8.47 us  [from_z(): lax.ppermute(array, z_axes, [((i + step) % NZ, i) for i in range(NZ)])]
    ppermute x4, starting transfers between devices: 13.1 us -> 15.7 us  [from_z(): lax.ppermute(array, z_axes, [((i + step) % NZ, i) for i in range(NZ)])]
  transfers between devices with their start and end apart: 9 -> 13, of which waited for: 4 -> 5; matrix products, arithmetic and copies ran while one was open for 1% -> 5% of each run, Pallas kernels for 6% -> 7%
where the time goes in v3:
time: 166 us; the launch traced here: 164 us
  starting transfers between devices  59 us (36%)
  blocking collectives  36.5 us (22%)
  Pallas kernels  26.5 us (16%)
  waiting for transfers between devices  16.1 us (10%)
  between operations  13.6 us (8%)
  local copies, waits for them, and re-layouts  12.1 us (7%)
    all_to_all x3, starting transfers between devices, exchange(): return lax.all_to_all(array, axes, 0, 0, tiled=True)  26.9 us
    pallas_call x7, Pallas kernels, call(): pl.pallas_call(kernel, out_shape=outs, in_specs=specs, out_specs=VMEM if...  26.5 us
    all_to_all x2, blocking collectives, exchange(): return lax.all_to_all(array, axes, 0, 0, tiled=True)  22.8 us
    ppermute x4, starting transfers between devices, from_z(): lax.ppermute(array, z_axes, [((i + step) % NZ, i) for i in range(NZ)])  15.7 us
    ppermute x4, starting transfers between devices, from_x(): return lax.ppermute(array, 'x', [((i + step) % NX, i) for i in range(NX)])  14.4 us
    all_gather x1, blocking collectives, shards(): by_y = lax.all_gather(tokens, 'y')  13.7 us
    ppermute x4, waiting for transfers between devices, from_z(): lax.ppermute(array, z_axes, [((i + step) % NZ, i) for i in range(NZ)])  8.47 us
    unnamed x21, local copies, waits for them, and re-layouts  7.12 us
  transfers between devices with their start and end apart: 13, of which 5 were waited for; matrix products, arithmetic and copies ran while one was open for 5% of the time, Pallas kernels for 7%

profile of v3, /device:TPU:24, one launch (start us, length us, event | category | flops | bytes accessed | tf_op | source)
XLA Modules:
  0.0 164.0 jit_solution(8772017891349524877)
XLA Ops:
  9.6 17.7 %all-to-all-start.1 = ((bf16[16,96,128]{2,1,0:T(8,128)(2,1)}), bf16[16,96,128]{2,1,0:T(8,128)(2,1)S(1)}, u32[]{:S(2)}, u32[]{:S(2)}) async-start(bf16[16,96,128]{2,1,0:T(8,128)(2,1)} %bitcast.9), calls=%async_computation.1 | async-start | bytes 786432 | tf_op jit(solution)/shard_map/all_to_all | solution.py:236
  28.0 13.7 %all-gather = bf16[512,512]{1,0:T(8,128)(2,1)} all-gather(bf16[128,512]{1,0:T(8,128)(2,1)} %param.9), channel_id=2, replica_groups=mesh['x'=4,'zh'=4,'zl'=4,'y'=4,'core'=2] {'y'}, dimensions={0}, use_global_device_ids=true | all-gather | bytes 655360 | tf_op jit(solution)/shard_map/all_gather | solution.py:257
  41.8 5.2 %collective-permute-start = (bf16[4,128,512]{2,1,0:T(8,128)(2,1)}, bf16[4,128,512]{2,1,0:T(8,128)(2,1)}, u32[]{:S(2)}, u32[]{:S(2)}) collective-permute-start(bf16[4,128,512]{2,1,0:T(8,128)(2,1)} %bitcast.5), channel_id=1, source_target_pairs={{128,0},{256,128},{384,256},{0,384},{129,1},{257,129},{385,257},{1... | collective-permute-start | bytes 1572872 | tf_op jit(solution)/shard_map/ppermute | solution.py:259
  46.9 1.9 %collective-permute-start.3 = (bf16[4,128,512]{2,1,0:T(8,128)(2,1)}, bf16[4,128,512]{2,1,0:T(8,128)(2,1)}, u32[]{:S(2)}, u32[]{:S(2)}) collective-permute-start(bf16[4,128,512]{2,1,0:T(8,128)(2,1)} %bitcast.5), channel_id=1, source_target_pairs={{384,0},{0,128},{128,256},{256,384},{385,1},{1,129},{129,257},{257... | collective-permute-start | bytes 1572872 | tf_op jit(solution)/shard_map/ppermute | solution.py:259
  48.9 1.9 %fusion = (bf16[256,512]{1,0:T(8,128)(2,1)}, bf16[256,512]{1,0:T(8,128)(2,1)}) fusion(bf16[512,512]{1,0:T(8,128)(2,1)} %all-gather), kind=kLoop, calls=%fused_computation.6 | loop fusion | bytes 1048576 | tf_op jit(solution)/shard_map/slice | solution.py:262
  50.7 4.2 %collective-permute-start.1 = (bf16[2,128,512]{2,1,0:T(8,128)(2,1)}, bf16[2,128,512]{2,1,0:T(8,128)(2,1)}, u32[]{:S(2)}, u32[]{:S(2)}) collective-permute-start(bf16[2,128,512]{2,1,0:T(8,128)(2,1)} %bitcast.6), channel_id=1, source_target_pairs={{256,0},{384,128},{0,256},{128,384},{257,1},{385,129},{1,257},{129... | collective-permute-start | bytes 786440 | tf_op jit(solution)/shard_map/ppermute | solution.py:259
  55.0 3.1 %collective-permute-start.2 = (bf16[2,128,512]{2,1,0:T(8,128)(2,1)}, bf16[2,128,512]{2,1,0:T(8,128)(2,1)S(1)}, u32[]{:S(2)}, u32[]{:S(2)}) collective-permute-start(bf16[2,128,512]{2,1,0:T(8,128)(2,1)} %bitcast.7), channel_id=1, source_target_pairs={{256,0},{384,128},{0,256},{128,384},{257,1},{385,129},{1,257},{129... | collective-permute-start | bytes 786440 | tf_op jit(solution)/shard_map/ppermute | solution.py:259
  59.2 5.8 %collective-permute-start.4 = (bf16[16,96,128]{2,1,0:T(8,128)(2,1)S(1)}, bf16[16,96,128]{2,1,0:T(8,128)(2,1)S(1)}, u32[]{:S(2)}, u32[]{:S(2)}) collective-permute-start(bf16[16,96,128]{2,1,0:T(8,128)(2,1)S(1)} %all-to-all-done.1.near), channel_id=1, source_target_pairs={{8,0},{16,8},{24,16},{32,24},{40,32},{48,40},{56,48},{64,56},{72,6... | collective-permute-start | bytes 1179656 | tf_op jit(solution)/shard_map/ppermute | solution.py:254
  65.0 2.0 %collective-permute-done = bf16[4,128,512]{2,1,0:T(8,128)(2,1)} collective-permute-done((bf16[4,128,512]{2,1,0:T(8,128)(2,1)}, bf16[4,128,512]{2,1,0:T(8,128)(2,1)}, u32[]{:S(2)}, u32[]{:S(2)}) %collective-permute-start) | collective-permute-done | bytes 524320 | tf_op jit(solution)/shard_map/ppermute | solution.py:259
  67.0 4.1 %collective-permute-start.5 = (bf16[16,96,128]{2,1,0:T(8,128)(2,1)S(1)}, bf16[16,96,128]{2,1,0:T(8,128)(2,1)S(1)}, u32[]{:S(2)}, u32[]{:S(2)}) collective-permute-start(bf16[16,96,128]{2,1,0:T(8,128)(2,1)S(1)} %all-to-all-done.1.near), channel_id=1, source_target_pairs={{120,0},{0,8},{8,16},{16,24},{24,32},{32,40},{40,48},{48,56},{56,6... | collective-permute-start | bytes 1179656 | tf_op jit(solution)/shard_map/ppermute | solution.py:254
  75.3 7.2 %collective-permute-done.5.behind = bf16[16,96,128]{2,1,0:T(8,128)(2,1)S(1)} collective-permute-done((bf16[16,96,128]{2,1,0:T(8,128)(2,1)S(1)}, bf16[16,96,128]{2,1,0:T(8,128)(2,1)S(1)}, u32[]{:S(2)}, u32[]{:S(2)}) %collective-permute-start.5) | collective-permute-done | bytes 393248 | tf_op jit(solution)/shard_map/ppermute | solution.py:254
  82.4 1.9 %collective-permute-start.6 = (bf16[4,4,128,512]{3,2,1,0:T(8,128)(2,1)S(1)}, bf16[4,4,128,512]{3,2,1,0:T(8,128)(2,1)}, u32[]{:S(2)}, u32[]{:S(2)}) collective-permute-start(bf16[4,4,128,512]{3,2,1,0:T(8,128)(2,1)S(1)} %bitcast.11), channel_id=1, source_target_pairs={{0,1},{1,0},{2,3},{3,2},{4,5},{5,4},{6,7},{7,6},{8,9},{9,8},{10,11... | collective-permute-start | bytes 6291464 | tf_op jit(solution)/shard_map/ppermute | solution.py:267
  85.0 3.3 %collective-permute-start.7 = (bf16[8,96,128]{2,1,0:T(8,128)(2,1)}, bf16[8,96,128]{2,1,0:T(8,128)(2,1)S(1)}, u32[]{:S(2)}, u32[]{:S(2)}) collective-permute-start(bf16[8,96,128]{2,1,0:T(8,128)(2,1)} %slice.14), channel_id=1, source_target_pairs={{8,0},{16,8},{24,16},{32,24},{40,32},{48,40},{56,48},{64,56},{72,6... | collective-permute-start | bytes 589832 | tf_op jit(solution)/shard_map/ppermute | solution.py:254
  89.0 2.5 %collective-permute-start.8 = (bf16[8,96,128]{2,1,0:T(8,128)(2,1)}, bf16[8,96,128]{2,1,0:T(8,128)(2,1)}, u32[]{:S(2)}, u32[]{:S(2)}) collective-permute-start(bf16[8,96,128]{2,1,0:T(8,128)(2,1)} %slice.15), channel_id=1, source_target_pairs={{120,0},{0,8},{8,16},{16,24},{24,32},{32,40},{40,48},{48,56},{56,6... | collective-permute-start | bytes 589832 | tf_op jit(solution)/shard_map/ppermute | solution.py:254
  92.2 4.8 %all-to-all-start = ((s32[4,2,16]{2,1,0:T(2,128)}), s32[4,2,16]{2,1,0:T(2,128)S(1)}, u32[]{:S(2)}, u32[]{:S(2)}) async-start(s32[4,2,16]{2,1,0:T(2,128)} %broadcast_in_dim.2), calls=%async_computation | async-start | bytes 8192 | tf_op jit(solution)/shard_map/all_to_all | solution.py:236
  97.1 3.7 %shard_map.93.normed = bf16[8,512,512]{2,1,0:T(8,128)(2,1)S(1)} custom-call(s32[4]{0:T(128)S(1)} %pad_add_fusion.where, bf16[4,4,128,512]{3,2,1,0:T(8,128)(2,1)S(1)} %bitcast.12, bf16[4,4,128,512]{3,2,1,0:T(8,128)(2,1)} %collective-permute-done.6.other, f32[8,1,512]{2,1,0:T(1,128)S(1)} %bitcast.13), custom_call_target="tpu_custom_call" | custom-call | flops 16777216 | bytes 8388608 | tf_op jit(solution)/shard_map/pallas_call | solution.py:30
  101.2 3.5 %shard_map.94 = bf16[4,576,128]{2,1,0:T(8,128)(2,1)} custom-call(s32[4]{0:T(128)S(1)} %pad_add_fusion.where, bf16[8,512,512]{2,1,0:T(8,128)(2,1)S(1)} %shard_map.93.normed, bf16[16,96,128]{2,1,0:T(8,128)(2,1)S(1)} %all-to-all-done.1.near, bf16[16,96,128]{2,1,0:T(8,128)(2,1)S(1)} %collective-permute-done.4.ahead, ...), custom_call_target="tpu_custom_call" | custom-call | flops 1073741824 | bytes 8388608 | tf_op jit(solution)/shard_map/pallas_call | solution.py:30
  104.7 4.4 %all-to-all-start.2 = ((bf16[4,576,128]{2,1,0:T(8,128)(2,1)}), bf16[4,576,128]{2,1,0:T(8,128)(2,1)S(1)}, u32[]{:S(2)}, u32[]{:S(2)}) async-start(bf16[4,576,128]{2,1,0:T(8,128)(2,1)} %shard_map.94), calls=%async_computation.2 | async-start | bytes 1179648 | tf_op jit(solution)/shard_map/all_to_all | solution.py:236
  109.2 4.7 %shard_map.91.units = s32[128]{0:T(128)S(1)} custom-call(s32[4]{0:T(128)S(1)} %pad_add_fusion.where, s32[64,16]{1,0:T(8,128)S(1)} %copy.11.lists, s32[128]{0:T(128)S(1)} %copy-done.4, s32[8,16]{1,0:T(8,128)S(1)} %bitcast.14), custom_call_target="tpu_custom_call" | custom-call | tf_op jit(solution)/shard_map/pallas_call | solution.py:30
  114.0 4.9 %all-to-all-done.2.got = bf16[4,576,128]{2,1,0:T(8,128)(2,1)S(1)} async-done(((bf16[4,576,128]{2,1,0:T(8,128)(2,1)}), bf16[4,576,128]{2,1,0:T(8,128)(2,1)S(1)}, u32[]{:S(2)}, u32[]{:S(2)}) %all-to-all-start.2) | async-done | bytes 589856 | tf_op jit(solution)/shard_map/all_to_all | solution.py:236
  120.5 5.8 %shard_map.95 = f32[4,8,512]{2,1,0:T(8,128)S(1)} custom-call(s32[4]{0:T(128)S(1)} %pad_add_fusion.where, s32[128]{0:T(128)S(1)} %shard_map.91.units, bf16[4,576,128]{2,1,0:T(8,128)(2,1)S(1)} %all-to-all-done.2.got, bf16[32,128,256]{2,1,0:T(8,128)(2,1)S(1)} %copy-done), custom_call_target="tpu_custom_call" | custom-call | tf_op jit(solution)/shard_map/pallas_call | solution.py:30
  126.3 8.0 %all_to_all.25.all_stats = f32[4,8,512]{2,1,0:T(8,128)S(1)} all-to-all(f32[4,8,512]{2,1,0:T(8,128)S(1)} %shard_map.95), channel_id=1, replica_groups=mesh['x'=4,'zh'=4,'zl'=4,'y'=4,'core'=2] {'x'}, dimensions={0} | all-to-all | bytes 131072 | tf_op jit(solution)/shard_map/all_to_all | solution.py:236
  134.3 7.3 %shard_map.96 = f32[4,128,512]{2,1,0:T(8,128)S(1)} custom-call(s32[4]{0:T(128)S(1)} %pad_add_fusion.where, s32[128]{0:T(128)S(1)} %shard_map.91.units, bf16[4,576,128]{2,1,0:T(8,128)(2,1)S(1)} %all-to-all-done.2.got, bf16[32,128,256]{2,1,0:T(8,128)(2,1)S(1)} %copy-done, f32[4,8,512]{2,1,0:T(8,128)S(1)} %all_to_all.25.all_stats), custom_call_target="tpu_custom_call" | custom-call | tf_op jit(solution)/shard_map/pallas_call | solution.py:30
  141.5 14.8 %all_to_all.26.got = f32[4,128,512]{2,1,0:T(8,128)S(1)} all-to-all(f32[4,128,512]{2,1,0:T(8,128)S(1)} %shard_map.96), channel_id=1, replica_groups=mesh['x'=4,'zh'=4,'zl'=4,'y'=4,'core'=2] {'x'}, dimensions={0} | all-to-all | bytes 2097152 | tf_op jit(solution)/shard_map/all_to_all | solution.py:236
  (41 shorter events, 13.9 us)
Async XLA Ops:
  6.5 0.8 copy-start.1
  7.4 0.7 copy-start.2
  8.1 0.7 copy-start.3
  9.6 49.6 %all-to-all-start.1 = ((bf16[16,96,128]{2,1,0:T(8,128)(2,1)}), bf16[16,96,128]{2,1,0:T(8,128)(2,1)S(1)}, u32[]{:S(2)}, u32[]{:S(2)}) async-start(bf16[16,96,128]{2,1,0:T(8,128)(2,1)} %bitcast.9), calls=%async_computation.1 | async-start | bytes 786432 | tf_op jit(solution)/shard_map/all_to_all | solution.py:236
  27.3 86.7 %all-gather.3.cloned.1.call-start = ((), (), s32[]{:S(2)}) async-start(), calls=%async_computation.5 | async-start | bytes 2228224 | tf_op jit(solution)/shard_map/all_gather | solution.py:246
  41.8 25.3 %collective-permute-start = (bf16[4,128,512]{2,1,0:T(8,128)(2,1)}, bf16[4,128,512]{2,1,0:T(8,128)(2,1)}, u32[]{:S(2)}, u32[]{:S(2)}) collective-permute-start(bf16[4,128,512]{2,1,0:T(8,128)(2,1)} %bitcast.5), channel_id=1, source_target_pairs={{128,0},{256,128},{384,256},{0,384},{129,1},{257,129},{385,257},{1... | collective-permute-start | bytes 1572872 | tf_op jit(solution)/shard_map/ppermute | solution.py:259
  46.9 26.3 %collective-permute-start.3 = (bf16[4,128,512]{2,1,0:T(8,128)(2,1)}, bf16[4,128,512]{2,1,0:T(8,128)(2,1)}, u32[]{:S(2)}, u32[]{:S(2)}) collective-permute-start(bf16[4,128,512]{2,1,0:T(8,128)(2,1)} %bitcast.5), channel_id=1, source_target_pairs={{384,0},{0,128},{128,256},{256,384},{385,1},{1,129},{129,257},{257... | collective-permute-start | bytes 1572872 | tf_op jit(solution)/shard_map/ppermute | solution.py:259
  50.7 21.5 %collective-permute-start.1 = (bf16[2,128,512]{2,1,0:T(8,128)(2,1)}, bf16[2,128,512]{2,1,0:T(8,128)(2,1)}, u32[]{:S(2)}, u32[]{:S(2)}) collective-permute-start(bf16[2,128,512]{2,1,0:T(8,128)(2,1)} %bitcast.6), channel_id=1, source_target_pairs={{256,0},{384,128},{0,256},{128,384},{257,1},{385,129},{1,257},{129... | collective-permute-start | bytes 786440 | tf_op jit(solution)/shard_map/ppermute | solution.py:259
  55.0 18.3 %collective-permute-start.2 = (bf16[2,128,512]{2,1,0:T(8,128)(2,1)}, bf16[2,128,512]{2,1,0:T(8,128)(2,1)S(1)}, u32[]{:S(2)}, u32[]{:S(2)}) collective-permute-start(bf16[2,128,512]{2,1,0:T(8,128)(2,1)} %bitcast.7), channel_id=1, source_target_pairs={{256,0},{384,128},{0,256},{128,384},{257,1},{385,129},{1,257},{129... | collective-permute-start | bytes 786440 | tf_op jit(solution)/shard_map/ppermute | solution.py:259
  59.2 32.4 %copy-start.7 = (s32[2,16]{1,0:T(2,128)S(1)}, s32[2,16]{1,0:T(2,128)}, u32[]{:S(2)}) copy-start(s32[2,16]{1,0:T(2,128)} %param.17) | copy-start | bytes 388
  59.2 37.8 %copy-start.5 = (bf16[4096]{0:T(1024)(128)(2,1)S(1)}, bf16[4096]{0:T(1024)(128)(2,1)}, u32[]{:S(2)}) copy-start(bf16[4096]{0:T(1024)(128)(2,1)} %param.10) | copy-start | bytes 24580
  59.2 16.0 %collective-permute-start.4 = (bf16[16,96,128]{2,1,0:T(8,128)(2,1)S(1)}, bf16[16,96,128]{2,1,0:T(8,128)(2,1)S(1)}, u32[]{:S(2)}, u32[]{:S(2)}) collective-permute-start(bf16[16,96,128]{2,1,0:T(8,128)(2,1)S(1)} %all-to-all-done.1.near), channel_id=1, source_target_pairs={{8,0},{16,8},{24,16},{32,24},{40,32},{48,40},{56,48},{64,56},{72,6... | collective-permute-start | bytes 1179656 | tf_op jit(solution)/shard_map/ppermute | solution.py:254
  67.0 15.4 %collective-permute-start.5 = (bf16[16,96,128]{2,1,0:T(8,128)(2,1)S(1)}, bf16[16,96,128]{2,1,0:T(8,128)(2,1)S(1)}, u32[]{:S(2)}, u32[]{:S(2)}) collective-permute-start(bf16[16,96,128]{2,1,0:T(8,128)(2,1)S(1)} %all-to-all-done.1.near), channel_id=1, source_target_pairs={{120,0},{0,8},{8,16},{16,24},{24,32},{32,40},{40,48},{48,56},{56,6... | collective-permute-start | bytes 1179656 | tf_op jit(solution)/shard_map/ppermute | solution.py:254
  82.4 14.7 %collective-permute-start.6 = (bf16[4,4,128,512]{3,2,1,0:T(8,128)(2,1)S(1)}, bf16[4,4,128,512]{3,2,1,0:T(8,128)(2,1)}, u32[]{:S(2)}, u32[]{:S(2)}) collective-permute-start(bf16[4,4,128,512]{3,2,1,0:T(8,128)(2,1)S(1)} %bitcast.11), channel_id=1, source_target_pairs={{0,1},{1,0},{2,3},{3,2},{4,5},{5,4},{6,7},{7,6},{8,9},{9,8},{10,11... | collective-permute-start | bytes 6291464 | tf_op jit(solution)/shard_map/ppermute | solution.py:267
  85.0 15.8 %collective-permute-start.7 = (bf16[8,96,128]{2,1,0:T(8,128)(2,1)}, bf16[8,96,128]{2,1,0:T(8,128)(2,1)S(1)}, u32[]{:S(2)}, u32[]{:S(2)}) collective-permute-start(bf16[8,96,128]{2,1,0:T(8,128)(2,1)} %slice.14), channel_id=1, source_target_pairs={{8,0},{16,8},{24,16},{32,24},{40,32},{48,40},{56,48},{64,56},{72,6... | collective-permute-start | bytes 589832 | tf_op jit(solution)/shard_map/ppermute | solution.py:254
  89.0 12.2 %collective-permute-start.8 = (bf16[8,96,128]{2,1,0:T(8,128)(2,1)}, bf16[8,96,128]{2,1,0:T(8,128)(2,1)}, u32[]{:S(2)}, u32[]{:S(2)}) collective-permute-start(bf16[8,96,128]{2,1,0:T(8,128)(2,1)} %slice.15), channel_id=1, source_target_pairs={{120,0},{0,8},{8,16},{16,24},{24,32},{32,40},{40,48},{48,56},{56,6... | collective-permute-start | bytes 589832 | tf_op jit(solution)/shard_map/ppermute | solution.py:254
  92.2 12.5 %all-to-all-start = ((s32[4,2,16]{2,1,0:T(2,128)}), s32[4,2,16]{2,1,0:T(2,128)S(1)}, u32[]{:S(2)}, u32[]{:S(2)}) async-start(s32[4,2,16]{2,1,0:T(2,128)} %broadcast_in_dim.2), calls=%async_computation | async-start | bytes 8192 | tf_op jit(solution)/shard_map/all_to_all | solution.py:236
  100.8 8.3 %copy-start.6 = (s32[64,16]{0,1:T(8,128)S(1)}, s32[64,16]{0,1:T(8,128)}, u32[]{:S(2)}) copy-start(s32[64,16]{0,1:T(8,128)} %param.15) | copy-start | bytes 12292
  100.8 8.4 %copy-start.4 = (s32[128]{0:T(128)S(1)}, s32[128]{0:T(128)}, u32[]{:S(2)}) copy-start(s32[128]{0:T(128)} %place.1) | copy-start | bytes 1540
  104.7 14.2 %all-to-all-start.2 = ((bf16[4,576,128]{2,1,0:T(8,128)(2,1)}), bf16[4,576,128]{2,1,0:T(8,128)(2,1)S(1)}, u32[]{:S(2)}, u32[]{:S(2)}) async-start(bf16[4,576,128]{2,1,0:T(8,128)(2,1)} %shard_map.94), calls=%async_computation.2 | async-start | bytes 1179648 | tf_op jit(solution)/shard_map/all_to_all | solution.py:236
  118.9 1.6 copy-start
Sparse Core Ops, SparseCore 0:
  30.2 76.2 all-gather.2

commit v4 on v3

--- a/solution.py
+++ b/solution.py
@@ -46,33 +46,31 @@
     return jnp.where(lane < HALF, left, right).astype(BF16)
 
 
-def pack_kernel(wq, wk, wv, out):
+def pack_kernel(wq, wk, wv, use, out):
     for part in range(NX):
         src = wk if part < 2 else wv
         at = HALF * (part % 2)
-        packed = side_by_side(src[0:32, :], src[32:64, :], at, at)
-        for copy in range(4):
-            out[part, copy, 0:64, :] = wq[:, part * HEAD : (part + 1) * HEAD]
-            out[part, copy, 64:96, :] = packed
+        out[part, 0:64, :] = wq[:, part * HEAD : (part + 1) * HEAD]
+        out[part, 64:96, :] = side_by_side(src[0:32, :], src[32:64, :], at, at)
+        out[part, 96:112, :] = use[...]
 
 
 def norm_kernel(where, mine, other, gain, out):
     core = where[3]
-    for row in range(NX):
-        rows = pl.ds(pl.multiple_of(lax.rem(where[0] + row, NX) * SEQ, SEQ), SEQ)
+    for x in range(NX):
+        rows = pl.ds(x * SEQ, SEQ)
         total = jnp.zeros((SEQ, HEAD), F32)
         for src in (mine, other):
             for y in range(4):
                 for c in range(4):
-                    feats = src[row, y, :, c * HEAD : (c + 1) * HEAD].astype(F32)
+                    feats = src[x * 4 + y, :, c * HEAD : (c + 1) * HEAD].astype(F32)
                     total = total + feats * feats
         power = jnp.sum(total, axis=-1, keepdims=True) * (1.0 / 4096.0)
         factor = lax.rsqrt(power + 1e-05)
-        for src, flip in ((mine, 0), (other, 1)):
-            side = core if flip == 0 else 1 - core
+        for src, side in ((mine, core), (other, 1 - core)):
             for y in range(4):
                 slot = 2 * y + side
-                feats = src[row, y].astype(F32)
+                feats = src[x * 4 + y].astype(F32)
                 out[slot, rows, :] = (feats * factor * gain[slot]).astype(BF16)
 
 
@@ -105,20 +103,14 @@
     units[0] = lax.fori_loop(0, NX * NZ, compact, 0)
 
 
-def project_kernel(where, normed, near, ahead, far_a, far_b, behind, send, weights):
-    lane_part = where[2]
-    for step in range(4):
-        row = lax.rem(lane_part + step, 4) * HALF
+def project_kernel(where, normed, near, ahead, far, behind, send, weights):
+    z = where[1]
+    for step, blocks in ((0, near), (1, ahead), (2, far), (NZ - 1, behind)):
+        at = lax.rem(z + step, NZ)
         for b in range(16):
-            if step == 0:
-                block = near[b]
-            elif step == 1:
-                block = ahead[b]
-            elif step == 3:
-                block = behind[b]
-            else:
-                block = far_a[b] if b < 8 else far_b[b - 8]
-            base = pl.multiple_of(b * 256 + row, HALF)
+            block = blocks[b]
+            depth = (b % 4) * 1024 + lax.rem(at + (b // 4) * 4, NZ) * HALF
+            base = pl.multiple_of(depth, HALF)
             packed = block[64:96, :]
             weights[pl.ds(base, 64), 0:HEAD] = block[0:64, :]
             weights[pl.ds(base, 32), HEAD : 2 * HEAD] = packed
@@ -245,25 +237,28 @@
     z_axes = ("zh", "zl")
     docs = lax.all_gather(doc_cache, z_axes, axis=0, tiled=True)
     x, zh, zl = lax.axis_index("x"), lax.axis_index("zh"), lax.axis_index("zl")
-    where = jnp.stack([x, zh * 4 + zl, zl, lax.axis_index("core")]).astype(jnp.int32)
-
-    parts = call(pack_kernel, shape((4, 4, 96, HEAD), BF16), (wq, wk, wv), [VMEM] * 3)
-    near = exchange(parts.reshape(16, 96, HEAD), ("x", "zh"))
+    y, core = lax.axis_index("y"), lax.axis_index("core")
+    where = jnp.stack([x, zh * 4 + zl, zl, core, y]).astype(jnp.int32)
 
     def from_z(array, step):
         return lax.ppermute(array, z_axes, [((i + step) % NZ, i) for i in range(NZ)])
 
-    tokens, _ = lax.optimization_barrier((tokens, parts))
-    by_y = lax.all_gather(tokens, "y")
-    def from_x(array, step):
-        return lax.ppermute(array, "x", [((i + step) % NX, i) for i in range(NX)])
-
-    mine = jnp.concatenate(
-        [by_y, from_x(by_y, 1), from_x(by_y[0:2], 2), from_x(by_y[2:4], -2), from_x(by_y, -1)]
-    ).reshape(4, 4, SEQ, 512)
+    def from_y(array, step):
+        return lax.ppermute(array, "y", [((i + step) % 4, i) for i in range(4)])
+
+    flags = jnp.pad(block_use.astype(BF16), ((0, 14), (0, HEAD - PICKS)))
+    packed = call(
+        pack_kernel, shape((NX, 112, HEAD), BF16), (wq, wk, wv, flags), [VMEM] * 4
+    )
+    by_x = exchange(packed, "x")
+    part = by_x[:, 0:96]
+    near = jnp.concatenate([part, from_z(part, 4), from_z(part, 8), from_z(part, 12)])
+
+    tokens, _ = lax.optimization_barrier((tokens, by_x))
+    mine = spread(tokens, ("x", "y"), 16)
     ahead = from_z(near, 1)
     behind = from_z(near, -1)
-    mine, ahead, behind = lax.optimization_barrier((mine, ahead, behind))
+    mine, _, _ = lax.optimization_barrier((mine, ahead, behind))
     other = lax.ppermute(mine, "core", [(0, 1), (1, 0)])
     gain = norm_gain.astype(F32).reshape(8, 1, 512)
     normed = call(
@@ -274,7 +269,7 @@
         flops=ROWS * 4096 * 8,
         moved=8 << 20,
     )
-    use = spread(block_use, "x", NX).reshape(8, PICKS)
+    use = by_x[:, 96:98, 0:PICKS].astype(jnp.int32).reshape(8, PICKS)
     units = call(
         route_kernel,
         shape((UNITS,), jnp.int32),
@@ -284,13 +279,12 @@
         scratch=[pltpu.SMEM((NX * NZ,), jnp.int32)],
     )
 
-    far_a = from_z(ahead[0:8], 1)
-    far_b = from_z(behind[8:16], -1)
+    far = from_z(ahead, 1)
     send = call(
         project_kernel,
         shape((NX, ROWS + HALF, HEAD), BF16),
-        (where, normed, near, ahead, far_a, far_b, behind),
-        [SMEM] + [VMEM] * 6,
+        (where, normed, near, ahead, far, behind),
+        [SMEM] + [VMEM] * 5,
         scratch=[pltpu.VMEM((4096, 2 * HEAD), BF16)],
         flops=2 * ROWS * 4096 * 256,
         moved=8 << 20,

time: 166 us -> 171 us (1.030)
  waiting for transfers between devices: 16.1 us -> 46.8 us
  starting transfers between devices: 59 us -> 46.4 us
  Pallas kernels: 26.5 us -> 17 us
  local copies, waits for them, and re-layouts: 12.1 us -> 6.49 us
  blocking collectives: 36.5 us -> 38.7 us
    ppermute x4 -> x6, waiting for transfers between devices: 8.47 us -> 38.9 us  [from_z(): lax.ppermute(array, z_axes, [((i + step) % NZ, i) for i in range(NZ)])]
    ppermute x4 -> x6, starting transfers between devices: 15.7 us -> 32.5 us  [from_z(): lax.ppermute(array, z_axes, [((i + step) % NZ, i) for i in range(NZ)])]
    all_to_all x2 -> x3, blocking collectives: 22.8 us -> 38.7 us  [exchange(): return lax.all_to_all(array, axes, 0, 0, tiled=True)]
    all_to_all x3 -> x2, starting transfers between devices: 26.9 us -> 11.9 us  [exchange(): return lax.all_to_all(array, axes, 0, 0, tiled=True)]
    ppermute x4 -> x0, starting transfers between devices: 14.4 us -> none  [from_x(): return lax.ppermute(array, 'x', [((i + step) % NX, i) for i in range(NX)])]
    all_gather x1 -> x0, blocking collectives: 13.7 us -> none  [shards(): by_y = lax.all_gather(tokens, 'y')]
    pallas_call x7, Pallas kernels: 26.5 us -> 17 us  [call(): pl.pallas_call(kernel, out_shape=outs, in_specs=specs, out_specs=VMEM if...]
    slice x3 -> x2, local copies, waits for them, and re-layouts: 3.25 us -> 0.01 us  [the longest x1 0.01 us: shards(): part = by_x[:, 0:96]]
  transfers between devices with their start and end apart: 13 -> 10, of which waited for: 5 -> 7; matrix products, arithmetic and copies ran while one was open for 5% -> 0% of each run, Pallas kernels for 7% -> 7%
where the time goes in v4:
time: 171 us; the launch traced here: 170 us
  waiting for transfers between devices  46.8 us (27%)
  starting transfers between devices  46.4 us (27%)
  blocking collectives  38.7 us (23%)
  Pallas kernels  17 us (10%)
  between operations  13.6 us (8%)
  local copies, waits for them, and re-layouts  6.49 us (4%)
    ppermute x6, waiting for transfers between devices, from_z(): lax.ppermute(array, z_axes, [((i + step) % NZ, i) for i in range(NZ)])  38.9 us
    all_to_all x3, blocking collectives, exchange(): return lax.all_to_all(array, axes, 0, 0, tiled=True)  38.7 us
    ppermute x6, starting transfers between devices, from_z(): lax.ppermute(array, z_axes, [((i + step) % NZ, i) for i in range(NZ)])  32.5 us
    pallas_call x7, Pallas kernels, call(): pl.pallas_call(kernel, out_shape=outs, in_specs=specs, out_specs=VMEM if...  17 us
    all_to_all x2, starting transfers between devices, exchange(): return lax.all_to_all(array, axes, 0, 0, tiled=True)  11.9 us
    all_to_all x2, waiting for transfers between devices, exchange(): return lax.all_to_all(array, axes, 0, 0, tiled=True)  5.08 us
    unnamed x15, local copies, waits for them, and re-layouts  3.96 us
  transfers between devices with their start and end apart: 10, of which 7 were waited for; matrix products, arithmetic and copies ran while one was open for 0% of the time, Pallas kernels for 7%

profile of v4, /device:TPU:24, one launch (start us, length us, event | category | flops | bytes accessed | tf_op | source)
XLA Modules:
  0.0 169.8 jit_solution(7870652444460957536)
XLA Ops:
  9.6 10.0 %all_to_all.25 = bf16[4,112,128]{2,1,0:T(8,128)(2,1)S(1)} all-to-all(bf16[4,112,128]{2,1,0:T(8,128)(2,1)S(1)} %shard_map.91), channel_id=1, replica_groups=mesh['x'=4,'zh'=4,'zl'=4,'y'=4,'core'=2] {'x'}, dimensions={0} | all-to-all | bytes 229376 | tf_op jit(solution)/shard_map/all_to_all | solution.py:228
  19.6 2.4 %broadcast_in_dim.2 = bf16[16,128,512]{2,1,0:T(8,128)(2,1)} broadcast(bf16[128,512]{1,0:T(8,128)(2,1)} %param.9), dimensions={1,2} | broadcast | bytes 2228224 | tf_op jit(solution)/shard_map/broadcast_in_dim | solution.py:232
  22.0 7.5 %all-to-all-start.1 = ((bf16[16,128,512]{2,1,0:T(8,128)(2,1)}), bf16[16,128,512]{2,1,0:T(8,128)(2,1)S(1)}, u32[]{:S(2)}, u32[]{:S(2)}) async-start(bf16[16,128,512]{2,1,0:T(8,128)(2,1)} %broadcast_in_dim.2), calls=%async_computation.1 | async-start | bytes 4194304 | tf_op jit(solution)/shard_map/all_to_all | solution.py:228
  30.3 7.0 %collective-permute-start.2 = (bf16[4,96,128]{2,1,0:T(8,128)(2,1)S(1)}, bf16[4,96,128]{2,1,0:T(8,128)(2,1)S(1)}, u32[]{:S(2)}, u32[]{:S(2)}) collective-permute-start(bf16[4,96,128]{2,1,0:T(8,128)(2,1)S(1)} %slice.9), channel_id=1, source_target_pairs={{96,0},{104,8},{112,16},{120,24},{0,32},{8,40},{16,48},{24,56},{32... | collective-permute-start | bytes 294920 | tf_op jit(solution)/shard_map/ppermute | solution.py:244
  37.3 10.9 %collective-permute-start.1 = (bf16[4,96,128]{2,1,0:T(8,128)(2,1)S(1)}, bf16[4,96,128]{2,1,0:T(8,128)(2,1)S(1)}, u32[]{:S(2)}, u32[]{:S(2)}) collective-permute-start(bf16[4,96,128]{2,1,0:T(8,128)(2,1)S(1)} %slice.9), channel_id=1, source_target_pairs={{64,0},{72,8},{80,16},{88,24},{96,32},{104,40},{112,48},{120,56},{... | collective-permute-start | bytes 294920 | tf_op jit(solution)/shard_map/ppermute | solution.py:244
  48.2 5.5 %collective-permute-start = (bf16[4,96,128]{2,1,0:T(8,128)(2,1)S(1)}, bf16[4,96,128]{2,1,0:T(8,128)(2,1)S(1)}, u32[]{:S(2)}, u32[]{:S(2)}) collective-permute-start(bf16[4,96,128]{2,1,0:T(8,128)(2,1)S(1)} %slice.9), channel_id=1, source_target_pairs={{32,0},{40,8},{48,16},{56,24},{64,32},{72,40},{80,48},{88,56},{96,... | collective-permute-start | bytes 294920 | tf_op jit(solution)/shard_map/ppermute | solution.py:244
  53.7 3.2 %collective-permute-done.1 = bf16[4,96,128]{2,1,0:T(8,128)(2,1)S(1)} collective-permute-done((bf16[4,96,128]{2,1,0:T(8,128)(2,1)S(1)}, bf16[4,96,128]{2,1,0:T(8,128)(2,1)S(1)}, u32[]{:S(2)}, u32[]{:S(2)}) %collective-permute-start.1) | collective-permute-done | bytes 98336 | tf_op jit(solution)/shard_map/ppermute | solution.py:244
  56.9 8.9 %collective-permute-done = bf16[4,96,128]{2,1,0:T(8,128)(2,1)S(1)} collective-permute-done((bf16[4,96,128]{2,1,0:T(8,128)(2,1)S(1)}, bf16[4,96,128]{2,1,0:T(8,128)(2,1)S(1)}, u32[]{:S(2)}, u32[]{:S(2)}) %collective-permute-start) | collective-permute-done | bytes 98336 | tf_op jit(solution)/shard_map/ppermute | solution.py:244
  65.9 5.3 %collective-permute-start.3 = (bf16[16,96,128]{2,1,0:T(8,128)(2,1)S(1)}, bf16[16,96,128]{2,1,0:T(8,128)(2,1)S(1)}, u32[]{:S(2)}, u32[]{:S(2)}) collective-permute-start(bf16[16,96,128]{2,1,0:T(8,128)(2,1)S(1)} %pad_maximum_fusion.near), channel_id=1, source_target_pairs={{8,0},{16,8},{24,16},{32,24},{40,32},{48,40},{56,48},{64,56},{72,6... | collective-permute-start | bytes 1179656 | tf_op jit(solution)/shard_map/ppermute | solution.py:244
  71.2 1.9 %collective-permute-start.4 = (bf16[16,96,128]{2,1,0:T(8,128)(2,1)S(1)}, bf16[16,96,128]{2,1,0:T(8,128)(2,1)S(1)}, u32[]{:S(2)}, u32[]{:S(2)}) collective-permute-start(bf16[16,96,128]{2,1,0:T(8,128)(2,1)S(1)} %pad_maximum_fusion.near), channel_id=1, source_target_pairs={{120,0},{0,8},{8,16},{16,24},{24,32},{32,40},{40,48},{48,56},{56,6... | collective-permute-start | bytes 1179656 | tf_op jit(solution)/shard_map/ppermute | solution.py:244
  73.2 11.9 %collective-permute-done.3.ahead = bf16[16,96,128]{2,1,0:T(8,128)(2,1)S(1)} collective-permute-done((bf16[16,96,128]{2,1,0:T(8,128)(2,1)S(1)}, bf16[16,96,128]{2,1,0:T(8,128)(2,1)S(1)}, u32[]{:S(2)}, u32[]{:S(2)}) %collective-permute-start.3) | collective-permute-done | bytes 393248 | tf_op jit(solution)/shard_map/ppermute | solution.py:244
  85.0 5.2 %collective-permute-done.4.behind = bf16[16,96,128]{2,1,0:T(8,128)(2,1)S(1)} collective-permute-done((bf16[16,96,128]{2,1,0:T(8,128)(2,1)S(1)}, bf16[16,96,128]{2,1,0:T(8,128)(2,1)S(1)}, u32[]{:S(2)}, u32[]{:S(2)}) %collective-permute-start.4) | collective-permute-done | bytes 393248 | tf_op jit(solution)/shard_map/ppermute | solution.py:244
  90.2 1.9 %collective-permute-start.5 = (bf16[16,128,512]{2,1,0:T(8,128)(2,1)S(1)}, bf16[16,128,512]{2,1,0:T(8,128)(2,1)}, u32[]{:S(2)}, u32[]{:S(2)}) collective-permute-start(bf16[16,128,512]{2,1,0:T(8,128)(2,1)S(1)} %all-to-all-done.1.mine), channel_id=1, source_target_pairs={{0,1},{1,0},{2,3},{3,2},{4,5},{5,4},{6,7},{7,6},{8,9},{9,8},{10,11... | collective-permute-start | bytes 6291464 | tf_op jit(solution)/shard_map/ppermute | solution.py:262
  92.1 1.9 %collective-permute-start.6 = (bf16[16,96,128]{2,1,0:T(8,128)(2,1)S(1)}, bf16[16,96,128]{2,1,0:T(8,128)(2,1)}, u32[]{:S(2)}, u32[]{:S(2)}) collective-permute-start(bf16[16,96,128]{2,1,0:T(8,128)(2,1)S(1)} %collective-permute-done.3.ahead), channel_id=1, source_target_pairs={{8,0},{16,8},{24,16},{32,24},{40,32},{48,40},{56,48},{64,56},{72,6... | collective-permute-start | bytes 1179656 | tf_op jit(solution)/shard_map/ppermute | solution.py:244
  94.2 2.2 %collective-permute-done.5.other = bf16[16,128,512]{2,1,0:T(8,128)(2,1)} collective-permute-done((bf16[16,128,512]{2,1,0:T(8,128)(2,1)S(1)}, bf16[16,128,512]{2,1,0:T(8,128)(2,1)}, u32[]{:S(2)}, u32[]{:S(2)}) %collective-permute-start.5) | collective-permute-done | bytes 2097184 | tf_op jit(solution)/shard_map/ppermute | solution.py:262
  96.4 3.6 %shard_map.93.normed = bf16[8,512,512]{2,1,0:T(8,128)(2,1)S(1)} custom-call(s32[5]{0:T(128)S(1)} %stack.23.where, bf16[16,128,512]{2,1,0:T(8,128)(2,1)S(1)} %all-to-all-done.1.mine, bf16[16,128,512]{2,1,0:T(8,128)(2,1)} %collective-permute-done.5.other, f32[8,1,512]{2,1,0:T(1,128)S(1)} %bitcast.8), custom_call_target="tpu_custom_call" | custom-call | flops 16777216 | bytes 8388608 | tf_op jit(solution)/shard_map/pallas_call | solution.py:30
  100.1 9.6 %collective-permute-done.6.far = bf16[16,96,128]{2,1,0:T(8,128)(2,1)} collective-permute-done((bf16[16,96,128]{2,1,0:T(8,128)(2,1)S(1)}, bf16[16,96,128]{2,1,0:T(8,128)(2,1)}, u32[]{:S(2)}, u32[]{:S(2)}) %collective-permute-start.6) | collective-permute-done | bytes 393248 | tf_op jit(solution)/shard_map/ppermute | solution.py:244
  109.7 3.6 %shard_map.94 = bf16[4,576,128]{2,1,0:T(8,128)(2,1)} custom-call(s32[5]{0:T(128)S(1)} %stack.23.where, bf16[8,512,512]{2,1,0:T(8,128)(2,1)S(1)} %shard_map.93.normed, bf16[16,96,128]{2,1,0:T(8,128)(2,1)S(1)} %pad_maximum_fusion.near, bf16[16,96,128]{2,1,0:T(8,128)(2,1)S(1)} %collective-permute-done.3.ahead, bf16[16,96,128]{2,1,0:T(8,128)(2,1)} %collective-permute-done.6.far, ...), custom_call_target="tpu_custom_call" | custom-call | flops 1073741824 | bytes 8388608 | tf_op jit(solution)/shard_map/pallas_call | solution.py:30
  113.3 4.4 %all-to-all-start.2 = ((bf16[4,576,128]{2,1,0:T(8,128)(2,1)}), bf16[4,576,128]{2,1,0:T(8,128)(2,1)S(1)}, u32[]{:S(2)}, u32[]{:S(2)}) async-start(bf16[4,576,128]{2,1,0:T(8,128)(2,1)} %shard_map.94), calls=%async_computation.2 | async-start | bytes 1179648 | tf_op jit(solution)/shard_map/all_to_all | solution.py:228
  117.8 4.7 %shard_map.92.units = s32[128]{0:T(128)S(1)} custom-call(s32[5]{0:T(128)S(1)} %stack.23.where, s32[64,16]{1,0:T(8,128)S(1)} %copy.11.lists, s32[128]{0:T(128)S(1)} %copy-done.4, s32[8,16]{1,0:T(8,128)S(1)} %convert.2.use), custom_call_target="tpu_custom_call" | custom-call | tf_op jit(solution)/shard_map/pallas_call | solution.py:30
  122.6 5.1 %all-to-all-done.2.got = bf16[4,576,128]{2,1,0:T(8,128)(2,1)S(1)} async-done(((bf16[4,576,128]{2,1,0:T(8,128)(2,1)}), bf16[4,576,128]{2,1,0:T(8,128)(2,1)S(1)}, u32[]{:S(2)}, u32[]{:S(2)}) %all-to-all-start.2) | async-done | bytes 589856 | tf_op jit(solution)/shard_map/all_to_all | solution.py:228
  131.1 10.4 %all_to_all.26.all_stats = f32[4,8,512]{2,1,0:T(8,128)S(1)} all-to-all(f32[4,8,512]{2,1,0:T(8,128)S(1)} %shard_map.95), channel_id=1, replica_groups=mesh['x'=4,'zh'=4,'zl'=4,'y'=4,'core'=2] {'x'}, dimensions={0} | all-to-all | bytes 131072 | tf_op jit(solution)/shard_map/all_to_all | solution.py:228
  141.5 2.3 %shard_map.96 = f32[4,128,512]{2,1,0:T(8,128)S(1)} custom-call(s32[5]{0:T(128)S(1)} %stack.23.where, s32[128]{0:T(128)S(1)} %shard_map.92.units, bf16[4,576,128]{2,1,0:T(8,128)(2,1)S(1)} %all-to-all-done.2.got, bf16[32,128,256]{2,1,0:T(8,128)(2,1)S(1)} %copy-done, f32[4,8,512]{2,1,0:T(8,128)S(1)} %all_to_all.26.all_stats), custom_call_target="tpu_custom_call" | custom-call | tf_op jit(solution)/shard_map/pallas_call | solution.py:30
  143.8 18.4 %all_to_all.27.got = f32[4,128,512]{2,1,0:T(8,128)S(1)} all-to-all(f32[4,128,512]{2,1,0:T(8,128)S(1)} %shard_map.96), channel_id=1, replica_groups=mesh['x'=4,'zh'=4,'zl'=4,'y'=4,'core'=2] {'x'}, dimensions={0} | all-to-all | bytes 2097152 | tf_op jit(solution)/shard_map/all_to_all | solution.py:228
  (31 shorter events, 8.3 us)
Async XLA Ops:
  7.2 0.8 copy-start.1
  8.1 0.7 copy-start.2
  8.8 0.7 copy-start.3
  22.0 72.1 %copy-start.5 = (bf16[4096]{0:T(1024)(128)(2,1)S(1)}, bf16[4096]{0:T(1024)(128)(2,1)}, u32[]{:S(2)}) copy-start(bf16[4096]{0:T(1024)(128)(2,1)} %param.10) | copy-start | bytes 24580
  22.0 68.2 %all-to-all-start.1 = ((bf16[16,128,512]{2,1,0:T(8,128)(2,1)}), bf16[16,128,512]{2,1,0:T(8,128)(2,1)S(1)}, u32[]{:S(2)}, u32[]{:S(2)}) async-start(bf16[16,128,512]{2,1,0:T(8,128)(2,1)} %broadcast_in_dim.2), calls=%async_computation.1 | async-start | bytes 4194304 | tf_op jit(solution)/shard_map/all_to_all | solution.py:228
  29.5 93.1 %all-gather.2.cloned.1.call-start = ((), (), s32[]{:S(2)}) async-start(), calls=%async_computation.5 | async-start | bytes 2228224 | tf_op jit(solution)/shard_map/all_gather | solution.py:238
  30.3 23.4 %collective-permute-start.2 = (bf16[4,96,128]{2,1,0:T(8,128)(2,1)S(1)}, bf16[4,96,128]{2,1,0:T(8,128)(2,1)S(1)}, u32[]{:S(2)}, u32[]{:S(2)}) collective-permute-start(bf16[4,96,128]{2,1,0:T(8,128)(2,1)S(1)} %slice.9), channel_id=1, source_target_pairs={{96,0},{104,8},{112,16},{120,24},{0,32},{8,40},{16,48},{24,56},{32... | collective-permute-start | bytes 294920 | tf_op jit(solution)/shard_map/ppermute | solution.py:244
  37.3 19.6 %collective-permute-start.1 = (bf16[4,96,128]{2,1,0:T(8,128)(2,1)S(1)}, bf16[4,96,128]{2,1,0:T(8,128)(2,1)S(1)}, u32[]{:S(2)}, u32[]{:S(2)}) collective-permute-start(bf16[4,96,128]{2,1,0:T(8,128)(2,1)S(1)} %slice.9), channel_id=1, source_target_pairs={{64,0},{72,8},{80,16},{88,24},{96,32},{104,40},{112,48},{120,56},{... | collective-permute-start | bytes 294920 | tf_op jit(solution)/shard_map/ppermute | solution.py:244
  48.2 17.7 %collective-permute-start = (bf16[4,96,128]{2,1,0:T(8,128)(2,1)S(1)}, bf16[4,96,128]{2,1,0:T(8,128)(2,1)S(1)}, u32[]{:S(2)}, u32[]{:S(2)}) collective-permute-start(bf16[4,96,128]{2,1,0:T(8,128)(2,1)S(1)} %slice.9), channel_id=1, source_target_pairs={{32,0},{40,8},{48,16},{56,24},{64,32},{72,40},{80,48},{88,56},{96,... | collective-permute-start | bytes 294920 | tf_op jit(solution)/shard_map/ppermute | solution.py:244
  65.9 19.1 %collective-permute-start.3 = (bf16[16,96,128]{2,1,0:T(8,128)(2,1)S(1)}, bf16[16,96,128]{2,1,0:T(8,128)(2,1)S(1)}, u32[]{:S(2)}, u32[]{:S(2)}) collective-permute-start(bf16[16,96,128]{2,1,0:T(8,128)(2,1)S(1)} %pad_maximum_fusion.near), channel_id=1, source_target_pairs={{8,0},{16,8},{24,16},{32,24},{40,32},{48,40},{56,48},{64,56},{72,6... | collective-permute-start | bytes 1179656 | tf_op jit(solution)/shard_map/ppermute | solution.py:244
  71.2 19.0 %collective-permute-start.4 = (bf16[16,96,128]{2,1,0:T(8,128)(2,1)S(1)}, bf16[16,96,128]{2,1,0:T(8,128)(2,1)S(1)}, u32[]{:S(2)}, u32[]{:S(2)}) collective-permute-start(bf16[16,96,128]{2,1,0:T(8,128)(2,1)S(1)} %pad_maximum_fusion.near), channel_id=1, source_target_pairs={{120,0},{0,8},{8,16},{16,24},{24,32},{32,40},{40,48},{48,56},{56,6... | collective-permute-start | bytes 1179656 | tf_op jit(solution)/shard_map/ppermute | solution.py:244
  90.2 6.2 %collective-permute-start.5 = (bf16[16,128,512]{2,1,0:T(8,128)(2,1)S(1)}, bf16[16,128,512]{2,1,0:T(8,128)(2,1)}, u32[]{:S(2)}, u32[]{:S(2)}) collective-permute-start(bf16[16,128,512]{2,1,0:T(8,128)(2,1)S(1)} %all-to-all-done.1.mine), channel_id=1, source_target_pairs={{0,1},{1,0},{2,3},{3,2},{4,5},{5,4},{6,7},{7,6},{8,9},{9,8},{10,11... | collective-permute-start | bytes 6291464 | tf_op jit(solution)/shard_map/ppermute | solution.py:262
  92.1 17.6 %collective-permute-start.6 = (bf16[16,96,128]{2,1,0:T(8,128)(2,1)S(1)}, bf16[16,96,128]{2,1,0:T(8,128)(2,1)}, u32[]{:S(2)}, u32[]{:S(2)}) collective-permute-start(bf16[16,96,128]{2,1,0:T(8,128)(2,1)S(1)} %collective-permute-done.3.ahead), channel_id=1, source_target_pairs={{8,0},{16,8},{24,16},{32,24},{40,32},{48,40},{56,48},{64,56},{72,6... | collective-permute-start | bytes 1179656 | tf_op jit(solution)/shard_map/ppermute | solution.py:244
  100.0 17.7 %copy-start.6 = (s32[64,16]{0,1:T(8,128)S(1)}, s32[64,16]{0,1:T(8,128)}, u32[]{:S(2)}) copy-start(s32[64,16]{0,1:T(8,128)} %param.15) | copy-start | bytes 12292
  100.0 17.8 %copy-start.4 = (s32[128]{0:T(128)S(1)}, s32[128]{0:T(128)}, u32[]{:S(2)}) copy-start(s32[128]{0:T(128)} %place.1) | copy-start | bytes 1540
  113.3 14.4 %all-to-all-start.2 = ((bf16[4,576,128]{2,1,0:T(8,128)(2,1)}), bf16[4,576,128]{2,1,0:T(8,128)(2,1)S(1)}, u32[]{:S(2)}, u32[]{:S(2)}) async-start(bf16[4,576,128]{2,1,0:T(8,128)(2,1)} %shard_map.94), calls=%async_computation.2 | async-start | bytes 1179648 | tf_op jit(solution)/shard_map/all_to_all | solution.py:228
  127.7 1.6 copy-start
Sparse Core Ops, SparseCore 0:
  32.4 81.8 all-gather.1

commit v5 on v4

--- a/solution.py
+++ b/solution.py
@@ -52,25 +52,26 @@
         at = HALF * (part % 2)
         out[part, 0:64, :] = wq[:, part * HEAD : (part + 1) * HEAD]
         out[part, 64:96, :] = side_by_side(src[0:32, :], src[32:64, :], at, at)
-        out[part, 96:112, :] = use[...]
+        out[part, 96:128, :] = use[...]
 
 
 def norm_kernel(where, mine, other, gain, out):
     core = where[3]
-    for x in range(NX):
-        rows = pl.ds(x * SEQ, SEQ)
+    for row in range(NX):
+        rows = pl.ds(pl.multiple_of(lax.rem(where[0] + row, NX) * SEQ, SEQ), SEQ)
         total = jnp.zeros((SEQ, HEAD), F32)
         for src in (mine, other):
             for y in range(4):
                 for c in range(4):
-                    feats = src[x * 4 + y, :, c * HEAD : (c + 1) * HEAD].astype(F32)
+                    feats = src[row, y, :, c * HEAD : (c + 1) * HEAD].astype(F32)
                     total = total + feats * feats
         power = jnp.sum(total, axis=-1, keepdims=True) * (1.0 / 4096.0)
         factor = lax.rsqrt(power + 1e-05)
-        for src, side in ((mine, core), (other, 1 - core)):
+        for src, flip in ((mine, 0), (other, 1)):
+            side = core if flip == 0 else 1 - core
             for y in range(4):
                 slot = 2 * y + side
-                feats = src[x * 4 + y].astype(F32)
+                feats = src[row, y].astype(F32)
                 out[slot, rows, :] = (feats * factor * gain[slot]).astype(BF16)
 
 
@@ -103,14 +104,16 @@
     units[0] = lax.fori_loop(0, NX * NZ, compact, 0)
 
 
-def project_kernel(where, normed, near, ahead, far, behind, send, weights):
-    z = where[1]
-    for step, blocks in ((0, near), (1, ahead), (2, far), (NZ - 1, behind)):
-        at = lax.rem(z + step, NZ)
-        for b in range(16):
-            block = blocks[b]
-            depth = (b % 4) * 1024 + lax.rem(at + (b // 4) * 4, NZ) * HALF
-            base = pl.multiple_of(depth, HALF)
+def project_kernel(where, normed, mine, up, down, send, weights):
+    parity = where[1] % 2
+    for i in range(8):
+        for b in range(8):
+            x = b % 4
+            if b < 4:
+                block, z = mine[i, x], 2 * i + parity
+            else:
+                block, z = (up[i, x] if i < 4 else down[i - 4, x]), 2 * i + 1 - parity
+            base = pl.multiple_of(x * 1024 + z * HALF, HALF)
             packed = block[64:96, :]
             weights[pl.ds(base, 64), 0:HEAD] = block[0:64, :]
             weights[pl.ds(base, 32), HEAD : 2 * HEAD] = packed
@@ -152,10 +155,17 @@
     return jnp.where(row_at >= key_at, scores, LOW)
 
 
-def unit_scores(code, got, docs):
+def documents(docs, owner, z, part):
+    cols, rows = slice(part * HEAD, (part + 1) * HEAD), pl.ds((owner // 4) * 2, 2)
+    step = lax.rem(owner - z + NZ, 4)
+    near, ahead, far, behind = (ref[rows, :, cols].reshape(2 * SEQ, HEAD) for ref in docs)
+    return jnp.where(step < 2, jnp.where(step == 0, near, ahead), jnp.where(step == 2, far, behind))
+
+
+def unit_scores(code, got, docs, z):
     entry, bits = code // 16, code % 16
     group, owner = entry // NZ, entry % NZ
-    keys = docs[pl.ds(owner * 2, 2), :, 0:HEAD].reshape(2 * SEQ, HEAD)
+    keys = documents(docs, owner, z, 0)
     scores = scores_of(keys, queries(got, group))
     second = (lax.broadcasted_iota(jnp.int32, (1, COLS), 1) % SEQ) // HALF
     kept = []
@@ -166,7 +176,8 @@
     return group, owner, jnp.concatenate(kept, axis=0)
 
 
-def stats_kernel(where, units, got, docs, send, stats):
+def stats_kernel(where, units, got, near, ahead, far, behind, send, stats):
+    docs = (near, ahead, far, behind)
     x = where[0]
     scores = own_scores(got, x)
     top = jnp.max(scores, axis=0, keepdims=True)
@@ -176,7 +187,7 @@
     stats[pl.ds(x + 4, 1), :] = jnp.sum(jnp.exp(scores - top), axis=0, keepdims=True)
 
     def unit(i, carry):
-        group, owner, scores = unit_scores(units[i + 1], got, docs)
+        group, owner, scores = unit_scores(units[i + 1], got, docs, where[1])
         before = stats[pl.ds(group, 1), :]
         top = jnp.maximum(before, jnp.max(scores, axis=0, keepdims=True))
         part = jnp.sum(jnp.exp(scores - top), axis=0, keepdims=True)
@@ -189,7 +200,8 @@
         send[dest] = stats[...]
 
 
-def values_kernel(where, units, got, docs, all_stats, send, total):
+def values_kernel(where, units, got, near, ahead, far, behind, all_stats, send, total):
+    docs = (near, ahead, far, behind)
     x = where[0]
     tops = [all_stats[src, 0:4, :] for src in range(NX)]
     top = jnp.maximum(jnp.maximum(tops[0], tops[1]), jnp.maximum(tops[2], tops[3]))
@@ -209,8 +221,8 @@
     add(x, own_scores(got, x), own_part(got, 2))
 
     def unit(i, carry):
-        group, owner, scores = unit_scores(units[i + 1], got, docs)
-        values = docs[pl.ds(owner * 2, 2), :, HEAD : 2 * HEAD].reshape(2 * SEQ, HEAD)
+        group, owner, scores = unit_scores(units[i + 1], got, docs, where[1])
+        values = documents(docs, owner, where[1], 1)
         add(group, scores, values)
         return carry
 
@@ -234,31 +246,38 @@
 
 def shards(tokens, norm_gain, wq, wk, wv, doc_cache, doc_lists, doc_place, block_use):
     shape = jax.ShapeDtypeStruct
-    z_axes = ("zh", "zl")
-    docs = lax.all_gather(doc_cache, z_axes, axis=0, tiled=True)
-    x, zh, zl = lax.axis_index("x"), lax.axis_index("zh"), lax.axis_index("zl")
+    z_axes = ("zh", "zm", "zp")
+    x, zh = lax.axis_index("x"), lax.axis_index("zh")
+    zl = lax.axis_index("zm") * 2 + lax.axis_index("zp")
     y, core = lax.axis_index("y"), lax.axis_index("core")
     where = jnp.stack([x, zh * 4 + zl, zl, core, y]).astype(jnp.int32)
 
     def from_z(array, step):
         return lax.ppermute(array, z_axes, [((i + step) % NZ, i) for i in range(NZ)])
 
-    def from_y(array, step):
-        return lax.ppermute(array, "y", [((i + step) % 4, i) for i in range(4)])
-
-    flags = jnp.pad(block_use.astype(BF16), ((0, 14), (0, HEAD - PICKS)))
+    def from_x(array, step):
+        return lax.ppermute(array, "x", [((i + step) % NX, i) for i in range(NX)])
+
+    flags = jnp.pad(block_use.astype(BF16), ((0, 30), (0, HEAD - PICKS)))
     packed = call(
-        pack_kernel, shape((NX, 112, HEAD), BF16), (wq, wk, wv, flags), [VMEM] * 4
+        pack_kernel, shape((NX, 128, HEAD), BF16), (wq, wk, wv, flags), [VMEM] * 4
     )
     by_x = exchange(packed, "x")
-    part = by_x[:, 0:96]
-    near = jnp.concatenate([part, from_z(part, 4), from_z(part, 8), from_z(part, 12)])
-
-    tokens, _ = lax.optimization_barrier((tokens, by_x))
-    mine = spread(tokens, ("x", "y"), 16)
+    w_mine = lax.all_gather(by_x, ("zh", "zm"))
+
+    tokens, doc_cache, _ = lax.optimization_barrier((tokens, doc_cache, by_x))
+    near = spread(doc_cache, "zh", 4).reshape(8, SEQ, 2 * HEAD)
     ahead = from_z(near, 1)
     behind = from_z(near, -1)
-    mine, _, _ = lax.optimization_barrier((mine, ahead, behind))
+
+    by_y = lax.all_gather(tokens, "y")
+    mine = jnp.concatenate([by_y, from_x(by_y, 1), from_x(by_y, 2), from_x(by_y, 3)])
+    mine = mine.reshape(4, 4, SEQ, 512)
+    mine, ahead, behind, w_mine = lax.optimization_barrier((mine, ahead, behind, w_mine))
+    w_up = from_z(w_mine[0:4, :, 0:96], 1)
+    w_down = from_z(w_mine[4:8, :, 0:96], -1)
+    far = from_z(ahead, 1)
+    docs = (near, ahead, far, behind)
     other = lax.ppermute(mine, "core", [(0, 1), (1, 0)])
     gain = norm_gain.astype(F32).reshape(8, 1, 512)
     normed = call(
@@ -279,12 +298,11 @@
         scratch=[pltpu.SMEM((NX * NZ,), jnp.int32)],
     )
 
-    far = from_z(ahead, 1)
     send = call(
         project_kernel,
         shape((NX, ROWS + HALF, HEAD), BF16),
-        (where, normed, near, ahead, far, behind),
-        [SMEM] + [VMEM] * 5,
+        (where, normed, w_mine, w_up, w_down),
+        [SMEM] + [VMEM] * 4,
         scratch=[pltpu.VMEM((4096, 2 * HEAD), BF16)],
         flops=2 * ROWS * 4096 * 256,
         moved=8 << 20,
@@ -293,16 +311,16 @@
     stats = call(
         stats_kernel,
         shape((NX, 8, COLS), F32),
-        (where, units, got, docs),
-        [SMEM, SMEM, VMEM, VMEM],
+        (where, units, got, *docs),
+        [SMEM, SMEM] + [VMEM] * 5,
         scratch=[pltpu.VMEM((8, COLS), F32)],
     )
     all_stats = exchange(stats, "x")
     partial = call(
         values_kernel,
         shape((NX, HEAD, COLS), F32),
-        (where, units, got, docs, all_stats),
-        [SMEM, SMEM, VMEM, VMEM, VMEM],
+        (where, units, got, *docs, all_stats),
+        [SMEM, SMEM] + [VMEM] * 6,
         scratch=[pltpu.VMEM((8, COLS), F32)],
     )
     returned = exchange(partial, "x")
@@ -310,8 +328,8 @@
 
 
 def solution(mesh):
-    fine = Mesh(mesh.devices.reshape(4, 4, 4, 4, 2), ("x", "zh", "zl", "y", "core"))
-    pairs, tensor = ("x", "zh", "zl"), ("y", "core")
+    fine = Mesh(mesh.devices.reshape(4, 4, 2, 2, 4, 2), ("x", "zh", "zm", "zp", "y", "core"))
+    pairs, tensor = ("x", "zh", "zm", "zp"), ("y", "core")
     placed = (
         P(pairs, tensor),
         P(),

time: 171 us -> 181 us (1.058)
  waiting for transfers between devices: 46.8 us -> 34.5 us
  blocking collectives: 38.7 us -> 47.1 us
  Pallas kernels: 17 us -> 23.3 us
  local copies, waits for them, and re-layouts: 6.49 us -> 9.72 us
  other arithmetic: 0.75 us -> 3.18 us
    ppermute x6 -> x5, waiting for transfers between devices: 38.9 us -> 1.89 us  [from_z(): lax.ppermute(array, z_axes, [((i + step) % NZ, i) for i in range(NZ)])]
    all_gather x1, waiting for transfers between devices: 0.02 us -> 18.7 us  [shards(): w_mine = lax.all_gather(by_x, ('zh', 'zm'))]
    ppermute x6 -> x5, starting transfers between devices: 32.5 us -> 17.8 us  [from_z(): lax.ppermute(array, z_axes, [((i + step) % NZ, i) for i in range(NZ)])]
    all_gather x0 -> x1, blocking collectives: none -> 12.8 us  [shards(): by_y = lax.all_gather(tokens, 'y')]
    ppermute x0 -> x3, starting transfers between devices: none -> 9.16 us  [from_x(): return lax.ppermute(array, 'x', [((i + step) % NX, i) for i in range(NX)])]
    all_to_all x2, starting transfers between devices: 11.9 us -> 18.6 us  [exchange(): return lax.all_to_all(array, axes, 0, 0, tiled=True)]
    all_to_all x2, waiting for transfers between devices: 5.08 us -> 11.4 us  [exchange(): return lax.all_to_all(array, axes, 0, 0, tiled=True)]
    pallas_call x7, Pallas kernels: 17 us -> 23.3 us  [call(): pl.pallas_call(kernel, out_shape=outs, in_specs=specs, out_specs=VMEM if...]
  transfers between devices with their start and end apart: 10 -> 12, of which waited for: 7 -> 6; matrix products, arithmetic and copies ran while one was open for 0% -> 3% of each run, Pallas kernels for 7% -> 7%
where the time goes in v5:
time: 181 us; the launch traced here: 179 us
  starting transfers between devices  47.4 us (26%)
  blocking collectives  47.1 us (26%)
  waiting for transfers between devices  34.5 us (19%)
  Pallas kernels  23.3 us (13%)
  between operations  13.6 us (8%)
  local copies, waits for them, and re-layouts  9.72 us (5%)
  other arithmetic  3.18 us (2%)
    all_to_all x3, blocking collectives, exchange(): return lax.all_to_all(array, axes, 0, 0, tiled=True)  34.3 us
    pallas_call x7, Pallas kernels, call(): pl.pallas_call(kernel, out_shape=outs, in_specs=specs, out_specs=VMEM if...  23.3 us
    all_gather x1, waiting for transfers between devices, shards(): w_mine = lax.all_gather(by_x, ('zh', 'zm'))  18.7 us
    all_to_all x2, starting transfers between devices, exchange(): return lax.all_to_all(array, axes, 0, 0, tiled=True)  18.6 us
    ppermute x5, starting transfers between devices, from_z(): lax.ppermute(array, z_axes, [((i + step) % NZ, i) for i in range(NZ)])  17.8 us
    all_gather x1, blocking collectives, shards(): by_y = lax.all_gather(tokens, 'y')  12.8 us
    all_to_all x2, waiting for transfers between devices, exchange(): return lax.all_to_all(array, axes, 0, 0, tiled=True)  11.4 us
    ppermute x3, starting transfers between devices, from_x(): return lax.ppermute(array, 'x', [((i + step) % NX, i) for i in range(NX)])  9.16 us
  transfers between devices with their start and end apart: 12, of which 6 were waited for; matrix products, arithmetic and copies ran while one was open for 3% of the time, Pallas kernels for 7%

profile of v5, /device:TPU:24, one launch (start us, length us, event | category | flops | bytes accessed | tf_op | source)
XLA Modules:
  0.0 178.9 jit_solution(3346175355232171019)
XLA Ops:
  9.6 10.2 %all_to_all.25 = bf16[4,128,128]{2,1,0:T(8,128)(2,1)} all-to-all(bf16[4,128,128]{2,1,0:T(8,128)(2,1)S(1)} %shard_map.91), channel_id=1, replica_groups=mesh['x'=4,'zh'=4,'zm'=2,'zp'=2,'y'=4,'core'=2] {'x'}, dimensions={0} | all-to-all | bytes 262144 | tf_op jit(solution)/shard_map/all_to_all | solution.py:240
  21.5 15.1 %all-to-all-start.1 = ((bf16[4,2,128,256]{3,2,1,0:T(8,128)(2,1)}), bf16[4,2,128,256]{3,2,1,0:T(8,128)(2,1)S(1)}, u32[]{:S(2)}, u32[]{:S(2)}) async-start(bf16[4,2,128,256]{3,2,1,0:T(8,128)(2,1)} %broadcast_in_dim.2), calls=%async_computation.1 | async-start | bytes 1048576 | tf_op jit(solution)/shard_map/all_to_all | solution.py:240
  37.3 12.8 %all-gather = bf16[512,512]{1,0:T(8,128)(2,1)S(1)} all-gather(bf16[128,512]{1,0:T(8,128)(2,1)S(1)} %copy-done.11), channel_id=2, replica_groups=mesh['x'=4,'zh'=4,'zm'=2,'zp'=2,'y'=4,'core'=2] {'y'}, dimensions={0}, use_global_device_ids=true | all-gather | bytes 655360 | tf_op jit(solution)/shard_map/all_gather | solution.py:273
  50.1 2.5 %collective-permute-start.2 = (bf16[4,128,512]{2,1,0:T(8,128)(2,1)S(1)}, bf16[4,128,512]{2,1,0:T(8,128)(2,1)S(1)}, u32[]{:S(2)}, u32[]{:S(2)}) collective-permute-start(bf16[4,128,512]{2,1,0:T(8,128)(2,1)S(1)} %bitcast.21), channel_id=1, source_target_pairs={{384,0},{0,128},{128,256},{256,384},{385,1},{1,129},{129,257},{257... | collective-permute-start | bytes 1572872 | tf_op jit(solution)/shard_map/ppermute | solution.py:259
  52.6 4.0 %collective-permute-start.1 = (bf16[4,128,512]{2,1,0:T(8,128)(2,1)S(1)}, bf16[4,128,512]{2,1,0:T(8,128)(2,1)S(1)}, u32[]{:S(2)}, u32[]{:S(2)}) collective-permute-start(bf16[4,128,512]{2,1,0:T(8,128)(2,1)S(1)} %bitcast.22), channel_id=1, source_target_pairs={{256,0},{384,128},{0,256},{128,384},{257,1},{385,129},{1,257},{129... | collective-permute-start | bytes 1572872 | tf_op jit(solution)/shard_map/ppermute | solution.py:259
  56.6 2.7 %collective-permute-start = (bf16[4,128,512]{2,1,0:T(8,128)(2,1)S(1)}, bf16[4,128,512]{2,1,0:T(8,128)(2,1)}, u32[]{:S(2)}, u32[]{:S(2)}) collective-permute-start(bf16[4,128,512]{2,1,0:T(8,128)(2,1)S(1)} %bitcast.23), channel_id=1, source_target_pairs={{128,0},{256,128},{384,256},{0,384},{129,1},{257,129},{385,257},{1... | collective-permute-start | bytes 1572872 | tf_op jit(solution)/shard_map/ppermute | solution.py:259
  59.3 7.0 %all-to-all-done.1 = bf16[4,2,128,256]{3,2,1,0:T(8,128)(2,1)S(1)} async-done(((bf16[4,2,128,256]{3,2,1,0:T(8,128)(2,1)}), bf16[4,2,128,256]{3,2,1,0:T(8,128)(2,1)S(1)}, u32[]{:S(2)}, u32[]{:S(2)}) %all-to-all-start.1) | async-done | bytes 524320 | tf_op jit(solution)/shard_map/all_to_all | solution.py:240
  66.3 5.9 %collective-permute-start.3 = (bf16[8,128,256]{2,1,0:T(8,128)(2,1)S(1)}, bf16[8,128,256]{2,1,0:T(8,128)(2,1)S(1)}, u32[]{:S(2)}, u32[]{:S(2)}) collective-permute-start(bf16[8,128,256]{2,1,0:T(8,128)(2,1)S(1)} %bitcast.14), channel_id=1, source_target_pairs={{8,0},{16,8},{24,16},{32,24},{40,32},{48,40},{56,48},{64,56},{72,6... | collective-permute-start | bytes 1572872 | tf_op jit(solution)/shard_map/ppermute | solution.py:256
  72.3 1.9 %collective-permute-start.4 = (bf16[8,128,256]{2,1,0:T(8,128)(2,1)S(1)}, bf16[8,128,256]{2,1,0:T(8,128)(2,1)}, u32[]{:S(2)}, u32[]{:S(2)}) collective-permute-start(bf16[8,128,256]{2,1,0:T(8,128)(2,1)S(1)} %bitcast.15), channel_id=1, source_target_pairs={{120,0},{0,8},{8,16},{16,24},{24,32},{32,40},{40,48},{48,56},{56,6... | collective-permute-start | bytes 1572872 | tf_op jit(solution)/shard_map/ppermute | solution.py:256
  79.3 18.7 %all-gather.4.cloned.1.call-done = bf16[32,128,128]{2,1,0:T(8,128)(2,1)} async-done(((bf16[4,128,128]{2,1,0:T(8,128)(2,1)}), bf16[32,128,128]{2,1,0:T(8,128)(2,1)}) %all-gather.4.cloned.1.call-update) | async-done | bytes 1048592 | tf_op jit(solution)/shard_map/all_gather | solution.py:266
  98.0 1.9 %collective-permute-start.5 = (bf16[4,4,128,512]{3,2,1,0:T(8,128)(2,1)S(1)}, bf16[4,4,128,512]{3,2,1,0:T(8,128)(2,1)}, u32[]{:S(2)}, u32[]{:S(2)}) collective-permute-start(bf16[4,4,128,512]{3,2,1,0:T(8,128)(2,1)S(1)} %bitcast.12), channel_id=1, source_target_pairs={{0,1},{1,0},{2,3},{3,2},{4,5},{5,4},{6,7},{7,6},{8,9},{9,8},{10,11... | collective-permute-start | bytes 6291464 | tf_op jit(solution)/shard_map/ppermute | solution.py:281
  100.0 2.1 %fusion = (bf16[4,4,96,128]{3,2,1,0:T(8,128)(2,1)}, bf16[4,4,96,128]{3,2,1,0:T(8,128)(2,1)}) fusion(bf16[8,4,128,128]{3,2,1,0:T(8,128)(2,1)} %bitcast.18), kind=kLoop, calls=%fused_computation.1 | loop fusion | bytes 1572864 | tf_op jit(solution)/shard_map/slice | solution.py:278
  102.0 2.9 %collective-permute-start.6 = (bf16[4,4,96,128]{3,2,1,0:T(8,128)(2,1)}, bf16[4,4,96,128]{3,2,1,0:T(8,128)(2,1)S(1)}, u32[]{:S(2)}, u32[]{:S(2)}) collective-permute-start(bf16[4,4,96,128]{3,2,1,0:T(8,128)(2,1)} %get-tuple-element.18), channel_id=1, source_target_pairs={{8,0},{16,8},{24,16},{32,24},{40,32},{48,40},{56,48},{64,56},{72,6... | collective-permute-start | bytes 1179656 | tf_op jit(solution)/shard_map/ppermute | solution.py:256
  105.0 2.9 %collective-permute-start.7 = (bf16[4,4,96,128]{3,2,1,0:T(8,128)(2,1)}, bf16[4,4,96,128]{3,2,1,0:T(8,128)(2,1)}, u32[]{:S(2)}, u32[]{:S(2)}) collective-permute-start(bf16[4,4,96,128]{3,2,1,0:T(8,128)(2,1)} %get-tuple-element.17), channel_id=1, source_target_pairs={{120,0},{0,8},{8,16},{16,24},{24,32},{32,40},{40,48},{48,56},{56,6... | collective-permute-start | bytes 1179656 | tf_op jit(solution)/shard_map/ppermute | solution.py:256
  109.2 4.1 %collective-permute-start.8 = (bf16[8,128,256]{2,1,0:T(8,128)(2,1)S(1)}, bf16[8,128,256]{2,1,0:T(8,128)(2,1)}, u32[]{:S(2)}, u32[]{:S(2)}) collective-permute-start(bf16[8,128,256]{2,1,0:T(8,128)(2,1)S(1)} %collective-permute-done.3.ahead), channel_id=1, source_target_pairs={{8,0},{16,8},{24,16},{32,24},{40,32},{48,40},{56,48},{64,56},{72,6... | collective-permute-start | bytes 1572872 | tf_op jit(solution)/shard_map/ppermute | solution.py:256
  114.0 3.7 %shard_map.93.normed = bf16[8,512,512]{2,1,0:T(8,128)(2,1)S(1)} custom-call(s32[5]{0:T(128)S(1)} %copy-done.2, bf16[4,4,128,512]{3,2,1,0:T(8,128)(2,1)S(1)} %bitcast.13, bf16[4,4,128,512]{3,2,1,0:T(8,128)(2,1)} %collective-permute-done.5.other, f32[8,1,512]{2,1,0:T(1,128)S(1)} %bitcast.20), custom_call_target="tpu_custom_call" | custom-call | flops 16777216 | bytes 8388608 | tf_op jit(solution)/shard_map/pallas_call | solution.py:30
  119.6 3.5 %shard_map.94 = bf16[4,576,128]{2,1,0:T(8,128)(2,1)} custom-call(s32[5]{0:T(128)S(1)} %copy-done.3, bf16[8,512,512]{2,1,0:T(8,128)(2,1)S(1)} %shard_map.93.normed, bf16[8,4,128,128]{3,2,1,0:T(8,128)(2,1)S(1)} %bitcast.19, bf16[4,4,96,128]{3,2,1,0:T(8,128)(2,1)S(1)} %collective-permute-done.6.up, bf16[4,4,96,128]{3,2,1,0:T(8,128)(2,1)} %collective-permute-done.7.down), custom_call_target="tpu_custom_call" | custom-call | flops 1073741824 | bytes 8388608 | tf_op jit(solution)/shard_map/pallas_call | solution.py:30
  123.2 3.5 %all-to-all-start.2 = ((bf16[4,576,128]{2,1,0:T(8,128)(2,1)}), bf16[4,576,128]{2,1,0:T(8,128)(2,1)S(1)}, u32[]{:S(2)}, u32[]{:S(2)}) async-start(bf16[4,576,128]{2,1,0:T(8,128)(2,1)} %shard_map.94), calls=%async_computation.2 | async-start | bytes 1179648 | tf_op jit(solution)/shard_map/all_to_all | solution.py:240
  127.5 4.7 %shard_map.92.units = s32[128]{0:T(128)S(1)} custom-call(s32[5]{0:T(128)S(1)} %copy-done.4, s32[64,16]{1,0:T(8,128)S(1)} %copy.11.lists, s32[128]{0:T(128)S(1)} %copy-done.7, s32[8,16]{1,0:T(8,128)S(1)} %convert.2.use), custom_call_target="tpu_custom_call" | custom-call | tf_op jit(solution)/shard_map/pallas_call | solution.py:30
  132.2 4.4 %all-to-all-done.2.got = bf16[4,576,128]{2,1,0:T(8,128)(2,1)S(1)} async-done(((bf16[4,576,128]{2,1,0:T(8,128)(2,1)}), bf16[4,576,128]{2,1,0:T(8,128)(2,1)S(1)}, u32[]{:S(2)}, u32[]{:S(2)}) %all-to-all-start.2) | async-done | bytes 589856 | tf_op jit(solution)/shard_map/all_to_all | solution.py:240
  136.6 4.7 %shard_map.95 = f32[4,8,512]{2,1,0:T(8,128)S(1)} custom-call(s32[5]{0:T(128)S(1)} %copy-done.4, s32[128]{0:T(128)S(1)} %shard_map.92.units, bf16[4,576,128]{2,1,0:T(8,128)(2,1)S(1)} %all-to-all-done.2.got, bf16[8,128,256]{2,1,0:T(8,128)(2,1)S(1)} %bitcast.16, bf16[8,128,256]{2,1,0:T(8,128)(2,1)S(1)} %collective-permute-done.3.ahead, ...), custom_call_target="tpu_custom_call" | custom-call | tf_op jit(solution)/shard_map/pallas_call | solution.py:30
  141.3 8.6 %all_to_all.26.all_stats = f32[4,8,512]{2,1,0:T(8,128)S(1)} all-to-all(f32[4,8,512]{2,1,0:T(8,128)S(1)} %shard_map.95), channel_id=1, replica_groups=mesh['x'=4,'zh'=4,'zm'=2,'zp'=2,'y'=4,'core'=2] {'x'}, dimensions={0} | all-to-all | bytes 131072 | tf_op jit(solution)/shard_map/all_to_all | solution.py:240
  149.9 5.8 %shard_map.96 = f32[4,128,512]{2,1,0:T(8,128)S(1)} custom-call(s32[5]{0:T(128)S(1)} %copy-done.4, s32[128]{0:T(128)S(1)} %shard_map.92.units, bf16[4,576,128]{2,1,0:T(8,128)(2,1)S(1)} %all-to-all-done.2.got, bf16[8,128,256]{2,1,0:T(8,128)(2,1)S(1)} %bitcast.17, bf16[8,128,256]{2,1,0:T(8,128)(2,1)S(1)} %collective-permute-done.3.ahead, ...), custom_call_target="tpu_custom_call" | custom-call | tf_op jit(solution)/shard_map/pallas_call | solution.py:30
  155.7 15.5 %all_to_all.27.got = f32[4,128,512]{2,1,0:T(8,128)S(1)} all-to-all(f32[4,128,512]{2,1,0:T(8,128)S(1)} %shard_map.96), channel_id=1, replica_groups=mesh['x'=4,'zh'=4,'zm'=2,'zp'=2,'y'=4,'core'=2] {'x'}, dimensions={0} | all-to-all | bytes 2097152 | tf_op jit(solution)/shard_map/all_to_all | solution.py:240
  (48 shorter events, 16.0 us)
Async XLA Ops:
  7.2 0.8 copy-start.1
  8.1 0.7 copy-start.5
  8.8 0.7 copy-start.6
  9.5 27.8 %copy-start.11 = (bf16[128,512]{1,0:T(8,128)(2,1)S(1)}, bf16[128,512]{1,0:T(8,128)(2,1)}, u32[]{:S(2)}) copy-start(bf16[128,512]{1,0:T(8,128)(2,1)} %param.9) | copy-start | bytes 393220
  21.5 44.8 %all-to-all-start.1 = ((bf16[4,2,128,256]{3,2,1,0:T(8,128)(2,1)}), bf16[4,2,128,256]{3,2,1,0:T(8,128)(2,1)S(1)}, u32[]{:S(2)}, u32[]{:S(2)}) async-start(bf16[4,2,128,256]{3,2,1,0:T(8,128)(2,1)} %broadcast_in_dim.2), calls=%async_computation.1 | async-start | bytes 1048576 | tf_op jit(solution)/shard_map/all_to_all | solution.py:240
  36.6 61.4 %all-gather.4.cloned.1.call-start = ((), (), s32[]{:S(2)}) async-start(), calls=%async_computation.5 | async-start | bytes 1179648 | tf_op jit(solution)/shard_map/all_gather | solution.py:266
  50.1 24.8 %copy-start.8 = (bf16[512,512]{1,0:T(8,128)(2,1)}, bf16[512,512]{1,0:T(8,128)(2,1)S(1)}, u32[]{:S(2)}) copy-start(bf16[512,512]{1,0:T(8,128)(2,1)S(1)} %all-gather) | copy-start | bytes 1572868
  50.1 24.8 %collective-permute-start.2 = (bf16[4,128,512]{2,1,0:T(8,128)(2,1)S(1)}, bf16[4,128,512]{2,1,0:T(8,128)(2,1)S(1)}, u32[]{:S(2)}, u32[]{:S(2)}) collective-permute-start(bf16[4,128,512]{2,1,0:T(8,128)(2,1)S(1)} %bitcast.21), channel_id=1, source_target_pairs={{384,0},{0,128},{128,256},{256,384},{385,1},{1,129},{129,257},{257... | collective-permute-start | bytes 1572872 | tf_op jit(solution)/shard_map/ppermute | solution.py:259
  52.6 22.3 %collective-permute-start.1 = (bf16[4,128,512]{2,1,0:T(8,128)(2,1)S(1)}, bf16[4,128,512]{2,1,0:T(8,128)(2,1)S(1)}, u32[]{:S(2)}, u32[]{:S(2)}) collective-permute-start(bf16[4,128,512]{2,1,0:T(8,128)(2,1)S(1)} %bitcast.22), channel_id=1, source_target_pairs={{256,0},{384,128},{0,256},{128,384},{257,1},{385,129},{1,257},{129... | collective-permute-start | bytes 1572872 | tf_op jit(solution)/shard_map/ppermute | solution.py:259
  56.6 21.0 %collective-permute-start = (bf16[4,128,512]{2,1,0:T(8,128)(2,1)S(1)}, bf16[4,128,512]{2,1,0:T(8,128)(2,1)}, u32[]{:S(2)}, u32[]{:S(2)}) collective-permute-start(bf16[4,128,512]{2,1,0:T(8,128)(2,1)S(1)} %bitcast.23), channel_id=1, source_target_pairs={{128,0},{256,128},{384,256},{0,384},{129,1},{257,129},{385,257},{1... | collective-permute-start | bytes 1572872 | tf_op jit(solution)/shard_map/ppermute | solution.py:259
  66.3 31.7 %collective-permute-start.3 = (bf16[8,128,256]{2,1,0:T(8,128)(2,1)S(1)}, bf16[8,128,256]{2,1,0:T(8,128)(2,1)S(1)}, u32[]{:S(2)}, u32[]{:S(2)}) collective-permute-start(bf16[8,128,256]{2,1,0:T(8,128)(2,1)S(1)} %bitcast.14), channel_id=1, source_target_pairs={{8,0},{16,8},{24,16},{32,24},{40,32},{48,40},{56,48},{64,56},{72,6... | collective-permute-start | bytes 1572872 | tf_op jit(solution)/shard_map/ppermute | solution.py:256
  72.3 25.8 %collective-permute-start.4 = (bf16[8,128,256]{2,1,0:T(8,128)(2,1)S(1)}, bf16[8,128,256]{2,1,0:T(8,128)(2,1)}, u32[]{:S(2)}, u32[]{:S(2)}) collective-permute-start(bf16[8,128,256]{2,1,0:T(8,128)(2,1)S(1)} %bitcast.15), channel_id=1, source_target_pairs={{120,0},{0,8},{8,16},{16,24},{24,32},{32,40},{40,48},{48,56},{56,6... | collective-permute-start | bytes 1572872 | tf_op jit(solution)/shard_map/ppermute | solution.py:256
  74.9 0.8 copy-start.9
  75.7 0.8 copy-start.10
  98.0 15.3 %collective-permute-start.5 = (bf16[4,4,128,512]{3,2,1,0:T(8,128)(2,1)S(1)}, bf16[4,4,128,512]{3,2,1,0:T(8,128)(2,1)}, u32[]{:S(2)}, u32[]{:S(2)}) collective-permute-start(bf16[4,4,128,512]{3,2,1,0:T(8,128)(2,1)S(1)} %bitcast.12), channel_id=1, source_target_pairs={{0,1},{1,0},{2,3},{3,2},{4,5},{5,4},{6,7},{7,6},{8,9},{9,8},{10,11... | collective-permute-start | bytes 6291464 | tf_op jit(solution)/shard_map/ppermute | solution.py:281
  102.0 15.7 %collective-permute-start.6 = (bf16[4,4,96,128]{3,2,1,0:T(8,128)(2,1)}, bf16[4,4,96,128]{3,2,1,0:T(8,128)(2,1)S(1)}, u32[]{:S(2)}, u32[]{:S(2)}) collective-permute-start(bf16[4,4,96,128]{3,2,1,0:T(8,128)(2,1)} %get-tuple-element.18), channel_id=1, source_target_pairs={{8,0},{16,8},{24,16},{32,24},{40,32},{48,40},{56,48},{64,56},{72,6... | collective-permute-start | bytes 1179656 | tf_op jit(solution)/shard_map/ppermute | solution.py:256
  105.0 14.7 %collective-permute-start.7 = (bf16[4,4,96,128]{3,2,1,0:T(8,128)(2,1)}, bf16[4,4,96,128]{3,2,1,0:T(8,128)(2,1)}, u32[]{:S(2)}, u32[]{:S(2)}) collective-permute-start(bf16[4,4,96,128]{3,2,1,0:T(8,128)(2,1)} %get-tuple-element.17), channel_id=1, source_target_pairs={{120,0},{0,8},{8,16},{16,24},{24,32},{32,40},{40,48},{48,56},{56,6... | collective-permute-start | bytes 1179656 | tf_op jit(solution)/shard_map/ppermute | solution.py:256
  109.2 23.0 %collective-permute-start.8 = (bf16[8,128,256]{2,1,0:T(8,128)(2,1)S(1)}, bf16[8,128,256]{2,1,0:T(8,128)(2,1)}, u32[]{:S(2)}, u32[]{:S(2)}) collective-permute-start(bf16[8,128,256]{2,1,0:T(8,128)(2,1)S(1)} %collective-permute-done.3.ahead), channel_id=1, source_target_pairs={{8,0},{16,8},{24,16},{32,24},{40,32},{48,40},{56,48},{64,56},{72,6... | collective-permute-start | bytes 1572872 | tf_op jit(solution)/shard_map/ppermute | solution.py:256
  114.0 5.7 %copy-start = (bf16[32,128,128]{2,1,0:T(8,128)(2,1)S(1)}, bf16[32,128,128]{2,1,0:T(8,128)(2,1)}, u32[]{:S(2)}) copy-start(bf16[32,128,128]{2,1,0:T(8,128)(2,1)} %all-gather.4.cloned.1.call-done) | copy-start | bytes 3145732
  114.0 5.7 %copy-start.3 = (s32[5]{0:T(128)S(1)}, s32[5]{0:T(128)}, u32[]{:S(2)}) copy-start(s32[5]{0:T(128)} %stack.23.where) | copy-start | bytes 64
  117.7 9.0 %copy-start.12 = (s32[64,16]{0,1:T(8,128)S(1)}, s32[64,16]{0,1:T(8,128)}, u32[]{:S(2)}) copy-start(s32[64,16]{0,1:T(8,128)} %param.15) | copy-start | bytes 12292
  117.7 9.8 %copy-start.4 = (s32[5]{0:T(128)S(1)}, s32[5]{0:T(128)}, u32[]{:S(2)}) copy-start(s32[5]{0:T(128)} %stack.23.where) | copy-start | bytes 64
  117.7 9.7 %copy-start.7 = (s32[128]{0:T(128)S(1)}, s32[128]{0:T(128)}, u32[]{:S(2)}) copy-start(s32[128]{0:T(128)} %place.1) | copy-start | bytes 1540
  123.2 13.5 %all-to-all-start.2 = ((bf16[4,576,128]{2,1,0:T(8,128)(2,1)}), bf16[4,576,128]{2,1,0:T(8,128)(2,1)S(1)}, u32[]{:S(2)}, u32[]{:S(2)}) async-start(bf16[4,576,128]{2,1,0:T(8,128)(2,1)} %shard_map.94), calls=%async_computation.2 | async-start | bytes 1179648 | tf_op jit(solution)/shard_map/all_to_all | solution.py:240
  (1 other events, 0.6 us)
Sparse Core Ops, SparseCore 0:
  39.5 58.4 all-gather.3

commit v6 on v3

--- a/solution.py
+++ b/solution.py
@@ -1,3 +1,5 @@
+import math
+
 import jax
 import jax.numpy as jnp
 from jax import lax
@@ -17,12 +19,13 @@
 PICKS = 16
 ROWS = NX * SEQ
 COLS = RATIO * SEQ
-SCALE = HEAD ** (-0.5)
+RATE = HEAD ** (-0.5) * math.log2(math.e)
 LOW = -1e30
 UNITS = 128
 
 VMEM = pl.BlockSpec(memory_space=pltpu.VMEM)
 SMEM = pl.BlockSpec(memory_space=pltpu.SMEM)
+ANY = pl.BlockSpec(memory_space=pl.ANY)
 PARAMS = pltpu.CompilerParams(vmem_limit_bytes=24 * 1024 * 1024)
 
 
@@ -46,7 +49,17 @@
     return jnp.where(lane < HALF, left, right).astype(BF16)
 
 
-def pack_kernel(wq, wk, wv, out):
+def pack_kernel(*refs):
+    sources, (out, tagged), copies, done = refs[:5], refs[5:7], refs[7:12], refs[12]
+    moves = [
+        pltpu.make_async_copy(src, dst, done.at[i])
+        for i, (src, dst) in enumerate(zip(sources, copies))
+    ]
+    for move in moves:
+        move.start()
+    for move in moves:
+        move.wait()
+    wq, wk, wv, tokens, flags = copies
     for part in range(NX):
         src = wk if part < 2 else wv
         at = HALF * (part % 2)
@@ -54,6 +67,8 @@
         for copy in range(4):
             out[part, copy, 0:64, :] = wq[:, part * HEAD : (part + 1) * HEAD]
             out[part, copy, 64:96, :] = packed
+    tagged[0:SEQ, :] = tokens[...]
+    tagged[SEQ : SEQ + 16, :] = flags[...]
 
 
 def norm_kernel(where, mine, other, gain, out):
@@ -64,15 +79,14 @@
         for src in (mine, other):
             for y in range(4):
                 for c in range(4):
-                    feats = src[row, y, :, c * HEAD : (c + 1) * HEAD].astype(F32)
+                    feats = src[row, y, 0:SEQ, c * HEAD : (c + 1) * HEAD].astype(F32)
                     total = total + feats * feats
         power = jnp.sum(total, axis=-1, keepdims=True) * (1.0 / 4096.0)
         factor = lax.rsqrt(power + 1e-05)
-        for src, flip in ((mine, 0), (other, 1)):
-            side = core if flip == 0 else 1 - core
+        for src, side in ((mine, core), (other, 1 - core)):
             for y in range(4):
                 slot = 2 * y + side
-                feats = src[row, y].astype(F32)
+                feats = src[row, y, 0:SEQ, :].astype(F32)
                 out[slot, rows, :] = (feats * factor * gain[slot]).astype(BF16)
 
 
@@ -89,7 +103,8 @@
         row, pick = i // PICKS, i % PICKS
         at = place[lists[row * NZ + z, pick]]
         owner, local = at // 2, at % 2
-        bits = use[row * 2, pick] + 2 * use[row * 2 + 1, pick]
+        step = lax.rem(row - x + NX, NX) * 2
+        bits = use[step, pick] + 2 * use[step + 1, pick]
         entry = row * NZ + owner % NZ
         mine = jnp.where(owner // NZ == x, 1, 0)
         table[entry] = table[entry] + mine * bits * jnp.where(local == 1, 4, 1)
@@ -102,22 +117,17 @@
         units[count + 1] = i * 16 + bits
         return count + jnp.where(bits > 0, 1, 0)
 
-    units[0] = lax.fori_loop(0, NX * NZ, compact, 0)
-
-
-def project_kernel(where, normed, near, ahead, far_a, far_b, behind, send, weights):
+    count = lax.fori_loop(0, NX * NZ, compact, 0)
+    units[0] = count
+    units[count + 1] = 0
+
+
+def project_kernel(where, normed, near, ahead, far, behind, send, weights):
     lane_part = where[2]
-    for step in range(4):
+    for step, blocks in enumerate((near, ahead, far, behind)):
         row = lax.rem(lane_part + step, 4) * HALF
         for b in range(16):
-            if step == 0:
-                block = near[b]
-            elif step == 1:
-                block = ahead[b]
-            elif step == 3:
-                block = behind[b]
-            else:
-                block = far_a[b] if b < 8 else far_b[b - 8]
+            block = blocks[b]
             base = pl.multiple_of(b * 256 + row, HALF)
             packed = block[64:96, :]
             weights[pl.ds(base, 64), 0:HEAD] = block[0:64, :]
@@ -148,9 +158,7 @@
 
 
 def scores_of(keys, query):
-    return (
-        lax.dot_general(keys, query, (((1,), (1,)), ((), ())), preferred_element_type=F32) * SCALE
-    )
+    return lax.dot_general(keys, query, (((1,), (1,)), ((), ())), preferred_element_type=F32)
 
 
 def own_scores(got, group):
@@ -166,12 +174,16 @@
     keys = docs[pl.ds(owner * 2, 2), :, 0:HEAD].reshape(2 * SEQ, HEAD)
     scores = scores_of(keys, queries(got, group))
     second = (lax.broadcasted_iota(jnp.int32, (1, COLS), 1) % SEQ) // HALF
-    kept = []
+    parts = []
     for local in range(2):
         use_a, use_b = (bits // (4**local)) % 2, (bits // (2 * 4**local)) % 2
-        keep = jnp.where(second == 0, use_a, use_b)
-        kept.append(jnp.where(keep > 0, scores[local * SEQ : (local + 1) * SEQ], LOW))
-    return group, owner, jnp.concatenate(kept, axis=0)
+        keep = jnp.where(second == 0, use_a, use_b) > 0
+        parts.append((scores[local * SEQ : (local + 1) * SEQ], keep))
+    return group, owner, parts
+
+
+def weigh(scores, shift):
+    return jnp.exp2((scores - shift) * RATE)
 
 
 def stats_kernel(where, units, got, docs, send, stats):
@@ -181,18 +193,28 @@
     stats[0:4, :] = jnp.full((4, COLS), LOW, F32)
     stats[4:8, :] = jnp.zeros((4, COLS), F32)
     stats[pl.ds(x, 1), :] = top
-    stats[pl.ds(x + 4, 1), :] = jnp.sum(jnp.exp(scores - top), axis=0, keepdims=True)
-
-    def unit(i, carry):
-        group, owner, scores = unit_scores(units[i + 1], got, docs)
-        before = stats[pl.ds(group, 1), :]
-        top = jnp.maximum(before, jnp.max(scores, axis=0, keepdims=True))
-        part = jnp.sum(jnp.exp(scores - top), axis=0, keepdims=True)
-        stats[pl.ds(group, 1), :] = top
-        stats[pl.ds(group + 4, 1), :] = stats[pl.ds(group + 4, 1), :] * jnp.exp(before - top) + part
+    stats[pl.ds(x + 4, 1), :] = jnp.sum(weigh(scores, top), axis=0, keepdims=True)
+
+    def unit(code):
+        group, _, parts = unit_scores(code, got, docs)
+        tops = [jnp.where(keep, jnp.max(s, axis=0, keepdims=True), LOW) for s, keep in parts]
+        top = jnp.maximum(tops[0], tops[1])
+        sums = [
+            jnp.sum(weigh(s, jnp.where(keep, top, -LOW)), axis=0, keepdims=True)
+            for s, keep in parts
+        ]
+        return group, top, sums[0] + sums[1]
+
+    def pair(i, carry):
+        for group, top, part in [unit(units[2 * i + 1]), unit(units[2 * i + 2])]:
+            before = stats[pl.ds(group, 1), :]
+            new = jnp.maximum(before, top)
+            old = stats[pl.ds(group + 4, 1), :] * weigh(before, new)
+            stats[pl.ds(group, 1), :] = new
+            stats[pl.ds(group + 4, 1), :] = old + part * weigh(top, new)
         return carry
 
-    lax.fori_loop(0, units[0], unit, 0)
+    lax.fori_loop(0, (units[0] + 1) // 2, pair, 0)
     for dest in range(NX):
         send[dest] = stats[...]
 
@@ -203,26 +225,32 @@
     top = jnp.maximum(jnp.maximum(tops[0], tops[1]), jnp.maximum(tops[2], tops[3]))
     sums = jnp.zeros((4, COLS), F32)
     for src in range(NX):
-        sums = sums + all_stats[src, 4:8, :] * jnp.exp(tops[src] - top)
+        sums = sums + all_stats[src, 4:8, :] * weigh(tops[src], top)
     total[0:4, :] = top
-    total[4:8, :] = sums
+    total[4:8, :] = 1.0 / sums
     send[...] = jnp.zeros(send.shape, F32)
 
-    def add(group, scores, values):
-        expo = jnp.exp(scores - total[pl.ds(group, 1), :])
-        probs = (expo / total[pl.ds(group + 4, 1), :]).astype(BF16)
-        out = lax.dot_general(values, probs, (((0,), (0,)), ((), ())), preferred_element_type=F32)
-        send[pl.ds(group, 1)] = send[pl.ds(group, 1)] + out[None]
-
-    add(x, own_scores(got, x), own_part(got, 2))
-
-    def unit(i, carry):
-        group, owner, scores = unit_scores(units[i + 1], got, docs)
+    def apply(values, probs):
+        return lax.dot_general(values, probs, (((0,), (0,)), ((), ())), preferred_element_type=F32)
+
+    own = weigh(own_scores(got, x), total[pl.ds(x, 1), :]) * total[pl.ds(x + 4, 1), :]
+    send[pl.ds(x, 1)] = apply(own_part(got, 2), own.astype(BF16))[None]
+
+    def unit(code):
+        group, owner, parts = unit_scores(code, got, docs)
+        top, inverse = total[pl.ds(group, 1), :], total[pl.ds(group + 4, 1), :]
+        probs = [
+            (weigh(s, jnp.where(keep, top, -LOW)) * inverse).astype(BF16) for s, keep in parts
+        ]
         values = docs[pl.ds(owner * 2, 2), :, HEAD : 2 * HEAD].reshape(2 * SEQ, HEAD)
-        add(group, scores, values)
+        return group, apply(values, jnp.concatenate(probs, axis=0))
+
+    def pair(i, carry):
+        for group, out in [unit(units[2 * i + 1]), unit(units[2 * i + 2])]:
+            send[pl.ds(group, 1)] = send[pl.ds(group, 1)] + out[None]
         return carry
 
-    lax.fori_loop(0, units[0], unit, 0)
+    lax.fori_loop(0, (units[0] + 1) // 2, pair, 0)
 
 
 def finish_kernel(got, out):
@@ -234,10 +262,6 @@
 
 def exchange(array, axes):
     return lax.all_to_all(array, axes, 0, 0, tiled=True)
-
-
-def spread(array, axes, count):
-    return exchange(jnp.broadcast_to(array[None], (count, *array.shape)), axes)
 
 
 def shards(tokens, norm_gain, wq, wk, wv, doc_cache, doc_lists, doc_place, block_use):
@@ -247,20 +271,27 @@
     x, zh, zl = lax.axis_index("x"), lax.axis_index("zh"), lax.axis_index("zl")
     where = jnp.stack([x, zh * 4 + zl, zl, lax.axis_index("core")]).astype(jnp.int32)
 
-    parts = call(pack_kernel, shape((4, 4, 96, HEAD), BF16), (wq, wk, wv), [VMEM] * 3)
+    flags = jnp.pad(block_use.astype(BF16), ((0, 14), (0, 512 - PICKS)))
+    sources = (wq, wk, wv, tokens, flags)
+    parts, tagged = call(
+        pack_kernel,
+        [shape((4, 4, 96, HEAD), BF16), shape((SEQ + 16, 512), BF16)],
+        sources,
+        [ANY] * 5,
+        out_specs=[VMEM] * 2,
+        scratch=[pltpu.VMEM(a.shape, BF16) for a in sources] + [pltpu.SemaphoreType.DMA((5,))],
+    )
     near = exchange(parts.reshape(16, 96, HEAD), ("x", "zh"))
 
     def from_z(array, step):
         return lax.ppermute(array, z_axes, [((i + step) % NZ, i) for i in range(NZ)])
 
-    tokens, _ = lax.optimization_barrier((tokens, parts))
-    by_y = lax.all_gather(tokens, "y")
     def from_x(array, step):
         return lax.ppermute(array, "x", [((i + step) % NX, i) for i in range(NX)])
 
-    mine = jnp.concatenate(
-        [by_y, from_x(by_y, 1), from_x(by_y[0:2], 2), from_x(by_y[2:4], -2), from_x(by_y, -1)]
-    ).reshape(4, 4, SEQ, 512)
+    by_y = lax.all_gather(tagged, "y")
+    mine = jnp.concatenate([by_y, from_x(by_y, 1), from_x(by_y, 2), from_x(by_y, 3)])
+    mine = mine.reshape(NX, 4, SEQ + 16, 512)
     ahead = from_z(near, 1)
     behind = from_z(near, -1)
     mine, ahead, behind = lax.optimization_barrier((mine, ahead, behind))
@@ -274,7 +305,7 @@
         flops=ROWS * 4096 * 8,
         moved=8 << 20,
     )
-    use = spread(block_use, "x", NX).reshape(8, PICKS)
+    use = mine[:, 0, SEQ : SEQ + 2, 0:PICKS].astype(jnp.int32).reshape(8, PICKS)
     units = call(
         route_kernel,
         shape((UNITS,), jnp.int32),
@@ -284,13 +315,12 @@
         scratch=[pltpu.SMEM((NX * NZ,), jnp.int32)],
     )
 
-    far_a = from_z(ahead[0:8], 1)
-    far_b = from_z(behind[8:16], -1)
+    far = from_z(ahead, 1)
     send = call(
         project_kernel,
         shape((NX, ROWS + HALF, HEAD), BF16),
-        (where, normed, near, ahead, far_a, far_b, behind),
-        [SMEM] + [VMEM] * 6,
+        (where, normed, near, ahead, far, behind),
+        [SMEM] + [VMEM] * 5,
         scratch=[pltpu.VMEM((4096, 2 * HEAD), BF16)],
         flops=2 * ROWS * 4096 * 256,
         moved=8 << 20,

time: 166 us -> 162 us (0.976)
  starting transfers between devices: 59 us -> 49.3 us
  waiting for transfers between devices: 16.1 us -> 25.8 us
  local copies, waits for them, and re-layouts: 12.1 us -> 7.83 us
  other arithmetic: 0.08 us -> 3.37 us
  Pallas kernels: 26.5 us -> 23.8 us
    ppermute x4 -> x3, waiting for transfers between devices: 2 us -> 11.1 us  [from_x(): return lax.ppermute(array, 'x', [((i + step) % NX, i) for i in range(NX)])]
    all_to_all x3 -> x2, starting transfers between devices: 26.9 us -> 21.1 us  [exchange(): return lax.all_to_all(array, axes, 0, 0, tiled=True)]
    ppermute x4 -> x3, starting transfers between devices: 14.4 us -> 10.5 us  [from_x(): return lax.ppermute(array, 'x', [((i + step) % NX, i) for i in range(NX)])]
    slice x3 -> x1, local copies, waits for them, and re-layouts: 3.25 us -> 0.01 us  [shards(): use = mine[:, 0, SEQ:SEQ + 2, 0:PICKS].astype(jnp.int32).reshape(8, PICKS)]
    pallas_call x7, Pallas kernels: 26.5 us -> 23.8 us  [call(): pl.pallas_call(kernel, out_shape=outs, in_specs=specs, out_specs=VMEM if...]
    concatenate x0 -> x1, other arithmetic: none -> 1.91 us  [shards(): jnp.concatenate([by_y, from_x(by_y, 1), from_x(by_y, 2), from_x(by_y, 3)])]
    ppermute x4 -> x3, waiting for transfers between devices: 8.47 us -> 9.4 us  [from_z(): lax.ppermute(array, z_axes, [((i + step) % NZ, i) for i in range(NZ)])]
    unnamed x21 -> x27, local copies, waits for them, and re-layouts: 7.12 us -> 7.81 us
  transfers between devices with their start and end apart: 13 -> 10, of which waited for: 5 -> 4; matrix products, arithmetic and copies ran while one was open for 5% -> 2% of each run, Pallas kernels for 7% -> 8%
where the time goes in v6:
time: 162 us; the launch traced here: 161 us
  starting transfers between devices  49.3 us (30%)
  blocking collectives  37.2 us (23%)
  waiting for transfers between devices  25.8 us (16%)
  Pallas kernels  23.8 us (15%)
  between operations  13.6 us (8%)
  local copies, waits for them, and re-layouts  7.83 us (5%)
  other arithmetic  3.37 us (2%)
    pallas_call x7, Pallas kernels, call(): pl.pallas_call(kernel, out_shape=outs, in_specs=specs, out_specs=VMEM if...  23.8 us
    all_to_all x2, blocking collectives, exchange(): return lax.all_to_all(array, axes, 0, 0, tiled=True)  23.6 us
    all_to_all x2, starting transfers between devices, exchange(): return lax.all_to_all(array, axes, 0, 0, tiled=True)  21.1 us
    ppermute x3, starting transfers between devices, from_z(): lax.ppermute(array, z_axes, [((i + step) % NZ, i) for i in range(NZ)])  15.6 us
    all_gather x1, blocking collectives, shards(): by_y = lax.all_gather(tagged, 'y')  13.7 us
    ppermute x3, waiting for transfers between devices, from_x(): return lax.ppermute(array, 'x', [((i + step) % NX, i) for i in range(NX)])  11.1 us
    ppermute x3, starting transfers between devices, from_x(): return lax.ppermute(array, 'x', [((i + step) % NX, i) for i in range(NX)])  10.5 us
    ppermute x3, waiting for transfers between devices, from_z(): lax.ppermute(array, z_axes, [((i + step) % NZ, i) for i in range(NZ)])  9.4 us
  transfers between devices with their start and end apart: 10, of which 4 were waited for; matrix products, arithmetic and copies ran while one was open for 2% of the time, Pallas kernels for 8%

profile of v6, /device:TPU:24, one launch (start us, length us, event | category | flops | bytes accessed | tf_op | source)
XLA Modules:
  0.0 160.9 jit_solution(9737139798237327911)
XLA Ops:
  10.4 1.2 shard_map.91
  11.6 17.7 %all-to-all-start = ((bf16[16,96,128]{2,1,0:T(8,128)(2,1)}), bf16[16,96,128]{2,1,0:T(8,128)(2,1)S(1)}, u32[]{:S(2)}, u32[]{:S(2)}) async-start(bf16[16,96,128]{2,1,0:T(8,128)(2,1)} %bitcast.6), calls=%async_computation | async-start | bytes 786432 | tf_op jit(solution)/shard_map/all_to_all | solution.py:264
  30.0 13.7 %all-gather = bf16[576,512]{1,0:T(8,128)(2,1)S(1)} all-gather(bf16[144,512]{1,0:T(8,128)(2,1)S(1)} %get-tuple-element.10), channel_id=2, replica_groups=mesh['x'=4,'zh'=4,'zl'=4,'y'=4,'core'=2] {'y'}, dimensions={0}, use_global_device_ids=true | all-gather | bytes 737280 | tf_op jit(solution)/shard_map/all_gather | solution.py:292
  43.7 5.0 %collective-permute-start = (bf16[4,144,512]{2,1,0:T(8,128)(2,1)S(1)}, bf16[4,144,512]{2,1,0:T(8,128)(2,1)S(1)}, u32[]{:S(2)}, u32[]{:S(2)}) collective-permute-start(bf16[4,144,512]{2,1,0:T(8,128)(2,1)S(1)} %bitcast.14), channel_id=1, source_target_pairs={{128,0},{256,128},{384,256},{0,384},{129,1},{257,129},{385,257},{1... | collective-permute-start | bytes 1769480 | tf_op jit(solution)/shard_map/ppermute | solution.py:290
  48.7 2.8 %collective-permute-start.1 = (bf16[4,144,512]{2,1,0:T(8,128)(2,1)S(1)}, bf16[4,144,512]{2,1,0:T(8,128)(2,1)S(1)}, u32[]{:S(2)}, u32[]{:S(2)}) collective-permute-start(bf16[4,144,512]{2,1,0:T(8,128)(2,1)S(1)} %bitcast.15), channel_id=1, source_target_pairs={{256,0},{384,128},{0,256},{128,384},{257,1},{385,129},{1,257},{129... | collective-permute-start | bytes 1769480 | tf_op jit(solution)/shard_map/ppermute | solution.py:290
  51.4 2.8 %collective-permute-start.2 = (bf16[4,144,512]{2,1,0:T(8,128)(2,1)S(1)}, bf16[4,144,512]{2,1,0:T(8,128)(2,1)}, u32[]{:S(2)}, u32[]{:S(2)}) collective-permute-start(bf16[4,144,512]{2,1,0:T(8,128)(2,1)S(1)} %bitcast.16), channel_id=1, source_target_pairs={{384,0},{0,128},{128,256},{256,384},{385,1},{1,129},{129,257},{257... | collective-permute-start | bytes 1769480 | tf_op jit(solution)/shard_map/ppermute | solution.py:290
  54.2 5.9 %collective-permute-start.3 = (bf16[16,96,128]{2,1,0:T(8,128)(2,1)S(1)}, bf16[16,96,128]{2,1,0:T(8,128)(2,1)S(1)}, u32[]{:S(2)}, u32[]{:S(2)}) collective-permute-start(bf16[16,96,128]{2,1,0:T(8,128)(2,1)S(1)} %all-to-all-done.near), channel_id=1, source_target_pairs={{8,0},{16,8},{24,16},{32,24},{40,32},{48,40},{56,48},{64,56},{72,6... | collective-permute-start | bytes 1179656 | tf_op jit(solution)/shard_map/ppermute | solution.py:287
  60.1 3.4 %collective-permute-start.4 = (bf16[16,96,128]{2,1,0:T(8,128)(2,1)S(1)}, bf16[16,96,128]{2,1,0:T(8,128)(2,1)S(1)}, u32[]{:S(2)}, u32[]{:S(2)}) collective-permute-start(bf16[16,96,128]{2,1,0:T(8,128)(2,1)S(1)} %all-to-all-done.near), channel_id=1, source_target_pairs={{120,0},{0,8},{8,16},{16,24},{24,32},{32,40},{40,48},{48,56},{56,6... | collective-permute-start | bytes 1179656 | tf_op jit(solution)/shard_map/ppermute | solution.py:287
  63.5 7.4 %collective-permute-done = bf16[4,144,512]{2,1,0:T(8,128)(2,1)S(1)} collective-permute-done((bf16[4,144,512]{2,1,0:T(8,128)(2,1)S(1)}, bf16[4,144,512]{2,1,0:T(8,128)(2,1)S(1)}, u32[]{:S(2)}, u32[]{:S(2)}) %collective-permute-start) | collective-permute-done | bytes 589856 | tf_op jit(solution)/shard_map/ppermute | solution.py:290
  72.5 3.7 %collective-permute-done.2 = bf16[4,144,512]{2,1,0:T(8,128)(2,1)} collective-permute-done((bf16[4,144,512]{2,1,0:T(8,128)(2,1)S(1)}, bf16[4,144,512]{2,1,0:T(8,128)(2,1)}, u32[]{:S(2)}, u32[]{:S(2)}) %collective-permute-start.2) | collective-permute-done | bytes 589856 | tf_op jit(solution)/shard_map/ppermute | solution.py:290
  76.2 1.9 %pad_maximum_fusion = bf16[16,144,512]{2,1,0:T(8,128)(2,1)S(1)} fusion(bf16[4,144,512]{2,1,0:T(8,128)(2,1)} %collective-permute-done.2, bf16[4,144,512]{2,1,0:T(8,128)(2,1)} %copy-done.11, bf16[4,144,512]{2,1,0:T(8,128)(2,1)} %copy-done.10, bf16[4,144,512]{2,1,0:T(8,128)(2,1)} %bitcast.17), kind=kLoop, calls=%fused_computation | loop fusion | flops 3538944 | bytes 4718592 | tf_op jit(solution)/shard_map/concatenate | solution.py:293
  78.1 1.9 %collective-permute-start.5 = (bf16[4,4,144,512]{3,2,1,0:T(8,128)(2,1)S(1)}, bf16[4,4,144,512]{3,2,1,0:T(8,128)(2,1)}, u32[]{:S(2)}, u32[]{:S(2)}) collective-permute-start(bf16[4,4,144,512]{3,2,1,0:T(8,128)(2,1)S(1)} %bitcast.10), channel_id=1, source_target_pairs={{0,1},{1,0},{2,3},{3,2},{4,5},{5,4},{6,7},{7,6},{8,9},{9,8},{10,11... | collective-permute-start | bytes 7077896 | tf_op jit(solution)/shard_map/ppermute | solution.py:298
  80.1 6.4 %collective-permute-start.6 = (bf16[16,96,128]{2,1,0:T(8,128)(2,1)S(1)}, bf16[16,96,128]{2,1,0:T(8,128)(2,1)}, u32[]{:S(2)}, u32[]{:S(2)}) collective-permute-start(bf16[16,96,128]{2,1,0:T(8,128)(2,1)S(1)} %collective-permute-done.3.ahead), channel_id=1, source_target_pairs={{8,0},{16,8},{24,16},{32,24},{40,32},{48,40},{56,48},{64,56},{72,6... | collective-permute-start | bytes 1179656 | tf_op jit(solution)/shard_map/ppermute | solution.py:287
  87.3 3.7 %shard_map.93.normed = bf16[8,512,512]{2,1,0:T(8,128)(2,1)S(1)} custom-call(s32[4]{0:T(128)S(1)} %pad_add_fusion.where, bf16[4,4,144,512]{3,2,1,0:T(8,128)(2,1)S(1)} %bitcast.11, bf16[4,4,144,512]{3,2,1,0:T(8,128)(2,1)} %collective-permute-done.5.other, f32[8,1,512]{2,1,0:T(1,128)S(1)} %bitcast.13), custom_call_target="tpu_custom_call" | custom-call | flops 16777216 | bytes 8388608 | tf_op jit(solution)/shard_map/pallas_call | solution.py:33
  91.0 9.4 %collective-permute-done.6.far = bf16[16,96,128]{2,1,0:T(8,128)(2,1)} collective-permute-done((bf16[16,96,128]{2,1,0:T(8,128)(2,1)S(1)}, bf16[16,96,128]{2,1,0:T(8,128)(2,1)}, u32[]{:S(2)}, u32[]{:S(2)}) %collective-permute-start.6) | collective-permute-done | bytes 393248 | tf_op jit(solution)/shard_map/ppermute | solution.py:287
  100.4 3.6 %shard_map.94 = bf16[4,576,128]{2,1,0:T(8,128)(2,1)} custom-call(s32[4]{0:T(128)S(1)} %pad_add_fusion.where, bf16[8,512,512]{2,1,0:T(8,128)(2,1)S(1)} %shard_map.93.normed, bf16[16,96,128]{2,1,0:T(8,128)(2,1)S(1)} %all-to-all-done.near, bf16[16,96,128]{2,1,0:T(8,128)(2,1)S(1)} %collective-permute-done.3.ahead, ...), custom_call_target="tpu_custom_call" | custom-call | flops 1073741824 | bytes 8388608 | tf_op jit(solution)/shard_map/pallas_call | solution.py:33
  104.0 3.5 %all-to-all-start.1 = ((bf16[4,576,128]{2,1,0:T(8,128)(2,1)}), bf16[4,576,128]{2,1,0:T(8,128)(2,1)S(1)}, u32[]{:S(2)}, u32[]{:S(2)}) async-start(bf16[4,576,128]{2,1,0:T(8,128)(2,1)} %shard_map.94), calls=%async_computation.1 | async-start | bytes 1179648 | tf_op jit(solution)/shard_map/all_to_all | solution.py:264
  108.3 4.8 %shard_map.92.units = s32[128]{0:T(128)S(1)} custom-call(s32[4]{0:T(128)S(1)} %copy-done.4, s32[64,16]{1,0:T(8,128)S(1)} %copy.11.lists, s32[128]{0:T(128)S(1)} %copy-done.8, s32[8,16]{1,0:T(8,128)S(1)} %convert.2.use), custom_call_target="tpu_custom_call" | custom-call | tf_op jit(solution)/shard_map/pallas_call | solution.py:33
  113.1 4.7 %all-to-all-done.1.got = bf16[4,576,128]{2,1,0:T(8,128)(2,1)S(1)} async-done(((bf16[4,576,128]{2,1,0:T(8,128)(2,1)}), bf16[4,576,128]{2,1,0:T(8,128)(2,1)S(1)}, u32[]{:S(2)}, u32[]{:S(2)}) %all-to-all-start.1) | async-done | bytes 589856 | tf_op jit(solution)/shard_map/all_to_all | solution.py:264
  117.7 1.6 copy-done
  120.0 4.1 %shard_map.95 = f32[4,8,512]{2,1,0:T(8,128)S(1)} custom-call(s32[4]{0:T(128)S(1)} %copy-done.5, s32[128]{0:T(128)S(1)} %shard_map.92.units, bf16[4,576,128]{2,1,0:T(8,128)(2,1)S(1)} %all-to-all-done.1.got, bf16[32,128,256]{2,1,0:T(8,128)(2,1)S(1)} %copy-done), custom_call_target="tpu_custom_call" | custom-call | tf_op jit(solution)/shard_map/pallas_call | solution.py:33
  124.1 8.0 %all_to_all.20.all_stats = f32[4,8,512]{2,1,0:T(8,128)S(1)} all-to-all(f32[4,8,512]{2,1,0:T(8,128)S(1)} %shard_map.95), channel_id=1, replica_groups=mesh['x'=4,'zh'=4,'zl'=4,'y'=4,'core'=2] {'x'}, dimensions={0} | all-to-all | bytes 131072 | tf_op jit(solution)/shard_map/all_to_all | solution.py:264
  132.1 5.7 %shard_map.96 = f32[4,128,512]{2,1,0:T(8,128)S(1)} custom-call(s32[4]{0:T(128)S(1)} %copy-done.5, s32[128]{0:T(128)S(1)} %shard_map.92.units, bf16[4,576,128]{2,1,0:T(8,128)(2,1)S(1)} %all-to-all-done.1.got, bf16[32,128,256]{2,1,0:T(8,128)(2,1)S(1)} %copy-done, f32[4,8,512]{2,1,0:T(8,128)S(1)} %all_to_all.20.all_stats), custom_call_target="tpu_custom_call" | custom-call | tf_op jit(solution)/shard_map/pallas_call | solution.py:33
  137.7 15.6 %all_to_all.21.got = f32[4,128,512]{2,1,0:T(8,128)S(1)} all-to-all(f32[4,128,512]{2,1,0:T(8,128)S(1)} %shard_map.96), channel_id=1, replica_groups=mesh['x'=4,'zh'=4,'zl'=4,'y'=4,'core'=2] {'x'}, dimensions={0} | all-to-all | bytes 2097152 | tf_op jit(solution)/shard_map/all_to_all | solution.py:264
  (41 shorter events, 9.2 us)
Async XLA Ops:
  7.2 0.9 copy-start.1
  8.1 0.8 copy-start.2
  9.0 0.7 copy-start.6
  9.7 0.7 copy-start.7
  11.6 42.6 %all-to-all-start = ((bf16[16,96,128]{2,1,0:T(8,128)(2,1)}), bf16[16,96,128]{2,1,0:T(8,128)(2,1)S(1)}, u32[]{:S(2)}, u32[]{:S(2)}) async-start(bf16[16,96,128]{2,1,0:T(8,128)(2,1)} %bitcast.6), calls=%async_computation | async-start | bytes 786432 | tf_op jit(solution)/shard_map/all_to_all | solution.py:264
  29.3 83.8 %all-gather.3.cloned.1.call-start = ((), (), s32[]{:S(2)}) async-start(), calls=%async_computation.4 | async-start | bytes 2228224 | tf_op jit(solution)/shard_map/all_gather | solution.py:270
  43.7 27.2 %copy-start.9 = (bf16[576,512]{1,0:T(8,128)(2,1)}, bf16[576,512]{1,0:T(8,128)(2,1)S(1)}, u32[]{:S(2)}) copy-start(bf16[576,512]{1,0:T(8,128)(2,1)S(1)} %all-gather) | copy-start | bytes 1769476
  43.7 27.2 %collective-permute-start = (bf16[4,144,512]{2,1,0:T(8,128)(2,1)S(1)}, bf16[4,144,512]{2,1,0:T(8,128)(2,1)S(1)}, u32[]{:S(2)}, u32[]{:S(2)}) collective-permute-start(bf16[4,144,512]{2,1,0:T(8,128)(2,1)S(1)} %bitcast.14), channel_id=1, source_target_pairs={{128,0},{256,128},{384,256},{0,384},{129,1},{257,129},{385,257},{1... | collective-permute-start | bytes 1769480 | tf_op jit(solution)/shard_map/ppermute | solution.py:290
  48.7 22.2 %collective-permute-start.1 = (bf16[4,144,512]{2,1,0:T(8,128)(2,1)S(1)}, bf16[4,144,512]{2,1,0:T(8,128)(2,1)S(1)}, u32[]{:S(2)}, u32[]{:S(2)}) collective-permute-start(bf16[4,144,512]{2,1,0:T(8,128)(2,1)S(1)} %bitcast.15), channel_id=1, source_target_pairs={{256,0},{384,128},{0,256},{128,384},{257,1},{385,129},{1,257},{129... | collective-permute-start | bytes 1769480 | tf_op jit(solution)/shard_map/ppermute | solution.py:290
  51.4 24.8 %collective-permute-start.2 = (bf16[4,144,512]{2,1,0:T(8,128)(2,1)S(1)}, bf16[4,144,512]{2,1,0:T(8,128)(2,1)}, u32[]{:S(2)}, u32[]{:S(2)}) collective-permute-start(bf16[4,144,512]{2,1,0:T(8,128)(2,1)S(1)} %bitcast.16), channel_id=1, source_target_pairs={{384,0},{0,128},{128,256},{256,384},{385,1},{1,129},{129,257},{257... | collective-permute-start | bytes 1769480 | tf_op jit(solution)/shard_map/ppermute | solution.py:290
  54.2 23.9 %collective-permute-start.3 = (bf16[16,96,128]{2,1,0:T(8,128)(2,1)S(1)}, bf16[16,96,128]{2,1,0:T(8,128)(2,1)S(1)}, u32[]{:S(2)}, u32[]{:S(2)}) collective-permute-start(bf16[16,96,128]{2,1,0:T(8,128)(2,1)S(1)} %all-to-all-done.near), channel_id=1, source_target_pairs={{8,0},{16,8},{24,16},{32,24},{40,32},{48,40},{56,48},{64,56},{72,6... | collective-permute-start | bytes 1179656 | tf_op jit(solution)/shard_map/ppermute | solution.py:287
  60.1 18.0 %collective-permute-start.4 = (bf16[16,96,128]{2,1,0:T(8,128)(2,1)S(1)}, bf16[16,96,128]{2,1,0:T(8,128)(2,1)S(1)}, u32[]{:S(2)}, u32[]{:S(2)}) collective-permute-start(bf16[16,96,128]{2,1,0:T(8,128)(2,1)S(1)} %all-to-all-done.near), channel_id=1, source_target_pairs={{120,0},{0,8},{8,16},{16,24},{24,32},{32,40},{40,48},{48,56},{56,6... | collective-permute-start | bytes 1179656 | tf_op jit(solution)/shard_map/ppermute | solution.py:287
  70.9 0.8 copy-start.10
  71.7 0.8 copy-start.11
  78.1 9.1 %collective-permute-start.5 = (bf16[4,4,144,512]{3,2,1,0:T(8,128)(2,1)S(1)}, bf16[4,4,144,512]{3,2,1,0:T(8,128)(2,1)}, u32[]{:S(2)}, u32[]{:S(2)}) collective-permute-start(bf16[4,4,144,512]{3,2,1,0:T(8,128)(2,1)S(1)} %bitcast.10), channel_id=1, source_target_pairs={{0,1},{1,0},{2,3},{3,2},{4,5},{5,4},{6,7},{7,6},{8,9},{9,8},{10,11... | collective-permute-start | bytes 7077896 | tf_op jit(solution)/shard_map/ppermute | solution.py:298
  80.1 20.4 %collective-permute-start.6 = (bf16[16,96,128]{2,1,0:T(8,128)(2,1)S(1)}, bf16[16,96,128]{2,1,0:T(8,128)(2,1)}, u32[]{:S(2)}, u32[]{:S(2)}) collective-permute-start(bf16[16,96,128]{2,1,0:T(8,128)(2,1)S(1)} %collective-permute-done.3.ahead), channel_id=1, source_target_pairs={{8,0},{16,8},{24,16},{32,24},{40,32},{48,40},{56,48},{64,56},{72,6... | collective-permute-start | bytes 1179656 | tf_op jit(solution)/shard_map/ppermute | solution.py:287
  87.3 13.2 %copy-start.3 = (s32[4]{0:T(128)}, s32[4]{0:T(128)S(1)}, u32[]{:S(2)}) copy-start(s32[4]{0:T(128)S(1)} %pad_add_fusion.where) | copy-start | bytes 52
  91.0 16.5 %copy-start.12 = (s32[64,16]{0,1:T(8,128)S(1)}, s32[64,16]{0,1:T(8,128)}, u32[]{:S(2)}) copy-start(s32[64,16]{0,1:T(8,128)} %param.15) | copy-start | bytes 12292
  91.0 16.6 %copy-start.8 = (s32[128]{0:T(128)S(1)}, s32[128]{0:T(128)}, u32[]{:S(2)}) copy-start(s32[128]{0:T(128)} %place.1) | copy-start | bytes 1540
  104.0 13.7 %all-to-all-start.1 = ((bf16[4,576,128]{2,1,0:T(8,128)(2,1)}), bf16[4,576,128]{2,1,0:T(8,128)(2,1)S(1)}, u32[]{:S(2)}, u32[]{:S(2)}) async-start(bf16[4,576,128]{2,1,0:T(8,128)(2,1)} %shard_map.94), calls=%async_computation.1 | async-start | bytes 1179648 | tf_op jit(solution)/shard_map/all_to_all | solution.py:264
  107.6 0.7 copy-start.4
  117.7 1.6 copy-start
  119.3 0.7 copy-start.5
Sparse Core Ops, SparseCore 0:
  32.2 76.8 all-gather.2

commit v7 on v6

--- a/solution.py
+++ b/solution.py
@@ -26,17 +26,16 @@
 VMEM = pl.BlockSpec(memory_space=pltpu.VMEM)
 SMEM = pl.BlockSpec(memory_space=pltpu.SMEM)
 ANY = pl.BlockSpec(memory_space=pl.ANY)
-PARAMS = pltpu.CompilerParams(vmem_limit_bytes=24 * 1024 * 1024)
-
-
-def call(kernel, outs, args, specs, out_specs=None, scratch=(), flops=0, moved=0):
+
+
+def call(kernel, outs, args, specs, out_specs=None, scratch=(), flops=0, moved=0, limit=24):
     return pl.pallas_call(
         kernel,
         out_shape=outs,
         in_specs=specs,
         out_specs=VMEM if out_specs is None else out_specs,
         scratch_shapes=list(scratch),
-        compiler_params=PARAMS,
+        compiler_params=pltpu.CompilerParams(vmem_limit_bytes=limit * 1024 * 1024),
         cost_estimate=pl.CostEstimate(flops=flops, bytes_accessed=moved, transcendentals=0),
     )(*args)
 
@@ -50,16 +49,20 @@
 
 
 def pack_kernel(*refs):
-    sources, (out, tagged), copies, done = refs[:5], refs[5:7], refs[7:12], refs[12]
+    sources, use, (out, tagged), copies, flags, done = refs[:4], refs[4], refs[5:7], refs[7:11], refs[11], refs[12]
     moves = [
         pltpu.make_async_copy(src, dst, done.at[i])
         for i, (src, dst) in enumerate(zip(sources, copies))
     ]
     for move in moves:
         move.start()
+    flags[...] = jnp.zeros(flags.shape, jnp.int32)
+    flags[0:2, 0:PICKS] = use[...]
+    tagged[SEQ : SEQ + 16, :] = flags[...].astype(F32).astype(BF16)
     for move in moves:
         move.wait()
-    wq, wk, wv, tokens, flags = copies
+    wq, wk, wv, tokens = copies
+    tagged[0:SEQ, :] = tokens[...]
     for part in range(NX):
         src = wk if part < 2 else wv
         at = HALF * (part % 2)
@@ -67,14 +70,12 @@
         for copy in range(4):
             out[part, copy, 0:64, :] = wq[:, part * HEAD : (part + 1) * HEAD]
             out[part, copy, 64:96, :] = packed
-    tagged[0:SEQ, :] = tokens[...]
-    tagged[SEQ : SEQ + 16, :] = flags[...]
-
-
-def norm_kernel(where, mine, other, gain, out):
-    core = where[3]
+
+
+def norm_kernel(mine, other, gain, out):
+    core = lax.axis_index("core")
     for row in range(NX):
-        rows = pl.ds(pl.multiple_of(lax.rem(where[0] + row, NX) * SEQ, SEQ), SEQ)
+        rows = pl.ds(pl.multiple_of(lax.rem(lax.axis_index("x") + row, NX) * SEQ, SEQ), SEQ)
         total = jnp.zeros((SEQ, HEAD), F32)
         for src in (mine, other):
             for y in range(4):
@@ -90,8 +91,8 @@
                 out[slot, rows, :] = (feats * factor * gain[slot]).astype(BF16)
 
 
-def route_kernel(where, lists, place, use, units, table):
-    x, z = where[0], where[1]
+def route_kernel(lists, place, use, units, table):
+    x, z = lax.axis_index("x"), lax.axis_index("zh") * 4 + lax.axis_index("zl")
 
     def clear(i, carry):
         table[i] = 0
@@ -122,12 +123,11 @@
     units[count + 1] = 0
 
 
-def project_kernel(where, normed, near, ahead, far, behind, send, weights):
-    lane_part = where[2]
-    for step, blocks in enumerate((near, ahead, far, behind)):
-        row = lax.rem(lane_part + step, 4) * HALF
+def project_kernel(normed, near, ahead, far_a, far_b, behind, send, weights):
+    for step, blocks in enumerate((near, ahead, (far_a, far_b), behind)):
+        row = lax.rem(lax.axis_index("zl") + step, 4) * HALF
         for b in range(16):
-            block = blocks[b]
+            block = blocks[b // 8][b % 8] if step == 2 else blocks[b]
             base = pl.multiple_of(b * 256 + row, HALF)
             packed = block[64:96, :]
             weights[pl.ds(base, 64), 0:HEAD] = block[0:64, :]
@@ -186,8 +186,10 @@
     return jnp.exp2((scores - shift) * RATE)
 
 
-def stats_kernel(where, units, got, docs, send, stats):
-    x = where[0]
+def stats_kernel(units, got, far_docs, send, stats, docs, done):
+    fetch = pltpu.make_async_copy(far_docs, docs, done)
+    fetch.start()
+    x = lax.axis_index("x")
     scores = own_scores(got, x)
     top = jnp.max(scores, axis=0, keepdims=True)
     stats[0:4, :] = jnp.full((4, COLS), LOW, F32)
@@ -214,13 +216,16 @@
             stats[pl.ds(group + 4, 1), :] = old + part * weigh(top, new)
         return carry
 
+    fetch.wait()
     lax.fori_loop(0, (units[0] + 1) // 2, pair, 0)
     for dest in range(NX):
         send[dest] = stats[...]
 
 
-def values_kernel(where, units, got, docs, all_stats, send, total):
-    x = where[0]
+def values_kernel(units, got, far_docs, all_stats, send, total, docs, done):
+    fetch = pltpu.make_async_copy(far_docs, docs, done)
+    fetch.start()
+    x = lax.axis_index("x")
     tops = [all_stats[src, 0:4, :] for src in range(NX)]
     top = jnp.maximum(jnp.maximum(tops[0], tops[1]), jnp.maximum(tops[2], tops[3]))
     sums = jnp.zeros((4, COLS), F32)
@@ -250,6 +255,7 @@
             send[pl.ds(group, 1)] = send[pl.ds(group, 1)] + out[None]
         return carry
 
+    fetch.wait()
     lax.fori_loop(0, (units[0] + 1) // 2, pair, 0)
 
 
@@ -268,18 +274,17 @@
     shape = jax.ShapeDtypeStruct
     z_axes = ("zh", "zl")
     docs = lax.all_gather(doc_cache, z_axes, axis=0, tiled=True)
-    x, zh, zl = lax.axis_index("x"), lax.axis_index("zh"), lax.axis_index("zl")
-    where = jnp.stack([x, zh * 4 + zl, zl, lax.axis_index("core")]).astype(jnp.int32)
-
-    flags = jnp.pad(block_use.astype(BF16), ((0, 14), (0, 512 - PICKS)))
-    sources = (wq, wk, wv, tokens, flags)
+
+    sources = (wq, wk, wv, tokens)
     parts, tagged = call(
         pack_kernel,
         [shape((4, 4, 96, HEAD), BF16), shape((SEQ + 16, 512), BF16)],
-        sources,
-        [ANY] * 5,
+        (*sources, block_use),
+        [ANY] * 4 + [VMEM],
         out_specs=[VMEM] * 2,
-        scratch=[pltpu.VMEM(a.shape, BF16) for a in sources] + [pltpu.SemaphoreType.DMA((5,))],
+        scratch=[pltpu.VMEM(a.shape, BF16) for a in sources]
+        + [pltpu.VMEM((16, 512), jnp.int32), pltpu.SemaphoreType.DMA((4,))],
+        limit=62,
     )
     near = exchange(parts.reshape(16, 96, HEAD), ("x", "zh"))
 
@@ -294,14 +299,16 @@
     mine = mine.reshape(NX, 4, SEQ + 16, 512)
     ahead = from_z(near, 1)
     behind = from_z(near, -1)
-    mine, ahead, behind = lax.optimization_barrier((mine, ahead, behind))
+    far_a = from_z(near[0:8], 2)
+    far_b = from_z(near[8:16], -2)
+    mine, ahead, behind, far_a, far_b = lax.optimization_barrier((mine, ahead, behind, far_a, far_b))
     other = lax.ppermute(mine, "core", [(0, 1), (1, 0)])
     gain = norm_gain.astype(F32).reshape(8, 1, 512)
     normed = call(
         norm_kernel,
         shape((8, ROWS, 512), BF16),
-        (where, mine, other, gain),
-        [SMEM, VMEM, VMEM, VMEM],
+        (mine, other, gain),
+        [VMEM] * 3,
         flops=ROWS * 4096 * 8,
         moved=8 << 20,
     )
@@ -309,37 +316,43 @@
     units = call(
         route_kernel,
         shape((UNITS,), jnp.int32),
-        (where, doc_lists, doc_place, use),
-        [SMEM] * 4,
+        (doc_lists, doc_place, use),
+        [SMEM] * 3,
         out_specs=SMEM,
         scratch=[pltpu.SMEM((NX * NZ,), jnp.int32)],
     )
 
-    far = from_z(ahead, 1)
     send = call(
         project_kernel,
         shape((NX, ROWS + HALF, HEAD), BF16),
-        (where, normed, near, ahead, far, behind),
-        [SMEM] + [VMEM] * 5,
+        (normed, near, ahead, far_a, far_b, behind),
+        [VMEM] * 6,
         scratch=[pltpu.VMEM((4096, 2 * HEAD), BF16)],
         flops=2 * ROWS * 4096 * 256,
         moved=8 << 20,
     )
     got = exchange(send, "x")
+    scratch = [
+        pltpu.VMEM((8, COLS), F32),
+        pltpu.VMEM((2 * NZ, SEQ, 2 * HEAD), BF16),
+        pltpu.SemaphoreType.DMA,
+    ]
     stats = call(
         stats_kernel,
         shape((NX, 8, COLS), F32),
-        (where, units, got, docs),
-        [SMEM, SMEM, VMEM, VMEM],
-        scratch=[pltpu.VMEM((8, COLS), F32)],
+        (units, got, docs),
+        [SMEM, VMEM, ANY],
+        scratch=scratch,
+        limit=52,
     )
     all_stats = exchange(stats, "x")
     partial = call(
         values_kernel,
         shape((NX, HEAD, COLS), F32),
-        (where, units, got, docs, all_stats),
-        [SMEM, SMEM, VMEM, VMEM, VMEM],
-        scratch=[pltpu.VMEM((8, COLS), F32)],
+        (units, got, docs, all_stats),
+        [SMEM, VMEM, ANY, VMEM],
+        scratch=scratch,
+        limit=52,
     )
     returned = exchange(partial, "x")
     return call(finish_kernel, shape((SEQ, COLS), BF16), (returned,), [VMEM])

time: 162 us -> 159 us (0.981)
  local copies, waits for them, and re-layouts: 7.83 us -> 0.14 us
  starting transfers between devices: 49.3 us -> 52.5 us
  waiting for transfers between devices: 25.8 us -> 28.7 us
  Pallas kernels: 23.8 us -> 21.8 us
  other arithmetic: 3.37 us -> 1.73 us
    unnamed x27 -> x11, local copies, waits for them, and re-layouts: 7.81 us -> 0.11 us
    ppermute x1, waiting for transfers between devices: 0.01 us -> 4.48 us  [shards(): other = lax.ppermute(mine, 'core', [(0, 1), (1, 0)])]
    ppermute x3, waiting for transfers between devices: 11.1 us -> 7.56 us  [from_x(): return lax.ppermute(array, 'x', [((i + step) % NX, i) for i in range(NX)])]
    ppermute x3 -> x4, starting transfers between devices: 15.6 us -> 18.9 us  [from_z(): lax.ppermute(array, z_axes, [((i + step) % NZ, i) for i in range(NZ)])]
    pallas_call x7, Pallas kernels: 23.8 us -> 21.8 us  [call(): pl.pallas_call(kernel, out_shape=outs, in_specs=specs, out_specs=VMEM if...]
    ppermute x3 -> x4, waiting for transfers between devices: 9.4 us -> 10.1 us  [from_z(): lax.ppermute(array, z_axes, [((i + step) % NZ, i) for i in range(NZ)])]
  transfers between devices with their start and end apart: 10 -> 11, of which waited for: 4 -> 5; matrix products, arithmetic and copies ran while one was open for 2% -> 1% of each run, Pallas kernels for 8% -> 6%
where the time goes in v7:
time: 159 us; the launch traced here: 157 us
  starting transfers between devices  52.5 us (33%)
  blocking collectives  38.3 us (24%)
  waiting for transfers between devices  28.7 us (18%)
  Pallas kernels  21.8 us (14%)
  between operations  13.6 us (9%)
  other arithmetic  1.73 us (1%)
    all_to_all x2, blocking collectives, exchange(): return lax.all_to_all(array, axes, 0, 0, tiled=True)  24.4 us
    pallas_call x7, Pallas kernels, call(): pl.pallas_call(kernel, out_shape=outs, in_specs=specs, out_specs=VMEM if...  21.8 us
    all_to_all x2, starting transfers between devices, exchange(): return lax.all_to_all(array, axes, 0, 0, tiled=True)  21.1 us
    ppermute x4, starting transfers between devices, from_z(): lax.ppermute(array, z_axes, [((i + step) % NZ, i) for i in range(NZ)])  18.9 us
    all_gather x1, blocking collectives, shards(): by_y = lax.all_gather(tagged, 'y')  13.9 us
    ppermute x3, starting transfers between devices, from_x(): return lax.ppermute(array, 'x', [((i + step) % NX, i) for i in range(NX)])  10.5 us
    ppermute x4, waiting for transfers between devices, from_z(): lax.ppermute(array, z_axes, [((i + step) % NZ, i) for i in range(NZ)])  10.1 us
    ppermute x3, waiting for transfers between devices, from_x(): return lax.ppermute(array, 'x', [((i + step) % NX, i) for i in range(NX)])  7.56 us
  transfers between devices with their start and end apart: 11, of which 5 were waited for; matrix products, arithmetic and copies ran while one was open for 1% of the time, Pallas kernels for 6%

profile of v7, /device:TPU:24, one launch (start us, length us, event | category | flops | bytes accessed | tf_op | source)
XLA Modules:
  0.0 156.7 jit_solution(14789587646802831777)
XLA Ops:
  6.5 2.6 %shard_map.91 = (bf16[4,4,96,128]{3,2,1,0:T(8,128)(2,1)}, bf16[144,512]{1,0:T(8,128)(2,1)}) custom-call(bf16[64,512]{1,0:T(8,128)(2,1)} %refs_0_.1, bf16[64,128]{1,0:T(8,128)(2,1)} %refs_1_.1, bf16[64,128]{1,0:T(8,128)(2,1)} %refs_2_.1, bf16[128,512]{1,0:T(8,128)(2,1)} %refs_3_.1, s32[2,16]{1,0:T(2,128)} %refs_4_.1), custom_call_target="tpu_custom_call" | custom-call | tf_op jit(solution)/shard_map/pallas_call | solution.py:32
  9.1 17.7 %all-to-all-start = ((bf16[16,96,128]{2,1,0:T(8,128)(2,1)}), bf16[16,96,128]{2,1,0:T(8,128)(2,1)S(1)}, u32[]{:S(2)}, u32[]{:S(2)}) async-start(bf16[16,96,128]{2,1,0:T(8,128)(2,1)} %bitcast.14), calls=%async_computation | async-start | bytes 786432 | tf_op jit(solution)/shard_map/all_to_all | solution.py:270
  27.5 13.9 %all-gather = bf16[576,512]{1,0:T(8,128)(2,1)S(1)} all-gather(bf16[144,512]{1,0:T(8,128)(2,1)} %get-tuple-element.12), channel_id=2, replica_groups=mesh['x'=4,'zh'=4,'zl'=4,'y'=4,'core'=2] {'y'}, dimensions={0}, use_global_device_ids=true | all-gather | bytes 737280 | tf_op jit(solution)/shard_map/all_gather | solution.py:297
  41.4 5.0 %collective-permute-start = (bf16[4,144,512]{2,1,0:T(8,128)(2,1)S(1)}, bf16[4,144,512]{2,1,0:T(8,128)(2,1)S(1)}, u32[]{:S(2)}, u32[]{:S(2)}) collective-permute-start(bf16[4,144,512]{2,1,0:T(8,128)(2,1)S(1)} %bitcast.10), channel_id=1, source_target_pairs={{128,0},{256,128},{384,256},{0,384},{129,1},{257,129},{385,257},{1... | collective-permute-start | bytes 1769480 | tf_op jit(solution)/shard_map/ppermute | solution.py:295
  46.4 2.8 %collective-permute-start.1 = (bf16[4,144,512]{2,1,0:T(8,128)(2,1)S(1)}, bf16[4,144,512]{2,1,0:T(8,128)(2,1)S(1)}, u32[]{:S(2)}, u32[]{:S(2)}) collective-permute-start(bf16[4,144,512]{2,1,0:T(8,128)(2,1)S(1)} %bitcast.11), channel_id=1, source_target_pairs={{256,0},{384,128},{0,256},{128,384},{257,1},{385,129},{1,257},{129... | collective-permute-start | bytes 1769480 | tf_op jit(solution)/shard_map/ppermute | solution.py:295
  49.2 2.8 %collective-permute-start.2 = (bf16[4,144,512]{2,1,0:T(8,128)(2,1)S(1)}, bf16[4,144,512]{2,1,0:T(8,128)(2,1)}, u32[]{:S(2)}, u32[]{:S(2)}) collective-permute-start(bf16[4,144,512]{2,1,0:T(8,128)(2,1)S(1)} %bitcast.12), channel_id=1, source_target_pairs={{384,0},{0,128},{128,256},{256,384},{385,1},{1,129},{129,257},{257... | collective-permute-start | bytes 1769480 | tf_op jit(solution)/shard_map/ppermute | solution.py:295
  51.9 5.9 %collective-permute-start.3 = (bf16[16,96,128]{2,1,0:T(8,128)(2,1)S(1)}, bf16[16,96,128]{2,1,0:T(8,128)(2,1)S(1)}, u32[]{:S(2)}, u32[]{:S(2)}) collective-permute-start(bf16[16,96,128]{2,1,0:T(8,128)(2,1)S(1)} %all-to-all-done.near), channel_id=1, source_target_pairs={{8,0},{16,8},{24,16},{32,24},{40,32},{48,40},{56,48},{64,56},{72,6... | collective-permute-start | bytes 1179656 | tf_op jit(solution)/shard_map/ppermute | solution.py:292
  57.8 3.2 %collective-permute-start.4 = (bf16[16,96,128]{2,1,0:T(8,128)(2,1)S(1)}, bf16[16,96,128]{2,1,0:T(8,128)(2,1)S(1)}, u32[]{:S(2)}, u32[]{:S(2)}) collective-permute-start(bf16[16,96,128]{2,1,0:T(8,128)(2,1)S(1)} %all-to-all-done.near), channel_id=1, source_target_pairs={{120,0},{0,8},{8,16},{16,24},{24,32},{32,40},{40,48},{48,56},{56,6... | collective-permute-start | bytes 1179656 | tf_op jit(solution)/shard_map/ppermute | solution.py:292
  61.0 7.6 %collective-permute-done = bf16[4,144,512]{2,1,0:T(8,128)(2,1)S(1)} collective-permute-done((bf16[4,144,512]{2,1,0:T(8,128)(2,1)S(1)}, bf16[4,144,512]{2,1,0:T(8,128)(2,1)S(1)}, u32[]{:S(2)}, u32[]{:S(2)}) %collective-permute-start) | collective-permute-done | bytes 589856 | tf_op jit(solution)/shard_map/ppermute | solution.py:295
  68.6 7.8 %collective-permute-start.5 = (bf16[8,96,128]{2,1,0:T(8,128)(2,1)S(1)}, bf16[8,96,128]{2,1,0:T(8,128)(2,1)S(1)}, u32[]{:S(2)}, u32[]{:S(2)}) collective-permute-start(bf16[8,96,128]{2,1,0:T(8,128)(2,1)S(1)} %get-tuple-element.20), channel_id=1, source_target_pairs={{16,0},{24,8},{32,16},{40,24},{48,32},{56,40},{64,48},{72,56},{80,... | collective-permute-start | bytes 589832 | tf_op jit(solution)/shard_map/ppermute | solution.py:292
  76.4 2.1 %collective-permute-start.6 = (bf16[8,96,128]{2,1,0:T(8,128)(2,1)S(1)}, bf16[8,96,128]{2,1,0:T(8,128)(2,1)S(1)}, u32[]{:S(2)}, u32[]{:S(2)}) collective-permute-start(bf16[8,96,128]{2,1,0:T(8,128)(2,1)S(1)} %get-tuple-element.19), channel_id=1, source_target_pairs={{112,0},{120,8},{0,16},{8,24},{16,32},{24,40},{32,48},{40,56},{48,... | collective-permute-start | bytes 589832 | tf_op jit(solution)/shard_map/ppermute | solution.py:292
  80.2 3.2 %collective-permute-done.5.far_a = bf16[8,96,128]{2,1,0:T(8,128)(2,1)S(1)} collective-permute-done((bf16[8,96,128]{2,1,0:T(8,128)(2,1)S(1)}, bf16[8,96,128]{2,1,0:T(8,128)(2,1)S(1)}, u32[]{:S(2)}, u32[]{:S(2)}) %collective-permute-start.5) | collective-permute-done | bytes 196640 | tf_op jit(solution)/shard_map/ppermute | solution.py:292
  83.4 6.9 %collective-permute-done.6.far_b = bf16[8,96,128]{2,1,0:T(8,128)(2,1)S(1)} collective-permute-done((bf16[8,96,128]{2,1,0:T(8,128)(2,1)S(1)}, bf16[8,96,128]{2,1,0:T(8,128)(2,1)S(1)}, u32[]{:S(2)}, u32[]{:S(2)}) %collective-permute-start.6) | collective-permute-done | bytes 196640 | tf_op jit(solution)/shard_map/ppermute | solution.py:292
  90.4 1.9 %collective-permute-start.7 = (bf16[4,4,144,512]{3,2,1,0:T(8,128)(2,1)S(1)}, bf16[4,4,144,512]{3,2,1,0:T(8,128)(2,1)S(1)}, u32[]{:S(2)}, u32[]{:S(2)}) collective-permute-start(bf16[4,4,144,512]{3,2,1,0:T(8,128)(2,1)S(1)} %bitcast.6), channel_id=1, source_target_pairs={{0,1},{1,0},{2,3},{3,2},{4,5},{5,4},{6,7},{7,6},{8,9},{9,8},{10,11... | collective-permute-start | bytes 7077896 | tf_op jit(solution)/shard_map/ppermute | solution.py:305
  92.3 4.5 %collective-permute-done.7.other = bf16[4,4,144,512]{3,2,1,0:T(8,128)(2,1)S(1)} collective-permute-done((bf16[4,4,144,512]{3,2,1,0:T(8,128)(2,1)S(1)}, bf16[4,4,144,512]{3,2,1,0:T(8,128)(2,1)S(1)}, u32[]{:S(2)}, u32[]{:S(2)}) %collective-permute-start.7) | collective-permute-done | bytes 2359328 | tf_op jit(solution)/shard_map/ppermute | solution.py:305
  96.8 2.0 %shard_map.93.normed = bf16[8,512,512]{2,1,0:T(8,128)(2,1)S(1)} custom-call(bf16[4,4,144,512]{3,2,1,0:T(8,128)(2,1)S(1)} %bitcast.7, bf16[4,4,144,512]{3,2,1,0:T(8,128)(2,1)S(1)} %collective-permute-done.7.other, f32[8,1,512]{2,1,0:T(1,128)S(1)} %bitcast.9), custom_call_target="tpu_custom_call" | custom-call | flops 16777216 | bytes 8388608 | tf_op jit(solution)/shard_map/pallas_call | solution.py:32
  98.9 2.5 %shard_map.94 = bf16[4,576,128]{2,1,0:T(8,128)(2,1)} custom-call(bf16[8,512,512]{2,1,0:T(8,128)(2,1)S(1)} %shard_map.93.normed, bf16[16,96,128]{2,1,0:T(8,128)(2,1)S(1)} %all-to-all-done.near, bf16[16,96,128]{2,1,0:T(8,128)(2,1)S(1)} %collective-permute-done.3.ahead, bf16[8,96,128]{2,1,0:T(8,128)(2,1)S(1)} %collective-permute-done.5.far_a, ...), custom_call_target="tpu_custom_call" | custom-call | flops 1073741824 | bytes 8388608 | tf_op jit(solution)/shard_map/pallas_call | solution.py:32
  101.4 3.5 %all-to-all-start.1 = ((bf16[4,576,128]{2,1,0:T(8,128)(2,1)}), bf16[4,576,128]{2,1,0:T(8,128)(2,1)S(1)}, u32[]{:S(2)}, u32[]{:S(2)}) async-start(bf16[4,576,128]{2,1,0:T(8,128)(2,1)} %shard_map.94), calls=%async_computation.1 | async-start | bytes 1179648 | tf_op jit(solution)/shard_map/all_to_all | solution.py:270
  105.0 4.8 %shard_map.92.units = s32[128]{0:T(128)S(1)} custom-call(s32[64,16]{1,0:T(8,128)S(1)} %copy.11.lists, s32[128]{0:T(128)S(1)} %copy-done, s32[8,16]{1,0:T(8,128)S(1)} %convert.2.use), custom_call_target="tpu_custom_call" | custom-call | tf_op jit(solution)/shard_map/pallas_call | solution.py:32
  109.8 5.8 %all-to-all-done.1.got = bf16[4,576,128]{2,1,0:T(8,128)(2,1)S(1)} async-done(((bf16[4,576,128]{2,1,0:T(8,128)(2,1)}), bf16[4,576,128]{2,1,0:T(8,128)(2,1)S(1)}, u32[]{:S(2)}, u32[]{:S(2)}) %all-to-all-start.1) | async-done | bytes 589856 | tf_op jit(solution)/shard_map/all_to_all | solution.py:270
  115.6 4.0 %shard_map.95 = f32[4,8,512]{2,1,0:T(8,128)S(1)} custom-call(s32[128]{0:T(128)S(1)} %shard_map.92.units, bf16[4,576,128]{2,1,0:T(8,128)(2,1)S(1)} %all-to-all-done.1.got, bf16[32,128,256]{2,1,0:T(8,128)(2,1)} %all-gather.3.cloned.1.call-done.far_docs), custom_call_target="tpu_custom_call" | custom-call | tf_op jit(solution)/shard_map/pallas_call | solution.py:32
  119.6 8.2 %all_to_all.20.all_stats = f32[4,8,512]{2,1,0:T(8,128)S(1)} all-to-all(f32[4,8,512]{2,1,0:T(8,128)S(1)} %shard_map.95), channel_id=1, replica_groups=mesh['x'=4,'zh'=4,'zl'=4,'y'=4,'core'=2] {'x'}, dimensions={0} | all-to-all | bytes 131072 | tf_op jit(solution)/shard_map/all_to_all | solution.py:270
  127.8 5.1 %shard_map.96 = f32[4,128,512]{2,1,0:T(8,128)S(1)} custom-call(s32[128]{0:T(128)S(1)} %shard_map.92.units, bf16[4,576,128]{2,1,0:T(8,128)(2,1)S(1)} %all-to-all-done.1.got, bf16[32,128,256]{2,1,0:T(8,128)(2,1)} %all-gather.3.cloned.1.call-done.far_docs, f32[4,8,512]{2,1,0:T(8,128)S(1)} %all_to_all.20.all_stats), custom_call_target="tpu_custom_call" | custom-call | tf_op jit(solution)/shard_map/pallas_call | solution.py:32
  132.9 16.2 %all_to_all.21.got = f32[4,128,512]{2,1,0:T(8,128)S(1)} all-to-all(f32[4,128,512]{2,1,0:T(8,128)S(1)} %shard_map.96), channel_id=1, replica_groups=mesh['x'=4,'zh'=4,'zl'=4,'y'=4,'core'=2] {'x'}, dimensions={0} | all-to-all | bytes 2097152 | tf_op jit(solution)/shard_map/all_to_all | solution.py:270
  (25 shorter events, 3.4 us)
Async XLA Ops:
  9.1 42.8 %all-to-all-start = ((bf16[16,96,128]{2,1,0:T(8,128)(2,1)}), bf16[16,96,128]{2,1,0:T(8,128)(2,1)S(1)}, u32[]{:S(2)}, u32[]{:S(2)}) async-start(bf16[16,96,128]{2,1,0:T(8,128)(2,1)} %bitcast.14), calls=%async_computation | async-start | bytes 786432 | tf_op jit(solution)/shard_map/all_to_all | solution.py:270
  26.8 83.0 %all-gather.3.cloned.1.call-start = ((), (), s32[]{:S(2)}) async-start(), calls=%async_computation.4 | async-start | bytes 2228224 | tf_op jit(solution)/shard_map/all_gather | solution.py:276
  41.4 27.2 %collective-permute-start = (bf16[4,144,512]{2,1,0:T(8,128)(2,1)S(1)}, bf16[4,144,512]{2,1,0:T(8,128)(2,1)S(1)}, u32[]{:S(2)}, u32[]{:S(2)}) collective-permute-start(bf16[4,144,512]{2,1,0:T(8,128)(2,1)S(1)} %bitcast.10), channel_id=1, source_target_pairs={{128,0},{256,128},{384,256},{0,384},{129,1},{257,129},{385,257},{1... | collective-permute-start | bytes 1769480 | tf_op jit(solution)/shard_map/ppermute | solution.py:295
  46.4 30.0 %collective-permute-start.1 = (bf16[4,144,512]{2,1,0:T(8,128)(2,1)S(1)}, bf16[4,144,512]{2,1,0:T(8,128)(2,1)S(1)}, u32[]{:S(2)}, u32[]{:S(2)}) collective-permute-start(bf16[4,144,512]{2,1,0:T(8,128)(2,1)S(1)} %bitcast.11), channel_id=1, source_target_pairs={{256,0},{384,128},{0,256},{128,384},{257,1},{385,129},{1,257},{129... | collective-permute-start | bytes 1769480 | tf_op jit(solution)/shard_map/ppermute | solution.py:295
  49.2 29.4 %collective-permute-start.2 = (bf16[4,144,512]{2,1,0:T(8,128)(2,1)S(1)}, bf16[4,144,512]{2,1,0:T(8,128)(2,1)}, u32[]{:S(2)}, u32[]{:S(2)}) collective-permute-start(bf16[4,144,512]{2,1,0:T(8,128)(2,1)S(1)} %bitcast.12), channel_id=1, source_target_pairs={{384,0},{0,128},{128,256},{256,384},{385,1},{1,129},{129,257},{257... | collective-permute-start | bytes 1769480 | tf_op jit(solution)/shard_map/ppermute | solution.py:295
  51.9 38.4 %collective-permute-start.3 = (bf16[16,96,128]{2,1,0:T(8,128)(2,1)S(1)}, bf16[16,96,128]{2,1,0:T(8,128)(2,1)S(1)}, u32[]{:S(2)}, u32[]{:S(2)}) collective-permute-start(bf16[16,96,128]{2,1,0:T(8,128)(2,1)S(1)} %all-to-all-done.near), channel_id=1, source_target_pairs={{8,0},{16,8},{24,16},{32,24},{40,32},{48,40},{56,48},{64,56},{72,6... | collective-permute-start | bytes 1179656 | tf_op jit(solution)/shard_map/ppermute | solution.py:292
  57.8 32.6 %collective-permute-start.4 = (bf16[16,96,128]{2,1,0:T(8,128)(2,1)S(1)}, bf16[16,96,128]{2,1,0:T(8,128)(2,1)S(1)}, u32[]{:S(2)}, u32[]{:S(2)}) collective-permute-start(bf16[16,96,128]{2,1,0:T(8,128)(2,1)S(1)} %all-to-all-done.near), channel_id=1, source_target_pairs={{120,0},{0,8},{8,16},{16,24},{24,32},{32,40},{40,48},{48,56},{56,6... | collective-permute-start | bytes 1179656 | tf_op jit(solution)/shard_map/ppermute | solution.py:292
  68.6 9.9 %copy-start.1 = (bf16[4,144,512]{2,1,0:T(8,128)(2,1)}, bf16[4,144,512]{2,1,0:T(8,128)(2,1)S(1)}, u32[]{:S(2)}) copy-start(bf16[4,144,512]{2,1,0:T(8,128)(2,1)S(1)} %collective-permute-done) | copy-start | bytes 1769476
  68.6 14.9 %collective-permute-start.5 = (bf16[8,96,128]{2,1,0:T(8,128)(2,1)S(1)}, bf16[8,96,128]{2,1,0:T(8,128)(2,1)S(1)}, u32[]{:S(2)}, u32[]{:S(2)}) collective-permute-start(bf16[8,96,128]{2,1,0:T(8,128)(2,1)S(1)} %get-tuple-element.20), channel_id=1, source_target_pairs={{16,0},{24,8},{32,16},{40,24},{48,32},{56,40},{64,48},{72,56},{80,... | collective-permute-start | bytes 589832 | tf_op jit(solution)/shard_map/ppermute | solution.py:292
  76.4 2.1 %copy-start.2 = (bf16[4,144,512]{2,1,0:T(8,128)(2,1)}, bf16[4,144,512]{2,1,0:T(8,128)(2,1)S(1)}, u32[]{:S(2)}) copy-start(bf16[4,144,512]{2,1,0:T(8,128)(2,1)S(1)} %collective-permute-done.1) | copy-start | bytes 1769476
  76.4 15.9 %copy-start.3 = (bf16[4096]{0:T(1024)(128)(2,1)S(1)}, bf16[4096]{0:T(1024)(128)(2,1)}, u32[]{:S(2)}) copy-start(bf16[4096]{0:T(1024)(128)(2,1)} %param.10) | copy-start | bytes 24580
  76.4 13.9 %collective-permute-start.6 = (bf16[8,96,128]{2,1,0:T(8,128)(2,1)S(1)}, bf16[8,96,128]{2,1,0:T(8,128)(2,1)S(1)}, u32[]{:S(2)}, u32[]{:S(2)}) collective-permute-start(bf16[8,96,128]{2,1,0:T(8,128)(2,1)S(1)} %get-tuple-element.19), channel_id=1, source_target_pairs={{112,0},{120,8},{0,16},{8,24},{16,32},{24,40},{32,48},{40,56},{48,... | collective-permute-start | bytes 589832 | tf_op jit(solution)/shard_map/ppermute | solution.py:292
  90.4 6.4 %collective-permute-start.7 = (bf16[4,4,144,512]{3,2,1,0:T(8,128)(2,1)S(1)}, bf16[4,4,144,512]{3,2,1,0:T(8,128)(2,1)S(1)}, u32[]{:S(2)}, u32[]{:S(2)}) collective-permute-start(bf16[4,4,144,512]{3,2,1,0:T(8,128)(2,1)S(1)} %bitcast.6), channel_id=1, source_target_pairs={{0,1},{1,0},{2,3},{3,2},{4,5},{5,4},{6,7},{7,6},{8,9},{9,8},{10,11... | collective-permute-start | bytes 7077896 | tf_op jit(solution)/shard_map/ppermute | solution.py:305
  98.8 6.0 %copy-start.4 = (s32[64,16]{0,1:T(8,128)S(1)}, s32[64,16]{0,1:T(8,128)}, u32[]{:S(2)}) copy-start(s32[64,16]{0,1:T(8,128)} %param.15) | copy-start | bytes 12292
  98.9 6.1 %copy-start = (s32[128]{0:T(128)S(1)}, s32[128]{0:T(128)}, u32[]{:S(2)}) copy-start(s32[128]{0:T(128)} %place.1) | copy-start | bytes 1540
  101.4 14.2 %all-to-all-start.1 = ((bf16[4,576,128]{2,1,0:T(8,128)(2,1)}), bf16[4,576,128]{2,1,0:T(8,128)(2,1)S(1)}, u32[]{:S(2)}, u32[]{:S(2)}) async-start(bf16[4,576,128]{2,1,0:T(8,128)(2,1)} %shard_map.94), calls=%async_computation.1 | async-start | bytes 1179648 | tf_op jit(solution)/shard_map/all_to_all | solution.py:270
Sparse Core Ops, SparseCore 0:
  29.7 78.9 all-gather.2

commit v8 on v7

--- a/solution.py
+++ b/solution.py
@@ -123,11 +123,12 @@
     units[count + 1] = 0
 
 
-def project_kernel(normed, near, ahead, far_a, far_b, behind, send, weights):
-    for step, blocks in enumerate((near, ahead, (far_a, far_b), behind)):
+def project_kernel(normed, near, ahead, far, behind, *rest):
+    sends, weights, owns = rest[:NX], rest[NX], rest[NX + 1]
+    for step, blocks in enumerate((near, ahead, far, behind)):
         row = lax.rem(lax.axis_index("zl") + step, 4) * HALF
         for b in range(16):
-            block = blocks[b // 8][b % 8] if step == 2 else blocks[b]
+            block = blocks[b]
             base = pl.multiple_of(b * 256 + row, HALF)
             packed = block[64:96, :]
             weights[pl.ds(base, 64), 0:HEAD] = block[0:64, :]
@@ -141,10 +142,12 @@
             normed[slot], weights[slot * 512 : (slot + 1) * 512, :], preferred_element_type=F32
         )
     query = total[:, 0:HEAD].astype(BF16)
-    for dest in range(NX):
-        own = total[dest * SEQ : (dest + 1) * SEQ, HEAD : 2 * HEAD]
-        send[dest, 0:ROWS, :] = query
-        send[dest, ROWS : ROWS + HALF, :] = side_by_side(own[0:HALF], own[HALF:SEQ], 0, 0)
+    owns[...] = total[:, HEAD : 2 * HEAD]
+    for step, send in enumerate(sends):
+        dest = lax.rem(lax.axis_index("x") + step, NX)
+        own = owns[pl.ds(pl.multiple_of(dest * SEQ, SEQ), SEQ), :]
+        send[0:ROWS, :] = query
+        send[ROWS : ROWS + HALF, :] = side_by_side(own[0:HALF], own[HALF:SEQ], 0, 0)
 
 
 def own_part(got, first):
@@ -186,9 +189,15 @@
     return jnp.exp2((scores - shift) * RATE)
 
 
-def stats_kernel(units, got, far_docs, send, stats, docs, done):
+def in_order(pieces, got):
+    for step, piece in enumerate(pieces):
+        got[lax.rem(lax.axis_index("x") - step + NX, NX)] = piece[...]
+
+
+def stats_kernel(units, own, one, two, three, far_docs, send, stats, docs, got, done):
     fetch = pltpu.make_async_copy(far_docs, docs, done)
     fetch.start()
+    in_order((own, one, two, three), got)
     x = lax.axis_index("x")
     scores = own_scores(got, x)
     top = jnp.max(scores, axis=0, keepdims=True)
@@ -222,9 +231,10 @@
         send[dest] = stats[...]
 
 
-def values_kernel(units, got, far_docs, all_stats, send, total, docs, done):
+def values_kernel(units, own, one, two, three, far_docs, all_stats, send, total, docs, got, done):
     fetch = pltpu.make_async_copy(far_docs, docs, done)
     fetch.start()
+    in_order((own, one, two, three), got)
     x = lax.axis_index("x")
     tops = [all_stats[src, 0:4, :] for src in range(NX)]
     top = jnp.maximum(jnp.maximum(tops[0], tops[1]), jnp.maximum(tops[2], tops[3]))
@@ -299,9 +309,8 @@
     mine = mine.reshape(NX, 4, SEQ + 16, 512)
     ahead = from_z(near, 1)
     behind = from_z(near, -1)
-    far_a = from_z(near[0:8], 2)
-    far_b = from_z(near[8:16], -2)
-    mine, ahead, behind, far_a, far_b = lax.optimization_barrier((mine, ahead, behind, far_a, far_b))
+    far = lax.ppermute(near, z_axes, [((i + 2 - 4 * (i % 2)) % NZ, i) for i in range(NZ)])
+    mine, ahead, far, behind = lax.optimization_barrier((mine, ahead, far, behind))
     other = lax.ppermute(mine, "core", [(0, 1), (1, 0)])
     gain = norm_gain.astype(F32).reshape(8, 1, 512)
     normed = call(
@@ -322,26 +331,31 @@
         scratch=[pltpu.SMEM((NX * NZ,), jnp.int32)],
     )
 
-    send = call(
+    sends = call(
         project_kernel,
-        shape((NX, ROWS + HALF, HEAD), BF16),
-        (normed, near, ahead, far_a, far_b, behind),
-        [VMEM] * 6,
-        scratch=[pltpu.VMEM((4096, 2 * HEAD), BF16)],
+        [shape((ROWS + HALF, HEAD), BF16)] * NX,
+        (normed, near, ahead, far, behind),
+        [VMEM] * 5,
+        out_specs=[VMEM] * NX,
+        scratch=[pltpu.VMEM((4096, 2 * HEAD), BF16), pltpu.VMEM((ROWS, HEAD), F32)],
         flops=2 * ROWS * 4096 * 256,
         moved=8 << 20,
     )
-    got = exchange(send, "x")
+    got = [
+        lax.ppermute(sends[k], "x", [(i, (i + k) % NX) for i in range(NX)]) if k else sends[0]
+        for k in range(NX)
+    ]
     scratch = [
         pltpu.VMEM((8, COLS), F32),
         pltpu.VMEM((2 * NZ, SEQ, 2 * HEAD), BF16),
+        pltpu.VMEM((NX, ROWS + HALF, HEAD), BF16),
         pltpu.SemaphoreType.DMA,
     ]
     stats = call(
         stats_kernel,
         shape((NX, 8, COLS), F32),
-        (units, got, docs),
-        [SMEM, VMEM, ANY],
+        (units, *got, docs),
+        [SMEM] + [VMEM] * 4 + [ANY],
         scratch=scratch,
         limit=52,
     )
@@ -349,8 +363,8 @@
     partial = call(
         values_kernel,
         shape((NX, HEAD, COLS), F32),
-        (units, got, docs, all_stats),
-        [SMEM, VMEM, ANY, VMEM],
+        (units, *got, docs, all_stats),
+        [SMEM] + [VMEM] * 4 + [ANY, VMEM],
         scratch=scratch,
         limit=52,
     )

time: 159 us -> 157 us (0.987)
  waiting for transfers between devices: 28.7 us -> 26.2 us
  blocking collectives: 38.3 us -> 40.2 us
    ppermute x0 -> x4, starting transfers between devices: none -> 12.4 us  [the longest x3 8.98 us: shards(): lax.ppermute(sends[k], 'x', [(i, (i + k) % NX) for i in range(NX)])]
    ppermute x4 -> x2, starting transfers between devices: 18.9 us -> 9.24 us  [from_z(): lax.ppermute(array, z_axes, [((i + step) % NZ, i) for i in range(NZ)])]
    ppermute x0 -> x4, waiting for transfers between devices: none -> 7.06 us  [the longest x1 7.05 us: shards(): lax.ppermute(near, z_axes, [((i + 2 - 4 * (i % 2)) % NZ, i) for i in rang...]
    ppermute x4 -> x2, waiting for transfers between devices: 10.1 us -> 3.83 us  [from_z(): lax.ppermute(array, z_axes, [((i + step) % NZ, i) for i in range(NZ)])]
    all_to_all x2 -> x1, waiting for transfers between devices: 5.79 us -> 0.01 us  [exchange(): return lax.all_to_all(array, axes, 0, 0, tiled=True)]
    all_to_all x2 -> x1, starting transfers between devices: 21.1 us -> 17.7 us  [exchange(): return lax.all_to_all(array, axes, 0, 0, tiled=True)]
    all_to_all x2, blocking collectives: 24.4 us -> 26.4 us  [exchange(): return lax.all_to_all(array, axes, 0, 0, tiled=True)]
    all_gather x1, waiting for transfers between devices: 0.02 us -> 1.86 us  [shards(): docs = lax.all_gather(doc_cache, z_axes, axis=0, tiled=True)]
  transfers between devices with their start and end apart: 11 -> 12, of which waited for: 5 -> 6; matrix products, arithmetic and copies ran while one was open for 1% -> 1% of each run, Pallas kernels for 6% -> 5%
where the time goes in v8:
time: 157 us; the launch traced here: 156 us
  starting transfers between devices  51.9 us (33%)
  blocking collectives  40.2 us (26%)
  waiting for transfers between devices  26.2 us (17%)
  Pallas kernels  21.1 us (13%)
  between operations  13.6 us (9%)
  other arithmetic  1.74 us (1%)
    all_to_all x2, blocking collectives, exchange(): return lax.all_to_all(array, axes, 0, 0, tiled=True)  26.4 us
    pallas_call x7, Pallas kernels, call(): pl.pallas_call(kernel, out_shape=outs, in_specs=specs, out_specs=VMEM if...  21.1 us
    all_to_all x1, starting transfers between devices, exchange(): return lax.all_to_all(array, axes, 0, 0, tiled=True)  17.7 us
    all_gather x1, blocking collectives, shards(): by_y = lax.all_gather(tagged, 'y')  13.9 us
    ppermute x3, starting transfers between devices, from_x(): return lax.ppermute(array, 'x', [((i + step) % NX, i) for i in range(NX)])  10.7 us
    ppermute x2, starting transfers between devices, from_z(): lax.ppermute(array, z_axes, [((i + step) % NZ, i) for i in range(NZ)])  9.24 us
    ppermute x3, starting transfers between devices, shards(): lax.ppermute(sends[k], 'x', [(i, (i + k) % NX) for i in range(NX)])  8.98 us
    ppermute x3, waiting for transfers between devices, from_x(): return lax.ppermute(array, 'x', [((i + step) % NX, i) for i in range(NX)])  8.28 us
  transfers between devices with their start and end apart: 12, of which 6 were waited for; matrix products, arithmetic and copies ran while one was open for 1% of the time, Pallas kernels for 5%

profile of v8, /device:TPU:24, one launch (start us, length us, event | category | flops | bytes accessed | tf_op | source)
XLA Modules:
  0.0 155.7 jit_solution(14739067093520926204)
XLA Ops:
  6.5 2.6 %shard_map.91 = (bf16[4,4,96,128]{3,2,1,0:T(8,128)(2,1)}, bf16[144,512]{1,0:T(8,128)(2,1)}) custom-call(bf16[64,512]{1,0:T(8,128)(2,1)} %refs_0_.1, bf16[64,128]{1,0:T(8,128)(2,1)} %refs_1_.1, bf16[64,128]{1,0:T(8,128)(2,1)} %refs_2_.1, bf16[128,512]{1,0:T(8,128)(2,1)} %refs_3_.1, s32[2,16]{1,0:T(2,128)} %refs_4_.1), custom_call_target="tpu_custom_call" | custom-call | tf_op jit(solution)/shard_map/pallas_call | solution.py:32
  9.1 17.7 %all-to-all-start = ((bf16[16,96,128]{2,1,0:T(8,128)(2,1)}), bf16[16,96,128]{2,1,0:T(8,128)(2,1)S(1)}, u32[]{:S(2)}, u32[]{:S(2)}) async-start(bf16[16,96,128]{2,1,0:T(8,128)(2,1)} %bitcast.14), calls=%async_computation | async-start | bytes 786432 | tf_op jit(solution)/shard_map/all_to_all | solution.py:280
  27.5 13.9 %all-gather = bf16[576,512]{1,0:T(8,128)(2,1)S(1)} all-gather(bf16[144,512]{1,0:T(8,128)(2,1)} %get-tuple-element.15), channel_id=2, replica_groups=mesh['x'=4,'zh'=4,'zl'=4,'y'=4,'core'=2] {'y'}, dimensions={0}, use_global_device_ids=true | all-gather | bytes 737280 | tf_op jit(solution)/shard_map/all_gather | solution.py:307
  41.4 5.1 %collective-permute-start = (bf16[4,144,512]{2,1,0:T(8,128)(2,1)S(1)}, bf16[4,144,512]{2,1,0:T(8,128)(2,1)S(1)}, u32[]{:S(2)}, u32[]{:S(2)}) collective-permute-start(bf16[4,144,512]{2,1,0:T(8,128)(2,1)S(1)} %bitcast.10), channel_id=1, source_target_pairs={{128,0},{256,128},{384,256},{0,384},{129,1},{257,129},{385,257},{1... | collective-permute-start | bytes 1769480 | tf_op jit(solution)/shard_map/ppermute | solution.py:305
  46.5 2.8 %collective-permute-start.1 = (bf16[4,144,512]{2,1,0:T(8,128)(2,1)S(1)}, bf16[4,144,512]{2,1,0:T(8,128)(2,1)S(1)}, u32[]{:S(2)}, u32[]{:S(2)}) collective-permute-start(bf16[4,144,512]{2,1,0:T(8,128)(2,1)S(1)} %bitcast.11), channel_id=1, source_target_pairs={{256,0},{384,128},{0,256},{128,384},{257,1},{385,129},{1,257},{129... | collective-permute-start | bytes 1769480 | tf_op jit(solution)/shard_map/ppermute | solution.py:305
  49.3 2.8 %collective-permute-start.2 = (bf16[4,144,512]{2,1,0:T(8,128)(2,1)S(1)}, bf16[4,144,512]{2,1,0:T(8,128)(2,1)}, u32[]{:S(2)}, u32[]{:S(2)}) collective-permute-start(bf16[4,144,512]{2,1,0:T(8,128)(2,1)S(1)} %bitcast.12), channel_id=1, source_target_pairs={{384,0},{0,128},{128,256},{256,384},{385,1},{1,129},{129,257},{257... | collective-permute-start | bytes 1769480 | tf_op jit(solution)/shard_map/ppermute | solution.py:305
  52.1 5.9 %collective-permute-start.3 = (bf16[16,96,128]{2,1,0:T(8,128)(2,1)S(1)}, bf16[16,96,128]{2,1,0:T(8,128)(2,1)S(1)}, u32[]{:S(2)}, u32[]{:S(2)}) collective-permute-start(bf16[16,96,128]{2,1,0:T(8,128)(2,1)S(1)} %all-to-all-done.near), channel_id=1, source_target_pairs={{8,0},{16,8},{24,16},{32,24},{40,32},{48,40},{56,48},{64,56},{72,6... | collective-permute-start | bytes 1179656 | tf_op jit(solution)/shard_map/ppermute | solution.py:302
  58.0 3.4 %collective-permute-start.4 = (bf16[16,96,128]{2,1,0:T(8,128)(2,1)S(1)}, bf16[16,96,128]{2,1,0:T(8,128)(2,1)S(1)}, u32[]{:S(2)}, u32[]{:S(2)}) collective-permute-start(bf16[16,96,128]{2,1,0:T(8,128)(2,1)S(1)} %all-to-all-done.near), channel_id=1, source_target_pairs={{16,0},{120,8},{32,16},{8,24},{48,32},{24,40},{64,48},{40,56},{80,... | collective-permute-start | bytes 1179656 | tf_op jit(solution)/shard_map/ppermute | solution.py:312
  61.4 7.3 %collective-permute-done = bf16[4,144,512]{2,1,0:T(8,128)(2,1)S(1)} collective-permute-done((bf16[4,144,512]{2,1,0:T(8,128)(2,1)S(1)}, bf16[4,144,512]{2,1,0:T(8,128)(2,1)S(1)}, u32[]{:S(2)}, u32[]{:S(2)}) %collective-permute-start) | collective-permute-done | bytes 589856 | tf_op jit(solution)/shard_map/ppermute | solution.py:305
  68.7 3.4 %collective-permute-start.5 = (bf16[16,96,128]{2,1,0:T(8,128)(2,1)S(1)}, bf16[16,96,128]{2,1,0:T(8,128)(2,1)S(1)}, u32[]{:S(2)}, u32[]{:S(2)}) collective-permute-start(bf16[16,96,128]{2,1,0:T(8,128)(2,1)S(1)} %all-to-all-done.near), channel_id=1, source_target_pairs={{120,0},{0,8},{8,16},{16,24},{24,32},{32,40},{40,48},{48,56},{56,6... | collective-permute-start | bytes 1179656 | tf_op jit(solution)/shard_map/ppermute | solution.py:302
  75.7 7.0 %collective-permute-done.4.far = bf16[16,96,128]{2,1,0:T(8,128)(2,1)S(1)} collective-permute-done((bf16[16,96,128]{2,1,0:T(8,128)(2,1)S(1)}, bf16[16,96,128]{2,1,0:T(8,128)(2,1)S(1)}, u32[]{:S(2)}, u32[]{:S(2)}) %collective-permute-start.4) | collective-permute-done | bytes 393248 | tf_op jit(solution)/shard_map/ppermute | solution.py:312
  82.7 3.8 %collective-permute-done.5.behind = bf16[16,96,128]{2,1,0:T(8,128)(2,1)S(1)} collective-permute-done((bf16[16,96,128]{2,1,0:T(8,128)(2,1)S(1)}, bf16[16,96,128]{2,1,0:T(8,128)(2,1)S(1)}, u32[]{:S(2)}, u32[]{:S(2)}) %collective-permute-start.5) | collective-permute-done | bytes 393248 | tf_op jit(solution)/shard_map/ppermute | solution.py:302
  86.5 1.9 %collective-permute-start.6 = (bf16[4,4,144,512]{3,2,1,0:T(8,128)(2,1)S(1)}, bf16[4,4,144,512]{3,2,1,0:T(8,128)(2,1)S(1)}, u32[]{:S(2)}, u32[]{:S(2)}) collective-permute-start(bf16[4,4,144,512]{3,2,1,0:T(8,128)(2,1)S(1)} %bitcast.6), channel_id=1, source_target_pairs={{0,1},{1,0},{2,3},{3,2},{4,5},{5,4},{6,7},{7,6},{8,9},{9,8},{10,11... | collective-permute-start | bytes 7077896 | tf_op jit(solution)/shard_map/ppermute | solution.py:314
  88.5 4.5 %collective-permute-done.6.other = bf16[4,4,144,512]{3,2,1,0:T(8,128)(2,1)S(1)} collective-permute-done((bf16[4,4,144,512]{3,2,1,0:T(8,128)(2,1)S(1)}, bf16[4,4,144,512]{3,2,1,0:T(8,128)(2,1)S(1)}, u32[]{:S(2)}, u32[]{:S(2)}) %collective-permute-start.6) | collective-permute-done | bytes 2359328 | tf_op jit(solution)/shard_map/ppermute | solution.py:314
  92.9 2.0 %shard_map.93.normed = bf16[8,512,512]{2,1,0:T(8,128)(2,1)S(1)} custom-call(bf16[4,4,144,512]{3,2,1,0:T(8,128)(2,1)S(1)} %bitcast.7, bf16[4,4,144,512]{3,2,1,0:T(8,128)(2,1)S(1)} %collective-permute-done.6.other, f32[8,1,512]{2,1,0:T(1,128)S(1)} %bitcast.9), custom_call_target="tpu_custom_call" | custom-call | flops 16777216 | bytes 8388608 | tf_op jit(solution)/shard_map/pallas_call | solution.py:32
  96.8 1.9 %collective-permute-start.7 = (bf16[576,128]{1,0:T(8,128)(2,1)S(1)}, bf16[576,128]{1,0:T(8,128)(2,1)S(1)}, u32[]{:S(2)}, u32[]{:S(2)}) collective-permute-start(bf16[576,128]{1,0:T(8,128)(2,1)S(1)} %get-tuple-element.22), channel_id=1, source_target_pairs={{0,128},{128,256},{256,384},{384,0},{1,129},{129,257},{257,385},{3... | collective-permute-start | bytes 442376 | tf_op jit(solution)/shard_map/ppermute | solution.py:345
  98.7 4.4 %collective-permute-start.8 = (bf16[576,128]{1,0:T(8,128)(2,1)S(1)}, bf16[576,128]{1,0:T(8,128)(2,1)S(1)}, u32[]{:S(2)}, u32[]{:S(2)}) collective-permute-start(bf16[576,128]{1,0:T(8,128)(2,1)S(1)} %get-tuple-element.23), channel_id=1, source_target_pairs={{0,256},{128,384},{256,0},{384,128},{1,257},{129,385},{257,1},{385... | collective-permute-start | bytes 442376 | tf_op jit(solution)/shard_map/ppermute | solution.py:345
  103.2 2.6 %collective-permute-start.9 = (bf16[576,128]{1,0:T(8,128)(2,1)S(1)}, bf16[576,128]{1,0:T(8,128)(2,1)S(1)}, u32[]{:S(2)}, u32[]{:S(2)}) collective-permute-start(bf16[576,128]{1,0:T(8,128)(2,1)S(1)} %get-tuple-element.24), channel_id=1, source_target_pairs={{0,384},{128,0},{256,128},{384,256},{1,385},{129,1},{257,129},{385... | collective-permute-start | bytes 442376 | tf_op jit(solution)/shard_map/ppermute | solution.py:345
  105.9 4.8 %shard_map.92.units = s32[128]{0:T(128)S(1)} custom-call(s32[64,16]{1,0:T(8,128)S(1)} %copy.11.lists, s32[128]{0:T(128)S(1)} %copy-done, s32[8,16]{1,0:T(8,128)S(1)} %convert.2.use), custom_call_target="tpu_custom_call" | custom-call | tf_op jit(solution)/shard_map/pallas_call | solution.py:32
  110.7 1.9 %all-gather.3.cloned.1.call-done.far_docs = bf16[32,128,256]{2,1,0:T(8,128)(2,1)} async-done(((bf16[2,128,256]{2,1,0:T(8,128)(2,1)}), bf16[32,128,256]{2,1,0:T(8,128)(2,1)}) %all-gather.3.cloned.1.call-update) | async-done | bytes 2097168 | tf_op jit(solution)/shard_map/all_gather | solution.py:286
  112.6 4.0 %shard_map.95 = f32[4,8,512]{2,1,0:T(8,128)S(1)} custom-call(s32[128]{0:T(128)S(1)} %shard_map.92.units, bf16[576,128]{1,0:T(8,128)(2,1)S(1)} %get-tuple-element.21.own, bf16[576,128]{1,0:T(8,128)(2,1)S(1)} %collective-permute-done.7.one, bf16[576,128]{1,0:T(8,128)(2,1)S(1)} %collective-permute-done.8.two, ...), custom_call_target="tpu_custom_call" | custom-call | tf_op jit(solution)/shard_map/pallas_call | solution.py:32
  116.6 10.0 %all_to_all.15.all_stats = f32[4,8,512]{2,1,0:T(8,128)S(1)} all-to-all(f32[4,8,512]{2,1,0:T(8,128)S(1)} %shard_map.95), channel_id=1, replica_groups=mesh['x'=4,'zh'=4,'zl'=4,'y'=4,'core'=2] {'x'}, dimensions={0} | all-to-all | bytes 131072 | tf_op jit(solution)/shard_map/all_to_all | solution.py:280
  126.6 5.1 %shard_map.96 = f32[4,128,512]{2,1,0:T(8,128)S(1)} custom-call(s32[128]{0:T(128)S(1)} %shard_map.92.units, bf16[576,128]{1,0:T(8,128)(2,1)S(1)} %get-tuple-element.21.own, bf16[576,128]{1,0:T(8,128)(2,1)S(1)} %collective-permute-done.7.one, bf16[576,128]{1,0:T(8,128)(2,1)S(1)} %collective-permute-done.8.two, ...), custom_call_target="tpu_custom_call" | custom-call | tf_op jit(solution)/shard_map/pallas_call | solution.py:32
  131.8 16.3 %all_to_all.16.got = f32[4,128,512]{2,1,0:T(8,128)S(1)} all-to-all(f32[4,128,512]{2,1,0:T(8,128)S(1)} %shard_map.96), channel_id=1, replica_groups=mesh['x'=4,'zh'=4,'zl'=4,'y'=4,'core'=2] {'x'}, dimensions={0} | all-to-all | bytes 2097152 | tf_op jit(solution)/shard_map/all_to_all | solution.py:280
  (26 shorter events, 6.9 us)
Async XLA Ops:
  9.1 43.0 %all-to-all-start = ((bf16[16,96,128]{2,1,0:T(8,128)(2,1)}), bf16[16,96,128]{2,1,0:T(8,128)(2,1)S(1)}, u32[]{:S(2)}, u32[]{:S(2)}) async-start(bf16[16,96,128]{2,1,0:T(8,128)(2,1)} %bitcast.14), calls=%async_computation | async-start | bytes 786432 | tf_op jit(solution)/shard_map/all_to_all | solution.py:280
  26.8 85.8 %all-gather.3.cloned.1.call-start = ((), (), s32[]{:S(2)}) async-start(), calls=%async_computation.3 | async-start | bytes 2228224 | tf_op jit(solution)/shard_map/all_gather | solution.py:286
  41.4 47.1 %copy-start.3 = (bf16[4096]{0:T(1024)(128)(2,1)S(1)}, bf16[4096]{0:T(1024)(128)(2,1)}, u32[]{:S(2)}) copy-start(bf16[4096]{0:T(1024)(128)(2,1)} %param.10) | copy-start | bytes 24580
  41.4 27.3 %collective-permute-start = (bf16[4,144,512]{2,1,0:T(8,128)(2,1)S(1)}, bf16[4,144,512]{2,1,0:T(8,128)(2,1)S(1)}, u32[]{:S(2)}, u32[]{:S(2)}) collective-permute-start(bf16[4,144,512]{2,1,0:T(8,128)(2,1)S(1)} %bitcast.10), channel_id=1, source_target_pairs={{128,0},{256,128},{384,256},{0,384},{129,1},{257,129},{385,257},{1... | collective-permute-start | bytes 1769480 | tf_op jit(solution)/shard_map/ppermute | solution.py:305
  46.5 25.6 %collective-permute-start.1 = (bf16[4,144,512]{2,1,0:T(8,128)(2,1)S(1)}, bf16[4,144,512]{2,1,0:T(8,128)(2,1)S(1)}, u32[]{:S(2)}, u32[]{:S(2)}) collective-permute-start(bf16[4,144,512]{2,1,0:T(8,128)(2,1)S(1)} %bitcast.11), channel_id=1, source_target_pairs={{256,0},{384,128},{0,256},{128,384},{257,1},{385,129},{1,257},{129... | collective-permute-start | bytes 1769480 | tf_op jit(solution)/shard_map/ppermute | solution.py:305
  49.3 24.6 %collective-permute-start.2 = (bf16[4,144,512]{2,1,0:T(8,128)(2,1)S(1)}, bf16[4,144,512]{2,1,0:T(8,128)(2,1)}, u32[]{:S(2)}, u32[]{:S(2)}) collective-permute-start(bf16[4,144,512]{2,1,0:T(8,128)(2,1)S(1)} %bitcast.12), channel_id=1, source_target_pairs={{384,0},{0,128},{128,256},{256,384},{385,1},{1,129},{129,257},{257... | collective-permute-start | bytes 1769480 | tf_op jit(solution)/shard_map/ppermute | solution.py:305
  52.1 23.6 %collective-permute-start.3 = (bf16[16,96,128]{2,1,0:T(8,128)(2,1)S(1)}, bf16[16,96,128]{2,1,0:T(8,128)(2,1)S(1)}, u32[]{:S(2)}, u32[]{:S(2)}) collective-permute-start(bf16[16,96,128]{2,1,0:T(8,128)(2,1)S(1)} %all-to-all-done.near), channel_id=1, source_target_pairs={{8,0},{16,8},{24,16},{32,24},{40,32},{48,40},{56,48},{64,56},{72,6... | collective-permute-start | bytes 1179656 | tf_op jit(solution)/shard_map/ppermute | solution.py:302
  58.0 24.8 %collective-permute-start.4 = (bf16[16,96,128]{2,1,0:T(8,128)(2,1)S(1)}, bf16[16,96,128]{2,1,0:T(8,128)(2,1)S(1)}, u32[]{:S(2)}, u32[]{:S(2)}) collective-permute-start(bf16[16,96,128]{2,1,0:T(8,128)(2,1)S(1)} %all-to-all-done.near), channel_id=1, source_target_pairs={{16,0},{120,8},{32,16},{8,24},{48,32},{24,40},{64,48},{40,56},{80,... | collective-permute-start | bytes 1179656 | tf_op jit(solution)/shard_map/ppermute | solution.py:312
  68.7 3.4 %copy-start.1 = (bf16[4,144,512]{2,1,0:T(8,128)(2,1)}, bf16[4,144,512]{2,1,0:T(8,128)(2,1)S(1)}, u32[]{:S(2)}) copy-start(bf16[4,144,512]{2,1,0:T(8,128)(2,1)S(1)} %collective-permute-done) | copy-start | bytes 1769476
  68.7 17.8 %collective-permute-start.5 = (bf16[16,96,128]{2,1,0:T(8,128)(2,1)S(1)}, bf16[16,96,128]{2,1,0:T(8,128)(2,1)S(1)}, u32[]{:S(2)}, u32[]{:S(2)}) collective-permute-start(bf16[16,96,128]{2,1,0:T(8,128)(2,1)S(1)} %all-to-all-done.near), channel_id=1, source_target_pairs={{120,0},{0,8},{8,16},{16,24},{24,32},{32,40},{40,48},{48,56},{56,6... | collective-permute-start | bytes 1179656 | tf_op jit(solution)/shard_map/ppermute | solution.py:302
  72.1 0.8 copy-start.2
  86.5 6.4 %collective-permute-start.6 = (bf16[4,4,144,512]{3,2,1,0:T(8,128)(2,1)S(1)}, bf16[4,4,144,512]{3,2,1,0:T(8,128)(2,1)S(1)}, u32[]{:S(2)}, u32[]{:S(2)}) collective-permute-start(bf16[4,4,144,512]{3,2,1,0:T(8,128)(2,1)S(1)} %bitcast.6), channel_id=1, source_target_pairs={{0,1},{1,0},{2,3},{3,2},{4,5},{5,4},{6,7},{7,6},{8,9},{9,8},{10,11... | collective-permute-start | bytes 7077896 | tf_op jit(solution)/shard_map/ppermute | solution.py:314
  95.0 10.8 %copy-start.4 = (s32[64,16]{0,1:T(8,128)S(1)}, s32[64,16]{0,1:T(8,128)}, u32[]{:S(2)}) copy-start(s32[64,16]{0,1:T(8,128)} %param.15) | copy-start | bytes 12292
  95.0 10.9 %copy-start = (s32[128]{0:T(128)S(1)}, s32[128]{0:T(128)}, u32[]{:S(2)}) copy-start(s32[128]{0:T(128)} %place.1) | copy-start | bytes 1540
  96.8 15.8 %collective-permute-start.7 = (bf16[576,128]{1,0:T(8,128)(2,1)S(1)}, bf16[576,128]{1,0:T(8,128)(2,1)S(1)}, u32[]{:S(2)}, u32[]{:S(2)}) collective-permute-start(bf16[576,128]{1,0:T(8,128)(2,1)S(1)} %get-tuple-element.22), channel_id=1, source_target_pairs={{0,128},{128,256},{256,384},{384,0},{1,129},{129,257},{257,385},{3... | collective-permute-start | bytes 442376 | tf_op jit(solution)/shard_map/ppermute | solution.py:345
  98.7 13.9 %collective-permute-start.8 = (bf16[576,128]{1,0:T(8,128)(2,1)S(1)}, bf16[576,128]{1,0:T(8,128)(2,1)S(1)}, u32[]{:S(2)}, u32[]{:S(2)}) collective-permute-start(bf16[576,128]{1,0:T(8,128)(2,1)S(1)} %get-tuple-element.23), channel_id=1, source_target_pairs={{0,256},{128,384},{256,0},{384,128},{1,257},{129,385},{257,1},{385... | collective-permute-start | bytes 442376 | tf_op jit(solution)/shard_map/ppermute | solution.py:345
  103.2 9.4 %collective-permute-start.9 = (bf16[576,128]{1,0:T(8,128)(2,1)S(1)}, bf16[576,128]{1,0:T(8,128)(2,1)S(1)}, u32[]{:S(2)}, u32[]{:S(2)}) collective-permute-start(bf16[576,128]{1,0:T(8,128)(2,1)S(1)} %get-tuple-element.24), channel_id=1, source_target_pairs={{0,384},{128,0},{256,128},{384,256},{1,385},{129,1},{257,129},{385... | collective-permute-start | bytes 442376 | tf_op jit(solution)/shard_map/ppermute | solution.py:345
Sparse Core Ops, SparseCore 0:
  29.7 82.8 all-gather.2

commit v9 on v8

--- a/solution.py
+++ b/solution.py
@@ -120,7 +120,8 @@
 
     count = lax.fori_loop(0, NX * NZ, compact, 0)
     units[0] = count
-    units[count + 1] = 0
+    for step in range(1, 4):
+        units[count + step] = 0
 
 
 def project_kernel(normed, near, ahead, far, behind, *rest):
@@ -195,7 +196,7 @@
 
 
 def stats_kernel(units, own, one, two, three, far_docs, send, stats, docs, got, done):
-    fetch = pltpu.make_async_copy(far_docs, docs, done)
+    fetch = pltpu.make_async_copy(far_docs.at[:, :, 0:HEAD], docs, done)
     fetch.start()
     in_order((own, one, two, three), got)
     x = lax.axis_index("x")
@@ -217,7 +218,7 @@
         return group, top, sums[0] + sums[1]
 
     def pair(i, carry):
-        for group, top, part in [unit(units[2 * i + 1]), unit(units[2 * i + 2])]:
+        for group, top, part in [unit(units[4 * i + j]) for j in range(1, 5)]:
             before = stats[pl.ds(group, 1), :]
             new = jnp.maximum(before, top)
             old = stats[pl.ds(group + 4, 1), :] * weigh(before, new)
@@ -226,14 +227,12 @@
         return carry
 
     fetch.wait()
-    lax.fori_loop(0, (units[0] + 1) // 2, pair, 0)
+    lax.fori_loop(0, (units[0] + 3) // 4, pair, 0)
     for dest in range(NX):
         send[dest] = stats[...]
 
 
-def values_kernel(units, own, one, two, three, far_docs, all_stats, send, total, docs, got, done):
-    fetch = pltpu.make_async_copy(far_docs, docs, done)
-    fetch.start()
+def values_kernel(units, own, one, two, three, docs, all_stats, send, total, got):
     in_order((own, one, two, three), got)
     x = lax.axis_index("x")
     tops = [all_stats[src, 0:4, :] for src in range(NX)]
@@ -242,31 +241,30 @@
     for src in range(NX):
         sums = sums + all_stats[src, 4:8, :] * weigh(tops[src], top)
     total[0:4, :] = top
-    total[4:8, :] = 1.0 / sums
+    total[4:8, :] = top * RATE + jnp.log2(sums)
     send[...] = jnp.zeros(send.shape, F32)
 
     def apply(values, probs):
         return lax.dot_general(values, probs, (((0,), (0,)), ((), ())), preferred_element_type=F32)
 
-    own = weigh(own_scores(got, x), total[pl.ds(x, 1), :]) * total[pl.ds(x + 4, 1), :]
+    own = jnp.exp2(own_scores(got, x) * RATE - total[pl.ds(x + 4, 1), :])
     send[pl.ds(x, 1)] = apply(own_part(got, 2), own.astype(BF16))[None]
 
     def unit(code):
         group, owner, parts = unit_scores(code, got, docs)
-        top, inverse = total[pl.ds(group, 1), :], total[pl.ds(group + 4, 1), :]
+        shift = total[pl.ds(group + 4, 1), :]
         probs = [
-            (weigh(s, jnp.where(keep, top, -LOW)) * inverse).astype(BF16) for s, keep in parts
+            jnp.exp2(s * RATE - jnp.where(keep, shift, -LOW)).astype(BF16) for s, keep in parts
         ]
         values = docs[pl.ds(owner * 2, 2), :, HEAD : 2 * HEAD].reshape(2 * SEQ, HEAD)
         return group, apply(values, jnp.concatenate(probs, axis=0))
 
     def pair(i, carry):
-        for group, out in [unit(units[2 * i + 1]), unit(units[2 * i + 2])]:
+        for group, out in [unit(units[4 * i + j]) for j in range(1, 5)]:
             send[pl.ds(group, 1)] = send[pl.ds(group, 1)] + out[None]
         return carry
 
-    fetch.wait()
-    lax.fori_loop(0, (units[0] + 1) // 2, pair, 0)
+    lax.fori_loop(0, (units[0] + 3) // 4, pair, 0)
 
 
 def finish_kernel(got, out):
@@ -347,7 +345,7 @@
     ]
     scratch = [
         pltpu.VMEM((8, COLS), F32),
-        pltpu.VMEM((2 * NZ, SEQ, 2 * HEAD), BF16),
+        pltpu.VMEM((2 * NZ, SEQ, HEAD), BF16),
         pltpu.VMEM((NX, ROWS + HALF, HEAD), BF16),
         pltpu.SemaphoreType.DMA,
     ]
@@ -364,9 +362,8 @@
         values_kernel,
         shape((NX, HEAD, COLS), F32),
         (units, *got, docs, all_stats),
-        [SMEM] + [VMEM] * 4 + [ANY, VMEM],
-        scratch=scratch,
-        limit=52,
+        [SMEM] + [VMEM] * 6,
+        scratch=[scratch[0], scratch[2]],
     )
     returned = exchange(partial, "x")
     return call(finish_kernel, shape((SEQ, COLS), BF16), (returned,), [VMEM])

time: 157 us -> 154 us (0.981)
  Pallas kernels: 21.1 us -> 16.6 us
    pallas_call x7, Pallas kernels: 21.1 us -> 16.6 us  [call(): pl.pallas_call(kernel, out_shape=outs, in_specs=specs, out_specs=VMEM if...]
  transfers between devices with their start and end apart: 12 -> 12, of which waited for: 6 -> 6; matrix products, arithmetic and copies ran while one was open for 1% -> 1% of each run, Pallas kernels for 5% -> 6%
where the time goes in v9:
time: 154 us; the launch traced here: 153 us
  starting transfers between devices  51.9 us (34%)
  blocking collectives  41.7 us (27%)
  waiting for transfers between devices  26.2 us (17%)
  Pallas kernels  16.6 us (11%)
  between operations  13.6 us (9%)
  other arithmetic  1.74 us (1%)
    all_to_all x2, blocking collectives, exchange(): return lax.all_to_all(array, axes, 0, 0, tiled=True)  27.8 us
    all_to_all x1, starting transfers between devices, exchange(): return lax.all_to_all(array, axes, 0, 0, tiled=True)  17.7 us
    pallas_call x7, Pallas kernels, call(): pl.pallas_call(kernel, out_shape=outs, in_specs=specs, out_specs=VMEM if...  16.6 us
    all_gather x1, blocking collectives, shards(): by_y = lax.all_gather(tagged, 'y')  13.9 us
    ppermute x3, starting transfers between devices, from_x(): return lax.ppermute(array, 'x', [((i + step) % NX, i) for i in range(NX)])  10.7 us
    ppermute x2, starting transfers between devices, from_z(): lax.ppermute(array, z_axes, [((i + step) % NZ, i) for i in range(NZ)])  9.24 us
    ppermute x3, starting transfers between devices, shards(): lax.ppermute(sends[k], 'x', [(i, (i + k) % NX) for i in range(NX)])  8.98 us
    ppermute x3, waiting for transfers between devices, from_x(): return lax.ppermute(array, 'x', [((i + step) % NX, i) for i in range(NX)])  8.29 us
  transfers between devices with their start and end apart: 12, of which 6 were waited for; matrix products, arithmetic and copies ran while one was open for 1% of the time, Pallas kernels for 6%

profile of v9, /device:TPU:24, one launch (start us, length us, event | category | flops | bytes accessed | tf_op | source)
XLA Modules:
  0.0 152.7 jit_solution(5761215340176464841)
XLA Ops:
  6.5 2.6 %shard_map.91 = (bf16[4,4,96,128]{3,2,1,0:T(8,128)(2,1)}, bf16[144,512]{1,0:T(8,128)(2,1)}) custom-call(bf16[64,512]{1,0:T(8,128)(2,1)} %refs_0_.1, bf16[64,128]{1,0:T(8,128)(2,1)} %refs_1_.1, bf16[64,128]{1,0:T(8,128)(2,1)} %refs_2_.1, bf16[128,512]{1,0:T(8,128)(2,1)} %refs_3_.1, s32[2,16]{1,0:T(2,128)} %refs_4_.1), custom_call_target="tpu_custom_call" | custom-call | tf_op jit(solution)/shard_map/pallas_call | solution.py:32
  9.1 17.7 %all-to-all-start = ((bf16[16,96,128]{2,1,0:T(8,128)(2,1)}), bf16[16,96,128]{2,1,0:T(8,128)(2,1)S(1)}, u32[]{:S(2)}, u32[]{:S(2)}) async-start(bf16[16,96,128]{2,1,0:T(8,128)(2,1)} %bitcast.14), calls=%async_computation | async-start | bytes 786432 | tf_op jit(solution)/shard_map/all_to_all | solution.py:278
  27.5 13.9 %all-gather = bf16[576,512]{1,0:T(8,128)(2,1)S(1)} all-gather(bf16[144,512]{1,0:T(8,128)(2,1)} %get-tuple-element.15), channel_id=2, replica_groups=mesh['x'=4,'zh'=4,'zl'=4,'y'=4,'core'=2] {'y'}, dimensions={0}, use_global_device_ids=true | all-gather | bytes 737280 | tf_op jit(solution)/shard_map/all_gather | solution.py:305
  41.4 5.1 %collective-permute-start = (bf16[4,144,512]{2,1,0:T(8,128)(2,1)S(1)}, bf16[4,144,512]{2,1,0:T(8,128)(2,1)S(1)}, u32[]{:S(2)}, u32[]{:S(2)}) collective-permute-start(bf16[4,144,512]{2,1,0:T(8,128)(2,1)S(1)} %bitcast.10), channel_id=1, source_target_pairs={{128,0},{256,128},{384,256},{0,384},{129,1},{257,129},{385,257},{1... | collective-permute-start | bytes 1769480 | tf_op jit(solution)/shard_map/ppermute | solution.py:303
  46.5 2.8 %collective-permute-start.1 = (bf16[4,144,512]{2,1,0:T(8,128)(2,1)S(1)}, bf16[4,144,512]{2,1,0:T(8,128)(2,1)S(1)}, u32[]{:S(2)}, u32[]{:S(2)}) collective-permute-start(bf16[4,144,512]{2,1,0:T(8,128)(2,1)S(1)} %bitcast.11), channel_id=1, source_target_pairs={{256,0},{384,128},{0,256},{128,384},{257,1},{385,129},{1,257},{129... | collective-permute-start | bytes 1769480 | tf_op jit(solution)/shard_map/ppermute | solution.py:303
  49.3 2.8 %collective-permute-start.2 = (bf16[4,144,512]{2,1,0:T(8,128)(2,1)S(1)}, bf16[4,144,512]{2,1,0:T(8,128)(2,1)}, u32[]{:S(2)}, u32[]{:S(2)}) collective-permute-start(bf16[4,144,512]{2,1,0:T(8,128)(2,1)S(1)} %bitcast.12), channel_id=1, source_target_pairs={{384,0},{0,128},{128,256},{256,384},{385,1},{1,129},{129,257},{257... | collective-permute-start | bytes 1769480 | tf_op jit(solution)/shard_map/ppermute | solution.py:303
  52.1 5.9 %collective-permute-start.3 = (bf16[16,96,128]{2,1,0:T(8,128)(2,1)S(1)}, bf16[16,96,128]{2,1,0:T(8,128)(2,1)S(1)}, u32[]{:S(2)}, u32[]{:S(2)}) collective-permute-start(bf16[16,96,128]{2,1,0:T(8,128)(2,1)S(1)} %all-to-all-done.near), channel_id=1, source_target_pairs={{8,0},{16,8},{24,16},{32,24},{40,32},{48,40},{56,48},{64,56},{72,6... | collective-permute-start | bytes 1179656 | tf_op jit(solution)/shard_map/ppermute | solution.py:300
  58.0 3.4 %collective-permute-start.4 = (bf16[16,96,128]{2,1,0:T(8,128)(2,1)S(1)}, bf16[16,96,128]{2,1,0:T(8,128)(2,1)S(1)}, u32[]{:S(2)}, u32[]{:S(2)}) collective-permute-start(bf16[16,96,128]{2,1,0:T(8,128)(2,1)S(1)} %all-to-all-done.near), channel_id=1, source_target_pairs={{16,0},{120,8},{32,16},{8,24},{48,32},{24,40},{64,48},{40,56},{80,... | collective-permute-start | bytes 1179656 | tf_op jit(solution)/shard_map/ppermute | solution.py:310
  61.4 7.3 %collective-permute-done = bf16[4,144,512]{2,1,0:T(8,128)(2,1)S(1)} collective-permute-done((bf16[4,144,512]{2,1,0:T(8,128)(2,1)S(1)}, bf16[4,144,512]{2,1,0:T(8,128)(2,1)S(1)}, u32[]{:S(2)}, u32[]{:S(2)}) %collective-permute-start) | collective-permute-done | bytes 589856 | tf_op jit(solution)/shard_map/ppermute | solution.py:303
  68.7 3.4 %collective-permute-start.5 = (bf16[16,96,128]{2,1,0:T(8,128)(2,1)S(1)}, bf16[16,96,128]{2,1,0:T(8,128)(2,1)S(1)}, u32[]{:S(2)}, u32[]{:S(2)}) collective-permute-start(bf16[16,96,128]{2,1,0:T(8,128)(2,1)S(1)} %all-to-all-done.near), channel_id=1, source_target_pairs={{120,0},{0,8},{8,16},{16,24},{24,32},{32,40},{40,48},{48,56},{56,6... | collective-permute-start | bytes 1179656 | tf_op jit(solution)/shard_map/ppermute | solution.py:300
  75.7 7.0 %collective-permute-done.4.far = bf16[16,96,128]{2,1,0:T(8,128)(2,1)S(1)} collective-permute-done((bf16[16,96,128]{2,1,0:T(8,128)(2,1)S(1)}, bf16[16,96,128]{2,1,0:T(8,128)(2,1)S(1)}, u32[]{:S(2)}, u32[]{:S(2)}) %collective-permute-start.4) | collective-permute-done | bytes 393248 | tf_op jit(solution)/shard_map/ppermute | solution.py:310
  82.7 3.8 %collective-permute-done.5.behind = bf16[16,96,128]{2,1,0:T(8,128)(2,1)S(1)} collective-permute-done((bf16[16,96,128]{2,1,0:T(8,128)(2,1)S(1)}, bf16[16,96,128]{2,1,0:T(8,128)(2,1)S(1)}, u32[]{:S(2)}, u32[]{:S(2)}) %collective-permute-start.5) | collective-permute-done | bytes 393248 | tf_op jit(solution)/shard_map/ppermute | solution.py:300
  86.5 1.9 %collective-permute-start.6 = (bf16[4,4,144,512]{3,2,1,0:T(8,128)(2,1)S(1)}, bf16[4,4,144,512]{3,2,1,0:T(8,128)(2,1)S(1)}, u32[]{:S(2)}, u32[]{:S(2)}) collective-permute-start(bf16[4,4,144,512]{3,2,1,0:T(8,128)(2,1)S(1)} %bitcast.6), channel_id=1, source_target_pairs={{0,1},{1,0},{2,3},{3,2},{4,5},{5,4},{6,7},{7,6},{8,9},{9,8},{10,11... | collective-permute-start | bytes 7077896 | tf_op jit(solution)/shard_map/ppermute | solution.py:312
  88.5 4.5 %collective-permute-done.6.other = bf16[4,4,144,512]{3,2,1,0:T(8,128)(2,1)S(1)} collective-permute-done((bf16[4,4,144,512]{3,2,1,0:T(8,128)(2,1)S(1)}, bf16[4,4,144,512]{3,2,1,0:T(8,128)(2,1)S(1)}, u32[]{:S(2)}, u32[]{:S(2)}) %collective-permute-start.6) | collective-permute-done | bytes 2359328 | tf_op jit(solution)/shard_map/ppermute | solution.py:312
  93.0 2.0 %shard_map.93.normed = bf16[8,512,512]{2,1,0:T(8,128)(2,1)S(1)} custom-call(bf16[4,4,144,512]{3,2,1,0:T(8,128)(2,1)S(1)} %bitcast.7, bf16[4,4,144,512]{3,2,1,0:T(8,128)(2,1)S(1)} %collective-permute-done.6.other, f32[8,1,512]{2,1,0:T(1,128)S(1)} %bitcast.9), custom_call_target="tpu_custom_call" | custom-call | flops 16777216 | bytes 8388608 | tf_op jit(solution)/shard_map/pallas_call | solution.py:32
  96.8 1.9 %collective-permute-start.7 = (bf16[576,128]{1,0:T(8,128)(2,1)S(1)}, bf16[576,128]{1,0:T(8,128)(2,1)S(1)}, u32[]{:S(2)}, u32[]{:S(2)}) collective-permute-start(bf16[576,128]{1,0:T(8,128)(2,1)S(1)} %get-tuple-element.22), channel_id=1, source_target_pairs={{0,128},{128,256},{256,384},{384,0},{1,129},{129,257},{257,385},{3... | collective-permute-start | bytes 442376 | tf_op jit(solution)/shard_map/ppermute | solution.py:343
  98.7 4.4 %collective-permute-start.8 = (bf16[576,128]{1,0:T(8,128)(2,1)S(1)}, bf16[576,128]{1,0:T(8,128)(2,1)S(1)}, u32[]{:S(2)}, u32[]{:S(2)}) collective-permute-start(bf16[576,128]{1,0:T(8,128)(2,1)S(1)} %get-tuple-element.23), channel_id=1, source_target_pairs={{0,256},{128,384},{256,0},{384,128},{1,257},{129,385},{257,1},{385... | collective-permute-start | bytes 442376 | tf_op jit(solution)/shard_map/ppermute | solution.py:343
  103.2 2.6 %collective-permute-start.9 = (bf16[576,128]{1,0:T(8,128)(2,1)S(1)}, bf16[576,128]{1,0:T(8,128)(2,1)S(1)}, u32[]{:S(2)}, u32[]{:S(2)}) collective-permute-start(bf16[576,128]{1,0:T(8,128)(2,1)S(1)} %get-tuple-element.24), channel_id=1, source_target_pairs={{0,384},{128,0},{256,128},{384,256},{1,385},{129,1},{257,129},{385... | collective-permute-start | bytes 442376 | tf_op jit(solution)/shard_map/ppermute | solution.py:343
  105.9 4.8 %shard_map.92.units = s32[128]{0:T(128)S(1)} custom-call(s32[64,16]{1,0:T(8,128)S(1)} %copy.11.lists, s32[128]{0:T(128)S(1)} %copy-done.1, s32[8,16]{1,0:T(8,128)S(1)} %convert.2.use), custom_call_target="tpu_custom_call" | custom-call | tf_op jit(solution)/shard_map/pallas_call | solution.py:32
  110.7 1.9 %all-gather.3.cloned.1.call-done.far_docs.docs = bf16[32,128,256]{2,1,0:T(8,128)(2,1)} async-done(((bf16[2,128,256]{2,1,0:T(8,128)(2,1)}), bf16[32,128,256]{2,1,0:T(8,128)(2,1)}) %all-gather.3.cloned.1.call-update) | async-done | bytes 2097168 | tf_op jit(solution)/shard_map/all_gather | solution.py:284
  112.6 2.6 %shard_map.95 = f32[4,8,512]{2,1,0:T(8,128)S(1)} custom-call(s32[128]{0:T(128)S(1)} %shard_map.92.units, bf16[576,128]{1,0:T(8,128)(2,1)S(1)} %get-tuple-element.21.own, bf16[576,128]{1,0:T(8,128)(2,1)S(1)} %collective-permute-done.7.one, bf16[576,128]{1,0:T(8,128)(2,1)S(1)} %collective-permute-done.8.two, ...), custom_call_target="tpu_custom_call" | custom-call | tf_op jit(solution)/shard_map/pallas_call | solution.py:32
  115.2 10.3 %all_to_all.15.all_stats = f32[4,8,512]{2,1,0:T(8,128)S(1)} all-to-all(f32[4,8,512]{2,1,0:T(8,128)S(1)} %shard_map.95), channel_id=1, replica_groups=mesh['x'=4,'zh'=4,'zl'=4,'y'=4,'core'=2] {'x'}, dimensions={0} | all-to-all | bytes 131072 | tf_op jit(solution)/shard_map/all_to_all | solution.py:278
  125.5 2.2 %shard_map.96 = f32[4,128,512]{2,1,0:T(8,128)S(1)} custom-call(s32[128]{0:T(128)S(1)} %shard_map.92.units, bf16[576,128]{1,0:T(8,128)(2,1)S(1)} %get-tuple-element.21.own, bf16[576,128]{1,0:T(8,128)(2,1)S(1)} %collective-permute-done.7.one, bf16[576,128]{1,0:T(8,128)(2,1)S(1)} %collective-permute-done.8.two, ...), custom_call_target="tpu_custom_call" | custom-call | tf_op jit(solution)/shard_map/pallas_call | solution.py:32
  127.6 17.5 %all_to_all.16.got = f32[4,128,512]{2,1,0:T(8,128)S(1)} all-to-all(f32[4,128,512]{2,1,0:T(8,128)S(1)} %shard_map.96), channel_id=1, replica_groups=mesh['x'=4,'zh'=4,'zl'=4,'y'=4,'core'=2] {'x'}, dimensions={0} | all-to-all | bytes 2097152 | tf_op jit(solution)/shard_map/all_to_all | solution.py:278
  (28 shorter events, 6.9 us)
Async XLA Ops:
  9.1 43.0 %all-to-all-start = ((bf16[16,96,128]{2,1,0:T(8,128)(2,1)}), bf16[16,96,128]{2,1,0:T(8,128)(2,1)S(1)}, u32[]{:S(2)}, u32[]{:S(2)}) async-start(bf16[16,96,128]{2,1,0:T(8,128)(2,1)} %bitcast.14), calls=%async_computation | async-start | bytes 786432 | tf_op jit(solution)/shard_map/all_to_all | solution.py:278
  26.8 85.8 %all-gather.3.cloned.1.call-start = ((), (), s32[]{:S(2)}) async-start(), calls=%async_computation.3 | async-start | bytes 2228224 | tf_op jit(solution)/shard_map/all_gather | solution.py:284
  41.4 47.1 %copy-start.4 = (bf16[4096]{0:T(1024)(128)(2,1)S(1)}, bf16[4096]{0:T(1024)(128)(2,1)}, u32[]{:S(2)}) copy-start(bf16[4096]{0:T(1024)(128)(2,1)} %param.10) | copy-start | bytes 24580
  41.4 27.3 %collective-permute-start = (bf16[4,144,512]{2,1,0:T(8,128)(2,1)S(1)}, bf16[4,144,512]{2,1,0:T(8,128)(2,1)S(1)}, u32[]{:S(2)}, u32[]{:S(2)}) collective-permute-start(bf16[4,144,512]{2,1,0:T(8,128)(2,1)S(1)} %bitcast.10), channel_id=1, source_target_pairs={{128,0},{256,128},{384,256},{0,384},{129,1},{257,129},{385,257},{1... | collective-permute-start | bytes 1769480 | tf_op jit(solution)/shard_map/ppermute | solution.py:303
  46.5 25.6 %collective-permute-start.1 = (bf16[4,144,512]{2,1,0:T(8,128)(2,1)S(1)}, bf16[4,144,512]{2,1,0:T(8,128)(2,1)S(1)}, u32[]{:S(2)}, u32[]{:S(2)}) collective-permute-start(bf16[4,144,512]{2,1,0:T(8,128)(2,1)S(1)} %bitcast.11), channel_id=1, source_target_pairs={{256,0},{384,128},{0,256},{128,384},{257,1},{385,129},{1,257},{129... | collective-permute-start | bytes 1769480 | tf_op jit(solution)/shard_map/ppermute | solution.py:303
  49.3 24.6 %collective-permute-start.2 = (bf16[4,144,512]{2,1,0:T(8,128)(2,1)S(1)}, bf16[4,144,512]{2,1,0:T(8,128)(2,1)}, u32[]{:S(2)}, u32[]{:S(2)}) collective-permute-start(bf16[4,144,512]{2,1,0:T(8,128)(2,1)S(1)} %bitcast.12), channel_id=1, source_target_pairs={{384,0},{0,128},{128,256},{256,384},{385,1},{1,129},{129,257},{257... | collective-permute-start | bytes 1769480 | tf_op jit(solution)/shard_map/ppermute | solution.py:303
  52.1 23.6 %collective-permute-start.3 = (bf16[16,96,128]{2,1,0:T(8,128)(2,1)S(1)}, bf16[16,96,128]{2,1,0:T(8,128)(2,1)S(1)}, u32[]{:S(2)}, u32[]{:S(2)}) collective-permute-start(bf16[16,96,128]{2,1,0:T(8,128)(2,1)S(1)} %all-to-all-done.near), channel_id=1, source_target_pairs={{8,0},{16,8},{24,16},{32,24},{40,32},{48,40},{56,48},{64,56},{72,6... | collective-permute-start | bytes 1179656 | tf_op jit(solution)/shard_map/ppermute | solution.py:300
  58.0 24.8 %collective-permute-start.4 = (bf16[16,96,128]{2,1,0:T(8,128)(2,1)S(1)}, bf16[16,96,128]{2,1,0:T(8,128)(2,1)S(1)}, u32[]{:S(2)}, u32[]{:S(2)}) collective-permute-start(bf16[16,96,128]{2,1,0:T(8,128)(2,1)S(1)} %all-to-all-done.near), channel_id=1, source_target_pairs={{16,0},{120,8},{32,16},{8,24},{48,32},{24,40},{64,48},{40,56},{80,... | collective-permute-start | bytes 1179656 | tf_op jit(solution)/shard_map/ppermute | solution.py:310
  68.7 3.4 %copy-start.2 = (bf16[4,144,512]{2,1,0:T(8,128)(2,1)}, bf16[4,144,512]{2,1,0:T(8,128)(2,1)S(1)}, u32[]{:S(2)}) copy-start(bf16[4,144,512]{2,1,0:T(8,128)(2,1)S(1)} %collective-permute-done) | copy-start | bytes 1769476
  68.7 17.8 %collective-permute-start.5 = (bf16[16,96,128]{2,1,0:T(8,128)(2,1)S(1)}, bf16[16,96,128]{2,1,0:T(8,128)(2,1)S(1)}, u32[]{:S(2)}, u32[]{:S(2)}) collective-permute-start(bf16[16,96,128]{2,1,0:T(8,128)(2,1)S(1)} %all-to-all-done.near), channel_id=1, source_target_pairs={{120,0},{0,8},{8,16},{16,24},{24,32},{32,40},{40,48},{48,56},{56,6... | collective-permute-start | bytes 1179656 | tf_op jit(solution)/shard_map/ppermute | solution.py:300
  72.1 0.8 copy-start.3
  86.5 6.4 %collective-permute-start.6 = (bf16[4,4,144,512]{3,2,1,0:T(8,128)(2,1)S(1)}, bf16[4,4,144,512]{3,2,1,0:T(8,128)(2,1)S(1)}, u32[]{:S(2)}, u32[]{:S(2)}) collective-permute-start(bf16[4,4,144,512]{3,2,1,0:T(8,128)(2,1)S(1)} %bitcast.6), channel_id=1, source_target_pairs={{0,1},{1,0},{2,3},{3,2},{4,5},{5,4},{6,7},{7,6},{8,9},{9,8},{10,11... | collective-permute-start | bytes 7077896 | tf_op jit(solution)/shard_map/ppermute | solution.py:312
  95.0 10.8 %copy-start.5 = (s32[64,16]{0,1:T(8,128)S(1)}, s32[64,16]{0,1:T(8,128)}, u32[]{:S(2)}) copy-start(s32[64,16]{0,1:T(8,128)} %param.15) | copy-start | bytes 12292
  95.0 10.9 %copy-start.1 = (s32[128]{0:T(128)S(1)}, s32[128]{0:T(128)}, u32[]{:S(2)}) copy-start(s32[128]{0:T(128)} %place.1) | copy-start | bytes 1540
  96.8 15.8 %collective-permute-start.7 = (bf16[576,128]{1,0:T(8,128)(2,1)S(1)}, bf16[576,128]{1,0:T(8,128)(2,1)S(1)}, u32[]{:S(2)}, u32[]{:S(2)}) collective-permute-start(bf16[576,128]{1,0:T(8,128)(2,1)S(1)} %get-tuple-element.22), channel_id=1, source_target_pairs={{0,128},{128,256},{256,384},{384,0},{1,129},{129,257},{257,385},{3... | collective-permute-start | bytes 442376 | tf_op jit(solution)/shard_map/ppermute | solution.py:343
  98.7 13.9 %collective-permute-start.8 = (bf16[576,128]{1,0:T(8,128)(2,1)S(1)}, bf16[576,128]{1,0:T(8,128)(2,1)S(1)}, u32[]{:S(2)}, u32[]{:S(2)}) collective-permute-start(bf16[576,128]{1,0:T(8,128)(2,1)S(1)} %get-tuple-element.23), channel_id=1, source_target_pairs={{0,256},{128,384},{256,0},{384,128},{1,257},{129,385},{257,1},{385... | collective-permute-start | bytes 442376 | tf_op jit(solution)/shard_map/ppermute | solution.py:343
  103.2 9.4 %collective-permute-start.9 = (bf16[576,128]{1,0:T(8,128)(2,1)S(1)}, bf16[576,128]{1,0:T(8,128)(2,1)S(1)}, u32[]{:S(2)}, u32[]{:S(2)}) collective-permute-start(bf16[576,128]{1,0:T(8,128)(2,1)S(1)} %get-tuple-element.24), channel_id=1, source_target_pairs={{0,384},{128,0},{256,128},{384,256},{1,385},{129,1},{257,129},{385... | collective-permute-start | bytes 442376 | tf_op jit(solution)/shard_map/ppermute | solution.py:343
  112.6 12.9 %copy-start = (bf16[32,128,256]{2,1,0:T(8,128)(2,1)S(1)}, bf16[32,128,256]{2,1,0:T(8,128)(2,1)}, u32[]{:S(2)}) copy-start(bf16[32,128,256]{2,1,0:T(8,128)(2,1)} %all-gather.3.cloned.1.call-done.far_docs.docs) | copy-start | bytes 6291460
Sparse Core Ops, SparseCore 0:
  29.7 82.8 all-gather.2

commit v10 on v9

--- a/solution.py
+++ b/solution.py
@@ -307,9 +307,19 @@
     mine = mine.reshape(NX, 4, SEQ + 16, 512)
     ahead = from_z(near, 1)
     behind = from_z(near, -1)
-    far = lax.ppermute(near, z_axes, [((i + 2 - 4 * (i % 2)) % NZ, i) for i in range(NZ)])
+    far = from_z(ahead, 1)
     mine, ahead, far, behind = lax.optimization_barrier((mine, ahead, far, behind))
     other = lax.ppermute(mine, "core", [(0, 1), (1, 0)])
+    use = mine[:, 0, SEQ : SEQ + 2, 0:PICKS].astype(jnp.int32).reshape(8, PICKS)
+    units = call(
+        route_kernel,
+        shape((UNITS,), jnp.int32),
+        (doc_lists, doc_place, use),
+        [SMEM] * 3,
+        out_specs=SMEM,
+        scratch=[pltpu.SMEM((NX * NZ,), jnp.int32)],
+    )
+    other, units = lax.optimization_barrier((other, units))
     gain = norm_gain.astype(F32).reshape(8, 1, 512)
     normed = call(
         norm_kernel,
@@ -319,16 +329,6 @@
         flops=ROWS * 4096 * 8,
         moved=8 << 20,
     )
-    use = mine[:, 0, SEQ : SEQ + 2, 0:PICKS].astype(jnp.int32).reshape(8, PICKS)
-    units = call(
-        route_kernel,
-        shape((UNITS,), jnp.int32),
-        (doc_lists, doc_place, use),
-        [SMEM] * 3,
-        out_specs=SMEM,
-        scratch=[pltpu.SMEM((NX * NZ,), jnp.int32)],
-    )
-
     sends = call(
         project_kernel,
         [shape((ROWS + HALF, HEAD), BF16)] * NX,

time: 154 us -> 162 us (1.052)
  Pallas kernels: 16.6 us -> 22.1 us
  local copies, waits for them, and re-layouts: 0.92 us -> 3.86 us
  waiting for transfers between devices: 26.2 us -> 29.1 us
  blocking collectives: 41.7 us -> 39.1 us
  starting transfers between devices: 51.9 us -> 50.2 us
    ppermute x2 -> x3, waiting for transfers between devices: 3.83 us -> 22.5 us  [from_z(): lax.ppermute(array, z_axes, [((i + step) % NZ, i) for i in range(NZ)])]
    ppermute x3, waiting for transfers between devices: 8.29 us -> 0.01 us  [from_x(): return lax.ppermute(array, 'x', [((i + step) % NX, i) for i in range(NX)])]
    ppermute x1 -> x0, waiting for transfers between devices: 7.05 us -> none  [shards(): lax.ppermute(near, z_axes, [((i + 2 - 4 * (i % 2)) % NZ, i) for i in rang...]
    ppermute x3, waiting for transfers between devices: 0.01 us -> 5.95 us  [shards(): lax.ppermute(sends[k], 'x', [(i, (i + k) % NX) for i in range(NX)])]
    pallas_call x7, Pallas kernels: 16.6 us -> 22.1 us  [call(): pl.pallas_call(kernel, out_shape=outs, in_specs=specs, out_specs=VMEM if...]
    ppermute x1, waiting for transfers between devices: 4.48 us -> 0.01 us  [shards(): other = lax.ppermute(mine, 'core', [(0, 1), (1, 0)])]
    ppermute x1 -> x0, starting transfers between devices: 3.44 us -> none  [shards(): lax.ppermute(near, z_axes, [((i + 2 - 4 * (i % 2)) % NZ, i) for i in rang...]
    unnamed x13 -> x19, local copies, waits for them, and re-layouts: 0.91 us -> 3.85 us
  transfers between devices with their start and end apart: 12 -> 12, of which waited for: 6 -> 4; matrix products, arithmetic and copies ran while one was open for 1% -> 2% of each run, Pallas kernels for 6% -> 6%
where the time goes in v10:
time: 162 us; the launch traced here: 161 us
  starting transfers between devices  50.2 us (31%)
  blocking collectives  39.1 us (24%)
  waiting for transfers between devices  29.1 us (18%)
  Pallas kernels  22.1 us (14%)
  between operations  13.7 us (8%)
  local copies, waits for them, and re-layouts  3.86 us (2%)
  other arithmetic  2.61 us (2%)
    all_to_all x2, blocking collectives, exchange(): return lax.all_to_all(array, axes, 0, 0, tiled=True)  25.2 us
    ppermute x3, waiting for transfers between devices, from_z(): lax.ppermute(array, z_axes, [((i + step) % NZ, i) for i in range(NZ)])  22.5 us
    pallas_call x7, Pallas kernels, call(): pl.pallas_call(kernel, out_shape=outs, in_specs=specs, out_specs=VMEM if...  22.1 us
    all_to_all x1, starting transfers between devices, exchange(): return lax.all_to_all(array, axes, 0, 0, tiled=True)  17.7 us
    all_gather x1, blocking collectives, shards(): by_y = lax.all_gather(tagged, 'y')  13.9 us
    ppermute x3, starting transfers between devices, from_x(): return lax.ppermute(array, 'x', [((i + step) % NX, i) for i in range(NX)])  11.9 us
    ppermute x3, starting transfers between devices, from_z(): lax.ppermute(array, z_axes, [((i + step) % NZ, i) for i in range(NZ)])  9.69 us
    ppermute x3, starting transfers between devices, shards(): lax.ppermute(sends[k], 'x', [(i, (i + k) % NX) for i in range(NX)])  8.97 us
  transfers between devices with their start and end apart: 12, of which 4 were waited for; matrix products, arithmetic and copies ran while one was open for 2% of the time, Pallas kernels for 6%

profile of v10, /device:TPU:24, one launch (start us, length us, event | category | flops | bytes accessed | tf_op | source)
XLA Modules:
  0.0 160.6 jit_solution(8683614035598215585)
XLA Ops:
  6.5 2.5 %shard_map.91 = (bf16[4,4,96,128]{3,2,1,0:T(8,128)(2,1)}, bf16[144,512]{1,0:T(8,128)(2,1)}) custom-call(bf16[64,512]{1,0:T(8,128)(2,1)} %refs_0_.1, bf16[64,128]{1,0:T(8,128)(2,1)} %refs_1_.1, bf16[64,128]{1,0:T(8,128)(2,1)} %refs_2_.1, bf16[128,512]{1,0:T(8,128)(2,1)} %refs_3_.1, s32[2,16]{1,0:T(2,128)} %refs_4_.1), custom_call_target="tpu_custom_call" | custom-call | tf_op jit(solution)/shard_map/pallas_call | solution.py:32
  9.1 17.7 %all-to-all-start = ((bf16[16,96,128]{2,1,0:T(8,128)(2,1)}), bf16[16,96,128]{2,1,0:T(8,128)(2,1)S(1)}, u32[]{:S(2)}, u32[]{:S(2)}) async-start(bf16[16,96,128]{2,1,0:T(8,128)(2,1)} %bitcast.14), calls=%async_computation | async-start | bytes 786432 | tf_op jit(solution)/shard_map/all_to_all | solution.py:278
  27.5 13.9 %all-gather = bf16[576,512]{1,0:T(8,128)(2,1)S(1)} all-gather(bf16[144,512]{1,0:T(8,128)(2,1)} %get-tuple-element.17), channel_id=2, replica_groups=mesh['x'=4,'zh'=4,'zl'=4,'y'=4,'core'=2] {'y'}, dimensions={0}, use_global_device_ids=true | all-gather | bytes 737280 | tf_op jit(solution)/shard_map/all_gather | solution.py:305
  41.4 3.9 %collective-permute-start.2 = (bf16[4,144,512]{2,1,0:T(8,128)(2,1)S(1)}, bf16[4,144,512]{2,1,0:T(8,128)(2,1)S(1)}, u32[]{:S(2)}, u32[]{:S(2)}) collective-permute-start(bf16[4,144,512]{2,1,0:T(8,128)(2,1)S(1)} %bitcast.10), channel_id=1, source_target_pairs={{384,0},{0,128},{128,256},{256,384},{385,1},{1,129},{129,257},{257... | collective-permute-start | bytes 1769480 | tf_op jit(solution)/shard_map/ppermute | solution.py:303
  45.3 4.6 %collective-permute-start.1 = (bf16[4,144,512]{2,1,0:T(8,128)(2,1)S(1)}, bf16[4,144,512]{2,1,0:T(8,128)(2,1)S(1)}, u32[]{:S(2)}, u32[]{:S(2)}) collective-permute-start(bf16[4,144,512]{2,1,0:T(8,128)(2,1)S(1)} %bitcast.11), channel_id=1, source_target_pairs={{256,0},{384,128},{0,256},{128,384},{257,1},{385,129},{1,257},{129... | collective-permute-start | bytes 1769480 | tf_op jit(solution)/shard_map/ppermute | solution.py:303
  49.9 3.4 %collective-permute-start = (bf16[4,144,512]{2,1,0:T(8,128)(2,1)S(1)}, bf16[4,144,512]{2,1,0:T(8,128)(2,1)}, u32[]{:S(2)}, u32[]{:S(2)}) collective-permute-start(bf16[4,144,512]{2,1,0:T(8,128)(2,1)S(1)} %bitcast.12), channel_id=1, source_target_pairs={{128,0},{256,128},{384,256},{0,384},{129,1},{257,129},{385,257},{1... | collective-permute-start | bytes 1769480 | tf_op jit(solution)/shard_map/ppermute | solution.py:303
  53.3 5.9 %collective-permute-start.3 = (bf16[16,96,128]{2,1,0:T(8,128)(2,1)S(1)}, bf16[16,96,128]{2,1,0:T(8,128)(2,1)S(1)}, u32[]{:S(2)}, u32[]{:S(2)}) collective-permute-start(bf16[16,96,128]{2,1,0:T(8,128)(2,1)S(1)} %all-to-all-done.near), channel_id=1, source_target_pairs={{8,0},{16,8},{24,16},{32,24},{40,32},{48,40},{56,48},{64,56},{72,6... | collective-permute-start | bytes 1179656 | tf_op jit(solution)/shard_map/ppermute | solution.py:300
  59.1 1.9 %collective-permute-start.5 = (bf16[16,96,128]{2,1,0:T(8,128)(2,1)S(1)}, bf16[16,96,128]{2,1,0:T(8,128)(2,1)S(1)}, u32[]{:S(2)}, u32[]{:S(2)}) collective-permute-start(bf16[16,96,128]{2,1,0:T(8,128)(2,1)S(1)} %all-to-all-done.near), channel_id=1, source_target_pairs={{120,0},{0,8},{8,16},{16,24},{24,32},{32,40},{40,48},{48,56},{56,6... | collective-permute-start | bytes 1179656 | tf_op jit(solution)/shard_map/ppermute | solution.py:300
  61.1 11.1 %collective-permute-done.3.ahead = bf16[16,96,128]{2,1,0:T(8,128)(2,1)S(1)} collective-permute-done((bf16[16,96,128]{2,1,0:T(8,128)(2,1)S(1)}, bf16[16,96,128]{2,1,0:T(8,128)(2,1)S(1)}, u32[]{:S(2)}, u32[]{:S(2)}) %collective-permute-start.3) | collective-permute-done | bytes 393248 | tf_op jit(solution)/shard_map/ppermute | solution.py:300
  72.2 1.9 %collective-permute-start.4 = (bf16[16,96,128]{2,1,0:T(8,128)(2,1)S(1)}, bf16[16,96,128]{2,1,0:T(8,128)(2,1)S(1)}, u32[]{:S(2)}, u32[]{:S(2)}) collective-permute-start(bf16[16,96,128]{2,1,0:T(8,128)(2,1)S(1)} %collective-permute-done.3.ahead), channel_id=1, source_target_pairs={{8,0},{16,8},{24,16},{32,24},{40,32},{48,40},{56,48},{64,56},{72,6... | collective-permute-start | bytes 1179656 | tf_op jit(solution)/shard_map/ppermute | solution.py:300
  75.8 1.9 %pad_maximum_fusion = bf16[16,144,512]{2,1,0:T(8,128)(2,1)S(1)} fusion(bf16[4,144,512]{2,1,0:T(8,128)(2,1)} %copy-done.6, bf16[4,144,512]{2,1,0:T(8,128)(2,1)} %copy-done.7, bf16[4,144,512]{2,1,0:T(8,128)(2,1)} %collective-permute-done, bf16[4,144,512]{2,1,0:T(8,128)(2,1)} %bitcast.13), kind=kLoop, calls=%fused_computation | loop fusion | flops 3538944 | bytes 4718592 | tf_op jit(solution)/shard_map/concatenate | solution.py:306
  77.7 11.3 %collective-permute-done.4.far = bf16[16,96,128]{2,1,0:T(8,128)(2,1)S(1)} collective-permute-done((bf16[16,96,128]{2,1,0:T(8,128)(2,1)S(1)}, bf16[16,96,128]{2,1,0:T(8,128)(2,1)S(1)}, u32[]{:S(2)}, u32[]{:S(2)}) %collective-permute-start.4) | collective-permute-done | bytes 393248 | tf_op jit(solution)/shard_map/ppermute | solution.py:300
  89.8 1.9 %collective-permute-start.6 = (bf16[4,4,144,512]{3,2,1,0:T(8,128)(2,1)S(1)}, bf16[4,4,144,512]{3,2,1,0:T(8,128)(2,1)}, u32[]{:S(2)}, u32[]{:S(2)}) collective-permute-start(bf16[4,4,144,512]{3,2,1,0:T(8,128)(2,1)S(1)} %bitcast.6), channel_id=1, source_target_pairs={{0,1},{1,0},{2,3},{3,2},{4,5},{5,4},{6,7},{7,6},{8,9},{9,8},{10,11... | collective-permute-start | bytes 7077896 | tf_op jit(solution)/shard_map/ppermute | solution.py:312
  93.9 4.8 %shard_map.92.units = s32[128]{0:T(128)S(1)} custom-call(s32[64,16]{1,0:T(8,128)S(1)} %copy-done.3, s32[128]{0:T(128)S(1)} %copy-done.4, s32[8,16]{1,0:T(8,128)S(1)} %convert.2.use), custom_call_target="tpu_custom_call" | custom-call | tf_op jit(solution)/shard_map/pallas_call | solution.py:32
  98.7 3.8 %shard_map.93.normed = bf16[8,512,512]{2,1,0:T(8,128)(2,1)S(1)} custom-call(bf16[4,4,144,512]{3,2,1,0:T(8,128)(2,1)S(1)} %bitcast.8, bf16[4,4,144,512]{3,2,1,0:T(8,128)(2,1)} %collective-permute-done.6.other, f32[8,1,512]{2,1,0:T(1,128)S(1)} %bitcast.9), custom_call_target="tpu_custom_call" | custom-call | flops 16777216 | bytes 8388608 | tf_op jit(solution)/shard_map/pallas_call | solution.py:32
  104.3 1.9 %collective-permute-start.7 = (bf16[576,128]{1,0:T(8,128)(2,1)S(1)}, bf16[576,128]{1,0:T(8,128)(2,1)S(1)}, u32[]{:S(2)}, u32[]{:S(2)}) collective-permute-start(bf16[576,128]{1,0:T(8,128)(2,1)S(1)} %get-tuple-element.26), channel_id=1, source_target_pairs={{0,128},{128,256},{256,384},{384,0},{1,129},{129,257},{257,385},{3... | collective-permute-start | bytes 442376 | tf_op jit(solution)/shard_map/ppermute | solution.py:343
  106.2 3.8 %collective-permute-start.8 = (bf16[576,128]{1,0:T(8,128)(2,1)S(1)}, bf16[576,128]{1,0:T(8,128)(2,1)S(1)}, u32[]{:S(2)}, u32[]{:S(2)}) collective-permute-start(bf16[576,128]{1,0:T(8,128)(2,1)S(1)} %get-tuple-element.27), channel_id=1, source_target_pairs={{0,256},{128,384},{256,0},{384,128},{1,257},{129,385},{257,1},{385... | collective-permute-start | bytes 442376 | tf_op jit(solution)/shard_map/ppermute | solution.py:343
  110.0 3.3 %collective-permute-start.9 = (bf16[576,128]{1,0:T(8,128)(2,1)S(1)}, bf16[576,128]{1,0:T(8,128)(2,1)S(1)}, u32[]{:S(2)}, u32[]{:S(2)}) collective-permute-start(bf16[576,128]{1,0:T(8,128)(2,1)S(1)} %get-tuple-element.28), channel_id=1, source_target_pairs={{0,384},{128,0},{256,128},{384,256},{1,385},{129,1},{257,129},{385... | collective-permute-start | bytes 442376 | tf_op jit(solution)/shard_map/ppermute | solution.py:343
  113.3 3.5 %collective-permute-done.7.one = bf16[576,128]{1,0:T(8,128)(2,1)S(1)} collective-permute-done((bf16[576,128]{1,0:T(8,128)(2,1)S(1)}, bf16[576,128]{1,0:T(8,128)(2,1)S(1)}, u32[]{:S(2)}, u32[]{:S(2)}) %collective-permute-start.7) | collective-permute-done | bytes 147488 | tf_op jit(solution)/shard_map/ppermute | solution.py:343
  116.8 2.5 %collective-permute-done.9.three = bf16[576,128]{1,0:T(8,128)(2,1)S(1)} collective-permute-done((bf16[576,128]{1,0:T(8,128)(2,1)S(1)}, bf16[576,128]{1,0:T(8,128)(2,1)S(1)}, u32[]{:S(2)}, u32[]{:S(2)}) %collective-permute-start.9) | collective-permute-done | bytes 147488 | tf_op jit(solution)/shard_map/ppermute | solution.py:343
  119.3 4.0 %shard_map.95 = f32[4,8,512]{2,1,0:T(8,128)S(1)} custom-call(s32[128]{0:T(128)S(1)} %shard_map.92.units, bf16[576,128]{1,0:T(8,128)(2,1)S(1)} %get-tuple-element.25.own, bf16[576,128]{1,0:T(8,128)(2,1)S(1)} %collective-permute-done.7.one, bf16[576,128]{1,0:T(8,128)(2,1)S(1)} %collective-permute-done.8.two, ...), custom_call_target="tpu_custom_call" | custom-call | tf_op jit(solution)/shard_map/pallas_call | solution.py:32
  123.3 8.6 %all_to_all.15.all_stats = f32[4,8,512]{2,1,0:T(8,128)S(1)} all-to-all(f32[4,8,512]{2,1,0:T(8,128)S(1)} %shard_map.95), channel_id=1, replica_groups=mesh['x'=4,'zh'=4,'zl'=4,'y'=4,'core'=2] {'x'}, dimensions={0} | all-to-all | bytes 131072 | tf_op jit(solution)/shard_map/all_to_all | solution.py:278
  131.9 4.5 %shard_map.96 = f32[4,128,512]{2,1,0:T(8,128)S(1)} custom-call(s32[128]{0:T(128)S(1)} %shard_map.92.units, bf16[576,128]{1,0:T(8,128)(2,1)S(1)} %get-tuple-element.25.own, bf16[576,128]{1,0:T(8,128)(2,1)S(1)} %collective-permute-done.7.one, bf16[576,128]{1,0:T(8,128)(2,1)S(1)} %collective-permute-done.8.two, ...), custom_call_target="tpu_custom_call" | custom-call | tf_op jit(solution)/shard_map/pallas_call | solution.py:32
  136.4 16.6 %all_to_all.16.got = f32[4,128,512]{2,1,0:T(8,128)S(1)} all-to-all(f32[4,128,512]{2,1,0:T(8,128)S(1)} %shard_map.96), channel_id=1, replica_groups=mesh['x'=4,'zh'=4,'zl'=4,'y'=4,'core'=2] {'x'}, dimensions={0} | all-to-all | bytes 2097152 | tf_op jit(solution)/shard_map/all_to_all | solution.py:278
  (34 shorter events, 7.8 us)
Async XLA Ops:
  9.1 44.2 %all-to-all-start = ((bf16[16,96,128]{2,1,0:T(8,128)(2,1)}), bf16[16,96,128]{2,1,0:T(8,128)(2,1)S(1)}, u32[]{:S(2)}, u32[]{:S(2)}) async-start(bf16[16,96,128]{2,1,0:T(8,128)(2,1)} %bitcast.14), calls=%async_computation | async-start | bytes 786432 | tf_op jit(solution)/shard_map/all_to_all | solution.py:278
  26.8 86.5 %all-gather.3.cloned.1.call-start = ((), (), s32[]{:S(2)}) async-start(), calls=%async_computation.3 | async-start | bytes 2228224 | tf_op jit(solution)/shard_map/all_gather | solution.py:284
  41.4 32.8 %copy-start.5 = (bf16[576,512]{1,0:T(8,128)(2,1)}, bf16[576,512]{1,0:T(8,128)(2,1)S(1)}, u32[]{:S(2)}) copy-start(bf16[576,512]{1,0:T(8,128)(2,1)S(1)} %all-gather) | copy-start | bytes 1769476
  41.4 50.4 %copy-start.8 = (s32[64,16]{0,1:T(8,128)S(1)}, s32[64,16]{0,1:T(8,128)}, u32[]{:S(2)}) copy-start(s32[64,16]{0,1:T(8,128)} %param.15) | copy-start | bytes 12292
  41.4 51.8 %copy-start.4 = (s32[128]{0:T(128)S(1)}, s32[128]{0:T(128)}, u32[]{:S(2)}) copy-start(s32[128]{0:T(128)} %place.1) | copy-start | bytes 1540
  41.4 32.8 %collective-permute-start.2 = (bf16[4,144,512]{2,1,0:T(8,128)(2,1)S(1)}, bf16[4,144,512]{2,1,0:T(8,128)(2,1)S(1)}, u32[]{:S(2)}, u32[]{:S(2)}) collective-permute-start(bf16[4,144,512]{2,1,0:T(8,128)(2,1)S(1)} %bitcast.10), channel_id=1, source_target_pairs={{384,0},{0,128},{128,256},{256,384},{385,1},{1,129},{129,257},{257... | collective-permute-start | bytes 1769480 | tf_op jit(solution)/shard_map/ppermute | solution.py:303
  45.3 28.9 %collective-permute-start.1 = (bf16[4,144,512]{2,1,0:T(8,128)(2,1)S(1)}, bf16[4,144,512]{2,1,0:T(8,128)(2,1)S(1)}, u32[]{:S(2)}, u32[]{:S(2)}) collective-permute-start(bf16[4,144,512]{2,1,0:T(8,128)(2,1)S(1)} %bitcast.11), channel_id=1, source_target_pairs={{256,0},{384,128},{0,256},{128,384},{257,1},{385,129},{1,257},{129... | collective-permute-start | bytes 1769480 | tf_op jit(solution)/shard_map/ppermute | solution.py:303
  49.9 25.9 %collective-permute-start = (bf16[4,144,512]{2,1,0:T(8,128)(2,1)S(1)}, bf16[4,144,512]{2,1,0:T(8,128)(2,1)}, u32[]{:S(2)}, u32[]{:S(2)}) collective-permute-start(bf16[4,144,512]{2,1,0:T(8,128)(2,1)S(1)} %bitcast.12), channel_id=1, source_target_pairs={{128,0},{256,128},{384,256},{0,384},{129,1},{257,129},{385,257},{1... | collective-permute-start | bytes 1769480 | tf_op jit(solution)/shard_map/ppermute | solution.py:303
  53.3 18.9 %collective-permute-start.3 = (bf16[16,96,128]{2,1,0:T(8,128)(2,1)S(1)}, bf16[16,96,128]{2,1,0:T(8,128)(2,1)S(1)}, u32[]{:S(2)}, u32[]{:S(2)}) collective-permute-start(bf16[16,96,128]{2,1,0:T(8,128)(2,1)S(1)} %all-to-all-done.near), channel_id=1, source_target_pairs={{8,0},{16,8},{24,16},{32,24},{40,32},{48,40},{56,48},{64,56},{72,6... | collective-permute-start | bytes 1179656 | tf_op jit(solution)/shard_map/ppermute | solution.py:300
  59.1 18.5 %collective-permute-start.5 = (bf16[16,96,128]{2,1,0:T(8,128)(2,1)S(1)}, bf16[16,96,128]{2,1,0:T(8,128)(2,1)S(1)}, u32[]{:S(2)}, u32[]{:S(2)}) collective-permute-start(bf16[16,96,128]{2,1,0:T(8,128)(2,1)S(1)} %all-to-all-done.near), channel_id=1, source_target_pairs={{120,0},{0,8},{8,16},{16,24},{24,32},{32,40},{40,48},{48,56},{56,6... | collective-permute-start | bytes 1179656 | tf_op jit(solution)/shard_map/ppermute | solution.py:300
  72.2 16.8 %collective-permute-start.4 = (bf16[16,96,128]{2,1,0:T(8,128)(2,1)S(1)}, bf16[16,96,128]{2,1,0:T(8,128)(2,1)S(1)}, u32[]{:S(2)}, u32[]{:S(2)}) collective-permute-start(bf16[16,96,128]{2,1,0:T(8,128)(2,1)S(1)} %collective-permute-done.3.ahead), channel_id=1, source_target_pairs={{8,0},{16,8},{24,16},{32,24},{40,32},{48,40},{56,48},{64,56},{72,6... | collective-permute-start | bytes 1179656 | tf_op jit(solution)/shard_map/ppermute | solution.py:300
  74.1 0.8 copy-start.6
  75.0 0.8 copy-start.7
  89.0 0.8 copy-start.1
  89.8 8.9 %collective-permute-start.6 = (bf16[4,4,144,512]{3,2,1,0:T(8,128)(2,1)S(1)}, bf16[4,4,144,512]{3,2,1,0:T(8,128)(2,1)}, u32[]{:S(2)}, u32[]{:S(2)}) collective-permute-start(bf16[4,4,144,512]{3,2,1,0:T(8,128)(2,1)S(1)} %bitcast.6), channel_id=1, source_target_pairs={{0,1},{1,0},{2,3},{3,2},{4,5},{5,4},{6,7},{7,6},{8,9},{9,8},{10,11... | collective-permute-start | bytes 7077896 | tf_op jit(solution)/shard_map/ppermute | solution.py:312
  93.2 0.8 copy-start.3
  98.7 3.8 %copy-start.2 = (bf16[16,96,128]{2,1,0:T(8,128)(2,1)S(1)}, bf16[16,96,128]{2,1,0:T(8,128)(2,1)}, u32[]{:S(2)}) copy-start(bf16[16,96,128]{2,1,0:T(8,128)(2,1)} %copy-done.1) | copy-start | bytes 1179652
  104.3 12.5 %collective-permute-start.7 = (bf16[576,128]{1,0:T(8,128)(2,1)S(1)}, bf16[576,128]{1,0:T(8,128)(2,1)S(1)}, u32[]{:S(2)}, u32[]{:S(2)}) collective-permute-start(bf16[576,128]{1,0:T(8,128)(2,1)S(1)} %get-tuple-element.26), channel_id=1, source_target_pairs={{0,128},{128,256},{256,384},{384,0},{1,129},{129,257},{257,385},{3... | collective-permute-start | bytes 442376 | tf_op jit(solution)/shard_map/ppermute | solution.py:343
  106.2 10.6 %collective-permute-start.8 = (bf16[576,128]{1,0:T(8,128)(2,1)S(1)}, bf16[576,128]{1,0:T(8,128)(2,1)S(1)}, u32[]{:S(2)}, u32[]{:S(2)}) collective-permute-start(bf16[576,128]{1,0:T(8,128)(2,1)S(1)} %get-tuple-element.27), channel_id=1, source_target_pairs={{0,256},{128,384},{256,0},{384,128},{1,257},{129,385},{257,1},{385... | collective-permute-start | bytes 442376 | tf_op jit(solution)/shard_map/ppermute | solution.py:343
  110.0 9.3 %collective-permute-start.9 = (bf16[576,128]{1,0:T(8,128)(2,1)S(1)}, bf16[576,128]{1,0:T(8,128)(2,1)S(1)}, u32[]{:S(2)}, u32[]{:S(2)}) collective-permute-start(bf16[576,128]{1,0:T(8,128)(2,1)S(1)} %get-tuple-element.28), channel_id=1, source_target_pairs={{0,384},{128,0},{256,128},{384,256},{1,385},{129,1},{257,129},{385... | collective-permute-start | bytes 442376 | tf_op jit(solution)/shard_map/ppermute | solution.py:343
  113.3 18.6 %copy-start = (bf16[32,128,256]{2,1,0:T(8,128)(2,1)S(1)}, bf16[32,128,256]{2,1,0:T(8,128)(2,1)}, u32[]{:S(2)}) copy-start(bf16[32,128,256]{2,1,0:T(8,128)(2,1)} %all-gather.3.cloned.1.call-done.far_docs.docs) | copy-start | bytes 6291460
Sparse Core Ops, SparseCore 0:
  29.7 77.1 all-gather.2

commit v11 on v9

--- a/solution.py
+++ b/solution.py
@@ -49,20 +49,16 @@
 
 
 def pack_kernel(*refs):
-    sources, use, (out, tagged), copies, flags, done = refs[:4], refs[4], refs[5:7], refs[7:11], refs[11], refs[12]
+    sources, out, copies, done = refs[:3], refs[3], refs[4:7], refs[7]
     moves = [
         pltpu.make_async_copy(src, dst, done.at[i])
         for i, (src, dst) in enumerate(zip(sources, copies))
     ]
     for move in moves:
         move.start()
-    flags[...] = jnp.zeros(flags.shape, jnp.int32)
-    flags[0:2, 0:PICKS] = use[...]
-    tagged[SEQ : SEQ + 16, :] = flags[...].astype(F32).astype(BF16)
     for move in moves:
         move.wait()
-    wq, wk, wv, tokens = copies
-    tagged[0:SEQ, :] = tokens[...]
+    wq, wk, wv = copies
     for part in range(NX):
         src = wk if part < 2 else wv
         at = HALF * (part % 2)
@@ -70,6 +66,13 @@
         for copy in range(4):
             out[part, copy, 0:64, :] = wq[:, part * HEAD : (part + 1) * HEAD]
             out[part, copy, 64:96, :] = packed
+
+
+def tag_kernel(tokens, use, out, flags):
+    flags[...] = jnp.zeros(flags.shape, jnp.int32)
+    flags[0:2, 0:PICKS] = use[...]
+    out[0:SEQ, :] = tokens[...]
+    out[SEQ : SEQ + 16, :] = flags[...].astype(F32).astype(BF16)
 
 
 def norm_kernel(mine, other, gain, out):
@@ -186,6 +189,20 @@
     return group, owner, parts
 
 
+def in_steps(units, unit, merge):
+    def steps(width, first):
+        def step(i, carry):
+            for result in [unit(units[first + width * i + j]) for j in range(1, width + 1)]:
+                merge(*result)
+            return carry
+
+        return step
+
+    eights = units[0] // 8
+    lax.fori_loop(0, eights, steps(8, 0), 0)
+    lax.fori_loop(0, (units[0] - 8 * eights + 3) // 4, steps(4, 8 * eights), 0)
+
+
 def weigh(scores, shift):
     return jnp.exp2((scores - shift) * RATE)
 
@@ -217,17 +234,15 @@
         ]
         return group, top, sums[0] + sums[1]
 
-    def pair(i, carry):
-        for group, top, part in [unit(units[4 * i + j]) for j in range(1, 5)]:
-            before = stats[pl.ds(group, 1), :]
-            new = jnp.maximum(before, top)
-            old = stats[pl.ds(group + 4, 1), :] * weigh(before, new)
-            stats[pl.ds(group, 1), :] = new
-            stats[pl.ds(group + 4, 1), :] = old + part * weigh(top, new)
-        return carry
+    def merge(group, top, part):
+        before = stats[pl.ds(group, 1), :]
+        new = jnp.maximum(before, top)
+        old = stats[pl.ds(group + 4, 1), :] * weigh(before, new)
+        stats[pl.ds(group, 1), :] = new
+        stats[pl.ds(group + 4, 1), :] = old + part * weigh(top, new)
 
     fetch.wait()
-    lax.fori_loop(0, (units[0] + 3) // 4, pair, 0)
+    in_steps(units, unit, merge)
     for dest in range(NX):
         send[dest] = stats[...]
 
@@ -259,12 +274,10 @@
         values = docs[pl.ds(owner * 2, 2), :, HEAD : 2 * HEAD].reshape(2 * SEQ, HEAD)
         return group, apply(values, jnp.concatenate(probs, axis=0))
 
-    def pair(i, carry):
-        for group, out in [unit(units[4 * i + j]) for j in range(1, 5)]:
-            send[pl.ds(group, 1)] = send[pl.ds(group, 1)] + out[None]
-        return carry
-
-    lax.fori_loop(0, (units[0] + 3) // 4, pair, 0)
+    def merge(group, out):
+        send[pl.ds(group, 1)] = send[pl.ds(group, 1)] + out[None]
+
+    in_steps(units, unit, merge)
 
 
 def finish_kernel(got, out):
@@ -283,15 +296,22 @@
     z_axes = ("zh", "zl")
     docs = lax.all_gather(doc_cache, z_axes, axis=0, tiled=True)
 
-    sources = (wq, wk, wv, tokens)
-    parts, tagged = call(
+    sources = (wq, wk, wv)
+    parts = call(
         pack_kernel,
-        [shape((4, 4, 96, HEAD), BF16), shape((SEQ + 16, 512), BF16)],
-        (*sources, block_use),
-        [ANY] * 4 + [VMEM],
-        out_specs=[VMEM] * 2,
-        scratch=[pltpu.VMEM(a.shape, BF16) for a in sources]
-        + [pltpu.VMEM((16, 512), jnp.int32), pltpu.SemaphoreType.DMA((4,))],
+        shape((4, 4, 96, HEAD), BF16),
+        sources,
+        [ANY] * 3,
+        scratch=[pltpu.VMEM(a.shape, BF16) for a in sources] + [pltpu.SemaphoreType.DMA((3,))],
+        limit=62,
+    )
+    tagged = call(
+        tag_kernel,
+        shape((SEQ + 16, 512), BF16),
+        (tokens, block_use),
+        [VMEM] * 2,
+        scratch=[pltpu.VMEM((16, 512), jnp.int32)],
+        flops=0,
         limit=62,
     )
     near = exchange(parts.reshape(16, 96, HEAD), ("x", "zh"))

time: 154 us -> 153 us (level)
  Pallas kernels: 16.6 us -> 20.8 us
  blocking collectives: 41.7 us -> 39.5 us
  waiting for transfers between devices: 26.2 us -> 24.5 us
    pallas_call x7 -> x8, Pallas kernels: 16.6 us -> 20.8 us  [call(): pl.pallas_call(kernel, out_shape=outs, in_specs=specs, out_specs=VMEM if...]
    all_to_all x2, blocking collectives: 27.8 us -> 25.8 us  [exchange(): return lax.all_to_all(array, axes, 0, 0, tiled=True)]
    all_gather x1, waiting for transfers between devices: 1.86 us -> 0.02 us  [shards(): docs = lax.all_gather(doc_cache, z_axes, axis=0, tiled=True)]
  transfers between devices with their start and end apart: 12 -> 12, of which waited for: 6 -> 6; matrix products, arithmetic and copies ran while one was open for 1% -> 1% of each run, Pallas kernels for 6% -> 7%
where the time goes in v11:
time: 153 us; the launch traced here: 152 us
  starting transfers between devices  52.2 us (34%)
  blocking collectives  39.5 us (26%)
  waiting for transfers between devices  24.5 us (16%)
  Pallas kernels  20.8 us (14%)
  between operations  13.6 us (9%)
  other arithmetic  1.73 us (1%)
    all_to_all x2, blocking collectives, exchange(): return lax.all_to_all(array, axes, 0, 0, tiled=True)  25.8 us
    pallas_call x8, Pallas kernels, call(): pl.pallas_call(kernel, out_shape=outs, in_specs=specs, out_specs=VMEM if...  20.8 us
    all_to_all x1, starting transfers between devices, exchange(): return lax.all_to_all(array, axes, 0, 0, tiled=True)  17.7 us
    all_gather x1, blocking collectives, shards(): by_y = lax.all_gather(tagged, 'y')  13.7 us
    ppermute x3, starting transfers between devices, from_x(): return lax.ppermute(array, 'x', [((i + step) % NX, i) for i in range(NX)])  10.7 us
    ppermute x2, starting transfers between devices, from_z(): lax.ppermute(array, z_axes, [((i + step) % NZ, i) for i in range(NZ)])  9.41 us
    ppermute x3, starting transfers between devices, shards(): lax.ppermute(sends[k], 'x', [(i, (i + k) % NX) for i in range(NX)])  9.07 us
    ppermute x3, waiting for transfers between devices, from_x(): return lax.ppermute(array, 'x', [((i + step) % NX, i) for i in range(NX)])  9.03 us
  transfers between devices with their start and end apart: 12, of which 6 were waited for; matrix products, arithmetic and copies ran while one was open for 1% of the time, Pallas kernels for 7%

profile of v11, /device:TPU:24, one launch (start us, length us, event | category | flops | bytes accessed | tf_op | source)
XLA Modules:
  0.0 152.5 jit_solution(2297044508134781127)
XLA Ops:
  8.2 17.7 %all-to-all-start = ((bf16[16,96,128]{2,1,0:T(8,128)(2,1)}), bf16[16,96,128]{2,1,0:T(8,128)(2,1)S(1)}, u32[]{:S(2)}, u32[]{:S(2)}) async-start(bf16[16,96,128]{2,1,0:T(8,128)(2,1)} %bitcast.14), calls=%async_computation | async-start | bytes 786432 | tf_op jit(solution)/shard_map/all_to_all | solution.py:291
  28.2 13.7 %all-gather = bf16[576,512]{1,0:T(8,128)(2,1)S(1)} all-gather(bf16[144,512]{1,0:T(8,128)(2,1)} %shard_map.91), channel_id=2, replica_groups=mesh['x'=4,'zh'=4,'zl'=4,'y'=4,'core'=2] {'y'}, dimensions={0}, use_global_device_ids=true | all-gather | bytes 737280 | tf_op jit(solution)/shard_map/all_gather | solution.py:325
  42.0 5.3 %collective-permute-start = (bf16[4,144,512]{2,1,0:T(8,128)(2,1)S(1)}, bf16[4,144,512]{2,1,0:T(8,128)(2,1)}, u32[]{:S(2)}, u32[]{:S(2)}) collective-permute-start(bf16[4,144,512]{2,1,0:T(8,128)(2,1)S(1)} %bitcast.10), channel_id=1, source_target_pairs={{128,0},{256,128},{384,256},{0,384},{129,1},{257,129},{385,257},{1... | collective-permute-start | bytes 1769480 | tf_op jit(solution)/shard_map/ppermute | solution.py:323
  47.2 2.8 %collective-permute-start.1 = (bf16[4,144,512]{2,1,0:T(8,128)(2,1)S(1)}, bf16[4,144,512]{2,1,0:T(8,128)(2,1)}, u32[]{:S(2)}, u32[]{:S(2)}) collective-permute-start(bf16[4,144,512]{2,1,0:T(8,128)(2,1)S(1)} %bitcast.11), channel_id=1, source_target_pairs={{256,0},{384,128},{0,256},{128,384},{257,1},{385,129},{1,257},{129... | collective-permute-start | bytes 1769480 | tf_op jit(solution)/shard_map/ppermute | solution.py:323
  50.0 2.7 %collective-permute-start.2 = (bf16[4,144,512]{2,1,0:T(8,128)(2,1)S(1)}, bf16[4,144,512]{2,1,0:T(8,128)(2,1)}, u32[]{:S(2)}, u32[]{:S(2)}) collective-permute-start(bf16[4,144,512]{2,1,0:T(8,128)(2,1)S(1)} %bitcast.12), channel_id=1, source_target_pairs={{384,0},{0,128},{128,256},{256,384},{385,1},{1,129},{129,257},{257... | collective-permute-start | bytes 1769480 | tf_op jit(solution)/shard_map/ppermute | solution.py:323
  52.7 6.0 %collective-permute-start.3 = (bf16[16,96,128]{2,1,0:T(8,128)(2,1)S(1)}, bf16[16,96,128]{2,1,0:T(8,128)(2,1)S(1)}, u32[]{:S(2)}, u32[]{:S(2)}) collective-permute-start(bf16[16,96,128]{2,1,0:T(8,128)(2,1)S(1)} %all-to-all-done.near), channel_id=1, source_target_pairs={{8,0},{16,8},{24,16},{32,24},{40,32},{48,40},{56,48},{64,56},{72,6... | collective-permute-start | bytes 1179656 | tf_op jit(solution)/shard_map/ppermute | solution.py:320
  58.7 3.4 %collective-permute-start.4 = (bf16[16,96,128]{2,1,0:T(8,128)(2,1)S(1)}, bf16[16,96,128]{2,1,0:T(8,128)(2,1)S(1)}, u32[]{:S(2)}, u32[]{:S(2)}) collective-permute-start(bf16[16,96,128]{2,1,0:T(8,128)(2,1)S(1)} %all-to-all-done.near), channel_id=1, source_target_pairs={{16,0},{120,8},{32,16},{8,24},{48,32},{24,40},{64,48},{40,56},{80,... | collective-permute-start | bytes 1179656 | tf_op jit(solution)/shard_map/ppermute | solution.py:330
  62.1 7.1 %collective-permute-done = bf16[4,144,512]{2,1,0:T(8,128)(2,1)} collective-permute-done((bf16[4,144,512]{2,1,0:T(8,128)(2,1)S(1)}, bf16[4,144,512]{2,1,0:T(8,128)(2,1)}, u32[]{:S(2)}, u32[]{:S(2)}) %collective-permute-start) | collective-permute-done | bytes 589856 | tf_op jit(solution)/shard_map/ppermute | solution.py:323
  69.2 3.5 %collective-permute-start.5 = (bf16[16,96,128]{2,1,0:T(8,128)(2,1)S(1)}, bf16[16,96,128]{2,1,0:T(8,128)(2,1)S(1)}, u32[]{:S(2)}, u32[]{:S(2)}) collective-permute-start(bf16[16,96,128]{2,1,0:T(8,128)(2,1)S(1)} %all-to-all-done.near), channel_id=1, source_target_pairs={{120,0},{0,8},{8,16},{16,24},{24,32},{32,40},{40,48},{48,56},{56,6... | collective-permute-start | bytes 1179656 | tf_op jit(solution)/shard_map/ppermute | solution.py:320
  72.7 2.0 %collective-permute-done.2 = bf16[4,144,512]{2,1,0:T(8,128)(2,1)} collective-permute-done((bf16[4,144,512]{2,1,0:T(8,128)(2,1)S(1)}, bf16[4,144,512]{2,1,0:T(8,128)(2,1)}, u32[]{:S(2)}, u32[]{:S(2)}) %collective-permute-start.2) | collective-permute-done | bytes 589856 | tf_op jit(solution)/shard_map/ppermute | solution.py:323
  76.4 6.0 %collective-permute-done.4.far = bf16[16,96,128]{2,1,0:T(8,128)(2,1)S(1)} collective-permute-done((bf16[16,96,128]{2,1,0:T(8,128)(2,1)S(1)}, bf16[16,96,128]{2,1,0:T(8,128)(2,1)S(1)}, u32[]{:S(2)}, u32[]{:S(2)}) %collective-permute-start.4) | collective-permute-done | bytes 393248 | tf_op jit(solution)/shard_map/ppermute | solution.py:330
  82.4 3.7 %collective-permute-done.5.behind = bf16[16,96,128]{2,1,0:T(8,128)(2,1)S(1)} collective-permute-done((bf16[16,96,128]{2,1,0:T(8,128)(2,1)S(1)}, bf16[16,96,128]{2,1,0:T(8,128)(2,1)S(1)}, u32[]{:S(2)}, u32[]{:S(2)}) %collective-permute-start.5) | collective-permute-done | bytes 393248 | tf_op jit(solution)/shard_map/ppermute | solution.py:320
  86.0 1.9 %collective-permute-start.6 = (bf16[4,4,144,512]{3,2,1,0:T(8,128)(2,1)S(1)}, bf16[4,4,144,512]{3,2,1,0:T(8,128)(2,1)S(1)}, u32[]{:S(2)}, u32[]{:S(2)}) collective-permute-start(bf16[4,4,144,512]{3,2,1,0:T(8,128)(2,1)S(1)} %bitcast.6), channel_id=1, source_target_pairs={{0,1},{1,0},{2,3},{3,2},{4,5},{5,4},{6,7},{7,6},{8,9},{9,8},{10,11... | collective-permute-start | bytes 7077896 | tf_op jit(solution)/shard_map/ppermute | solution.py:332
  88.0 4.5 %collective-permute-done.6.other = bf16[4,4,144,512]{3,2,1,0:T(8,128)(2,1)S(1)} collective-permute-done((bf16[4,4,144,512]{3,2,1,0:T(8,128)(2,1)S(1)}, bf16[4,4,144,512]{3,2,1,0:T(8,128)(2,1)S(1)}, u32[]{:S(2)}, u32[]{:S(2)}) %collective-permute-start.6) | collective-permute-done | bytes 2359328 | tf_op jit(solution)/shard_map/ppermute | solution.py:332
  92.4 2.0 %shard_map.94.normed = bf16[8,512,512]{2,1,0:T(8,128)(2,1)S(1)} custom-call(bf16[4,4,144,512]{3,2,1,0:T(8,128)(2,1)S(1)} %bitcast.7, bf16[4,4,144,512]{3,2,1,0:T(8,128)(2,1)S(1)} %collective-permute-done.6.other, f32[8,1,512]{2,1,0:T(1,128)S(1)} %bitcast.9), custom_call_target="tpu_custom_call" | custom-call | flops 16777216 | bytes 8388608 | tf_op jit(solution)/shard_map/pallas_call | solution.py:32
  94.5 1.7 %shard_map.95 = (bf16[576,128]{1,0:T(8,128)(2,1)S(1)}, bf16[576,128]{1,0:T(8,128)(2,1)S(1)}, bf16[576,128]{1,0:T(8,128)(2,1)S(1)}, bf16[576,128]{1,0:T(8,128)(2,1)S(1)}) custom-call(bf16[8,512,512]{2,1,0:T(8,128)(2,1)S(1)} %shard_map.94.normed, bf16[16,96,128]{2,1,0:T(8,128)(2,1)S(1)} %all-to-all-done.near, ...), custom_call_target="tpu_custom_call" | custom-call | flops 1073741824 | bytes 8388608 | tf_op jit(solution)/shard_map/pallas_call | solution.py:32
  96.3 1.9 %collective-permute-start.7 = (bf16[576,128]{1,0:T(8,128)(2,1)S(1)}, bf16[576,128]{1,0:T(8,128)(2,1)S(1)}, u32[]{:S(2)}, u32[]{:S(2)}) collective-permute-start(bf16[576,128]{1,0:T(8,128)(2,1)S(1)} %get-tuple-element.18), channel_id=1, source_target_pairs={{0,128},{128,256},{256,384},{384,0},{1,129},{129,257},{257,385},{3... | collective-permute-start | bytes 442376 | tf_op jit(solution)/shard_map/ppermute | solution.py:363
  98.2 4.6 %collective-permute-start.8 = (bf16[576,128]{1,0:T(8,128)(2,1)S(1)}, bf16[576,128]{1,0:T(8,128)(2,1)S(1)}, u32[]{:S(2)}, u32[]{:S(2)}) collective-permute-start(bf16[576,128]{1,0:T(8,128)(2,1)S(1)} %get-tuple-element.19), channel_id=1, source_target_pairs={{0,256},{128,384},{256,0},{384,128},{1,257},{129,385},{257,1},{385... | collective-permute-start | bytes 442376 | tf_op jit(solution)/shard_map/ppermute | solution.py:363
  102.8 2.5 %collective-permute-start.9 = (bf16[576,128]{1,0:T(8,128)(2,1)S(1)}, bf16[576,128]{1,0:T(8,128)(2,1)S(1)}, u32[]{:S(2)}, u32[]{:S(2)}) collective-permute-start(bf16[576,128]{1,0:T(8,128)(2,1)S(1)} %get-tuple-element.20), channel_id=1, source_target_pairs={{0,384},{128,0},{256,128},{384,256},{1,385},{129,1},{257,129},{385... | collective-permute-start | bytes 442376 | tf_op jit(solution)/shard_map/ppermute | solution.py:363
  105.5 4.8 %shard_map.93.units = s32[128]{0:T(128)S(1)} custom-call(s32[64,16]{1,0:T(8,128)S(1)} %copy.11.lists, s32[128]{0:T(128)S(1)} %copy-done.1, s32[8,16]{1,0:T(8,128)S(1)} %convert.2.use), custom_call_target="tpu_custom_call" | custom-call | tf_op jit(solution)/shard_map/pallas_call | solution.py:32
  110.9 3.9 %shard_map.96 = f32[4,8,512]{2,1,0:T(8,128)S(1)} custom-call(s32[128]{0:T(128)S(1)} %shard_map.93.units, bf16[576,128]{1,0:T(8,128)(2,1)S(1)} %get-tuple-element.17.own, bf16[576,128]{1,0:T(8,128)(2,1)S(1)} %collective-permute-done.7.one, bf16[576,128]{1,0:T(8,128)(2,1)S(1)} %collective-permute-done.8.two, ...), custom_call_target="tpu_custom_call" | custom-call | tf_op jit(solution)/shard_map/pallas_call | solution.py:32
  114.8 9.4 %all_to_all.15.all_stats = f32[4,8,512]{2,1,0:T(8,128)S(1)} all-to-all(f32[4,8,512]{2,1,0:T(8,128)S(1)} %shard_map.96), channel_id=1, replica_groups=mesh['x'=4,'zh'=4,'zl'=4,'y'=4,'core'=2] {'x'}, dimensions={0} | all-to-all | bytes 131072 | tf_op jit(solution)/shard_map/all_to_all | solution.py:291
  124.2 4.3 %shard_map.97 = f32[4,128,512]{2,1,0:T(8,128)S(1)} custom-call(s32[128]{0:T(128)S(1)} %shard_map.93.units, bf16[576,128]{1,0:T(8,128)(2,1)S(1)} %get-tuple-element.17.own, bf16[576,128]{1,0:T(8,128)(2,1)S(1)} %collective-permute-done.7.one, bf16[576,128]{1,0:T(8,128)(2,1)S(1)} %collective-permute-done.8.two, ...), custom_call_target="tpu_custom_call" | custom-call | tf_op jit(solution)/shard_map/pallas_call | solution.py:32
  128.5 16.4 %all_to_all.16.got = f32[4,128,512]{2,1,0:T(8,128)S(1)} all-to-all(f32[4,128,512]{2,1,0:T(8,128)S(1)} %shard_map.97), channel_id=1, replica_groups=mesh['x'=4,'zh'=4,'zl'=4,'y'=4,'core'=2] {'x'}, dimensions={0} | all-to-all | bytes 2097152 | tf_op jit(solution)/shard_map/all_to_all | solution.py:291
  (25 shorter events, 7.2 us)
Async XLA Ops:
  8.2 44.4 %all-to-all-start = ((bf16[16,96,128]{2,1,0:T(8,128)(2,1)}), bf16[16,96,128]{2,1,0:T(8,128)(2,1)S(1)}, u32[]{:S(2)}, u32[]{:S(2)}) async-start(bf16[16,96,128]{2,1,0:T(8,128)(2,1)} %bitcast.14), calls=%async_computation | async-start | bytes 786432 | tf_op jit(solution)/shard_map/all_to_all | solution.py:291
  25.9 84.4 %all-gather.3.cloned.1.call-start = ((), (), s32[]{:S(2)}) async-start(), calls=%async_computation.3 | async-start | bytes 2228224 | tf_op jit(solution)/shard_map/all_gather | solution.py:297
  42.0 46.0 %copy-start.2 = (bf16[4096]{0:T(1024)(128)(2,1)S(1)}, bf16[4096]{0:T(1024)(128)(2,1)}, u32[]{:S(2)}) copy-start(bf16[4096]{0:T(1024)(128)(2,1)} %param.10) | copy-start | bytes 24580
  42.0 27.2 %collective-permute-start = (bf16[4,144,512]{2,1,0:T(8,128)(2,1)S(1)}, bf16[4,144,512]{2,1,0:T(8,128)(2,1)}, u32[]{:S(2)}, u32[]{:S(2)}) collective-permute-start(bf16[4,144,512]{2,1,0:T(8,128)(2,1)S(1)} %bitcast.10), channel_id=1, source_target_pairs={{128,0},{256,128},{384,256},{0,384},{129,1},{257,129},{385,257},{1... | collective-permute-start | bytes 1769480 | tf_op jit(solution)/shard_map/ppermute | solution.py:323
  47.2 25.4 %collective-permute-start.1 = (bf16[4,144,512]{2,1,0:T(8,128)(2,1)S(1)}, bf16[4,144,512]{2,1,0:T(8,128)(2,1)}, u32[]{:S(2)}, u32[]{:S(2)}) collective-permute-start(bf16[4,144,512]{2,1,0:T(8,128)(2,1)S(1)} %bitcast.11), channel_id=1, source_target_pairs={{256,0},{384,128},{0,256},{128,384},{257,1},{385,129},{1,257},{129... | collective-permute-start | bytes 1769480 | tf_op jit(solution)/shard_map/ppermute | solution.py:323
  50.0 24.6 %collective-permute-start.2 = (bf16[4,144,512]{2,1,0:T(8,128)(2,1)S(1)}, bf16[4,144,512]{2,1,0:T(8,128)(2,1)}, u32[]{:S(2)}, u32[]{:S(2)}) collective-permute-start(bf16[4,144,512]{2,1,0:T(8,128)(2,1)S(1)} %bitcast.12), channel_id=1, source_target_pairs={{384,0},{0,128},{128,256},{256,384},{385,1},{1,129},{129,257},{257... | collective-permute-start | bytes 1769480 | tf_op jit(solution)/shard_map/ppermute | solution.py:323
  52.7 23.6 %collective-permute-start.3 = (bf16[16,96,128]{2,1,0:T(8,128)(2,1)S(1)}, bf16[16,96,128]{2,1,0:T(8,128)(2,1)S(1)}, u32[]{:S(2)}, u32[]{:S(2)}) collective-permute-start(bf16[16,96,128]{2,1,0:T(8,128)(2,1)S(1)} %all-to-all-done.near), channel_id=1, source_target_pairs={{8,0},{16,8},{24,16},{32,24},{40,32},{48,40},{56,48},{64,56},{72,6... | collective-permute-start | bytes 1179656 | tf_op jit(solution)/shard_map/ppermute | solution.py:320
  58.7 23.7 %collective-permute-start.4 = (bf16[16,96,128]{2,1,0:T(8,128)(2,1)S(1)}, bf16[16,96,128]{2,1,0:T(8,128)(2,1)S(1)}, u32[]{:S(2)}, u32[]{:S(2)}) collective-permute-start(bf16[16,96,128]{2,1,0:T(8,128)(2,1)S(1)} %all-to-all-done.near), channel_id=1, source_target_pairs={{16,0},{120,8},{32,16},{8,24},{48,32},{24,40},{64,48},{40,56},{80,... | collective-permute-start | bytes 1179656 | tf_op jit(solution)/shard_map/ppermute | solution.py:330
  69.2 16.8 %collective-permute-start.5 = (bf16[16,96,128]{2,1,0:T(8,128)(2,1)S(1)}, bf16[16,96,128]{2,1,0:T(8,128)(2,1)S(1)}, u32[]{:S(2)}, u32[]{:S(2)}) collective-permute-start(bf16[16,96,128]{2,1,0:T(8,128)(2,1)S(1)} %all-to-all-done.near), channel_id=1, source_target_pairs={{120,0},{0,8},{8,16},{16,24},{24,32},{32,40},{40,48},{48,56},{56,6... | collective-permute-start | bytes 1179656 | tf_op jit(solution)/shard_map/ppermute | solution.py:320
  86.0 6.4 %collective-permute-start.6 = (bf16[4,4,144,512]{3,2,1,0:T(8,128)(2,1)S(1)}, bf16[4,4,144,512]{3,2,1,0:T(8,128)(2,1)S(1)}, u32[]{:S(2)}, u32[]{:S(2)}) collective-permute-start(bf16[4,4,144,512]{3,2,1,0:T(8,128)(2,1)S(1)} %bitcast.6), channel_id=1, source_target_pairs={{0,1},{1,0},{2,3},{3,2},{4,5},{5,4},{6,7},{7,6},{8,9},{9,8},{10,11... | collective-permute-start | bytes 7077896 | tf_op jit(solution)/shard_map/ppermute | solution.py:332
  94.5 10.9 %copy-start.3 = (s32[64,16]{0,1:T(8,128)S(1)}, s32[64,16]{0,1:T(8,128)}, u32[]{:S(2)}) copy-start(s32[64,16]{0,1:T(8,128)} %param.15) | copy-start | bytes 12292
  94.5 11.0 %copy-start.1 = (s32[128]{0:T(128)S(1)}, s32[128]{0:T(128)}, u32[]{:S(2)}) copy-start(s32[128]{0:T(128)} %place.1) | copy-start | bytes 1540
  96.3 14.0 %collective-permute-start.7 = (bf16[576,128]{1,0:T(8,128)(2,1)S(1)}, bf16[576,128]{1,0:T(8,128)(2,1)S(1)}, u32[]{:S(2)}, u32[]{:S(2)}) collective-permute-start(bf16[576,128]{1,0:T(8,128)(2,1)S(1)} %get-tuple-element.18), channel_id=1, source_target_pairs={{0,128},{128,256},{256,384},{384,0},{1,129},{129,257},{257,385},{3... | collective-permute-start | bytes 442376 | tf_op jit(solution)/shard_map/ppermute | solution.py:363
  98.2 12.1 %collective-permute-start.8 = (bf16[576,128]{1,0:T(8,128)(2,1)S(1)}, bf16[576,128]{1,0:T(8,128)(2,1)S(1)}, u32[]{:S(2)}, u32[]{:S(2)}) collective-permute-start(bf16[576,128]{1,0:T(8,128)(2,1)S(1)} %get-tuple-element.19), channel_id=1, source_target_pairs={{0,256},{128,384},{256,0},{384,128},{1,257},{129,385},{257,1},{385... | collective-permute-start | bytes 442376 | tf_op jit(solution)/shard_map/ppermute | solution.py:363
  102.8 8.1 %collective-permute-start.9 = (bf16[576,128]{1,0:T(8,128)(2,1)S(1)}, bf16[576,128]{1,0:T(8,128)(2,1)S(1)}, u32[]{:S(2)}, u32[]{:S(2)}) collective-permute-start(bf16[576,128]{1,0:T(8,128)(2,1)S(1)} %get-tuple-element.20), channel_id=1, source_target_pairs={{0,384},{128,0},{256,128},{384,256},{1,385},{129,1},{257,129},{385... | collective-permute-start | bytes 442376 | tf_op jit(solution)/shard_map/ppermute | solution.py:363
  110.3 13.9 %copy-start = (bf16[32,128,256]{2,1,0:T(8,128)(2,1)S(1)}, bf16[32,128,256]{2,1,0:T(8,128)(2,1)}, u32[]{:S(2)}) copy-start(bf16[32,128,256]{2,1,0:T(8,128)(2,1)} %all-gather.3.cloned.1.call-done.far_docs.docs) | copy-start | bytes 6291460
Sparse Core Ops, SparseCore 0:
  28.8 81.2 all-gather.2

commit v12 on v11

--- a/solution.py
+++ b/solution.py
@@ -328,7 +328,16 @@
     ahead = from_z(near, 1)
     behind = from_z(near, -1)
     far = lax.ppermute(near, z_axes, [((i + 2 - 4 * (i % 2)) % NZ, i) for i in range(NZ)])
-    mine, ahead, far, behind = lax.optimization_barrier((mine, ahead, far, behind))
+    use = mine[:, 0, SEQ : SEQ + 2, 0:PICKS].astype(jnp.int32).reshape(8, PICKS)
+    units = call(
+        route_kernel,
+        shape((UNITS,), jnp.int32),
+        (doc_lists, doc_place, use),
+        [SMEM] * 3,
+        out_specs=SMEM,
+        scratch=[pltpu.SMEM((NX * NZ,), jnp.int32)],
+    )
+    mine, units, ahead, far, behind = lax.optimization_barrier((mine, units, ahead, far, behind))
     other = lax.ppermute(mine, "core", [(0, 1), (1, 0)])
     gain = norm_gain.astype(F32).reshape(8, 1, 512)
     normed = call(
@@ -339,16 +348,6 @@
         flops=ROWS * 4096 * 8,
         moved=8 << 20,
     )
-    use = mine[:, 0, SEQ : SEQ + 2, 0:PICKS].astype(jnp.int32).reshape(8, PICKS)
-    units = call(
-        route_kernel,
-        shape((UNITS,), jnp.int32),
-        (doc_lists, doc_place, use),
-        [SMEM] * 3,
-        out_specs=SMEM,
-        scratch=[pltpu.SMEM((NX * NZ,), jnp.int32)],
-    )
-
     sends = call(
         project_kernel,
         [shape((ROWS + HALF, HEAD), BF16)] * NX,
@@ -359,10 +358,10 @@
         flops=2 * ROWS * 4096 * 256,
         moved=8 << 20,
     )
-    got = [
-        lax.ppermute(sends[k], "x", [(i, (i + k) % NX) for i in range(NX)]) if k else sends[0]
-        for k in range(NX)
-    ]
+    got = {
+        k: lax.ppermute(sends[k], "x", [(i, (i + k) % NX) for i in range(NX)]) for k in (2, 1, 3)
+    }
+    got = [sends[0], got[1], got[2], got[3]]
     scratch = [
         pltpu.VMEM((8, COLS), F32),
         pltpu.VMEM((2 * NZ, SEQ, HEAD), BF16),

time: 153 us -> 155 us (1.013)
  blocking collectives: 39.5 us -> 42.4 us
    all_gather x1, waiting for transfers between devices: 0.02 us -> 5.01 us  [shards(): docs = lax.all_gather(doc_cache, z_axes, axis=0, tiled=True)]
    ppermute x1, waiting for transfers between devices: 6 us -> 1.52 us  [shards(): lax.ppermute(near, z_axes, [((i + 2 - 4 * (i % 2)) % NZ, i) for i in rang...]
    all_to_all x2, blocking collectives: 25.8 us -> 28.7 us  [exchange(): return lax.all_to_all(array, axes, 0, 0, tiled=True)]
  transfers between devices with their start and end apart: 12 -> 12, of which waited for: 6 -> 7; matrix products, arithmetic and copies ran while one was open for 1% -> 1% of each run, Pallas kernels for 7% -> 7%
where the time goes in v12:
time: 155 us; the launch traced here: 154 us
  starting transfers between devices  52.1 us (34%)
  blocking collectives  42.4 us (27%)
  waiting for transfers between devices  25.3 us (16%)
  Pallas kernels  19.3 us (12%)
  between operations  13.6 us (9%)
    all_to_all x2, blocking collectives, exchange(): return lax.all_to_all(array, axes, 0, 0, tiled=True)  28.7 us
    pallas_call x8, Pallas kernels, call(): pl.pallas_call(kernel, out_shape=outs, in_specs=specs, out_specs=VMEM if...  19.3 us
    all_to_all x1, starting transfers between devices, exchange(): return lax.all_to_all(array, axes, 0, 0, tiled=True)  17.7 us
    all_gather x1, blocking collectives, shards(): by_y = lax.all_gather(tagged, 'y')  13.7 us
    ppermute x3, starting transfers between devices, from_x(): return lax.ppermute(array, 'x', [((i + step) % NX, i) for i in range(NX)])  10.6 us
    ppermute x2, starting transfers between devices, from_z(): lax.ppermute(array, z_axes, [((i + step) % NZ, i) for i in range(NZ)])  9.51 us
    ppermute x3, starting transfers between devices, shards(): lax.ppermute(sends[k], 'x', [(i, (i + k) % NX) for i in range(NX)])  8.97 us
    ppermute x3, waiting for transfers between devices, from_x(): return lax.ppermute(array, 'x', [((i + step) % NX, i) for i in range(NX)])  8.83 us
  transfers between devices with their start and end apart: 12, of which 7 were waited for; matrix products, arithmetic and copies ran while one was open for 1% of the time, Pallas kernels for 7%

profile of v12, /device:TPU:24, one launch (start us, length us, event | category | flops | bytes accessed | tf_op | source)
XLA Modules:
  0.0 154.2 jit_solution(13258742640541130746)
XLA Ops:
  8.3 17.7 %all-to-all-start = ((bf16[16,96,128]{2,1,0:T(8,128)(2,1)}), bf16[16,96,128]{2,1,0:T(8,128)(2,1)S(1)}, u32[]{:S(2)}, u32[]{:S(2)}) async-start(bf16[16,96,128]{2,1,0:T(8,128)(2,1)} %bitcast.14), calls=%async_computation | async-start | bytes 786432 | tf_op jit(solution)/shard_map/all_to_all | solution.py:291
  28.3 13.7 %all-gather = bf16[576,512]{1,0:T(8,128)(2,1)S(1)} all-gather(bf16[144,512]{1,0:T(8,128)(2,1)} %shard_map.91), channel_id=2, replica_groups=mesh['x'=4,'zh'=4,'zl'=4,'y'=4,'core'=2] {'y'}, dimensions={0}, use_global_device_ids=true | all-gather | bytes 737280 | tf_op jit(solution)/shard_map/all_gather | solution.py:325
  42.0 5.1 %collective-permute-start = (bf16[4,144,512]{2,1,0:T(8,128)(2,1)S(1)}, bf16[4,144,512]{2,1,0:T(8,128)(2,1)S(1)}, u32[]{:S(2)}, u32[]{:S(2)}) collective-permute-start(bf16[4,144,512]{2,1,0:T(8,128)(2,1)S(1)} %bitcast.10), channel_id=1, source_target_pairs={{128,0},{256,128},{384,256},{0,384},{129,1},{257,129},{385,257},{1... | collective-permute-start | bytes 1769480 | tf_op jit(solution)/shard_map/ppermute | solution.py:323
  47.1 2.8 %collective-permute-start.1 = (bf16[4,144,512]{2,1,0:T(8,128)(2,1)S(1)}, bf16[4,144,512]{2,1,0:T(8,128)(2,1)S(1)}, u32[]{:S(2)}, u32[]{:S(2)}) collective-permute-start(bf16[4,144,512]{2,1,0:T(8,128)(2,1)S(1)} %bitcast.11), channel_id=1, source_target_pairs={{256,0},{384,128},{0,256},{128,384},{257,1},{385,129},{1,257},{129... | collective-permute-start | bytes 1769480 | tf_op jit(solution)/shard_map/ppermute | solution.py:323
  49.9 2.7 %collective-permute-start.2 = (bf16[4,144,512]{2,1,0:T(8,128)(2,1)S(1)}, bf16[4,144,512]{2,1,0:T(8,128)(2,1)}, u32[]{:S(2)}, u32[]{:S(2)}) collective-permute-start(bf16[4,144,512]{2,1,0:T(8,128)(2,1)S(1)} %bitcast.12), channel_id=1, source_target_pairs={{384,0},{0,128},{128,256},{256,384},{385,1},{1,129},{129,257},{257... | collective-permute-start | bytes 1769480 | tf_op jit(solution)/shard_map/ppermute | solution.py:323
  52.6 6.0 %collective-permute-start.3 = (bf16[16,96,128]{2,1,0:T(8,128)(2,1)S(1)}, bf16[16,96,128]{2,1,0:T(8,128)(2,1)S(1)}, u32[]{:S(2)}, u32[]{:S(2)}) collective-permute-start(bf16[16,96,128]{2,1,0:T(8,128)(2,1)S(1)} %all-to-all-done.near), channel_id=1, source_target_pairs={{8,0},{16,8},{24,16},{32,24},{40,32},{48,40},{56,48},{64,56},{72,6... | collective-permute-start | bytes 1179656 | tf_op jit(solution)/shard_map/ppermute | solution.py:320
  58.6 3.4 %collective-permute-start.4 = (bf16[16,96,128]{2,1,0:T(8,128)(2,1)S(1)}, bf16[16,96,128]{2,1,0:T(8,128)(2,1)S(1)}, u32[]{:S(2)}, u32[]{:S(2)}) collective-permute-start(bf16[16,96,128]{2,1,0:T(8,128)(2,1)S(1)} %all-to-all-done.near), channel_id=1, source_target_pairs={{16,0},{120,8},{32,16},{8,24},{48,32},{24,40},{64,48},{40,56},{80,... | collective-permute-start | bytes 1179656 | tf_op jit(solution)/shard_map/ppermute | solution.py:330
  62.0 7.1 %collective-permute-done = bf16[4,144,512]{2,1,0:T(8,128)(2,1)S(1)} collective-permute-done((bf16[4,144,512]{2,1,0:T(8,128)(2,1)S(1)}, bf16[4,144,512]{2,1,0:T(8,128)(2,1)S(1)}, u32[]{:S(2)}, u32[]{:S(2)}) %collective-permute-start) | collective-permute-done | bytes 589856 | tf_op jit(solution)/shard_map/ppermute | solution.py:323
  69.1 3.6 %collective-permute-start.5 = (bf16[16,96,128]{2,1,0:T(8,128)(2,1)S(1)}, bf16[16,96,128]{2,1,0:T(8,128)(2,1)S(1)}, u32[]{:S(2)}, u32[]{:S(2)}) collective-permute-start(bf16[16,96,128]{2,1,0:T(8,128)(2,1)S(1)} %all-to-all-done.near), channel_id=1, source_target_pairs={{120,0},{0,8},{8,16},{16,24},{24,32},{32,40},{40,48},{48,56},{56,6... | collective-permute-start | bytes 1179656 | tf_op jit(solution)/shard_map/ppermute | solution.py:320
  72.8 1.7 %collective-permute-done.2 = bf16[4,144,512]{2,1,0:T(8,128)(2,1)} collective-permute-done((bf16[4,144,512]{2,1,0:T(8,128)(2,1)S(1)}, bf16[4,144,512]{2,1,0:T(8,128)(2,1)}, u32[]{:S(2)}, u32[]{:S(2)}) %collective-permute-start.2) | collective-permute-done | bytes 589856 | tf_op jit(solution)/shard_map/ppermute | solution.py:323
  75.9 4.8 %shard_map.92.units = s32[128]{0:T(128)S(1)} custom-call(s32[64,16]{1,0:T(8,128)S(1)} %copy.11.lists, s32[128]{0:T(128)S(1)} %copy-done.1, s32[8,16]{1,0:T(8,128)S(1)} %convert.2.use), custom_call_target="tpu_custom_call" | custom-call | tf_op jit(solution)/shard_map/pallas_call | solution.py:32
  82.2 4.1 %collective-permute-done.5.behind = bf16[16,96,128]{2,1,0:T(8,128)(2,1)S(1)} collective-permute-done((bf16[16,96,128]{2,1,0:T(8,128)(2,1)S(1)}, bf16[16,96,128]{2,1,0:T(8,128)(2,1)S(1)}, u32[]{:S(2)}, u32[]{:S(2)}) %collective-permute-start.5) | collective-permute-done | bytes 393248 | tf_op jit(solution)/shard_map/ppermute | solution.py:320
  86.3 1.9 %collective-permute-start.6 = (bf16[4,4,144,512]{3,2,1,0:T(8,128)(2,1)S(1)}, bf16[4,4,144,512]{3,2,1,0:T(8,128)(2,1)S(1)}, u32[]{:S(2)}, u32[]{:S(2)}) collective-permute-start(bf16[4,4,144,512]{3,2,1,0:T(8,128)(2,1)S(1)} %bitcast.7), channel_id=1, source_target_pairs={{0,1},{1,0},{2,3},{3,2},{4,5},{5,4},{6,7},{7,6},{8,9},{9,8},{10,11... | collective-permute-start | bytes 7077896 | tf_op jit(solution)/shard_map/ppermute | solution.py:341
  88.3 4.5 %collective-permute-done.6.other = bf16[4,4,144,512]{3,2,1,0:T(8,128)(2,1)S(1)} collective-permute-done((bf16[4,4,144,512]{3,2,1,0:T(8,128)(2,1)S(1)}, bf16[4,4,144,512]{3,2,1,0:T(8,128)(2,1)S(1)}, u32[]{:S(2)}, u32[]{:S(2)}) %collective-permute-start.6) | collective-permute-done | bytes 2359328 | tf_op jit(solution)/shard_map/ppermute | solution.py:341
  92.8 2.1 %shard_map.94.normed = bf16[8,512,512]{2,1,0:T(8,128)(2,1)S(1)} custom-call(bf16[4,4,144,512]{3,2,1,0:T(8,128)(2,1)S(1)} %bitcast.8, bf16[4,4,144,512]{3,2,1,0:T(8,128)(2,1)S(1)} %collective-permute-done.6.other, f32[8,1,512]{2,1,0:T(1,128)S(1)} %bitcast.9), custom_call_target="tpu_custom_call" | custom-call | flops 16777216 | bytes 8388608 | tf_op jit(solution)/shard_map/pallas_call | solution.py:32
  94.9 1.7 %shard_map.95 = (bf16[576,128]{1,0:T(8,128)(2,1)S(1)}, bf16[576,128]{1,0:T(8,128)(2,1)S(1)}, bf16[576,128]{1,0:T(8,128)(2,1)S(1)}, bf16[576,128]{1,0:T(8,128)(2,1)S(1)}) custom-call(bf16[8,512,512]{2,1,0:T(8,128)(2,1)S(1)} %shard_map.94.normed, bf16[16,96,128]{2,1,0:T(8,128)(2,1)S(1)} %all-to-all-done.near, ...), custom_call_target="tpu_custom_call" | custom-call | flops 1073741824 | bytes 8388608 | tf_op jit(solution)/shard_map/pallas_call | solution.py:32
  96.6 1.9 %collective-permute-start.7 = (bf16[576,128]{1,0:T(8,128)(2,1)S(1)}, bf16[576,128]{1,0:T(8,128)(2,1)S(1)}, u32[]{:S(2)}, u32[]{:S(2)}) collective-permute-start(bf16[576,128]{1,0:T(8,128)(2,1)S(1)} %get-tuple-element.20), channel_id=1, source_target_pairs={{0,128},{128,256},{256,384},{384,0},{1,129},{129,257},{257,385},{3... | collective-permute-start | bytes 442376 | tf_op jit(solution)/shard_map/ppermute | solution.py:362
  98.5 4.0 %collective-permute-start.8 = (bf16[576,128]{1,0:T(8,128)(2,1)S(1)}, bf16[576,128]{1,0:T(8,128)(2,1)S(1)}, u32[]{:S(2)}, u32[]{:S(2)}) collective-permute-start(bf16[576,128]{1,0:T(8,128)(2,1)S(1)} %get-tuple-element.21), channel_id=1, source_target_pairs={{0,256},{128,384},{256,0},{384,128},{1,257},{129,385},{257,1},{385... | collective-permute-start | bytes 442376 | tf_op jit(solution)/shard_map/ppermute | solution.py:362
  102.5 3.1 %collective-permute-start.9 = (bf16[576,128]{1,0:T(8,128)(2,1)S(1)}, bf16[576,128]{1,0:T(8,128)(2,1)S(1)}, u32[]{:S(2)}, u32[]{:S(2)}) collective-permute-start(bf16[576,128]{1,0:T(8,128)(2,1)S(1)} %get-tuple-element.22), channel_id=1, source_target_pairs={{0,384},{128,0},{256,128},{384,256},{1,385},{129,1},{257,129},{385... | collective-permute-start | bytes 442376 | tf_op jit(solution)/shard_map/ppermute | solution.py:362
  105.6 5.0 %all-gather.3.cloned.1.call-done.far_docs.docs = bf16[32,128,256]{2,1,0:T(8,128)(2,1)} async-done(((bf16[2,128,256]{2,1,0:T(8,128)(2,1)}), bf16[32,128,256]{2,1,0:T(8,128)(2,1)}) %all-gather.3.cloned.1.call-update) | async-done | bytes 2097168 | tf_op jit(solution)/shard_map/all_gather | solution.py:297
  111.3 3.3 %shard_map.96 = f32[4,8,512]{2,1,0:T(8,128)S(1)} custom-call(s32[128]{0:T(128)S(1)} %shard_map.92.units, bf16[576,128]{1,0:T(8,128)(2,1)S(1)} %get-tuple-element.19.own, bf16[576,128]{1,0:T(8,128)(2,1)S(1)} %collective-permute-done.7.one, bf16[576,128]{1,0:T(8,128)(2,1)S(1)} %collective-permute-done.8.two, ...), custom_call_target="tpu_custom_call" | custom-call | tf_op jit(solution)/shard_map/pallas_call | solution.py:32
  114.5 10.7 %all_to_all.15.all_stats = f32[4,8,512]{2,1,0:T(8,128)S(1)} all-to-all(f32[4,8,512]{2,1,0:T(8,128)S(1)} %shard_map.96), channel_id=1, replica_groups=mesh['x'=4,'zh'=4,'zl'=4,'y'=4,'core'=2] {'x'}, dimensions={0} | all-to-all | bytes 131072 | tf_op jit(solution)/shard_map/all_to_all | solution.py:291
  125.3 3.3 %shard_map.97 = f32[4,128,512]{2,1,0:T(8,128)S(1)} custom-call(s32[128]{0:T(128)S(1)} %shard_map.92.units, bf16[576,128]{1,0:T(8,128)(2,1)S(1)} %get-tuple-element.19.own, bf16[576,128]{1,0:T(8,128)(2,1)S(1)} %collective-permute-done.7.one, bf16[576,128]{1,0:T(8,128)(2,1)S(1)} %collective-permute-done.8.two, ...), custom_call_target="tpu_custom_call" | custom-call | tf_op jit(solution)/shard_map/pallas_call | solution.py:32
  128.6 18.0 %all_to_all.16.got = f32[4,128,512]{2,1,0:T(8,128)S(1)} all-to-all(f32[4,128,512]{2,1,0:T(8,128)S(1)} %shard_map.97), channel_id=1, replica_groups=mesh['x'=4,'zh'=4,'zl'=4,'y'=4,'core'=2] {'x'}, dimensions={0} | all-to-all | bytes 2097152 | tf_op jit(solution)/shard_map/all_to_all | solution.py:291
  (25 shorter events, 8.4 us)
Async XLA Ops:
  6.5 66.1 %copy-start.2 = (s32[64,16]{0,1:T(8,128)S(1)}, s32[64,16]{0,1:T(8,128)}, u32[]{:S(2)}) copy-start(s32[64,16]{0,1:T(8,128)} %param.15) | copy-start | bytes 12292
  8.3 44.3 %all-to-all-start = ((bf16[16,96,128]{2,1,0:T(8,128)(2,1)}), bf16[16,96,128]{2,1,0:T(8,128)(2,1)S(1)}, u32[]{:S(2)}, u32[]{:S(2)}) async-start(bf16[16,96,128]{2,1,0:T(8,128)(2,1)} %bitcast.14), calls=%async_computation | async-start | bytes 786432 | tf_op jit(solution)/shard_map/all_to_all | solution.py:291
  26.0 84.7 %all-gather.3.cloned.1.call-start = ((), (), s32[]{:S(2)}) async-start(), calls=%async_computation.3 | async-start | bytes 2228224 | tf_op jit(solution)/shard_map/all_gather | solution.py:297
  42.0 27.1 %collective-permute-start = (bf16[4,144,512]{2,1,0:T(8,128)(2,1)S(1)}, bf16[4,144,512]{2,1,0:T(8,128)(2,1)S(1)}, u32[]{:S(2)}, u32[]{:S(2)}) collective-permute-start(bf16[4,144,512]{2,1,0:T(8,128)(2,1)S(1)} %bitcast.10), channel_id=1, source_target_pairs={{128,0},{256,128},{384,256},{0,384},{129,1},{257,129},{385,257},{1... | collective-permute-start | bytes 1769480 | tf_op jit(solution)/shard_map/ppermute | solution.py:323
  47.1 25.6 %collective-permute-start.1 = (bf16[4,144,512]{2,1,0:T(8,128)(2,1)S(1)}, bf16[4,144,512]{2,1,0:T(8,128)(2,1)S(1)}, u32[]{:S(2)}, u32[]{:S(2)}) collective-permute-start(bf16[4,144,512]{2,1,0:T(8,128)(2,1)S(1)} %bitcast.11), channel_id=1, source_target_pairs={{256,0},{384,128},{0,256},{128,384},{257,1},{385,129},{1,257},{129... | collective-permute-start | bytes 1769480 | tf_op jit(solution)/shard_map/ppermute | solution.py:323
  49.9 24.6 %collective-permute-start.2 = (bf16[4,144,512]{2,1,0:T(8,128)(2,1)S(1)}, bf16[4,144,512]{2,1,0:T(8,128)(2,1)}, u32[]{:S(2)}, u32[]{:S(2)}) collective-permute-start(bf16[4,144,512]{2,1,0:T(8,128)(2,1)S(1)} %bitcast.12), channel_id=1, source_target_pairs={{384,0},{0,128},{128,256},{256,384},{385,1},{1,129},{129,257},{257... | collective-permute-start | bytes 1769480 | tf_op jit(solution)/shard_map/ppermute | solution.py:323
  52.6 28.1 %collective-permute-start.3 = (bf16[16,96,128]{2,1,0:T(8,128)(2,1)S(1)}, bf16[16,96,128]{2,1,0:T(8,128)(2,1)S(1)}, u32[]{:S(2)}, u32[]{:S(2)}) collective-permute-start(bf16[16,96,128]{2,1,0:T(8,128)(2,1)S(1)} %all-to-all-done.near), channel_id=1, source_target_pairs={{8,0},{16,8},{24,16},{32,24},{40,32},{48,40},{56,48},{64,56},{72,6... | collective-permute-start | bytes 1179656 | tf_op jit(solution)/shard_map/ppermute | solution.py:320
  58.6 23.7 %collective-permute-start.4 = (bf16[16,96,128]{2,1,0:T(8,128)(2,1)S(1)}, bf16[16,96,128]{2,1,0:T(8,128)(2,1)S(1)}, u32[]{:S(2)}, u32[]{:S(2)}) collective-permute-start(bf16[16,96,128]{2,1,0:T(8,128)(2,1)S(1)} %all-to-all-done.near), channel_id=1, source_target_pairs={{16,0},{120,8},{32,16},{8,24},{48,32},{24,40},{64,48},{40,56},{80,... | collective-permute-start | bytes 1179656 | tf_op jit(solution)/shard_map/ppermute | solution.py:330
  69.1 17.3 %collective-permute-start.5 = (bf16[16,96,128]{2,1,0:T(8,128)(2,1)S(1)}, bf16[16,96,128]{2,1,0:T(8,128)(2,1)S(1)}, u32[]{:S(2)}, u32[]{:S(2)}) collective-permute-start(bf16[16,96,128]{2,1,0:T(8,128)(2,1)S(1)} %all-to-all-done.near), channel_id=1, source_target_pairs={{120,0},{0,8},{8,16},{16,24},{24,32},{32,40},{40,48},{48,56},{56,6... | collective-permute-start | bytes 1179656 | tf_op jit(solution)/shard_map/ppermute | solution.py:320
  72.7 3.2 %copy-start.1 = (s32[128]{0:T(128)S(1)}, s32[128]{0:T(128)}, u32[]{:S(2)}) copy-start(s32[128]{0:T(128)} %place.1) | copy-start | bytes 1540
  72.8 15.5 %copy-start.3 = (bf16[4096]{0:T(1024)(128)(2,1)S(1)}, bf16[4096]{0:T(1024)(128)(2,1)}, u32[]{:S(2)}) copy-start(bf16[4096]{0:T(1024)(128)(2,1)} %param.10) | copy-start | bytes 24580
  86.3 6.4 %collective-permute-start.6 = (bf16[4,4,144,512]{3,2,1,0:T(8,128)(2,1)S(1)}, bf16[4,4,144,512]{3,2,1,0:T(8,128)(2,1)S(1)}, u32[]{:S(2)}, u32[]{:S(2)}) collective-permute-start(bf16[4,4,144,512]{3,2,1,0:T(8,128)(2,1)S(1)} %bitcast.7), channel_id=1, source_target_pairs={{0,1},{1,0},{2,3},{3,2},{4,5},{5,4},{6,7},{7,6},{8,9},{9,8},{10,11... | collective-permute-start | bytes 7077896 | tf_op jit(solution)/shard_map/ppermute | solution.py:341
  96.6 14.0 %collective-permute-start.7 = (bf16[576,128]{1,0:T(8,128)(2,1)S(1)}, bf16[576,128]{1,0:T(8,128)(2,1)S(1)}, u32[]{:S(2)}, u32[]{:S(2)}) collective-permute-start(bf16[576,128]{1,0:T(8,128)(2,1)S(1)} %get-tuple-element.20), channel_id=1, source_target_pairs={{0,128},{128,256},{256,384},{384,0},{1,129},{129,257},{257,385},{3... | collective-permute-start | bytes 442376 | tf_op jit(solution)/shard_map/ppermute | solution.py:362
  98.5 12.1 %collective-permute-start.8 = (bf16[576,128]{1,0:T(8,128)(2,1)S(1)}, bf16[576,128]{1,0:T(8,128)(2,1)S(1)}, u32[]{:S(2)}, u32[]{:S(2)}) collective-permute-start(bf16[576,128]{1,0:T(8,128)(2,1)S(1)} %get-tuple-element.21), channel_id=1, source_target_pairs={{0,256},{128,384},{256,0},{384,128},{1,257},{129,385},{257,1},{385... | collective-permute-start | bytes 442376 | tf_op jit(solution)/shard_map/ppermute | solution.py:362
  102.5 8.7 %collective-permute-start.9 = (bf16[576,128]{1,0:T(8,128)(2,1)S(1)}, bf16[576,128]{1,0:T(8,128)(2,1)S(1)}, u32[]{:S(2)}, u32[]{:S(2)}) collective-permute-start(bf16[576,128]{1,0:T(8,128)(2,1)S(1)} %get-tuple-element.22), channel_id=1, source_target_pairs={{0,384},{128,0},{256,128},{384,256},{1,385},{129,1},{257,129},{385... | collective-permute-start | bytes 442376 | tf_op jit(solution)/shard_map/ppermute | solution.py:362
  110.6 14.6 %copy-start = (bf16[32,128,256]{2,1,0:T(8,128)(2,1)S(1)}, bf16[32,128,256]{2,1,0:T(8,128)(2,1)}, u32[]{:S(2)}) copy-start(bf16[32,128,256]{2,1,0:T(8,128)(2,1)} %all-gather.3.cloned.1.call-done.far_docs.docs) | copy-start | bytes 6291460
Sparse Core Ops, SparseCore 0:
  28.9 81.6 all-gather.2

commit v13 on v12

--- a/solution.py
+++ b/solution.py
@@ -327,7 +327,7 @@
     mine = mine.reshape(NX, 4, SEQ + 16, 512)
     ahead = from_z(near, 1)
     behind = from_z(near, -1)
-    far = lax.ppermute(near, z_axes, [((i + 2 - 4 * (i % 2)) % NZ, i) for i in range(NZ)])
+    far = from_z(ahead, 1)
     use = mine[:, 0, SEQ : SEQ + 2, 0:PICKS].astype(jnp.int32).reshape(8, PICKS)
     units = call(
         route_kernel,

time: 155 us -> 156 us (level); the launches traced: 154 us -> 154 us
  waiting for transfers between devices: 25.3 us -> 30.5 us
  starting transfers between devices: 52.1 us -> 48.9 us
  Pallas kernels: 19.3 us -> 17.4 us
    ppermute x2 -> x3, waiting for transfers between devices: 4.11 us -> 18.7 us  [from_z(): lax.ppermute(array, z_axes, [((i + step) % NZ, i) for i in range(NZ)])]
    ppermute x3, waiting for transfers between devices: 8.83 us -> 0.99 us  [from_x(): return lax.ppermute(array, 'x', [((i + step) % NX, i) for i in range(NX)])]
    all_gather x1, waiting for transfers between devices: 5.01 us -> 0.02 us  [shards(): docs = lax.all_gather(doc_cache, z_axes, axis=0, tiled=True)]
    ppermute x3, waiting for transfers between devices: 0.64 us -> 5.61 us  [shards(): lax.ppermute(sends[k], 'x', [(i, (i + k) % NX) for i in range(NX)])]
    ppermute x1 -> x0, starting transfers between devices: 3.44 us -> none  [shards(): lax.ppermute(near, z_axes, [((i + 2 - 4 * (i % 2)) % NZ, i) for i in rang...]
    pallas_call x8, Pallas kernels: 19.3 us -> 17.4 us  [call(): pl.pallas_call(kernel, out_shape=outs, in_specs=specs, out_specs=VMEM if...]
    ppermute x2 -> x3, starting transfers between devices: 9.51 us -> 9.78 us  [from_z(): lax.ppermute(array, z_axes, [((i + step) % NZ, i) for i in range(NZ)])]
  transfers between devices with their start and end apart: 12 -> 12, of which waited for: 7 -> 6; matrix products, arithmetic and copies ran while one was open for 1% -> 1% of each run, Pallas kernels for 7% -> 7%
where the time goes in v13:
time: 156 us; the launch traced here: 154 us
  starting transfers between devices  48.9 us (31%)
  blocking collectives  41.6 us (27%)
  waiting for transfers between devices  30.5 us (20%)
  Pallas kernels  17.4 us (11%)
  between operations  13.6 us (9%)
    all_to_all x2, blocking collectives, exchange(): return lax.all_to_all(array, axes, 0, 0, tiled=True)  27.9 us
    ppermute x3, waiting for transfers between devices, from_z(): lax.ppermute(array, z_axes, [((i + step) % NZ, i) for i in range(NZ)])  18.7 us
    all_to_all x1, starting transfers between devices, exchange(): return lax.all_to_all(array, axes, 0, 0, tiled=True)  17.7 us
    pallas_call x8, Pallas kernels, call(): pl.pallas_call(kernel, out_shape=outs, in_specs=specs, out_specs=VMEM if...  17.4 us
    all_gather x1, blocking collectives, shards(): by_y = lax.all_gather(tagged, 'y')  13.7 us
    ppermute x3, starting transfers between devices, from_x(): return lax.ppermute(array, 'x', [((i + step) % NX, i) for i in range(NX)])  10.6 us
    ppermute x3, starting transfers between devices, from_z(): lax.ppermute(array, z_axes, [((i + step) % NZ, i) for i in range(NZ)])  9.78 us
    ppermute x3, starting transfers between devices, shards(): lax.ppermute(sends[k], 'x', [(i, (i + k) % NX) for i in range(NX)])  8.97 us
  transfers between devices with their start and end apart: 12, of which 6 were waited for; matrix products, arithmetic and copies ran while one was open for 1% of the time, Pallas kernels for 7%

profile of v13, /device:TPU:24, one launch (start us, length us, event | category | flops | bytes accessed | tf_op | source)
XLA Modules:
  0.0 153.5 jit_solution(1968321428317494605)
XLA Ops:
  8.3 17.7 %all-to-all-start = ((bf16[16,96,128]{2,1,0:T(8,128)(2,1)}), bf16[16,96,128]{2,1,0:T(8,128)(2,1)S(1)}, u32[]{:S(2)}, u32[]{:S(2)}) async-start(bf16[16,96,128]{2,1,0:T(8,128)(2,1)} %bitcast.14), calls=%async_computation | async-start | bytes 786432 | tf_op jit(solution)/shard_map/all_to_all | solution.py:291
  28.3 13.7 %all-gather = bf16[576,512]{1,0:T(8,128)(2,1)S(1)} all-gather(bf16[144,512]{1,0:T(8,128)(2,1)} %shard_map.91), channel_id=2, replica_groups=mesh['x'=4,'zh'=4,'zl'=4,'y'=4,'core'=2] {'y'}, dimensions={0}, use_global_device_ids=true | all-gather | bytes 737280 | tf_op jit(solution)/shard_map/all_gather | solution.py:325
  42.0 5.1 %collective-permute-start = (bf16[4,144,512]{2,1,0:T(8,128)(2,1)S(1)}, bf16[4,144,512]{2,1,0:T(8,128)(2,1)S(1)}, u32[]{:S(2)}, u32[]{:S(2)}) collective-permute-start(bf16[4,144,512]{2,1,0:T(8,128)(2,1)S(1)} %bitcast.10), channel_id=1, source_target_pairs={{128,0},{256,128},{384,256},{0,384},{129,1},{257,129},{385,257},{1... | collective-permute-start | bytes 1769480 | tf_op jit(solution)/shard_map/ppermute | solution.py:323
  47.1 2.8 %collective-permute-start.1 = (bf16[4,144,512]{2,1,0:T(8,128)(2,1)S(1)}, bf16[4,144,512]{2,1,0:T(8,128)(2,1)S(1)}, u32[]{:S(2)}, u32[]{:S(2)}) collective-permute-start(bf16[4,144,512]{2,1,0:T(8,128)(2,1)S(1)} %bitcast.11), channel_id=1, source_target_pairs={{256,0},{384,128},{0,256},{128,384},{257,1},{385,129},{1,257},{129... | collective-permute-start | bytes 1769480 | tf_op jit(solution)/shard_map/ppermute | solution.py:323
  49.9 2.7 %collective-permute-start.2 = (bf16[4,144,512]{2,1,0:T(8,128)(2,1)S(1)}, bf16[4,144,512]{2,1,0:T(8,128)(2,1)}, u32[]{:S(2)}, u32[]{:S(2)}) collective-permute-start(bf16[4,144,512]{2,1,0:T(8,128)(2,1)S(1)} %bitcast.12), channel_id=1, source_target_pairs={{384,0},{0,128},{128,256},{256,384},{385,1},{1,129},{129,257},{257... | collective-permute-start | bytes 1769480 | tf_op jit(solution)/shard_map/ppermute | solution.py:323
  52.6 6.0 %collective-permute-start.3 = (bf16[16,96,128]{2,1,0:T(8,128)(2,1)S(1)}, bf16[16,96,128]{2,1,0:T(8,128)(2,1)S(1)}, u32[]{:S(2)}, u32[]{:S(2)}) collective-permute-start(bf16[16,96,128]{2,1,0:T(8,128)(2,1)S(1)} %all-to-all-done.near), channel_id=1, source_target_pairs={{8,0},{16,8},{24,16},{32,24},{40,32},{48,40},{56,48},{64,56},{72,6... | collective-permute-start | bytes 1179656 | tf_op jit(solution)/shard_map/ppermute | solution.py:320
  58.6 1.9 %collective-permute-start.5 = (bf16[16,96,128]{2,1,0:T(8,128)(2,1)S(1)}, bf16[16,96,128]{2,1,0:T(8,128)(2,1)S(1)}, u32[]{:S(2)}, u32[]{:S(2)}) collective-permute-start(bf16[16,96,128]{2,1,0:T(8,128)(2,1)S(1)} %all-to-all-done.near), channel_id=1, source_target_pairs={{120,0},{0,8},{8,16},{16,24},{24,32},{32,40},{40,48},{48,56},{56,6... | collective-permute-start | bytes 1179656 | tf_op jit(solution)/shard_map/ppermute | solution.py:320
  60.5 11.0 %collective-permute-done.3.ahead = bf16[16,96,128]{2,1,0:T(8,128)(2,1)S(1)} collective-permute-done((bf16[16,96,128]{2,1,0:T(8,128)(2,1)S(1)}, bf16[16,96,128]{2,1,0:T(8,128)(2,1)S(1)}, u32[]{:S(2)}, u32[]{:S(2)}) %collective-permute-start.3) | collective-permute-done | bytes 393248 | tf_op jit(solution)/shard_map/ppermute | solution.py:320
  71.5 1.9 %collective-permute-start.4 = (bf16[16,96,128]{2,1,0:T(8,128)(2,1)S(1)}, bf16[16,96,128]{2,1,0:T(8,128)(2,1)S(1)}, u32[]{:S(2)}, u32[]{:S(2)}) collective-permute-start(bf16[16,96,128]{2,1,0:T(8,128)(2,1)S(1)} %collective-permute-done.3.ahead), channel_id=1, source_target_pairs={{8,0},{16,8},{24,16},{32,24},{40,32},{48,40},{56,48},{64,56},{72,6... | collective-permute-start | bytes 1179656 | tf_op jit(solution)/shard_map/ppermute | solution.py:320
  75.9 4.8 %shard_map.92.units = s32[128]{0:T(128)S(1)} custom-call(s32[64,16]{1,0:T(8,128)S(1)} %copy.11.lists, s32[128]{0:T(128)S(1)} %copy-done.1, s32[8,16]{1,0:T(8,128)S(1)} %convert.2.use), custom_call_target="tpu_custom_call" | custom-call | tf_op jit(solution)/shard_map/pallas_call | solution.py:32
  80.7 7.7 %collective-permute-done.4.far = bf16[16,96,128]{2,1,0:T(8,128)(2,1)S(1)} collective-permute-done((bf16[16,96,128]{2,1,0:T(8,128)(2,1)S(1)}, bf16[16,96,128]{2,1,0:T(8,128)(2,1)S(1)}, u32[]{:S(2)}, u32[]{:S(2)}) %collective-permute-start.4) | collective-permute-done | bytes 393248 | tf_op jit(solution)/shard_map/ppermute | solution.py:320
  88.4 1.9 %collective-permute-start.6 = (bf16[4,4,144,512]{3,2,1,0:T(8,128)(2,1)S(1)}, bf16[4,4,144,512]{3,2,1,0:T(8,128)(2,1)S(1)}, u32[]{:S(2)}, u32[]{:S(2)}) collective-permute-start(bf16[4,4,144,512]{3,2,1,0:T(8,128)(2,1)S(1)} %bitcast.7), channel_id=1, source_target_pairs={{0,1},{1,0},{2,3},{3,2},{4,5},{5,4},{6,7},{7,6},{8,9},{9,8},{10,11... | collective-permute-start | bytes 7077896 | tf_op jit(solution)/shard_map/ppermute | solution.py:341
  90.3 4.5 %collective-permute-done.6.other = bf16[4,4,144,512]{3,2,1,0:T(8,128)(2,1)S(1)} collective-permute-done((bf16[4,4,144,512]{3,2,1,0:T(8,128)(2,1)S(1)}, bf16[4,4,144,512]{3,2,1,0:T(8,128)(2,1)S(1)}, u32[]{:S(2)}, u32[]{:S(2)}) %collective-permute-start.6) | collective-permute-done | bytes 2359328 | tf_op jit(solution)/shard_map/ppermute | solution.py:341
  94.8 2.1 %shard_map.94.normed = bf16[8,512,512]{2,1,0:T(8,128)(2,1)S(1)} custom-call(bf16[4,4,144,512]{3,2,1,0:T(8,128)(2,1)S(1)} %bitcast.8, bf16[4,4,144,512]{3,2,1,0:T(8,128)(2,1)S(1)} %collective-permute-done.6.other, f32[8,1,512]{2,1,0:T(1,128)S(1)} %bitcast.9), custom_call_target="tpu_custom_call" | custom-call | flops 16777216 | bytes 8388608 | tf_op jit(solution)/shard_map/pallas_call | solution.py:32
  96.9 1.7 %shard_map.95 = (bf16[576,128]{1,0:T(8,128)(2,1)S(1)}, bf16[576,128]{1,0:T(8,128)(2,1)S(1)}, bf16[576,128]{1,0:T(8,128)(2,1)S(1)}, bf16[576,128]{1,0:T(8,128)(2,1)S(1)}) custom-call(bf16[8,512,512]{2,1,0:T(8,128)(2,1)S(1)} %shard_map.94.normed, bf16[16,96,128]{2,1,0:T(8,128)(2,1)S(1)} %all-to-all-done.near, ...), custom_call_target="tpu_custom_call" | custom-call | flops 1073741824 | bytes 8388608 | tf_op jit(solution)/shard_map/pallas_call | solution.py:32
  98.7 1.9 %collective-permute-start.7 = (bf16[576,128]{1,0:T(8,128)(2,1)S(1)}, bf16[576,128]{1,0:T(8,128)(2,1)S(1)}, u32[]{:S(2)}, u32[]{:S(2)}) collective-permute-start(bf16[576,128]{1,0:T(8,128)(2,1)S(1)} %get-tuple-element.20), channel_id=1, source_target_pairs={{0,128},{128,256},{256,384},{384,0},{1,129},{129,257},{257,385},{3... | collective-permute-start | bytes 442376 | tf_op jit(solution)/shard_map/ppermute | solution.py:362
  100.6 4.1 %collective-permute-start.8 = (bf16[576,128]{1,0:T(8,128)(2,1)S(1)}, bf16[576,128]{1,0:T(8,128)(2,1)S(1)}, u32[]{:S(2)}, u32[]{:S(2)}) collective-permute-start(bf16[576,128]{1,0:T(8,128)(2,1)S(1)} %get-tuple-element.21), channel_id=1, source_target_pairs={{0,256},{128,384},{256,0},{384,128},{1,257},{129,385},{257,1},{385... | collective-permute-start | bytes 442376 | tf_op jit(solution)/shard_map/ppermute | solution.py:362
  104.7 3.0 %collective-permute-start.9 = (bf16[576,128]{1,0:T(8,128)(2,1)S(1)}, bf16[576,128]{1,0:T(8,128)(2,1)S(1)}, u32[]{:S(2)}, u32[]{:S(2)}) collective-permute-start(bf16[576,128]{1,0:T(8,128)(2,1)S(1)} %get-tuple-element.22), channel_id=1, source_target_pairs={{0,384},{128,0},{256,128},{384,256},{1,385},{129,1},{257,129},{385... | collective-permute-start | bytes 442376 | tf_op jit(solution)/shard_map/ppermute | solution.py:362
  107.7 3.1 %collective-permute-done.7.one = bf16[576,128]{1,0:T(8,128)(2,1)S(1)} collective-permute-done((bf16[576,128]{1,0:T(8,128)(2,1)S(1)}, bf16[576,128]{1,0:T(8,128)(2,1)S(1)}, u32[]{:S(2)}, u32[]{:S(2)}) %collective-permute-start.7) | collective-permute-done | bytes 147488 | tf_op jit(solution)/shard_map/ppermute | solution.py:362
  110.8 2.5 %collective-permute-done.9.three = bf16[576,128]{1,0:T(8,128)(2,1)S(1)} collective-permute-done((bf16[576,128]{1,0:T(8,128)(2,1)S(1)}, bf16[576,128]{1,0:T(8,128)(2,1)S(1)}, u32[]{:S(2)}, u32[]{:S(2)}) %collective-permute-start.9) | collective-permute-done | bytes 147488 | tf_op jit(solution)/shard_map/ppermute | solution.py:362
  113.3 2.6 %shard_map.96 = f32[4,8,512]{2,1,0:T(8,128)S(1)} custom-call(s32[128]{0:T(128)S(1)} %shard_map.92.units, bf16[576,128]{1,0:T(8,128)(2,1)S(1)} %get-tuple-element.19.own, bf16[576,128]{1,0:T(8,128)(2,1)S(1)} %collective-permute-done.7.one, bf16[576,128]{1,0:T(8,128)(2,1)S(1)} %collective-permute-done.8.two, ...), custom_call_target="tpu_custom_call" | custom-call | tf_op jit(solution)/shard_map/pallas_call | solution.py:32
  115.9 10.1 %all_to_all.15.all_stats = f32[4,8,512]{2,1,0:T(8,128)S(1)} all-to-all(f32[4,8,512]{2,1,0:T(8,128)S(1)} %shard_map.96), channel_id=1, replica_groups=mesh['x'=4,'zh'=4,'zl'=4,'y'=4,'core'=2] {'x'}, dimensions={0} | all-to-all | bytes 131072 | tf_op jit(solution)/shard_map/all_to_all | solution.py:291
  126.0 2.2 %shard_map.97 = f32[4,128,512]{2,1,0:T(8,128)S(1)} custom-call(s32[128]{0:T(128)S(1)} %shard_map.92.units, bf16[576,128]{1,0:T(8,128)(2,1)S(1)} %get-tuple-element.19.own, bf16[576,128]{1,0:T(8,128)(2,1)S(1)} %collective-permute-done.7.one, bf16[576,128]{1,0:T(8,128)(2,1)S(1)} %collective-permute-done.8.two, ...), custom_call_target="tpu_custom_call" | custom-call | tf_op jit(solution)/shard_map/pallas_call | solution.py:32
  128.2 17.8 %all_to_all.16.got = f32[4,128,512]{2,1,0:T(8,128)S(1)} all-to-all(f32[4,128,512]{2,1,0:T(8,128)S(1)} %shard_map.97), channel_id=1, replica_groups=mesh['x'=4,'zh'=4,'zl'=4,'y'=4,'core'=2] {'x'}, dimensions={0} | all-to-all | bytes 2097152 | tf_op jit(solution)/shard_map/all_to_all | solution.py:291
  (25 shorter events, 7.3 us)
Async XLA Ops:
  6.5 66.9 %copy-start.2 = (s32[64,16]{0,1:T(8,128)S(1)}, s32[64,16]{0,1:T(8,128)}, u32[]{:S(2)}) copy-start(s32[64,16]{0,1:T(8,128)} %param.15) | copy-start | bytes 12292
  8.3 44.3 %all-to-all-start = ((bf16[16,96,128]{2,1,0:T(8,128)(2,1)}), bf16[16,96,128]{2,1,0:T(8,128)(2,1)S(1)}, u32[]{:S(2)}, u32[]{:S(2)}) async-start(bf16[16,96,128]{2,1,0:T(8,128)(2,1)} %bitcast.14), calls=%async_computation | async-start | bytes 786432 | tf_op jit(solution)/shard_map/all_to_all | solution.py:291
  26.0 81.7 %all-gather.3.cloned.1.call-start = ((), (), s32[]{:S(2)}) async-start(), calls=%async_computation.3 | async-start | bytes 2228224 | tf_op jit(solution)/shard_map/all_gather | solution.py:297
  42.0 31.5 %collective-permute-start = (bf16[4,144,512]{2,1,0:T(8,128)(2,1)S(1)}, bf16[4,144,512]{2,1,0:T(8,128)(2,1)S(1)}, u32[]{:S(2)}, u32[]{:S(2)}) collective-permute-start(bf16[4,144,512]{2,1,0:T(8,128)(2,1)S(1)} %bitcast.10), channel_id=1, source_target_pairs={{128,0},{256,128},{384,256},{0,384},{129,1},{257,129},{385,257},{1... | collective-permute-start | bytes 1769480 | tf_op jit(solution)/shard_map/ppermute | solution.py:323
  47.1 26.4 %collective-permute-start.1 = (bf16[4,144,512]{2,1,0:T(8,128)(2,1)S(1)}, bf16[4,144,512]{2,1,0:T(8,128)(2,1)S(1)}, u32[]{:S(2)}, u32[]{:S(2)}) collective-permute-start(bf16[4,144,512]{2,1,0:T(8,128)(2,1)S(1)} %bitcast.11), channel_id=1, source_target_pairs={{256,0},{384,128},{0,256},{128,384},{257,1},{385,129},{1,257},{129... | collective-permute-start | bytes 1769480 | tf_op jit(solution)/shard_map/ppermute | solution.py:323
  49.9 24.6 %collective-permute-start.2 = (bf16[4,144,512]{2,1,0:T(8,128)(2,1)S(1)}, bf16[4,144,512]{2,1,0:T(8,128)(2,1)}, u32[]{:S(2)}, u32[]{:S(2)}) collective-permute-start(bf16[4,144,512]{2,1,0:T(8,128)(2,1)S(1)} %bitcast.12), channel_id=1, source_target_pairs={{384,0},{0,128},{128,256},{256,384},{385,1},{1,129},{129,257},{257... | collective-permute-start | bytes 1769480 | tf_op jit(solution)/shard_map/ppermute | solution.py:323
  52.6 18.9 %collective-permute-start.3 = (bf16[16,96,128]{2,1,0:T(8,128)(2,1)S(1)}, bf16[16,96,128]{2,1,0:T(8,128)(2,1)S(1)}, u32[]{:S(2)}, u32[]{:S(2)}) collective-permute-start(bf16[16,96,128]{2,1,0:T(8,128)(2,1)S(1)} %all-to-all-done.near), channel_id=1, source_target_pairs={{8,0},{16,8},{24,16},{32,24},{40,32},{48,40},{56,48},{64,56},{72,6... | collective-permute-start | bytes 1179656 | tf_op jit(solution)/shard_map/ppermute | solution.py:320
  58.6 22.2 %collective-permute-start.5 = (bf16[16,96,128]{2,1,0:T(8,128)(2,1)S(1)}, bf16[16,96,128]{2,1,0:T(8,128)(2,1)S(1)}, u32[]{:S(2)}, u32[]{:S(2)}) collective-permute-start(bf16[16,96,128]{2,1,0:T(8,128)(2,1)S(1)} %all-to-all-done.near), channel_id=1, source_target_pairs={{120,0},{0,8},{8,16},{16,24},{24,32},{32,40},{40,48},{48,56},{56,6... | collective-permute-start | bytes 1179656 | tf_op jit(solution)/shard_map/ppermute | solution.py:320
  71.5 16.9 %collective-permute-start.4 = (bf16[16,96,128]{2,1,0:T(8,128)(2,1)S(1)}, bf16[16,96,128]{2,1,0:T(8,128)(2,1)S(1)}, u32[]{:S(2)}, u32[]{:S(2)}) collective-permute-start(bf16[16,96,128]{2,1,0:T(8,128)(2,1)S(1)} %collective-permute-done.3.ahead), channel_id=1, source_target_pairs={{8,0},{16,8},{24,16},{32,24},{40,32},{48,40},{56,48},{64,56},{72,6... | collective-permute-start | bytes 1179656 | tf_op jit(solution)/shard_map/ppermute | solution.py:320
  73.5 2.4 %copy-start.1 = (s32[128]{0:T(128)S(1)}, s32[128]{0:T(128)}, u32[]{:S(2)}) copy-start(s32[128]{0:T(128)} %place.1) | copy-start | bytes 1540
  73.5 16.8 %copy-start.3 = (bf16[4096]{0:T(1024)(128)(2,1)S(1)}, bf16[4096]{0:T(1024)(128)(2,1)}, u32[]{:S(2)}) copy-start(bf16[4096]{0:T(1024)(128)(2,1)} %param.10) | copy-start | bytes 24580
  88.4 6.4 %collective-permute-start.6 = (bf16[4,4,144,512]{3,2,1,0:T(8,128)(2,1)S(1)}, bf16[4,4,144,512]{3,2,1,0:T(8,128)(2,1)S(1)}, u32[]{:S(2)}, u32[]{:S(2)}) collective-permute-start(bf16[4,4,144,512]{3,2,1,0:T(8,128)(2,1)S(1)} %bitcast.7), channel_id=1, source_target_pairs={{0,1},{1,0},{2,3},{3,2},{4,5},{5,4},{6,7},{7,6},{8,9},{9,8},{10,11... | collective-permute-start | bytes 7077896 | tf_op jit(solution)/shard_map/ppermute | solution.py:341
  98.7 12.2 %collective-permute-start.7 = (bf16[576,128]{1,0:T(8,128)(2,1)S(1)}, bf16[576,128]{1,0:T(8,128)(2,1)S(1)}, u32[]{:S(2)}, u32[]{:S(2)}) collective-permute-start(bf16[576,128]{1,0:T(8,128)(2,1)S(1)} %get-tuple-element.20), channel_id=1, source_target_pairs={{0,128},{128,256},{256,384},{384,0},{1,129},{129,257},{257,385},{3... | collective-permute-start | bytes 442376 | tf_op jit(solution)/shard_map/ppermute | solution.py:362
  100.6 10.2 %collective-permute-start.8 = (bf16[576,128]{1,0:T(8,128)(2,1)S(1)}, bf16[576,128]{1,0:T(8,128)(2,1)S(1)}, u32[]{:S(2)}, u32[]{:S(2)}) collective-permute-start(bf16[576,128]{1,0:T(8,128)(2,1)S(1)} %get-tuple-element.21), channel_id=1, source_target_pairs={{0,256},{128,384},{256,0},{384,128},{1,257},{129,385},{257,1},{385... | collective-permute-start | bytes 442376 | tf_op jit(solution)/shard_map/ppermute | solution.py:362
  104.7 8.6 %collective-permute-start.9 = (bf16[576,128]{1,0:T(8,128)(2,1)S(1)}, bf16[576,128]{1,0:T(8,128)(2,1)S(1)}, u32[]{:S(2)}, u32[]{:S(2)}) collective-permute-start(bf16[576,128]{1,0:T(8,128)(2,1)S(1)} %get-tuple-element.22), channel_id=1, source_target_pairs={{0,384},{128,0},{256,128},{384,256},{1,385},{129,1},{257,129},{385... | collective-permute-start | bytes 442376 | tf_op jit(solution)/shard_map/ppermute | solution.py:362
  107.7 18.3 %copy-start = (bf16[32,128,256]{2,1,0:T(8,128)(2,1)S(1)}, bf16[32,128,256]{2,1,0:T(8,128)(2,1)}, u32[]{:S(2)}) copy-start(bf16[32,128,256]{2,1,0:T(8,128)(2,1)} %all-gather.3.cloned.1.call-done.far_docs.docs) | copy-start | bytes 6291460
Sparse Core Ops, SparseCore 0:
  28.9 76.8 all-gather.2
